TPU v7x, 32 devices: a whole 2x2x4 slice. The times are simulated.
32 devices in a mesh: wide: 4 (over y, x), narrow: 8 (over z, core).
Axes of the slice: x: 2, y: 2, z: 4, core: 2. Of those that a mesh axis runs over, the one named last changes fastest.
Arguments:
- saved_inputs: bfloat16 [3, 8192, 4096], P(None, 'wide', 'narrow'), may hold values from -6 to 6
- cotangent: bfloat16 [8192, 4096], P('wide', 'narrow'), may hold values from -6 to 6
- w_self: bfloat16 [3, 4096, 512], P(None, 'narrow'), may hold values from -0.1875 to 0.1875
- w_cross: bfloat16 [3, 4096, 512], P(None, 'narrow'), may hold values from -0.1875 to 0.1875
Outputs:
- grad_in: bfloat16 [8192, 4096], P('wide', 'narrow')
- grad_self: float32 [3, 4096, 512], P(None, ('narrow', 'wide'))
- grad_cross: float32 [3, 4096, 512], P(None, ('narrow', 'wide'))
All inputs are finite; a program needn't handle non-finite values.
Results may differ from a plain program's by a relative error of at most 0.0057.
Values may be sent and summed in bfloat16 or wider, within the bound.
No kernel may reach another device: no remote copies, remote signals or barrier semaphores. Data moves between devices by JAX's collectives and lax.ppermute only.
A program may use at most 128 MiB of HBM per device.

v0:
```python
import math

import jax
import jax.numpy as jnp
from jax import lax
from jax.sharding import PartitionSpec as P

LEVELS = 3


def from_partner(array, axis, bit):
    return lax.ppermute(array, axis, [(i, i ^ 1 << bit) for i in range(lax.axis_size(axis))])


def outer_sum(left, right):
    return lax.dot_general(
        left, right, (((0,), (0,)), ((), ())), preferred_element_type=jnp.float32
    )


def times_trans(left, right):
    return lax.dot_general(
        left, right, (((1,), (1,)), ((), ())), preferred_element_type=jnp.float32
    )


def wide_sum(pair):
    return (
        lax.psum_scatter(pair[0], "wide", scatter_dimension=1, tiled=True),
        lax.psum_scatter(pair[1], "wide", scatter_dimension=1, tiled=True),
    )


def return_cross(block, level):
    return from_partner(block, "narrow", level)


def local(saved_inputs, cotangent, w_self, w_cross):
    total_tokens = saved_inputs.shape[1] * lax.axis_size("wide")
    scale = 1.0 / math.sqrt(total_tokens)
    grad = cotangent
    self_terms = [None] * LEVELS
    cross_terms = [None] * LEVELS
    self_done = [None] * LEVELS
    cross_done = [None] * LEVELS
    for level in reversed(range(LEVELS)):
        inputs = saved_inputs[level]
        a_block = w_self[level]
        c_block = w_cross[level]
        own = times_trans(grad, a_block)
        far_grad, far_cross = from_partner((grad, c_block), "narrow", level)
        self_terms[level] = outer_sum(inputs, grad) * scale
        cross_terms[level] = outer_sum(inputs, far_grad) * scale
        far = times_trans(far_grad, far_cross)
        summed_self, summed_cross = wide_sum((self_terms[level][None], cross_terms[level][None]))
        summed_cross = return_cross(summed_cross, level)
        self_done[level] = summed_self
        cross_done[level] = summed_cross
        grad = (own + far).astype(jnp.bfloat16)
    grad_self = jnp.concatenate(self_done, axis=0)
    grad_cross = jnp.concatenate(cross_done, axis=0)
    return (grad, grad_self, grad_cross)


def solution(mesh):
    in_specs = (
        P(None, "wide", "narrow"),
        P("wide", "narrow"),
        P(None, "narrow", None),
        P(None, "narrow", None),
    )
    out_specs = (
        P("wide", "narrow"),
        P(None, ("narrow", "wide"), None),
        P(None, ("narrow", "wide"), None),
    )
    return jax.shard_map(local, mesh=mesh, in_specs=in_specs, out_specs=out_specs, check_vma=False)
```

profile of v0, /device:TPU:0, one launch (start us, length us, event | category | flops | bytes accessed | tf_op | source)
XLA Modules:
  0.0 307.4 jit_solution(17060545118793135118)
XLA Ops:
  7.2 0.0 reduce-scatter.17.cloned.1.call-start
  7.2 4.1 %collective-permute-start = (bf16[2048,512]{1,0:T(8,128)(2,1)}, bf16[2048,512]{1,0:T(8,128)(2,1)S(1)}, u32[]{:S(2)}, u32[]{:S(2)}) collective-permute-start(bf16[2048,512]{1,0:T(8,128)(2,1)} %param.5), channel_id=1, source_target_pairs={{0,4},{1,5},{2,6},{3,7},{4,0},{5,1},{6,2},{7,3},{8,12},{9,13},{10,... | collective-permute-start | bytes 6291464 | tf_op jit(solution)/shard_map/ppermute | solution.py:12
  11.3 90.8 %collective-permute-done = bf16[2048,512]{1,0:T(8,128)(2,1)S(1)} collective-permute-done((bf16[2048,512]{1,0:T(8,128)(2,1)}, bf16[2048,512]{1,0:T(8,128)(2,1)S(1)}, u32[]{:S(2)}, u32[]{:S(2)}) %collective-permute-start) | collective-permute-done | bytes 2097184 | tf_op jit(solution)/shard_map/ppermute | solution.py:12
  102.1 1.3 copy-done.1
  103.4 3.9 %fusion.51 = f32[1,512,512]{1,2,0:T(8,128)} fusion(bf16[2048,512]{1,0:T(8,128)(2,1)S(1)} %collective-permute-done, bf16[3,2048,512]{2,1,0:T(8,128)(2,1)} %param.4), kind=kOutput, calls=%fused_computation.32 | convolution fusion | flops 1074003968 | bytes 5242880 | tf_op jit(solution)/shard_map/dot_general | solution.py:16
  107.3 0.0 reduce-scatter.17.cloned.1.call-update
  107.3 0.0 reduce-scatter.9.cloned.1.call-start
  107.4 1.6 slice_bitcast_fusion
  109.0 0.0 copy-start.2
  109.0 0.1 collective-permute-start.1
  109.1 0.3 copy-done
  109.4 2.6 fusion.58
  111.9 22.4 %collective-permute-done.1 = bf16[512,512]{1,0:T(8,128)(2,1)S(1)} collective-permute-done((bf16[512,512]{1,0:T(8,128)(2,1)S(1)}, bf16[512,512]{1,0:T(8,128)(2,1)S(1)}, u32[]{:S(2)}, u32[]{:S(2)}) %collective-permute-start.1) | collective-permute-done | bytes 524320 | tf_op jit(solution)/shard_map/ppermute | solution.py:12
  134.3 1.3 add_convert_fusion.2
  135.6 3.9 %fusion.33 = f32[1,512,512]{2,1,0:T(8,128)} fusion(bf16[2048,512]{1,0:T(8,128)(2,1)S(1)} %add_convert_fusion.2, bf16[3,2048,512]{2,1,0:T(8,128)(2,1)} %param.4), kind=kOutput, calls=%fused_computation.26 | convolution fusion | flops 1074003968 | bytes 5242880 | tf_op jit(solution)/shard_map/dot_general | solution.py:16
  139.5 0.0 reduce-scatter.9.cloned.1.call-update
  139.5 0.0 reduce-scatter.11.cloned.1.call-start
  139.6 0.1 collective-permute-start.2
  139.7 4.5 %fusion.45 = f32[1,512,512]{1,2,0:T(8,128)} fusion(bf16[2048,512]{1,0:T(8,128)(2,1)} %param.5, bf16[3,2048,512]{2,1,0:T(8,128)(2,1)} %param.4), kind=kOutput, calls=%fused_computation.30 | convolution fusion | flops 1074003968 | bytes 5242880 | tf_op jit(solution)/shard_map/dot_general | solution.py:16
  144.2 0.0 reduce-scatter.11.cloned.1.call-update
  144.2 0.0 reduce-scatter.7.cloned.1.call-start
  144.2 2.1 collective-permute-start.3
  146.3 2.4 fusion.56
  148.7 48.1 %collective-permute-done.3 = bf16[512,512]{1,0:T(8,128)(2,1)S(1)} collective-permute-done((bf16[512,512]{1,0:T(8,128)(2,1)S(1)}, bf16[512,512]{1,0:T(8,128)(2,1)S(1)}, u32[]{:S(2)}, u32[]{:S(2)}) %collective-permute-start.3) | collective-permute-done | bytes 524320 | tf_op jit(solution)/shard_map/ppermute | solution.py:12
  196.8 2.9 add_convert_fusion.1
  199.7 3.9 %fusion.21 = f32[1,512,512]{1,2,0:T(8,128)} fusion(bf16[2048,512]{1,0:T(8,128)(2,1)S(1)} %add_convert_fusion.1, bf16[3,2048,512]{2,1,0:T(8,128)(2,1)} %param.4), kind=kOutput, calls=%fused_computation.22 | convolution fusion | flops 1074003968 | bytes 5242880 | tf_op jit(solution)/shard_map/dot_general | solution.py:16
  203.6 0.0 reduce-scatter.7.cloned.1.call-update
  203.6 0.0 reduce-scatter.15.cloned.1.call-start
  203.7 0.1 collective-permute-start.4
  203.8 4.5 %fusion.39 = f32[1,512,512]{1,2,0:T(8,128)} fusion(bf16[2048,512]{1,0:T(8,128)(2,1)} %collective-permute-done.2, bf16[3,2048,512]{2,1,0:T(8,128)(2,1)} %param.4), kind=kOutput, calls=%fused_computation.28 | convolution fusion | flops 1074003968 | bytes 5242880 | tf_op jit(solution)/shard_map/dot_general | solution.py:16
  208.3 0.0 reduce-scatter.15.cloned.1.call-update
  208.3 0.2 reduce-scatter.13.cloned.1.call-start
  208.5 0.0 collective-permute-done.4
  208.5 4.7 %fusion.27 = f32[1,512,512]{1,2,0:T(8,128)} fusion(bf16[2048,512]{1,0:T(8,128)(2,1)} %collective-permute-done.4, bf16[3,2048,512]{2,1,0:T(8,128)(2,1)} %param.4), kind=kOutput, calls=%fused_computation.24 | convolution fusion | flops 1074003968 | bytes 5242880 | tf_op jit(solution)/shard_map/dot_general | solution.py:16
  213.2 0.0 reduce-scatter.13.cloned.1.call-update
  213.2 0.6 collective-permute-start.5
  213.8 1.5 collective-permute-start.8
  215.3 1.1 copy.10
  216.4 4.3 %fusion.54 = f32[2048,512]{1,0:T(8,128)} fusion(bf16[2048,512]{1,0:T(8,128)(2,1)S(1)} %add_convert_fusion.1, bf16[3,512,512]{2,1,0:T(8,128)(2,1)} %param.6), kind=kOutput, calls=%fused_computation.35 | convolution fusion | flops 1073741824 | bytes 6815744 | tf_op jit(solution)/shard_map/dot_general | solution.py:22
  220.7 11.1 %reduce-scatter.7.cloned.1.call-done = f32[1,128,512]{1,2,0:T(8,128)} async-done(((f32[1,512,512]{1,2,0:T(8,128)}), f32[1,128,512]{1,2,0:T(8,128)}) %reduce-scatter.7.cloned.1.call-update) | async-done | bytes 262160 | tf_op jit(solution)/shard_map/reduce_scatter | solution.py:29
  231.8 1.1 pad_maximum_fusion
  232.8 1.1 copy.14
  234.0 28.2 %reduce-scatter.15.cloned.1.call-done = f32[1,128,512]{1,2,0:T(8,128)} async-done(((f32[1,512,512]{1,2,0:T(8,128)}), f32[1,128,512]{1,2,0:T(8,128)}) %reduce-scatter.15.cloned.1.call-update) | async-done | bytes 262160 | tf_op jit(solution)/shard_map/reduce_scatter | solution.py:30
  262.2 1.5 collective-permute-start.7
  263.7 29.2 %reduce-scatter.13.cloned.1.call-done = f32[1,128,512]{1,2,0:T(8,128)} async-done(((f32[1,512,512]{1,2,0:T(8,128)}), f32[1,128,512]{1,2,0:T(8,128)}) %reduce-scatter.13.cloned.1.call-update) | async-done | bytes 262160 | tf_op jit(solution)/shard_map/reduce_scatter | solution.py:30
  293.0 5.4 %add_convert_fusion = bf16[2048,512]{1,0:T(8,128)(2,1)} fusion(f32[2048,512]{1,0:T(8,128)} %fusion.54, bf16[2048,512]{1,0:T(8,128)(2,1)} %collective-permute-done.4, bf16[512,512]{1,0:T(8,128)(2,1)S(1)} %collective-permute-done.5), kind=kOutput, calls=%fused_computation | convolution fusion | flops 1075838976 | bytes 8912896 | tf_op jit(solution)/shard_map/dot_general | solution.py:22
  298.4 1.0 pad_maximum_fusion.1
  299.4 1.1 copy.15
  (12 shorter events, 0.0 us)
Async XLA Ops:
  7.2 206.7 %reduce-scatter.17.cloned.1.call-start = ((), (), s32[]{:S(2)}) async-start(), calls=%async_computation.11 | async-start | bytes 1310720 | tf_op jit(solution)/shard_map/reduce_scatter | solution.py:30
  7.2 94.9 %collective-permute-start = (bf16[2048,512]{1,0:T(8,128)(2,1)}, bf16[2048,512]{1,0:T(8,128)(2,1)S(1)}, u32[]{:S(2)}, u32[]{:S(2)}) collective-permute-start(bf16[2048,512]{1,0:T(8,128)(2,1)} %param.5), channel_id=1, source_target_pairs={{0,4},{1,5},{2,6},{3,7},{4,0},{5,1},{6,2},{7,3},{8,12},{9,13},{10,... | collective-permute-start | bytes 6291464 | tf_op jit(solution)/shard_map/ppermute | solution.py:12
  102.1 1.3 copy-start.1
  107.3 2.1 copy-start
  107.3 108.0 %reduce-scatter.9.cloned.1.call-start = ((), (), s32[]{:S(2)}) async-start(), calls=%async_computation.7 | async-start | bytes 1310720 | tf_op jit(solution)/shard_map/reduce_scatter | solution.py:29
  109.0 25.3 %copy-start.2 = (bf16[2048,512]{1,0:T(8,128)(2,1)S(1)}, bf16[2048,512]{1,0:T(8,128)(2,1)}, u32[]{:S(2)}) copy-start(bf16[2048,512]{1,0:T(8,128)(2,1)} %copy-done.1) | copy-start | bytes 6291460
  109.0 25.3 %collective-permute-start.1 = (bf16[512,512]{1,0:T(8,128)(2,1)S(1)}, bf16[512,512]{1,0:T(8,128)(2,1)S(1)}, u32[]{:S(2)}, u32[]{:S(2)}) collective-permute-start(bf16[512,512]{1,0:T(8,128)(2,1)S(1)} %get-tuple-element.7), channel_id=1, source_target_pairs={{0,4},{1,5},{2,6},{3,7},{4,0},{5,1},{6,2},{7,3},{8,12},{9,13},{10,... | collective-permute-start | bytes 1572872 | tf_op jit(solution)/shard_map/ppermute | solution.py:12
  139.5 81.1 %reduce-scatter.11.cloned.1.call-start = ((), (), s32[]{:S(2)}) async-start(), calls=%async_computation.8 | async-start | bytes 1310720 | tf_op jit(solution)/shard_map/reduce_scatter | solution.py:29
  139.6 57.2 %collective-permute-start.2 = (bf16[2048,512]{1,0:T(8,128)(2,1)S(1)}, bf16[2048,512]{1,0:T(8,128)(2,1)}, u32[]{:S(2)}, u32[]{:S(2)}) collective-permute-start(bf16[2048,512]{1,0:T(8,128)(2,1)S(1)} %add_convert_fusion.2), channel_id=1, source_target_pairs={{0,2},{1,3},{2,0},{3,1},{4,6},{5,7},{6,4},{7,5},{8,10},{9,11},{10,... | collective-permute-start | bytes 6291464 | tf_op jit(solution)/shard_map/ppermute | solution.py:12
  144.2 87.6 %reduce-scatter.7.cloned.1.call-start = ((), (), s32[]{:S(2)}) async-start(), calls=%async_computation.6 | async-start | bytes 1310720 | tf_op jit(solution)/shard_map/reduce_scatter | solution.py:29
  144.2 52.6 %collective-permute-start.3 = (bf16[512,512]{1,0:T(8,128)(2,1)S(1)}, bf16[512,512]{1,0:T(8,128)(2,1)S(1)}, u32[]{:S(2)}, u32[]{:S(2)}) collective-permute-start(bf16[512,512]{1,0:T(8,128)(2,1)S(1)} %get-tuple-element.8), channel_id=1, source_target_pairs={{0,2},{1,3},{2,0},{3,1},{4,6},{5,7},{6,4},{7,5},{8,10},{9,11},{10,... | collective-permute-start | bytes 1572872 | tf_op jit(solution)/shard_map/ppermute | solution.py:12
  203.6 58.6 %reduce-scatter.15.cloned.1.call-start = ((), (), s32[]{:S(2)}) async-start(), calls=%async_computation.10 | async-start | bytes 1310720 | tf_op jit(solution)/shard_map/reduce_scatter | solution.py:30
  203.7 4.8 %collective-permute-start.4 = (bf16[2048,512]{1,0:T(8,128)(2,1)S(1)}, bf16[2048,512]{1,0:T(8,128)(2,1)}, u32[]{:S(2)}, u32[]{:S(2)}) collective-permute-start(bf16[2048,512]{1,0:T(8,128)(2,1)S(1)} %add_convert_fusion.1), channel_id=1, source_target_pairs={{0,1},{1,0},{2,3},{3,2},{4,5},{5,4},{6,7},{7,6},{8,9},{9,8},{10,11... | collective-permute-start | bytes 6291464 | tf_op jit(solution)/shard_map/ppermute | solution.py:12
  208.3 84.7 %reduce-scatter.13.cloned.1.call-start = ((), (), s32[]{:S(2)}) async-start(), calls=%async_computation.9 | async-start | bytes 1310720 | tf_op jit(solution)/shard_map/reduce_scatter | solution.py:30
  213.2 79.8 %collective-permute-start.5 = (bf16[512,512]{1,0:T(8,128)(2,1)S(1)}, bf16[512,512]{1,0:T(8,128)(2,1)S(1)}, u32[]{:S(2)}, u32[]{:S(2)}) collective-permute-start(bf16[512,512]{1,0:T(8,128)(2,1)S(1)} %get-tuple-element.6), channel_id=1, source_target_pairs={{0,1},{1,0},{2,3},{3,2},{4,5},{5,4},{6,7},{7,6},{8,9},{9,8},{10,11... | collective-permute-start | bytes 1572872 | tf_op jit(solution)/shard_map/ppermute | solution.py:12
  213.8 84.6 %collective-permute-start.8 = (f32[1,128,512]{1,2,0:T(8,128)}, f32[1,128,512]{1,2,0:T(8,128)}, u32[]{:S(2)}, u32[]{:S(2)}) collective-permute-start(f32[1,128,512]{1,2,0:T(8,128)} %reduce-scatter.17.cloned.1.call-done), channel_id=1, source_target_pairs={{0,4},{1,5},{2,6},{3,7},{4,0},{5,1},{6,2},{7,3},{8,12},{9,13},{10,... | collective-permute-start | bytes 786440 | tf_op jit(solution)/shard_map/ppermute | solution.py:12
  262.2 36.2 %collective-permute-start.7 = (f32[1,128,512]{1,2,0:T(8,128)}, f32[1,128,512]{1,2,0:T(8,128)S(1)}, u32[]{:S(2)}, u32[]{:S(2)}) collective-permute-start(f32[1,128,512]{1,2,0:T(8,128)} %reduce-scatter.15.cloned.1.call-done), channel_id=1, source_target_pairs={{0,2},{1,3},{2,0},{3,1},{4,6},{5,7},{6,4},{7,5},{8,10},{9,11},{10,... | collective-permute-start | bytes 786440 | tf_op jit(solution)/shard_map/ppermute | solution.py:12
  293.0 5.4 %collective-permute-start.6 = (f32[1,128,512]{1,2,0:T(8,128)}, f32[1,128,512]{1,2,0:T(8,128)S(1)}, u32[]{:S(2)}, u32[]{:S(2)}) collective-permute-start(f32[1,128,512]{1,2,0:T(8,128)} %reduce-scatter.13.cloned.1.call-done), channel_id=1, source_target_pairs={{0,1},{1,0},{2,3},{3,2},{4,5},{5,4},{6,7},{7,6},{8,9},{9,8},{10,11... | collective-permute-start | bytes 786440 | tf_op jit(solution)/shard_map/ppermute | solution.py:12
Sparse Core Ops, SparseCore 0:
  107.4 28.8 reduce-scatter.16
  139.7 27.6 reduce-scatter.8
  170.8 27.7 reduce-scatter.10
  203.7 27.9 reduce-scatter.6
  234.5 27.6 reduce-scatter.14
  265.2 27.6 reduce-scatter.12
where the time goes:
time: 308 us; the launch traced here: 307 us
  waiting for transfers between devices  230 us (75%)
  matrix products  44.2 us (14%)
  between operations  14.2 us (5%)
  starting transfers between devices  10.4 us (3%)
  local copies, waits for them, and re-layouts  6.6 us (2%)
    ppermute x9, waiting for transfers between devices, from_partner(): lax.ppermute(array, axis, [(i, i ^ 1 << bit) for i in range(lax.axis_size...  161 us
    reduce_scatter x3, waiting for transfers between devices, wide_sum(): lax.psum_scatter(pair[1], 'wide', scatter_dimension=1, tiled=True)  57.5 us
    dot_general x6, matrix products, outer_sum(): lax.dot_general(left, right, (((0,), (0,)), ((), ())), preferred_element_...  25.3 us
    dot_general x6, matrix products, times_trans(): lax.dot_general(left, right, (((1,), (1,)), ((), ())), preferred_element_...  18.9 us
    reduce_scatter x3, waiting for transfers between devices, wide_sum(): lax.psum_scatter(pair[0], 'wide', scatter_dimension=1, tiled=True)  11.1 us
    ppermute x9, starting transfers between devices, from_partner(): lax.ppermute(array, axis, [(i, i ^ 1 << bit) for i in range(lax.axis_size...  9.98 us
  transfers between devices with their start and end apart: 15, of which 6 were waited for; matrix products, arithmetic and copies ran while one was open for 15% of the time, Pallas kernels for 0%

commit v1 on v0

v1 whole, which is shorter than its diff:
```python
import math

import jax
import jax.numpy as jnp
from jax import lax
from jax.experimental import pallas as pl
from jax.experimental.pallas import tpu as pltpu
from jax.sharding import PartitionSpec as P

LEVELS = 3
CUTS = (3, 3, 3, 3, 2, 2)
GROUPS = ((0, 1, 2), (3, 4), (5,))
ROW_TILE = 16
WINDOW = 2
VMEM_LIMIT = 40 * 1024 * 1024

ANY = pl.BlockSpec(memory_space=pl.ANY)
WHOLE = pl.BlockSpec(memory_space=pltpu.VMEM)


def swap(array, axis, mask):
    return lax.ppermute(array, axis, [(i, i ^ mask) for i in range(lax.axis_size(axis))])


def outer_sum(left, right):
    return lax.dot_general(
        left, right, (((0,), (0,)), ((), ())), preferred_element_type=jnp.float32
    )


def times_trans(left, right):
    return lax.dot_general(
        left, right, (((1,), (1,)), ((), ())), preferred_element_type=jnp.float32
    )


def params():
    return pltpu.CompilerParams(vmem_limit_bytes=VMEM_LIMIT)


def cost(flops, nbytes):
    return pl.CostEstimate(flops=flops, bytes_accessed=nbytes, transcendentals=0)


def row_cuts(tokens):
    unit = tokens // sum(CUTS)
    assert unit % ROW_TILE == 0
    cuts, start = [], 0
    for c in CUTS:
        cuts.append((start, c * unit))
        start += c * unit
    return cuts


def next_grad(grad, far, w_self, far_cross, level, deps=(), fetch=None):
    size, width = grad.shape
    n_in = 4 + len(deps)

    def body(*refs):
        grad_ref, far_ref, a_ref, c_ref = refs[:4]
        if fetch is None:
            out_ref = refs[n_in]
        else:
            src_ref, out_ref, cut_ref, sem = refs[n_in:]
            copy = pltpu.make_async_copy(
                src_ref.at[pl.ds(fetch[1], fetch[2])], cut_ref, sem
            )
            copy.start()
        total = times_trans(grad_ref[...], a_ref[0]) + times_trans(far_ref[...], c_ref[...])
        out_ref[...] = total.astype(jnp.bfloat16)
        if fetch is not None:
            copy.wait()

    weight = pl.BlockSpec((1,) + w_self.shape[1:], lambda i: (level, 0, 0))
    operands = [grad, far, w_self, far_cross, *deps]
    in_specs = [WHOLE, WHOLE, weight, WHOLE] + [ANY] * len(deps)
    out_shape = [jax.ShapeDtypeStruct((size, width), jnp.bfloat16)]
    scratch = []
    if fetch is not None:
        operands.append(fetch[0])
        in_specs.append(ANY)
        out_shape.append(jax.ShapeDtypeStruct((fetch[2], width), jnp.bfloat16))
        scratch.append(pltpu.SemaphoreType.DMA)
    out = pl.pallas_call(
        body,
        grid=(1,),
        out_shape=out_shape,
        in_specs=in_specs,
        out_specs=[WHOLE] * len(out_shape),
        scratch_shapes=scratch,
        compiler_params=params(),
        cost_estimate=cost(4 * size * width * width, 6 * size * width + 4 * width * width),
        name=f"next_grad_{level}",
    )(*operands)
    return out if fetch is not None else out[0]


def weight_sums(saved_inputs, level, start, grads, fars, before, scale, last, deps=()):
    sizes = [g.shape[0] for g in grads]
    rows, width = sum(sizes), saved_inputs.shape[2]
    blk = grads[0].shape[1]
    parts = lax.axis_size("wide")
    share = width // parts
    m = len(grads)
    n_before = 0 if before is None else 1

    def body(*refs):
        x_ref = refs[0]
        g_refs, f_refs = refs[1 : 1 + m], refs[1 + m : 1 + 2 * m]
        pos = 1 + 2 * m
        old = refs[pos] if n_before else None
        pos += n_before + len(deps)
        n_out = parts if last else 1
        outs = refs[pos : pos + n_out]
        scratch = refs[pos + n_out :]
        x_buf, sem = scratch[0], scratch[1]
        total = scratch[2] if last else outs[0]
        copy = pltpu.make_async_copy(x_ref.at[level, pl.ds(start, rows)], x_buf, sem)
        copy.start()
        copy.wait()
        for which, sides in enumerate((g_refs, f_refs)):
            at = 0
            acc = old[which] if n_before else None
            for size, side in zip(sizes, sides):
                term = outer_sum(x_buf[at : at + size], side[...])
                acc = term if acc is None else acc + term
                at += size
            total[which] = acc * scale if last else acc
        if last:
            me = lax.axis_index("wide")
            outs[0][...] = total[:, pl.ds(pl.multiple_of(me * share, share), share)]
            for k in range(1, parts):
                there = pl.multiple_of((me ^ k) * share, share)
                outs[k][...] = total[:, pl.ds(there, share)].astype(jnp.bfloat16)

    sums = jax.ShapeDtypeStruct((2, width, blk), jnp.float32)
    if last:
        out_shape = [jax.ShapeDtypeStruct((2, share, blk), jnp.float32)]
        out_shape += [jax.ShapeDtypeStruct((2, share, blk), jnp.bfloat16)] * (parts - 1)
    else:
        out_shape = [sums]
    scratch = [pltpu.VMEM((rows, width), saved_inputs.dtype), pltpu.SemaphoreType.DMA]
    if last:
        scratch.append(pltpu.VMEM(sums.shape, jnp.float32))
    operands = [saved_inputs, *grads, *fars] + ([before] if n_before else []) + list(deps)
    out = pl.pallas_call(
        body,
        grid=(1,),
        out_shape=out_shape,
        in_specs=[ANY] + [WHOLE] * (2 * m + n_before) + [ANY] * len(deps),
        out_specs=[WHOLE] * len(out_shape),
        scratch_shapes=scratch,
        compiler_params=params(),
        cost_estimate=cost(4 * rows * width * blk, 6 * rows * width + 16 * width * blk),
        name=f"weight_sums_{level}",
    )(*operands)
    return out if last else out[0]


def far_blocks(w_cross):
    parts = lax.axis_size("wide")
    rows = w_cross.shape[1] // parts
    me = lax.axis_index("wide")
    out = [None] * LEVELS
    for level in reversed(range(LEVELS)):
        share = lax.dynamic_slice_in_dim(w_cross[level], me * rows, rows, 0)
        share = swap(share, "narrow", 1 << level)
        block = lax.dynamic_update_slice_in_dim(jnp.zeros_like(w_cross[level]), share, me * rows, 0)
        for k in range(1, parts):
            block = lax.dynamic_update_slice_in_dim(block, swap(share, "wide", k), (me ^ k) * rows, 0)
        out[level] = block
    return out


def wide_sum(kept, *terms):
    for k, term in enumerate(terms, 1):
        kept = kept + swap(term, "wide", k).astype(jnp.float32)
    return kept


def local(saved_inputs, cotangent, w_self, w_cross):
    tokens = saved_inputs.shape[1]
    scale = 1.0 / math.sqrt(tokens * lax.axis_size("wide"))
    cuts = row_cuts(tokens)
    blocks = far_blocks(w_cross)
    n = len(cuts)
    near = [[None] * n for _ in range(LEVELS + 1)]
    far = [[None] * n for _ in range(LEVELS)]
    top = LEVELS - 1
    for k in range(min(WINDOW, n)):
        near[top][k] = cotangent[cuts[k][0] : cuts[k][0] + cuts[k][1]]
        far[top][k] = swap(near[top][k], "narrow", 1 << top)
    for t in range(n + top):
        for level in reversed(range(LEVELS)):
            k = t - (top - level)
            if not 0 <= k < n:
                continue
            ahead = k + WINDOW
            fetch = None
            if level == top and ahead < n:
                fetch = (cotangent, *cuts[ahead])
            if far[level][k] is None:
                far[level][k] = swap(near[level][k], "narrow", 1 << level)
            out = next_grad(near[level][k], far[level][k], w_self, blocks[level], level, (), fetch)
            if fetch is not None:
                out, near[top][ahead] = out
                far[top][ahead] = swap(near[top][ahead], "narrow", 1 << top)
            near[level - 1][k] = out
    grad_self, grad_cross = [None] * LEVELS, [None] * LEVELS
    for level in reversed(range(LEVELS)):
        sums = None
        for group in GROUPS:
            last = group is GROUPS[-1]
            sums = weight_sums(
                saved_inputs,
                level,
                cuts[group[0]][0],
                [near[level][k] for k in group],
                [far[level][k] for k in group],
                sums,
                scale,
                last,
            )
        both = wide_sum(*sums)
        grad_self[level] = both[0]
        grad_cross[level] = swap(both[1].astype(jnp.bfloat16), "narrow", 1 << level)
    return (
        jnp.concatenate(near[-1]),
        jnp.stack(grad_self),
        jnp.stack(grad_cross).astype(jnp.float32),
    )


def solution(mesh):
    in_specs = (
        P(None, "wide", "narrow"),
        P("wide", "narrow"),
        P(None, "narrow", None),
        P(None, "narrow", None),
    )
    out_specs = (
        P("wide", "narrow"),
        P(None, ("narrow", "wide"), None),
        P(None, ("narrow", "wide"), None),
    )
    return jax.shard_map(local, mesh=mesh, in_specs=in_specs, out_specs=out_specs, check_vma=False)
```

time: 308 us -> 187 us (0.61)
  waiting for transfers between devices: 230 us -> 108 us
  matrix products: 44.2 us -> 0 us
  starting transfers between devices: 10.4 us -> 40.3 us
  Pallas kernels: 0 us -> 22.3 us
  between operations: 14.2 us -> 1.44 us
  local copies, waits for them, and re-layouts: 6.6 us -> 11.8 us
    reduce_scatter x6 -> x0, waiting for transfers between devices: 68.6 us -> none  [the longest x3 57.5 us: wide_sum(): lax.psum_scatter(pair[1], 'wide', scatter_dimension=1, tiled=True)]
    ppermute x9 -> x42, waiting for transfers between devices: 161 us -> 108 us  [swap(): lax.ppermute(array, axis, [(i, i ^ mask) for i in range(lax.axis_size(axi...]
    dot_general x12 -> x0, matrix products: 44.2 us -> none  [the longest x6 25.3 us: outer_sum(): lax.dot_general(left, right, (((0,), (0,)), ((), ())), preferred_element_...]
    ppermute x9 -> x42, starting transfers between devices: 9.98 us -> 40.3 us  [swap(): lax.ppermute(array, axis, [(i, i ^ mask) for i in range(lax.axis_size(axi...]
    pallas_call x0 -> x27, Pallas kernels: none -> 22.3 us  [the longest x9 11.9 us: weight_sums(): pl.pallas_call(body, grid=(1,), out_shape=out_shape, in_specs=[ANY] + [WH...]
    dynamic_slice x0 -> x3, local copies, waits for them, and re-layouts: none -> 4.17 us  [far_blocks(): share = lax.dynamic_slice_in_dim(w_cross[level], me * rows, rows, 0)]
  transfers between devices with their start and end apart: 15 -> 42, of which waited for: 6 -> 18; matrix products, arithmetic and copies ran while one was open for 15% -> 6% of each run, Pallas kernels for 0% -> 12%
where the time goes in v1:
time: 187 us; the launch traced here: 186 us
  waiting for transfers between devices  108 us (58%)
  starting transfers between devices  40.3 us (22%)
  Pallas kernels  22.3 us (12%)
  local copies, waits for them, and re-layouts  11.8 us (6%)
  other arithmetic  2.27 us (1%)
    ppermute x42, waiting for transfers between devices, swap(): lax.ppermute(array, axis, [(i, i ^ mask) for i in range(lax.axis_size(axi...  108 us
    ppermute x42, starting transfers between devices, swap(): lax.ppermute(array, axis, [(i, i ^ mask) for i in range(lax.axis_size(axi...  40.3 us
    pallas_call x9, Pallas kernels, weight_sums(): pl.pallas_call(body, grid=(1,), out_shape=out_shape, in_specs=[ANY] + [WH...  11.9 us
    pallas_call x18, Pallas kernels, next_grad(): pl.pallas_call(body, grid=(1,), out_shape=out_shape, in_specs=in_specs, o...  10.5 us
    dynamic_slice x3, local copies, waits for them, and re-layouts, far_blocks(): share = lax.dynamic_slice_in_dim(w_cross[level], me * rows, rows, 0)  4.17 us
  transfers between devices with their start and end apart: 42, of which 18 were waited for; matrix products, arithmetic and copies ran while one was open for 6% of the time, Pallas kernels for 12%

profile of v1, /device:TPU:0, one launch (start us, length us, event | category | flops | bytes accessed | tf_op | source)
XLA Modules:
  0.0 186.5 jit_solution(1854037616702347258)
XLA Ops:
  0.6 1.3 fusion.3
  1.9 4.1 %collective-permute-start.15 = (bf16[384,512]{1,0:T(8,128)(2,1)S(1)}, bf16[384,512]{1,0:T(8,128)(2,1)S(1)}, u32[]{:S(2)}, u32[]{:S(2)}) collective-permute-start(bf16[384,512]{1,0:T(8,128)(2,1)S(1)} %get-tuple-element.43.refs_0_.refs_2_), channel_id=1, source_target_pairs={{0,4},{1,5},{2,6},{3,7},{4,0},{5,1},{6,2},{7,3},{8,12},{9,13},{10,... | collective-permute-start | bytes 1179656 | tf_op jit(solution)/shard_map/ppermute | solution.py:22
  6.1 1.2 fusion.4
  7.3 1.7 dynamic-slice_bitcast_fusion.1
  9.0 1.8 collective-permute-start.6
  10.8 1.6 dynamic-slice_bitcast_fusion.2
  12.4 2.6 %collective-permute-start.1 = (bf16[128,512]{1,0:T(8,128)(2,1)}, bf16[128,512]{1,0:T(8,128)(2,1)S(1)}, u32[]{:S(2)}, u32[]{:S(2)}) collective-permute-start(bf16[128,512]{1,0:T(8,128)(2,1)} %dynamic-slice_bitcast_fusion.2), channel_id=1, source_target_pairs={{0,4},{1,5},{2,6},{3,7},{4,0},{5,1},{6,2},{7,3},{8,12},{9,13},{10,... | collective-permute-start | bytes 393224 | tf_op jit(solution)/shard_map/ppermute | solution.py:22
  15.0 0.9 dynamic-slice_bitcast_fusion
  16.0 10.9 %collective-permute-done.6 = bf16[128,512]{1,0:T(8,128)(2,1)S(1)} collective-permute-done((bf16[128,512]{1,0:T(8,128)(2,1)}, bf16[128,512]{1,0:T(8,128)(2,1)S(1)}, u32[]{:S(2)}, u32[]{:S(2)}) %collective-permute-start.6) | collective-permute-done | bytes 131104 | tf_op jit(solution)/shard_map/ppermute | solution.py:22
  26.9 2.4 %collective-permute-start.9 = (bf16[128,512]{1,0:T(8,128)(2,1)S(1)}, bf16[128,512]{1,0:T(8,128)(2,1)S(1)}, u32[]{:S(2)}, u32[]{:S(2)}) collective-permute-start(bf16[128,512]{1,0:T(8,128)(2,1)S(1)} %collective-permute-done.6), channel_id=1, source_target_pairs={{0,24},{8,16},{16,8},{24,0},{1,25},{9,17},{17,9},{25,1},{2,26},{10... | collective-permute-start | bytes 393224 | tf_op jit(solution)/shard_map/ppermute | solution.py:22
  29.4 16.6 %collective-permute-done.1 = bf16[128,512]{1,0:T(8,128)(2,1)S(1)} collective-permute-done((bf16[128,512]{1,0:T(8,128)(2,1)}, bf16[128,512]{1,0:T(8,128)(2,1)S(1)}, u32[]{:S(2)}, u32[]{:S(2)}) %collective-permute-start.1) | collective-permute-done | bytes 131104 | tf_op jit(solution)/shard_map/ppermute | solution.py:22
  46.0 1.5 collective-permute-start.7
  48.3 0.9 constant_dynamic-update-slice_fusion.9
  49.2 2.9 %collective-permute-done.7 = bf16[128,512]{1,0:T(8,128)(2,1)S(1)} collective-permute-done((bf16[128,512]{1,0:T(8,128)(2,1)S(1)}, bf16[128,512]{1,0:T(8,128)(2,1)S(1)}, u32[]{:S(2)}, u32[]{:S(2)}) %collective-permute-start.7) | collective-permute-done | bytes 131104 | tf_op jit(solution)/shard_map/ppermute | solution.py:22
  52.1 1.3 collective-permute-start.3
  53.5 2.2 %collective-permute-start.4 = (bf16[128,512]{1,0:T(8,128)(2,1)S(1)}, bf16[128,512]{1,0:T(8,128)(2,1)S(1)}, u32[]{:S(2)}, u32[]{:S(2)}) collective-permute-start(bf16[128,512]{1,0:T(8,128)(2,1)S(1)} %collective-permute-done.1), channel_id=1, source_target_pairs={{0,24},{8,16},{16,8},{24,0},{1,25},{9,17},{17,9},{25,1},{2,26},{10... | collective-permute-start | bytes 393224 | tf_op jit(solution)/shard_map/ppermute | solution.py:22
  55.8 5.2 %collective-permute-done.3 = bf16[128,512]{1,0:T(8,128)(2,1)S(1)} collective-permute-done((bf16[128,512]{1,0:T(8,128)(2,1)S(1)}, bf16[128,512]{1,0:T(8,128)(2,1)S(1)}, u32[]{:S(2)}, u32[]{:S(2)}) %collective-permute-start.3) | collective-permute-done | bytes 131104 | tf_op jit(solution)/shard_map/ppermute | solution.py:22
  60.9 1.0 collective-permute-start.8
  62.0 1.0 collective-permute-start.13
  63.1 1.1 collective-permute-start.12
  65.9 4.2 %collective-permute-start.5 = (bf16[384,512]{1,0:T(8,128)(2,1)S(1)}, bf16[384,512]{1,0:T(8,128)(2,1)S(1)}, u32[]{:S(2)}, u32[]{:S(2)}) collective-permute-start(bf16[384,512]{1,0:T(8,128)(2,1)S(1)} %get-tuple-element.23.refs_0_.refs_1_), channel_id=1, source_target_pairs={{0,2},{1,3},{2,0},{3,1},{4,6},{5,7},{6,4},{7,5},{8,10},{9,11},{10,... | collective-permute-start | bytes 1179656 | tf_op jit(solution)/shard_map/ppermute | solution.py:22
  70.2 0.9 collective-permute-start.16
  71.1 1.6 collective-permute-start.14
  72.7 14.9 %collective-permute-done.21.refs_1_.refs_3_ = bf16[384,512]{1,0:T(8,128)(2,1)S(1)} collective-permute-done((bf16[384,512]{1,0:T(8,128)(2,1)S(1)}, bf16[384,512]{1,0:T(8,128)(2,1)S(1)}, u32[]{:S(2)}, u32[]{:S(2)}) %collective-permute-start.21) | collective-permute-done | bytes 393248 | tf_op jit(solution)/shard_map/ppermute | solution.py:22
  89.3 19.1 %collective-permute-done.18.refs_1_.refs_6_ = bf16[384,512]{1,0:T(8,128)(2,1)S(1)} collective-permute-done((bf16[384,512]{1,0:T(8,128)(2,1)S(1)}, bf16[384,512]{1,0:T(8,128)(2,1)S(1)}, u32[]{:S(2)}, u32[]{:S(2)}) %collective-permute-start.18) | collective-permute-done | bytes 393248 | tf_op jit(solution)/shard_map/ppermute | solution.py:22
  109.9 1.8 collective-permute-start.19
  111.7 2.1 %weight_sums_2.3.refs_5_ = f32[2,512,512]{2,1,0:T(8,128)S(1)} custom-call(bf16[3,2048,512]{2,1,0:T(8,128)(2,1)S(1)} %bitcast.16, bf16[384,512]{1,0:T(8,128)(2,1)S(1)} %get-tuple-element.44.refs_0_.refs_1_, bf16[384,512]{1,0:T(8,128)(2,1)S(1)} %get-tuple-element.43.refs_0_.refs_2_, bf16[384,512]{1,0:T(8,128)(2,1)S(1)} %get-tuple-element.25.refs_0_.refs_3_, ...), custom_call_target="tpu_custom_call" | custom-call | flops 1207959552 | bytes 7733248 | tf_op jit(solution)/shard_map/weight_sums_2/pallas_call | solution.py:146
  113.7 2.8 %collective-permute-done.27.refs_1_.refs_2_ = bf16[256,512]{1,0:T(8,128)(2,1)S(1)} collective-permute-done((bf16[256,512]{1,0:T(8,128)(2,1)S(1)}, bf16[256,512]{1,0:T(8,128)(2,1)S(1)}, u32[]{:S(2)}, u32[]{:S(2)}) %collective-permute-start.27) | collective-permute-done | bytes 262176 | tf_op jit(solution)/shard_map/ppermute | solution.py:22
  117.0 2.3 %collective-permute-done.24.refs_1_.refs_4_ = bf16[256,512]{1,0:T(8,128)(2,1)S(1)} collective-permute-done((bf16[256,512]{1,0:T(8,128)(2,1)S(1)}, bf16[256,512]{1,0:T(8,128)(2,1)S(1)}, u32[]{:S(2)}, u32[]{:S(2)}) %collective-permute-start.24) | collective-permute-done | bytes 262176 | tf_op jit(solution)/shard_map/ppermute | solution.py:22
  119.9 1.2 weight_sums_2.4.refs_3_
  123.0 3.4 %collective-permute-done.19.refs_1_.refs_6_ = bf16[384,512]{1,0:T(8,128)(2,1)S(1)} collective-permute-done((bf16[384,512]{1,0:T(8,128)(2,1)S(1)}, bf16[384,512]{1,0:T(8,128)(2,1)S(1)}, u32[]{:S(2)}, u32[]{:S(2)}) %collective-permute-start.19) | collective-permute-done | bytes 393248 | tf_op jit(solution)/shard_map/ppermute | solution.py:22
  126.4 2.1 %weight_sums_1.3.refs_5_ = f32[2,512,512]{2,1,0:T(8,128)S(1)} custom-call(bf16[3,2048,512]{2,1,0:T(8,128)(2,1)S(1)} %bitcast.16, bf16[384,512]{1,0:T(8,128)(2,1)S(1)} %copy-done.7, bf16[384,512]{1,0:T(8,128)(2,1)S(1)} %copy-done.5, bf16[384,512]{1,0:T(8,128)(2,1)S(1)} %get-tuple-element.26.refs_0_.refs_3_, bf16[384,512]{1,0:T(8,128)(2,1)S(1)} %copy-done.9, ...), custom_call_target="tpu_custom_call" | custom-call | flops 1207959552 | bytes 7733248 | tf_op jit(solution)/shard_map/weight_sums_1/pallas_call | solution.py:146
  129.5 5.3 %collective-permute-done.22.refs_1_.refs_3_ = bf16[384,512]{1,0:T(8,128)(2,1)S(1)} collective-permute-done((bf16[384,512]{1,0:T(8,128)(2,1)S(1)}, bf16[384,512]{1,0:T(8,128)(2,1)S(1)}, u32[]{:S(2)}, u32[]{:S(2)}) %collective-permute-start.22) | collective-permute-done | bytes 393248 | tf_op jit(solution)/shard_map/ppermute | solution.py:22
  134.8 0.8 collective-permute-start.38
  137.7 7.9 %collective-permute-done.25.refs_1_.refs_4_ = bf16[256,512]{1,0:T(8,128)(2,1)S(1)} collective-permute-done((bf16[256,512]{1,0:T(8,128)(2,1)S(1)}, bf16[256,512]{1,0:T(8,128)(2,1)S(1)}, u32[]{:S(2)}, u32[]{:S(2)}) %collective-permute-start.25) | collective-permute-done | bytes 262176 | tf_op jit(solution)/shard_map/ppermute | solution.py:22
  145.6 1.2 weight_sums_1.4.refs_3_
  148.8 1.1 collective-permute-start.34
  149.9 1.9 %collective-permute-start.35 = (bf16[2,128,512]{2,1,0:T(8,128)(2,1)S(1)}, bf16[2,128,512]{2,1,0:T(8,128)(2,1)S(1)}, u32[]{:S(2)}, u32[]{:S(2)}) collective-permute-start(bf16[2,128,512]{2,1,0:T(8,128)(2,1)S(1)} %get-tuple-element.38), channel_id=1, source_target_pairs={{0,24},{8,16},{16,8},{24,0},{1,25},{9,17},{17,9},{25,1},{2,26},{10... | collective-permute-start | bytes 786440 | tf_op jit(solution)/shard_map/ppermute | solution.py:22
  152.9 4.5 %collective-permute-done.33 = bf16[2,128,512]{2,1,0:T(8,128)(2,1)S(1)} collective-permute-done((bf16[2,128,512]{2,1,0:T(8,128)(2,1)S(1)}, bf16[2,128,512]{2,1,0:T(8,128)(2,1)S(1)}, u32[]{:S(2)}, u32[]{:S(2)}) %collective-permute-start.33) | collective-permute-done | bytes 262176 | tf_op jit(solution)/shard_map/ppermute | solution.py:22
  157.5 4.9 %collective-permute-done.34 = bf16[2,128,512]{2,1,0:T(8,128)(2,1)S(1)} collective-permute-done((bf16[2,128,512]{2,1,0:T(8,128)(2,1)S(1)}, bf16[2,128,512]{2,1,0:T(8,128)(2,1)S(1)}, u32[]{:S(2)}, u32[]{:S(2)}) %collective-permute-start.34) | collective-permute-done | bytes 262176 | tf_op jit(solution)/shard_map/ppermute | solution.py:22
  162.6 2.1 %collective-permute-start.40 = (bf16[128,512]{1,0:T(8,128)(2,1)S(1)}, bf16[128,512]{1,0:T(8,128)(2,1)S(1)}, u32[]{:S(2)}, u32[]{:S(2)}) collective-permute-start(bf16[128,512]{1,0:T(8,128)(2,1)S(1)} %fusion.1), channel_id=1, source_target_pairs={{0,2},{1,3},{2,0},{3,1},{4,6},{5,7},{6,4},{7,5},{8,10},{9,11},{10,... | collective-permute-start | bytes 393224 | tf_op jit(solution)/shard_map/ppermute | solution.py:22
  164.7 2.1 %weight_sums_0.3.refs_5_ = f32[2,512,512]{2,1,0:T(8,128)S(1)} custom-call(bf16[3,2048,512]{2,1,0:T(8,128)(2,1)S(1)} %bitcast.16, bf16[384,512]{1,0:T(8,128)(2,1)S(1)} %next_grad_1.6.refs_0_.refs_1_, bf16[384,512]{1,0:T(8,128)(2,1)S(1)} %next_grad_1.7.refs_0_.refs_2_, bf16[384,512]{1,0:T(8,128)(2,1)S(1)} %next_grad_1.8.refs_0_.refs_3_, ...), custom_call_target="tpu_custom_call" | custom-call | flops 1207959552 | bytes 7733248 | tf_op jit(solution)/shard_map/weight_sums_0/pallas_call | solution.py:146
  166.8 1.2 weight_sums_0.4.refs_3_
  168.6 1.5 collective-permute-start.30
  170.8 1.4 collective-permute-start.32
  177.8 6.1 %collective-permute-done.31 = bf16[2,128,512]{2,1,0:T(8,128)(2,1)S(1)} collective-permute-done((bf16[2,128,512]{2,1,0:T(8,128)(2,1)S(1)}, bf16[2,128,512]{2,1,0:T(8,128)(2,1)S(1)}, u32[]{:S(2)}, u32[]{:S(2)}) %collective-permute-start.31) | collective-permute-done | bytes 262176 | tf_op jit(solution)/shard_map/ppermute | solution.py:22
  184.2 0.9 pad_maximum_fusion
  185.5 0.9 maximum_convert_fusion
  (139 shorter events, 22.4 us)
Async XLA Ops:
  1.9 61.1 %collective-permute-start.15 = (bf16[384,512]{1,0:T(8,128)(2,1)S(1)}, bf16[384,512]{1,0:T(8,128)(2,1)S(1)}, u32[]{:S(2)}, u32[]{:S(2)}) collective-permute-start(bf16[384,512]{1,0:T(8,128)(2,1)S(1)} %get-tuple-element.43.refs_0_.refs_2_), channel_id=1, source_target_pairs={{0,4},{1,5},{2,6},{3,7},{4,0},{5,1},{6,2},{7,3},{8,12},{9,13},{10,... | collective-permute-start | bytes 1179656 | tf_op jit(solution)/shard_map/ppermute | solution.py:22
  6.0 58.9 %collective-permute-start = (bf16[384,512]{1,0:T(8,128)(2,1)S(1)}, bf16[384,512]{1,0:T(8,128)(2,1)S(1)}, u32[]{:S(2)}, u32[]{:S(2)}) collective-permute-start(bf16[384,512]{1,0:T(8,128)(2,1)S(1)} %get-tuple-element.44.refs_0_.refs_1_), channel_id=1, source_target_pairs={{0,4},{1,5},{2,6},{3,7},{4,0},{5,1},{6,2},{7,3},{8,12},{9,13},{10,... | collective-permute-start | bytes 1179656 | tf_op jit(solution)/shard_map/ppermute | solution.py:22
  7.3 56.9 %copy-start = (bf16[3,512,512]{2,1,0:T(8,128)(2,1)S(1)}, bf16[3,512,512]{2,1,0:T(8,128)(2,1)}, u32[]{:S(2)}) copy-start(bf16[3,512,512]{2,1,0:T(8,128)(2,1)} %refs_2_.35) | copy-start | bytes 4718596
  9.0 18.0 %collective-permute-start.6 = (bf16[128,512]{1,0:T(8,128)(2,1)}, bf16[128,512]{1,0:T(8,128)(2,1)S(1)}, u32[]{:S(2)}, u32[]{:S(2)}) collective-permute-start(bf16[128,512]{1,0:T(8,128)(2,1)} %dynamic-slice_bitcast_fusion.1), channel_id=1, source_target_pairs={{0,2},{1,3},{2,0},{3,1},{4,6},{5,7},{6,4},{7,5},{8,10},{9,11},{10,... | collective-permute-start | bytes 393224 | tf_op jit(solution)/shard_map/ppermute | solution.py:22
  12.4 33.7 %collective-permute-start.1 = (bf16[128,512]{1,0:T(8,128)(2,1)}, bf16[128,512]{1,0:T(8,128)(2,1)S(1)}, u32[]{:S(2)}, u32[]{:S(2)}) collective-permute-start(bf16[128,512]{1,0:T(8,128)(2,1)} %dynamic-slice_bitcast_fusion.2), channel_id=1, source_target_pairs={{0,4},{1,5},{2,6},{3,7},{4,0},{5,1},{6,2},{7,3},{8,12},{9,13},{10,... | collective-permute-start | bytes 393224 | tf_op jit(solution)/shard_map/ppermute | solution.py:22
  15.9 31.8 %collective-permute-start.11 = (bf16[128,512]{1,0:T(8,128)(2,1)S(1)}, bf16[128,512]{1,0:T(8,128)(2,1)}, u32[]{:S(2)}, u32[]{:S(2)}) collective-permute-start(bf16[128,512]{1,0:T(8,128)(2,1)S(1)} %dynamic-slice_bitcast_fusion), channel_id=1, source_target_pairs={{0,1},{1,0},{2,3},{3,2},{4,5},{5,4},{6,7},{7,6},{8,9},{9,8},{10,11... | collective-permute-start | bytes 393224 | tf_op jit(solution)/shard_map/ppermute | solution.py:22
  16.0 48.2 %copy-start.1 = (bf16[2048,512]{1,0:T(8,128)(2,1)S(1)}, bf16[2048,512]{1,0:T(8,128)(2,1)}, u32[]{:S(2)}) copy-start(bf16[2048,512]{1,0:T(8,128)(2,1)} %refs_4_.7) | copy-start | bytes 6291460
  26.9 43.1 %collective-permute-start.9 = (bf16[128,512]{1,0:T(8,128)(2,1)S(1)}, bf16[128,512]{1,0:T(8,128)(2,1)S(1)}, u32[]{:S(2)}, u32[]{:S(2)}) collective-permute-start(bf16[128,512]{1,0:T(8,128)(2,1)S(1)} %collective-permute-done.6), channel_id=1, source_target_pairs={{0,24},{8,16},{16,8},{24,0},{1,25},{9,17},{17,9},{25,1},{2,26},{10... | collective-permute-start | bytes 393224 | tf_op jit(solution)/shard_map/ppermute | solution.py:22
  46.0 6.1 %collective-permute-start.7 = (bf16[128,512]{1,0:T(8,128)(2,1)S(1)}, bf16[128,512]{1,0:T(8,128)(2,1)S(1)}, u32[]{:S(2)}, u32[]{:S(2)}) collective-permute-start(bf16[128,512]{1,0:T(8,128)(2,1)S(1)} %collective-permute-done.6), channel_id=1, source_target_pairs={{0,8},{8,0},{16,24},{24,16},{1,9},{9,1},{17,25},{25,17},{2,10},{10... | collective-permute-start | bytes 393224 | tf_op jit(solution)/shard_map/ppermute | solution.py:22
  47.7 5.9 %collective-permute-start.2 = (bf16[128,512]{1,0:T(8,128)(2,1)S(1)}, bf16[128,512]{1,0:T(8,128)(2,1)S(1)}, u32[]{:S(2)}, u32[]{:S(2)}) collective-permute-start(bf16[128,512]{1,0:T(8,128)(2,1)S(1)} %collective-permute-done.1), channel_id=1, source_target_pairs={{0,8},{8,0},{16,24},{24,16},{1,9},{9,1},{17,25},{25,17},{2,10},{10... | collective-permute-start | bytes 393224 | tf_op jit(solution)/shard_map/ppermute | solution.py:22
  52.1 8.8 %collective-permute-start.3 = (bf16[128,512]{1,0:T(8,128)(2,1)S(1)}, bf16[128,512]{1,0:T(8,128)(2,1)S(1)}, u32[]{:S(2)}, u32[]{:S(2)}) collective-permute-start(bf16[128,512]{1,0:T(8,128)(2,1)S(1)} %collective-permute-done.1), channel_id=1, source_target_pairs={{0,16},{8,24},{16,0},{24,8},{1,17},{9,25},{17,1},{25,9},{2,18},{10... | collective-permute-start | bytes 393224 | tf_op jit(solution)/shard_map/ppermute | solution.py:22
  53.5 8.5 %collective-permute-start.4 = (bf16[128,512]{1,0:T(8,128)(2,1)S(1)}, bf16[128,512]{1,0:T(8,128)(2,1)S(1)}, u32[]{:S(2)}, u32[]{:S(2)}) collective-permute-start(bf16[128,512]{1,0:T(8,128)(2,1)S(1)} %collective-permute-done.1), channel_id=1, source_target_pairs={{0,24},{8,16},{16,8},{24,0},{1,25},{9,17},{17,9},{25,1},{2,26},{10... | collective-permute-start | bytes 393224 | tf_op jit(solution)/shard_map/ppermute | solution.py:22
  60.9 5.0 %collective-permute-start.8 = (bf16[128,512]{1,0:T(8,128)(2,1)S(1)}, bf16[128,512]{1,0:T(8,128)(2,1)S(1)}, u32[]{:S(2)}, u32[]{:S(2)}) collective-permute-start(bf16[128,512]{1,0:T(8,128)(2,1)S(1)} %collective-permute-done.6), channel_id=1, source_target_pairs={{0,16},{8,24},{16,0},{24,8},{1,17},{9,25},{17,1},{25,9},{2,18},{10... | collective-permute-start | bytes 393224 | tf_op jit(solution)/shard_map/ppermute | solution.py:22
  62.0 9.1 %collective-permute-start.13 = (bf16[128,512]{1,0:T(8,128)(2,1)}, bf16[128,512]{1,0:T(8,128)(2,1)S(1)}, u32[]{:S(2)}, u32[]{:S(2)}) collective-permute-start(bf16[128,512]{1,0:T(8,128)(2,1)} %collective-permute-done.11), channel_id=1, source_target_pairs={{0,16},{8,24},{16,0},{24,8},{1,17},{9,25},{17,1},{25,9},{2,18},{10... | collective-permute-start | bytes 393224 | tf_op jit(solution)/shard_map/ppermute | solution.py:22
  63.1 7.1 %collective-permute-start.12 = (bf16[128,512]{1,0:T(8,128)(2,1)}, bf16[128,512]{1,0:T(8,128)(2,1)S(1)}, u32[]{:S(2)}, u32[]{:S(2)}) collective-permute-start(bf16[128,512]{1,0:T(8,128)(2,1)} %collective-permute-done.11), channel_id=1, source_target_pairs={{0,8},{8,0},{16,24},{24,16},{1,9},{9,1},{17,25},{25,17},{2,10},{10... | collective-permute-start | bytes 393224 | tf_op jit(solution)/shard_map/ppermute | solution.py:22
  65.0 44.2 %copy-start.4 = (bf16[384,512]{1,0:T(8,128)(2,1)}, bf16[384,512]{1,0:T(8,128)(2,1)S(1)}, u32[]{:S(2)}) copy-start(bf16[384,512]{1,0:T(8,128)(2,1)S(1)} %get-tuple-element.24.refs_0_.refs_2_) | copy-start | bytes 1179652
  65.0 22.6 %collective-permute-start.21 = (bf16[384,512]{1,0:T(8,128)(2,1)S(1)}, bf16[384,512]{1,0:T(8,128)(2,1)S(1)}, u32[]{:S(2)}, u32[]{:S(2)}) collective-permute-start(bf16[384,512]{1,0:T(8,128)(2,1)S(1)} %get-tuple-element.27.refs_0_.refs_1_), channel_id=1, source_target_pairs={{0,4},{1,5},{2,6},{3,7},{4,0},{5,1},{6,2},{7,3},{8,12},{9,13},{10,... | collective-permute-start | bytes 1179656 | tf_op jit(solution)/shard_map/ppermute | solution.py:22
  65.9 22.7 %copy-start.6 = (bf16[384,512]{1,0:T(8,128)(2,1)}, bf16[384,512]{1,0:T(8,128)(2,1)S(1)}, u32[]{:S(2)}) copy-start(bf16[384,512]{1,0:T(8,128)(2,1)S(1)} %get-tuple-element.23.refs_0_.refs_1_) | copy-start | bytes 1179652
  65.9 22.7 %collective-permute-start.5 = (bf16[384,512]{1,0:T(8,128)(2,1)S(1)}, bf16[384,512]{1,0:T(8,128)(2,1)S(1)}, u32[]{:S(2)}, u32[]{:S(2)}) collective-permute-start(bf16[384,512]{1,0:T(8,128)(2,1)S(1)} %get-tuple-element.23.refs_0_.refs_1_), channel_id=1, source_target_pairs={{0,2},{1,3},{2,0},{3,1},{4,6},{5,7},{6,4},{7,5},{8,10},{9,11},{10,... | collective-permute-start | bytes 1179656 | tf_op jit(solution)/shard_map/ppermute | solution.py:22
  70.1 38.3 %collective-permute-start.18 = (bf16[384,512]{1,0:T(8,128)(2,1)S(1)}, bf16[384,512]{1,0:T(8,128)(2,1)S(1)}, u32[]{:S(2)}, u32[]{:S(2)}) collective-permute-start(bf16[384,512]{1,0:T(8,128)(2,1)S(1)} %get-tuple-element.25.refs_0_.refs_3_), channel_id=1, source_target_pairs={{0,4},{1,5},{2,6},{3,7},{4,0},{5,1},{6,2},{7,3},{8,12},{9,13},{10,... | collective-permute-start | bytes 1179656 | tf_op jit(solution)/shard_map/ppermute | solution.py:22
  70.2 39.0 %collective-permute-start.16 = (bf16[384,512]{1,0:T(8,128)(2,1)S(1)}, bf16[384,512]{1,0:T(8,128)(2,1)S(1)}, u32[]{:S(2)}, u32[]{:S(2)}) collective-permute-start(bf16[384,512]{1,0:T(8,128)(2,1)S(1)} %get-tuple-element.24.refs_0_.refs_2_), channel_id=1, source_target_pairs={{0,2},{1,3},{2,0},{3,1},{4,6},{5,7},{6,4},{7,5},{8,10},{9,11},{10,... | collective-permute-start | bytes 1179656 | tf_op jit(solution)/shard_map/ppermute | solution.py:22
  71.1 38.0 %collective-permute-start.14 = (bf16[128,512]{1,0:T(8,128)(2,1)}, bf16[128,512]{1,0:T(8,128)(2,1)S(1)}, u32[]{:S(2)}, u32[]{:S(2)}) collective-permute-start(bf16[128,512]{1,0:T(8,128)(2,1)} %collective-permute-done.11), channel_id=1, source_target_pairs={{0,24},{8,16},{16,8},{24,0},{1,25},{9,17},{17,9},{25,1},{2,26},{10... | collective-permute-start | bytes 393224 | tf_op jit(solution)/shard_map/ppermute | solution.py:22
  88.2 28.3 %collective-permute-start.27 = (bf16[256,512]{1,0:T(8,128)(2,1)S(1)}, bf16[256,512]{1,0:T(8,128)(2,1)S(1)}, u32[]{:S(2)}, u32[]{:S(2)}) collective-permute-start(bf16[256,512]{1,0:T(8,128)(2,1)S(1)} %get-tuple-element.30.refs_0_.refs_1_), channel_id=1, source_target_pairs={{0,4},{1,5},{2,6},{3,7},{4,0},{5,1},{6,2},{7,3},{8,12},{9,13},{10,... | collective-permute-start | bytes 786440 | tf_op jit(solution)/shard_map/ppermute | solution.py:22
  88.6 23.1 %slice-start = ((s8[6291456]{0:T(1024)(128)(4,1)}), s8[4194304]{0:T(1024)(128)(4,1)S(1)}, s32[]{:S(2)}) async-start(s8[6291456]{0:T(1024)(128)(4,1)} %bitcast.15), calls=%async_computation | async-start | bytes 8388608
  89.2 22.5 %slice-start.1 = ((s8[6291456]{0:T(1024)(128)(4,1)}), s8[2097152]{0:T(1024)(128)(4,1)S(1)}, s32[]{:S(2)}) async-start(s8[6291456]{0:T(1024)(128)(4,1)} %bitcast.15), calls=%async_computation.1 | async-start | bytes 4194304
  89.2 32.6 %collective-permute-start.10 = (bf16[384,512]{1,0:T(8,128)(2,1)S(1)}, bf16[384,512]{1,0:T(8,128)(2,1)S(1)}, u32[]{:S(2)}, u32[]{:S(2)}) collective-permute-start(bf16[384,512]{1,0:T(8,128)(2,1)S(1)} %next_grad_1.6.refs_0_.refs_1_), channel_id=1, source_target_pairs={{0,1},{1,0},{2,3},{3,2},{4,5},{5,4},{6,7},{7,6},{8,9},{9,8},{10,11... | collective-permute-start | bytes 1179656 | tf_op jit(solution)/shard_map/ppermute | solution.py:22
  109.0 10.3 %collective-permute-start.24 = (bf16[256,512]{1,0:T(8,128)(2,1)S(1)}, bf16[256,512]{1,0:T(8,128)(2,1)S(1)}, u32[]{:S(2)}, u32[]{:S(2)}) collective-permute-start(bf16[256,512]{1,0:T(8,128)(2,1)S(1)} %get-tuple-element.29.refs_0_.refs_2_), channel_id=1, source_target_pairs={{0,4},{1,5},{2,6},{3,7},{4,0},{5,1},{6,2},{7,3},{8,12},{9,13},{10,... | collective-permute-start | bytes 786440 | tf_op jit(solution)/shard_map/ppermute | solution.py:22
  109.8 19.3 %collective-permute-start.17 = (bf16[384,512]{1,0:T(8,128)(2,1)S(1)}, bf16[384,512]{1,0:T(8,128)(2,1)S(1)}, u32[]{:S(2)}, u32[]{:S(2)}) collective-permute-start(bf16[384,512]{1,0:T(8,128)(2,1)S(1)} %next_grad_1.7.refs_0_.refs_2_), channel_id=1, source_target_pairs={{0,1},{1,0},{2,3},{3,2},{4,5},{5,4},{6,7},{7,6},{8,9},{9,8},{10,11... | collective-permute-start | bytes 1179656 | tf_op jit(solution)/shard_map/ppermute | solution.py:22
  109.9 16.5 %collective-permute-start.19 = (bf16[384,512]{1,0:T(8,128)(2,1)S(1)}, bf16[384,512]{1,0:T(8,128)(2,1)S(1)}, u32[]{:S(2)}, u32[]{:S(2)}) collective-permute-start(bf16[384,512]{1,0:T(8,128)(2,1)S(1)} %get-tuple-element.26.refs_0_.refs_3_), channel_id=1, source_target_pairs={{0,2},{1,3},{2,0},{3,1},{4,6},{5,7},{6,4},{7,5},{8,10},{9,11},{10,... | collective-permute-start | bytes 1179656 | tf_op jit(solution)/shard_map/ppermute | solution.py:22
  116.6 18.3 %collective-permute-start.22 = (bf16[384,512]{1,0:T(8,128)(2,1)S(1)}, bf16[384,512]{1,0:T(8,128)(2,1)S(1)}, u32[]{:S(2)}, u32[]{:S(2)}) collective-permute-start(bf16[384,512]{1,0:T(8,128)(2,1)S(1)} %get-tuple-element.28.refs_0_.refs_1_), channel_id=1, source_target_pairs={{0,2},{1,3},{2,0},{3,1},{4,6},{5,7},{6,4},{7,5},{8,10},{9,11},{10,... | collective-permute-start | bytes 1179656 | tf_op jit(solution)/shard_map/ppermute | solution.py:22
  119.4 27.5 %collective-permute-start.28 = (bf16[256,512]{1,0:T(8,128)(2,1)S(1)}, bf16[256,512]{1,0:T(8,128)(2,1)S(1)}, u32[]{:S(2)}, u32[]{:S(2)}) collective-permute-start(bf16[256,512]{1,0:T(8,128)(2,1)S(1)} %next_grad_2.11.refs_0_.refs_1_), channel_id=1, source_target_pairs={{0,2},{1,3},{2,0},{3,1},{4,6},{5,7},{6,4},{7,5},{8,10},{9,11},{10,... | collective-permute-start | bytes 786440 | tf_op jit(solution)/shard_map/ppermute | solution.py:22
  121.8 26.4 %collective-permute-start.36 = (bf16[2,128,512]{2,1,0:T(8,128)(2,1)S(1)}, bf16[2,128,512]{2,1,0:T(8,128)(2,1)S(1)}, u32[]{:S(2)}, u32[]{:S(2)}) collective-permute-start(bf16[2,128,512]{2,1,0:T(8,128)(2,1)S(1)} %get-tuple-element.40), channel_id=1, source_target_pairs={{0,8},{8,0},{16,24},{24,16},{1,9},{9,1},{17,25},{25,17},{2,10},{10... | collective-permute-start | bytes 786440 | tf_op jit(solution)/shard_map/ppermute | solution.py:22
  126.4 19.2 %collective-permute-start.25 = (bf16[256,512]{1,0:T(8,128)(2,1)S(1)}, bf16[256,512]{1,0:T(8,128)(2,1)S(1)}, u32[]{:S(2)}, u32[]{:S(2)}) collective-permute-start(bf16[256,512]{1,0:T(8,128)(2,1)S(1)} %next_grad_2.10.refs_0_.refs_2_), channel_id=1, source_target_pairs={{0,2},{1,3},{2,0},{3,1},{4,6},{5,7},{6,4},{7,5},{8,10},{9,11},{10,... | collective-permute-start | bytes 786440 | tf_op jit(solution)/shard_map/ppermute | solution.py:22
  129.1 19.7 %collective-permute-start.37 = (bf16[2,128,512]{2,1,0:T(8,128)(2,1)S(1)}, bf16[2,128,512]{2,1,0:T(8,128)(2,1)S(1)}, u32[]{:S(2)}, u32[]{:S(2)}) collective-permute-start(bf16[2,128,512]{2,1,0:T(8,128)(2,1)S(1)} %get-tuple-element.41), channel_id=1, source_target_pairs={{0,16},{8,24},{16,0},{24,8},{1,17},{9,25},{17,1},{25,9},{2,18},{10... | collective-permute-start | bytes 786440 | tf_op jit(solution)/shard_map/ppermute | solution.py:22
  134.8 15.1 %collective-permute-start.38 = (bf16[2,128,512]{2,1,0:T(8,128)(2,1)S(1)}, bf16[2,128,512]{2,1,0:T(8,128)(2,1)S(1)}, u32[]{:S(2)}, u32[]{:S(2)}) collective-permute-start(bf16[2,128,512]{2,1,0:T(8,128)(2,1)S(1)} %get-tuple-element.42), channel_id=1, source_target_pairs={{0,24},{8,16},{16,8},{24,0},{1,25},{9,17},{17,9},{25,1},{2,26},{10... | collective-permute-start | bytes 786440 | tf_op jit(solution)/shard_map/ppermute | solution.py:22
  145.6 21.1 %collective-permute-start.23 = (bf16[384,512]{1,0:T(8,128)(2,1)S(1)}, bf16[384,512]{1,0:T(8,128)(2,1)S(1)}, u32[]{:S(2)}, u32[]{:S(2)}) collective-permute-start(bf16[384,512]{1,0:T(8,128)(2,1)S(1)} %next_grad_1.9.refs_0_.refs_1_), channel_id=1, source_target_pairs={{0,1},{1,0},{2,3},{3,2},{4,5},{5,4},{6,7},{7,6},{8,9},{9,8},{10,11... | collective-permute-start | bytes 1179656 | tf_op jit(solution)/shard_map/ppermute | solution.py:22
  146.8 15.7 %collective-permute-start.20 = (bf16[384,512]{1,0:T(8,128)(2,1)S(1)}, bf16[384,512]{1,0:T(8,128)(2,1)S(1)}, u32[]{:S(2)}, u32[]{:S(2)}) collective-permute-start(bf16[384,512]{1,0:T(8,128)(2,1)S(1)} %next_grad_1.8.refs_0_.refs_3_), channel_id=1, source_target_pairs={{0,1},{1,0},{2,3},{3,2},{4,5},{5,4},{6,7},{7,6},{8,9},{9,8},{10,11... | collective-permute-start | bytes 1179656 | tf_op jit(solution)/shard_map/ppermute | solution.py:22
  148.2 9.2 %collective-permute-start.33 = (bf16[2,128,512]{2,1,0:T(8,128)(2,1)S(1)}, bf16[2,128,512]{2,1,0:T(8,128)(2,1)S(1)}, u32[]{:S(2)}, u32[]{:S(2)}) collective-permute-start(bf16[2,128,512]{2,1,0:T(8,128)(2,1)S(1)} %get-tuple-element.36), channel_id=1, source_target_pairs={{0,8},{8,0},{16,24},{24,16},{1,9},{9,1},{17,25},{25,17},{2,10},{10... | collective-permute-start | bytes 786440 | tf_op jit(solution)/shard_map/ppermute | solution.py:22
  148.8 13.6 %collective-permute-start.34 = (bf16[2,128,512]{2,1,0:T(8,128)(2,1)S(1)}, bf16[2,128,512]{2,1,0:T(8,128)(2,1)S(1)}, u32[]{:S(2)}, u32[]{:S(2)}) collective-permute-start(bf16[2,128,512]{2,1,0:T(8,128)(2,1)S(1)} %get-tuple-element.37), channel_id=1, source_target_pairs={{0,16},{8,24},{16,0},{24,8},{1,17},{9,25},{17,1},{25,9},{2,18},{10... | collective-permute-start | bytes 786440 | tf_op jit(solution)/shard_map/ppermute | solution.py:22
  149.9 12.5 %collective-permute-start.35 = (bf16[2,128,512]{2,1,0:T(8,128)(2,1)S(1)}, bf16[2,128,512]{2,1,0:T(8,128)(2,1)S(1)}, u32[]{:S(2)}, u32[]{:S(2)}) collective-permute-start(bf16[2,128,512]{2,1,0:T(8,128)(2,1)S(1)} %get-tuple-element.38), channel_id=1, source_target_pairs={{0,24},{8,16},{16,8},{24,0},{1,25},{9,17},{17,9},{25,1},{2,26},{10... | collective-permute-start | bytes 786440 | tf_op jit(solution)/shard_map/ppermute | solution.py:22
  157.5 10.5 %collective-permute-start.29 = (bf16[256,512]{1,0:T(8,128)(2,1)S(1)}, bf16[256,512]{1,0:T(8,128)(2,1)S(1)}, u32[]{:S(2)}, u32[]{:S(2)}) collective-permute-start(bf16[256,512]{1,0:T(8,128)(2,1)S(1)} %next_grad_1.11.refs_0_.refs_1_), channel_id=1, source_target_pairs={{0,1},{1,0},{2,3},{3,2},{4,5},{5,4},{6,7},{7,6},{8,9},{9,8},{10,11... | collective-permute-start | bytes 786440 | tf_op jit(solution)/shard_map/ppermute | solution.py:22
  162.4 22.8 %collective-permute-start.41 = (bf16[128,512]{1,0:T(8,128)(2,1)S(1)}, bf16[128,512]{1,0:T(8,128)(2,1)S(1)}, u32[]{:S(2)}, u32[]{:S(2)}) collective-permute-start(bf16[128,512]{1,0:T(8,128)(2,1)S(1)} %fusion.2), channel_id=1, source_target_pairs={{0,4},{1,5},{2,6},{3,7},{4,0},{5,1},{6,2},{7,3},{8,12},{9,13},{10,... | collective-permute-start | bytes 393224 | tf_op jit(solution)/shard_map/ppermute | solution.py:22
  162.4 4.4 %collective-permute-start.26 = (bf16[256,512]{1,0:T(8,128)(2,1)S(1)}, bf16[256,512]{1,0:T(8,128)(2,1)S(1)}, u32[]{:S(2)}, u32[]{:S(2)}) collective-permute-start(bf16[256,512]{1,0:T(8,128)(2,1)S(1)} %next_grad_1.10.refs_0_.refs_2_), channel_id=1, source_target_pairs={{0,1},{1,0},{2,3},{3,2},{4,5},{5,4},{6,7},{7,6},{8,9},{9,8},{10,11... | collective-permute-start | bytes 786440 | tf_op jit(solution)/shard_map/ppermute | solution.py:22
  162.6 22.6 %collective-permute-start.40 = (bf16[128,512]{1,0:T(8,128)(2,1)S(1)}, bf16[128,512]{1,0:T(8,128)(2,1)S(1)}, u32[]{:S(2)}, u32[]{:S(2)}) collective-permute-start(bf16[128,512]{1,0:T(8,128)(2,1)S(1)} %fusion.1), channel_id=1, source_target_pairs={{0,2},{1,3},{2,0},{3,1},{4,6},{5,7},{6,4},{7,5},{8,10},{9,11},{10,... | collective-permute-start | bytes 393224 | tf_op jit(solution)/shard_map/ppermute | solution.py:22
  168.6 9.2 %collective-permute-start.30 = (bf16[2,128,512]{2,1,0:T(8,128)(2,1)S(1)}, bf16[2,128,512]{2,1,0:T(8,128)(2,1)S(1)}, u32[]{:S(2)}, u32[]{:S(2)}) collective-permute-start(bf16[2,128,512]{2,1,0:T(8,128)(2,1)S(1)} %get-tuple-element.32), channel_id=1, source_target_pairs={{0,8},{8,0},{16,24},{24,16},{1,9},{9,1},{17,25},{25,17},{2,10},{10... | collective-permute-start | bytes 786440 | tf_op jit(solution)/shard_map/ppermute | solution.py:22
  170.2 13.8 %collective-permute-start.31 = (bf16[2,128,512]{2,1,0:T(8,128)(2,1)S(1)}, bf16[2,128,512]{2,1,0:T(8,128)(2,1)S(1)}, u32[]{:S(2)}, u32[]{:S(2)}) collective-permute-start(bf16[2,128,512]{2,1,0:T(8,128)(2,1)S(1)} %get-tuple-element.33), channel_id=1, source_target_pairs={{0,16},{8,24},{16,0},{24,8},{1,17},{9,25},{17,1},{25,9},{2,18},{10... | collective-permute-start | bytes 786440 | tf_op jit(solution)/shard_map/ppermute | solution.py:22
  170.8 13.2 %collective-permute-start.32 = (bf16[2,128,512]{2,1,0:T(8,128)(2,1)S(1)}, bf16[2,128,512]{2,1,0:T(8,128)(2,1)S(1)}, u32[]{:S(2)}, u32[]{:S(2)}) collective-permute-start(bf16[2,128,512]{2,1,0:T(8,128)(2,1)S(1)} %get-tuple-element.34), channel_id=1, source_target_pairs={{0,24},{8,16},{16,8},{24,0},{1,25},{9,17},{17,9},{25,1},{2,26},{10... | collective-permute-start | bytes 786440 | tf_op jit(solution)/shard_map/ppermute | solution.py:22
  184.1 1.4 collective-permute-start.39
  (14 other events, 91.4 us)

commit v2 on v0

v2 whole, which is shorter than its diff:
```python
import math

import jax
import jax.numpy as jnp
from jax import lax
from jax.experimental import pallas as pl
from jax.experimental.pallas import tpu as pltpu
from jax.sharding import PartitionSpec as P

LEVELS = 3
TOP = LEVELS - 1
CUTS = (3, 6, 6, 7, 6, 4)
ROW_TILE = 16
VMEM_LIMIT = 24 * 1024 * 1024
WHOLE_VMEM = 60 * 1024 * 1024

ANY = pl.BlockSpec(memory_space=pl.ANY)
WHOLE = pl.BlockSpec(memory_space=pltpu.VMEM)
TOKEN = jax.ShapeDtypeStruct((8, 128), jnp.float32)


def in_hbm(array):
    return pltpu.with_memory_space_constraint(array, pltpu.HBM)


def swap(array, axis, mask):
    return lax.ppermute(array, axis, [(i, i ^ mask) for i in range(lax.axis_size(axis))])


def swap_both(array, wide_mask, narrow_mask):
    wide, narrow = lax.axis_size("wide"), lax.axis_size("narrow")
    pairs = [
        (w * narrow + i, (w ^ wide_mask) * narrow + (i ^ narrow_mask))
        for w in range(wide)
        for i in range(narrow)
    ]
    return lax.ppermute(array, ("wide", "narrow"), pairs)


def outer_sum(left, right):
    return lax.dot_general(
        left, right, (((0,), (0,)), ((), ())), preferred_element_type=jnp.float32
    )


def times_trans(left, right):
    return lax.dot_general(
        left, right, (((1,), (1,)), ((), ())), preferred_element_type=jnp.float32
    )


class Chain:
    def __init__(self):
        self.token = None

    def __call__(self, body, name, operands, in_specs, out_shape, out_specs, scratch=(), aliases=None, limit=VMEM_LIMIT, grid=1):
        n_in, n_out = len(operands), len(out_shape)
        held = [] if self.token is None else [self.token]

        def whole(*refs):
            ins = refs[:n_in]
            rest = refs[n_in + len(held) :]
            body(*ins, *rest[:n_out], *rest[n_out + 1 :])

        *outs, self.token = pl.pallas_call(
            whole,
            grid=(grid,),
            out_shape=[*out_shape, TOKEN],
            in_specs=[*in_specs] + [ANY] * len(held),
            out_specs=[*out_specs, ANY],
            scratch_shapes=list(scratch),
            input_output_aliases=aliases or {},
            compiler_params=pltpu.CompilerParams(vmem_limit_bytes=limit),
            name=name,
        )(*operands, *held)
        return outs


def row_cuts(tokens):
    unit = tokens // sum(CUTS)
    assert unit * sum(CUTS) == tokens and unit % ROW_TILE == 0
    cuts, start = [], 0
    for c in CUTS:
        cuts.append((start, c * unit))
        start += c * unit
    return cuts


def cut_out(chain, blocks, name, limit=WHOLE_VMEM):
    flat = [piece for block in blocks for piece in block]
    n = len(flat)

    def body(*refs):
        copies = []
        for b, block in enumerate(blocks):
            at = 0
            for _, where, size in block:
                j = len(copies)
                target = refs[n + b].at[pl.ds(at, size)]
                copy = pltpu.make_async_copy(where(refs[j], size), target, refs[-1].at[j])
                copy.start()
                copies.append(copy)
                at += size
        for copy in copies:
            copy.wait()

    return chain(
        body,
        name,
        [piece[0] for piece in flat],
        [ANY] * n,
        [
            jax.ShapeDtypeStruct((sum(p[2] for p in block), block[0][0].shape[-1]), block[0][0].dtype)
            for block in blocks
        ],
        [WHOLE] * len(blocks),
        [pltpu.SemaphoreType.DMA((n,))],
        limit=limit,
    )


def rows_at(start):
    return lambda ref, size: ref.at[pl.ds(start, size)]


def block_of(level):
    return lambda ref, size: ref.at[level]


def my_share(level, parts):
    def where(ref, size):
        first = pl.multiple_of(lax.axis_index("wide") % parts * size, size)
        return ref.at[level, pl.ds(first, size)]

    return where


def place_of(mask, parts):
    return lambda: (lax.axis_index("wide") ^ mask) % parts


def join_shares(chain, blocks, name):
    flat = [piece for block in blocks for piece in block]

    def body(*refs):
        ins, outs = list(refs[: len(flat)]), refs[len(flat) :]
        for out, block in zip(outs, blocks):
            for share, place in block:
                size = share.shape[0]
                out[pl.ds(pl.multiple_of(place() * size, size), size)] = ins.pop(0)[...]

    return chain(
        body,
        name,
        [share for share, _ in flat],
        [WHOLE] * len(flat),
        [
            jax.ShapeDtypeStruct((sum(a.shape[0] for a, _ in block),) + block[0][0].shape[1:], block[0][0].dtype)
            for block in blocks
        ],
        [WHOLE] * len(blocks),
    )


def next_grads(chain, w_self, jobs, name, into=None, halve=False, fetch=None, deps=()):
    width = w_self.shape[2]
    operands, in_specs, out_shape, out_specs, scratch, aliases = [], [], [], [], [], {}
    for level, grad, far, far_cross in jobs:
        operands += [w_self, far_cross, grad, far]
        in_specs += [weight_block(w_self, level), WHOLE, WHOLE, WHOLE]
    rows = [job[1].shape[0] for job in jobs]
    pieces = [size for size, job in zip(rows, jobs) if job[0] != 1]
    if halve:
        pieces = [rows[0] // 2] * 2
    for size in pieces:
        out_shape.append(jax.ShapeDtypeStruct((size, width), jnp.bfloat16))
        out_specs.append(WHOLE)
    operands += deps
    in_specs += [ANY] * len(deps)
    if into is not None:
        if not isinstance(into[0], jax.ShapeDtypeStruct):
            aliases[len(operands)] = len(out_shape)
            operands.append(in_hbm(into[0]))
            in_specs.append(ANY)
        out_shape.append(jax.ShapeDtypeStruct(into[0].shape, into[0].dtype))
        out_specs.append(ANY)
        stored = sum(size for size, job in zip(rows, jobs) if job[0] == 1)
        scratch += [pltpu.VMEM((stored, width), jnp.bfloat16), pltpu.SemaphoreType.DMA]
    if fetch is not None:
        operands.append(fetch[0])
        in_specs.append(ANY)
        out_shape.append(jax.ShapeDtypeStruct((fetch[2], fetch[0].shape[1]), fetch[0].dtype))
        out_specs.append(WHOLE)
        scratch.append(pltpu.SemaphoreType.DMA)

    def body(*refs):
        ins, outs = refs[: len(operands)], refs[len(operands) :]
        outs, scr = outs[: len(out_shape)], outs[len(out_shape) :]
        if fetch is not None:
            cut = pltpu.make_async_copy(ins[-1].at[pl.ds(*fetch[1:])], outs[-1], scr[-1])
            cut.start()
        at = 0
        for j in range(len(jobs)):
            a_ref, c_ref, grad_ref, far_ref = ins[4 * j : 4 * j + 4]
            total = times_trans(grad_ref[...], a_ref[0]) + times_trans(far_ref[...], c_ref[...])
            total = total.astype(jnp.bfloat16)
            if jobs[j][0] == 1:
                scr[0][at : at + rows[j]] = total
                at += rows[j]
            elif halve:
                outs[0][...] = total[: pieces[0]]
                outs[1][...] = total[pieces[0] :]
            else:
                outs[j][...] = total
        if into is not None:
            store = pltpu.make_async_copy(
                scr[0], outs[len(pieces)].at[pl.ds(into[1], stored)], scr[1]
            )
            store.start()
            store.wait()
        if fetch is not None:
            cut.wait()

    return chain(body, name, operands, in_specs, out_shape, out_specs, scratch, aliases)


def last_grad(chain, grad, far, w_self, far_cross):
    tokens, width = grad.shape
    steps = max(1, tokens // 512)

    def body(grad_ref, far_ref, a_ref, c_ref, out_ref):
        total = times_trans(grad_ref[...], a_ref[0]) + times_trans(far_ref[...], c_ref[0, 0])
        out_ref[...] = total.astype(jnp.bfloat16)

    rows = pl.BlockSpec((tokens // steps, width), lambda i: (i, 0))
    return chain(
        body,
        "last_grad",
        [grad, far, w_self, far_cross],
        [rows, rows, weight_block(w_self, 0), cross_block(far_cross)],
        [jax.ShapeDtypeStruct(grad.shape, grad.dtype)],
        [rows],
        grid=steps,
    )[0]


def cross_block(far_cross):
    return pl.BlockSpec((1, 1) + far_cross.shape[2:], lambda i: (other_core(), 0, 0, 0))


def other_core():
    return 1 - lax.axis_index("narrow") % 2


def both_cores(array):
    size = lax.axis_size("narrow")
    pairs = [[i, i + 1] for i in range(0, size, 2)]
    return lax.all_gather(array, "narrow", axis=0, axis_index_groups=pairs)


def weight_block(w_self, level):
    return pl.BlockSpec((1,) + w_self.shape[1:], lambda i: (level, 0, 0))


def weight_sums(chain, xs, sides, pairs, start, before, scale, last, name):
    rows = sum(g.shape[0] for g in sides[0])
    width = xs[0][0].shape[-1]
    parts = lax.axis_size("wide")
    share = width // parts
    n = len(pairs)
    operands = [x for x, _ in xs]
    in_specs = [ANY] * len(xs)
    for side in sides:
        operands += side if isinstance(side, list) else [in_hbm(side)]
        in_specs += [WHOLE] * len(side) if isinstance(side, list) else [ANY]
    if before is not None:
        operands.append(before)
        in_specs.append(WHOLE)
    buffers = [x for x, _ in xs] + [side for side in sides if not isinstance(side, list)]

    def body(*refs):
        ins, rest = list(refs[: len(operands)]), refs[len(operands) :]
        outs, scratch = rest[: len(out_shape)], rest[len(out_shape) :]
        old = None if before is None else ins.pop()
        total = scratch[-1] if last else outs[0]
        copies = []

        def fetch(source):
            j = len(copies)
            copy = pltpu.make_async_copy(source, scratch[0].at[j], scratch[1].at[j])
            copy.start()
            copies.append(copy)
            return scratch[0].at[j]

        x_bufs = [fetch(ins.pop(0).at[(*where(), pl.ds(start, rows))]) for _, where in xs]
        side_refs = []
        for side in sides:
            if isinstance(side, list):
                side_refs.append([ins.pop(0) for _ in side])
            else:
                side_refs.append([fetch(ins.pop(0).at[pl.ds(start, rows)])])
        for copy in copies:
            copy.wait()
        for j, (x, side) in enumerate(pairs):
            at = 0
            acc = None if before is None else old[j]
            for ref in side_refs[side]:
                size = ref.shape[0]
                term = outer_sum(x_bufs[x][at : at + size], ref[...])
                acc = term if acc is None else acc + term
                at += size
            total[j] = acc * scale if last else acc
        if last:
            me = lax.axis_index("wide")
            at = 0
            for b, many in enumerate(last):
                for k in range(parts):
                    there = pl.multiple_of((me ^ k) * share, share)
                    out = outs[b * parts + k]
                    out[...] = total[at : at + many, pl.ds(there, share)].astype(out.dtype)
                at += many

    whole = jax.ShapeDtypeStruct((n, width, width), jnp.float32)
    out_shape = [whole]
    if last:
        out_shape = [
            jax.ShapeDtypeStruct((many, share, width), jnp.bfloat16 if k else jnp.float32)
            for many in last
            for k in range(parts)
        ]
    scratch = [
        pltpu.VMEM((len(buffers), rows, width), buffers[0].dtype),
        pltpu.SemaphoreType.DMA((len(buffers),)),
    ]
    if last:
        scratch.append(pltpu.VMEM(whole.shape, jnp.float32))
    return chain(
        body, name, operands, in_specs, out_shape, [WHOLE] * len(out_shape), scratch
    )


def add_terms(chain, terms, name, dtypes, hold=None):
    m = len(terms)
    n = m + (hold is not None)

    def body(*refs):
        for j, dtype in enumerate(dtypes):
            total = refs[0][j].astype(jnp.float32)
            for ref in refs[1:m]:
                total = total + ref[j].astype(jnp.float32)
            refs[n + j][...] = total.astype(dtype)

    out_shape = [jax.ShapeDtypeStruct(terms[0].shape[1:], d) for d in dtypes]
    out_specs = [WHOLE] * len(dtypes)
    if hold is None:
        return chain(body, name, terms, [WHOLE] * m, out_shape, out_specs)
    return chain(
        body,
        name,
        [*terms, in_hbm(hold)],
        [WHOLE] * m + [ANY],
        [*out_shape, jax.ShapeDtypeStruct(hold.shape, hold.dtype)],
        [*out_specs, ANY],
        aliases={m: len(dtypes)},
    )


def store_levels(chain, levels, name):
    flat, spans = [], []
    for entry in levels:
        entry = entry if isinstance(entry, list) else [entry]
        spans.append((len(flat), len(entry)))
        flat += entry
    shape = flat[0].shape[-2:]

    def body(*refs):
        out = refs[len(flat)]
        for j, (first, many) in enumerate(spans):
            total = None
            for ref in refs[first : first + many]:
                value = ref[...].reshape(shape).astype(jnp.float32)
                total = value if total is None else total + value
            out[j] = total

    return chain(
        body,
        name,
        flat,
        [WHOLE] * len(flat),
        [jax.ShapeDtypeStruct((len(levels),) + shape, jnp.float32)],
        [WHOLE],
    )[0]


def local(saved_inputs, cotangent, w_self, w_cross):
    tokens, width = cotangent.shape
    parts = lax.axis_size("wide")
    share = w_cross.shape[1] // parts
    scale = 1.0 / math.sqrt(tokens * parts)
    cuts = row_cuts(tokens)
    n = len(cuts)
    z = n - 1
    end = cuts[z][0]
    far_inputs, far_cross = both_cores(saved_inputs), both_cores(w_cross)
    saved_inputs, cotangent, w_cross = in_hbm(saved_inputs), in_hbm(cotangent), in_hbm(w_cross)
    far_inputs, far_cross = in_hbm(far_inputs), in_hbm(far_cross)
    chain = Chain()
    near = [[None] * n for _ in range(LEVELS)]
    far = [[None] * n for _ in range(LEVELS)]

    def spread(terms):
        return [terms[0]] + [swap(t, "wide", k) for k, t in enumerate(terms[1:], 1)]

    def send(level, k):
        far[level][k] = [swap(a, "narrow", 1 << level) for a in near[level][k]]

    def flat(arrays):
        return [a for group in arrays for a in group]

    def at_level(level):
        return lambda: (level,)

    halves_of = min(2, parts)
    first, half_1 = cut_out(
        chain,
        [
            [(w_cross, my_share(2, parts), share), (cotangent, rows_at(0), cuts[0][1])],
            [(w_cross, my_share(1, halves_of), width // halves_of)],
        ],
        "first_rows",
    )
    first = swap(first, "narrow", 1 << 2)
    half_1 = swap(half_1, "narrow", 1 << 1)
    share_2, rows, *starts = cut_out(
        chain,
        [
            [(first, rows_at(0), share)],
            [(first, rows_at(share), cuts[0][1])],
            [(cotangent, rows_at(cuts[0][0]), cuts[0][1])],
            [(cotangent, rows_at(cuts[1][0]), cuts[1][1])],
        ],
        "parted",
        VMEM_LIMIT,
    )
    far[2][0], near[2][0], near[2][1] = [rows], [starts[0]], [starts[1]]
    send(2, 1)
    shares_2 = [(share_2, place_of(0, parts))]
    shares_2 += [(swap(share_2, "wide", k), place_of(k, parts)) for k in range(1, parts)]
    shares_1 = [(half_1, place_of(0, halves_of))]
    shares_1 += [(swap(half_1, "wide", k), place_of(k, halves_of)) for k in range(1, halves_of)]
    self_2 = weight_sums(
        chain,
        [(saved_inputs, at_level(2))],
        [[cotangent]],
        [(0, 0)],
        0,
        None,
        scale,
        (1,),
        "self_sums_2",
    )
    self_2 = spread(self_2)
    blocks = [None, None, *join_shares(chain, [shares_2], "join_2")]

    def job(level, k):
        return (level, near[level][k][0], far[level][k][0], blocks[level])

    grad = jax.ShapeDtypeStruct(cotangent.shape, cotangent.dtype)

    def level_1(k):
        jobs = [(1, a, b, blocks[1]) for a, b in zip(near[1][k], far[1][k])]
        return next_grads(chain, w_self, jobs, f"next_grads_1_{k}", (grad, cuts[k][0]))[0]

    def sums_a(ks, before, last=None):
        xs = [(saved_inputs, at_level(2)), (saved_inputs, at_level(1))]
        sides = [flat(far[2][k] for k in ks), flat(near[1][k] for k in ks)]
        start, name = cuts[ks[0]][0], f"sums_a_{ks[0]}"
        return weight_sums(chain, xs, sides, [(0, 0), (1, 1)], start, before, scale, last, name)

    def sums_b(k, before, last=None):
        xs = [(saved_inputs, at_level(1)), (saved_inputs, at_level(0))]
        xs.append((far_inputs, lambda: (other_core(), 0)))
        pairs = [(0, 0), (1, 1), (2, 1)]
        start, name = cuts[k][0], f"sums_b_{k}"
        return weight_sums(
            chain, xs, [far[1][k], grad], pairs, start, before, scale, last, name
        )

    sum_a = sum_b = None
    for k in range(n):
        ahead = k + 2
        done = next_grads(
            chain,
            w_self,
            [job(2, k)] + ([job(1, 0)] if k == 1 else []),
            f"next_grads_{k}",
            (grad, 0) if k == 1 else None,
            False,
            (cotangent, *cuts[ahead]) if ahead < n else None,
        )
        if ahead < n:
            near[2][ahead] = [done.pop()]
            send(2, ahead)
        if k == 1:
            grad = done.pop()
        near[1][k] = done
        send(1, k)
        if k == 0:
            (self_2,) = add_terms(chain, self_2, "add_self_2", (jnp.float32,))
            (blocks[1],) = join_shares(chain, [shares_1], "join_1")
        if 2 <= k < z:
            grad = level_1(k - 1) if k < z - 1 else grad
        if 1 <= k < z - 1:
            (sum_b,) = sums_b(k - 1, sum_b)
        if 1 <= k < z:
            (sum_a,) = sums_a([0, 1] if k == 1 else [k], sum_a)
    sum_a = spread(sums_a([z], sum_a, (2,)))
    for k in (z - 2, z - 1):
        grad = level_1(k)
        (sum_b,) = sums_b(k, sum_b)
    grad = level_1(z)
    sum_b = spread(sums_b(z, sum_b, (3,)))
    cross_2, self_1, grad = add_terms(chain, sum_a, "add_a", (jnp.bfloat16, jnp.float32), grad)
    cross_2 = swap(cross_2, "narrow", 1 << 2)
    far_grad = swap(grad, "narrow", 1 << 0)
    out = last_grad(chain, grad, far_grad, w_self, far_cross)
    cross_1, self_0, cross_0 = add_terms(
        chain, sum_b, "add_b", (jnp.bfloat16, jnp.float32, jnp.float32)
    )
    cross_1 = swap(cross_1, "narrow", 1 << 1)
    grad_self = store_levels(chain, [self_0, self_1, self_2], "store_self")
    grad_cross = store_levels(chain, [cross_0, cross_1, cross_2], "store_cross")
    return out, grad_self, grad_cross


def solution(mesh):
    in_specs = (
        P(None, "wide", "narrow"),
        P("wide", "narrow"),
        P(None, "narrow", None),
        P(None, "narrow", None),
    )
    out_specs = (
        P("wide", "narrow"),
        P(None, ("narrow", "wide"), None),
        P(None, ("narrow", "wide"), None),
    )
    return jax.shard_map(local, mesh=mesh, in_specs=in_specs, out_specs=out_specs, check_vma=False)
```

time: 308 us -> 178 us (0.58)
  waiting for transfers between devices: 230 us -> 60.3 us
  Pallas kernels: 0 us -> 61.3 us
  matrix products: 44.2 us -> 0 us
  starting transfers between devices: 10.4 us -> 35.9 us
    ppermute x9 -> x29, waiting for transfers between devices: 161 us -> 59.5 us  [swap(): lax.ppermute(array, axis, [(i, i ^ mask) for i in range(lax.axis_size(axi...]
    reduce_scatter x6 -> x0, waiting for transfers between devices: 68.6 us -> none  [the longest x3 57.5 us: wide_sum(): lax.psum_scatter(pair[1], 'wide', scatter_dimension=1, tiled=True)]
    pallas_call x0 -> x33, Pallas kernels: none -> 61.3 us  [__call__(): pl.pallas_call(whole, grid=(grid,), out_shape=[*out_shape, TOKEN], in_spe...]
    dot_general x12 -> x0, matrix products: 44.2 us -> none  [the longest x6 25.3 us: outer_sum(): lax.dot_general(left, right, (((0,), (0,)), ((), ())), preferred_element_...]
    ppermute x9 -> x29, starting transfers between devices: 9.98 us -> 35.9 us  [swap(): lax.ppermute(array, axis, [(i, i ^ mask) for i in range(lax.axis_size(axi...]
  transfers between devices with their start and end apart: 15 -> 31, of which waited for: 6 -> 13; matrix products, arithmetic and copies ran while one was open for 15% -> 0% of each run, Pallas kernels for 0% -> 34%
where the time goes in v2:
time: 178 us; the launch traced here: 177 us
  Pallas kernels  61.3 us (34%)
  waiting for transfers between devices  60.3 us (34%)
  starting transfers between devices  35.9 us (20%)
  between operations  14.5 us (8%)
  local copies, waits for them, and re-layouts  5.26 us (3%)
    pallas_call x33, Pallas kernels, __call__(): pl.pallas_call(whole, grid=(grid,), out_shape=[*out_shape, TOKEN], in_spe...  61.3 us
    ppermute x29, waiting for transfers between devices, swap(): lax.ppermute(array, axis, [(i, i ^ mask) for i in range(lax.axis_size(axi...  59.5 us
    ppermute x29, starting transfers between devices, swap(): lax.ppermute(array, axis, [(i, i ^ mask) for i in range(lax.axis_size(axi...  35.9 us
    unnamed x32, local copies, waits for them, and re-layouts  5.26 us
  transfers between devices with their start and end apart: 31, of which 13 were waited for; matrix products, arithmetic and copies ran while one was open for 0% of the time, Pallas kernels for 34%

profile of v2, /device:TPU:0, one launch (start us, length us, event | category | flops | bytes accessed | tf_op | source)
XLA Modules:
  0.0 177.2 jit_solution(11116750739074734676)
XLA Ops:
  7.9 2.0 %first_rows.1 = (bf16[320,512]{1,0:T(8,128)(2,1)}, bf16[256,512]{1,0:T(8,128)(2,1)}, f32[8,128]{1,0:T(8,128)}) custom-call(bf16[3,512,512]{2,1,0:T(8,128)(2,1)} %refs_2_.3, bf16[2048,512]{1,0:T(8,128)(2,1)} %refs_4_.7, bf16[3,512,512]{2,1,0:T(8,128)(2,1)} %refs_2_.3), custom_call_target="tpu_custom_call" | custom-call | tf_op jit(solution)/shard_map/first_rows/pallas_call | solution.py:65
  9.9 4.1 %collective-permute-start = (bf16[320,512]{1,0:T(8,128)(2,1)}, bf16[320,512]{1,0:T(8,128)(2,1)S(1)}, u32[]{:S(2)}, u32[]{:S(2)}) collective-permute-start(bf16[320,512]{1,0:T(8,128)(2,1)} %get-tuple-element.90), channel_id=1, source_target_pairs={{0,4},{1,5},{2,6},{3,7},{4,0},{5,1},{6,2},{7,3},{8,12},{9,13},{10,... | collective-permute-start | bytes 983048 | tf_op jit(solution)/shard_map/ppermute | solution.py:27
  14.0 1.6 collective-permute-start.5
  15.6 13.4 %collective-permute-done.refs_0_.refs_1_ = bf16[320,512]{1,0:T(8,128)(2,1)S(1)} collective-permute-done((bf16[320,512]{1,0:T(8,128)(2,1)}, bf16[320,512]{1,0:T(8,128)(2,1)S(1)}, u32[]{:S(2)}, u32[]{:S(2)}) %collective-permute-start) | collective-permute-done | bytes 327712 | tf_op jit(solution)/shard_map/ppermute | solution.py:27
  29.7 1.5 parted.1
  31.2 1.7 collective-permute-start.1
  32.9 1.5 collective-permute-start.2
  34.8 4.6 %self_sums_2.1 = (f32[1,128,512]{2,1,0:T(8,128)S(1)}, bf16[1,128,512]{2,1,0:T(8,128)(2,1)S(1)}, bf16[1,128,512]{2,1,0:T(8,128)(2,1)S(1)}, bf16[1,128,512]{2,1,0:T(8,128)(2,1)S(1)}, f32[8,128]{1,0:T(8,128)S(1)}) custom-call(bf16[3,2048,512]{2,1,0:T(8,128)(2,1)} %refs_1_.25, bf16[2048,512]{1,0:T(8,128)(2,1)} %refs_4_.7, f32[8,128]{1,0:T(8,128)S(1)} %get-tuple-element.93.refs_2_), custom_call_target="tpu_custom_call" | custom-call | tf_op jit(solution)/shard_map/self_sums_2/pallas_call | solution.py:65
  39.4 1.7 collective-permute-start.7
  41.6 1.9 %next_grads_0.1 = (bf16[192,512]{1,0:T(8,128)(2,1)S(1)}, bf16[384,512]{1,0:T(8,128)(2,1)}, f32[8,128]{1,0:T(8,128)S(1)}) custom-call(bf16[3,512,512]{2,1,0:T(8,128)(2,1)S(1)} %copy-done.2, bf16[512,512]{1,0:T(8,128)(2,1)S(1)} %get-tuple-element.95.refs_1_, bf16[192,512]{1,0:T(8,128)(2,1)S(1)} %get-tuple-element.102.refs_2_, ...), custom_call_target="tpu_custom_call" | custom-call | tf_op jit(solution)/shard_map/next_grads_0/pallas_call | solution.py:65
  43.5 4.2 %collective-permute-start.10 = (bf16[192,512]{1,0:T(8,128)(2,1)S(1)}, bf16[192,512]{1,0:T(8,128)(2,1)S(1)}, u32[]{:S(2)}, u32[]{:S(2)}) collective-permute-start(bf16[192,512]{1,0:T(8,128)(2,1)S(1)} %get-tuple-element.108.refs_6_.refs_4_), channel_id=1, source_target_pairs={{0,2},{1,3},{2,0},{3,1},{4,6},{5,7},{6,4},{7,5},{8,10},{9,11},{10,... | collective-permute-start | bytes 589832 | tf_op jit(solution)/shard_map/ppermute | solution.py:27
  47.7 1.5 collective-permute-start.8
  49.2 1.4 collective-permute-start.9
  50.6 2.7 %collective-permute-done.8.refs_2_ = bf16[1,128,512]{2,1,0:T(8,128)(2,1)S(1)} collective-permute-done((bf16[1,128,512]{2,1,0:T(8,128)(2,1)S(1)}, bf16[1,128,512]{2,1,0:T(8,128)(2,1)S(1)}, u32[]{:S(2)}, u32[]{:S(2)}) %collective-permute-start.8) | collective-permute-done | bytes 131104 | tf_op jit(solution)/shard_map/ppermute | solution.py:27
  56.4 2.5 %next_grads_1.1 = (bf16[384,512]{1,0:T(8,128)(2,1)}, bf16[2048,512]{1,0:T(8,128)(2,1)S(1)}, bf16[448,512]{1,0:T(8,128)(2,1)}, f32[8,128]{1,0:T(8,128)S(1)}) custom-call(bf16[3,512,512]{2,1,0:T(8,128)(2,1)S(1)} %copy-done.2, bf16[512,512]{1,0:T(8,128)(2,1)S(1)} %get-tuple-element.95.refs_1_, bf16[384,512]{1,0:T(8,128)(2,1)S(1)} %get-tuple-element.96.refs_2_, ...), custom_call_target="tpu_custom_call" | custom-call | tf_op jit(solution)/shard_map/next_grads_1/pallas_call | solution.py:65
  61.0 2.5 %collective-permute-start.13 = (bf16[384,512]{1,0:T(8,128)(2,1)}, bf16[384,512]{1,0:T(8,128)(2,1)S(1)}, u32[]{:S(2)}, u32[]{:S(2)}) collective-permute-start(bf16[384,512]{1,0:T(8,128)(2,1)} %get-tuple-element.112.refs_5_.refs_2_), channel_id=1, source_target_pairs={{0,2},{1,3},{2,0},{3,1},{4,6},{5,7},{6,4},{7,5},{8,10},{9,11},{10,... | collective-permute-start | bytes 1179656 | tf_op jit(solution)/shard_map/ppermute | solution.py:27
  64.4 1.9 %sums_b_0.1 = (f32[3,512,512]{2,1,0:T(8,128)S(1)}, f32[8,128]{1,0:T(8,128)S(1)}) custom-call(bf16[3,2048,512]{2,1,0:T(8,128)(2,1)} %refs_1_.25, bf16[3,2048,512]{2,1,0:T(8,128)(2,1)} %refs_1_.25, bf16[2,3,2048,512]{3,2,1,0:T(8,128)(2,1)} %bitcast.2, bf16[192,512]{1,0:T(8,128)(2,1)S(1)} %copy-done.6, bf16[2048,512]{1,0:T(8,128)(2,1)} %copy-done, ...), custom_call_target="tpu_custom_call" | custom-call | tf_op jit(solution)/shard_map/sums_b_0/pallas_call | solution.py:65
  66.4 3.4 %sums_a_0.1 = (f32[2,512,512]{2,1,0:T(8,128)S(1)}, f32[8,128]{1,0:T(8,128)S(1)}) custom-call(bf16[3,2048,512]{2,1,0:T(8,128)(2,1)} %refs_1_.25, bf16[3,2048,512]{2,1,0:T(8,128)(2,1)} %refs_1_.25, bf16[192,512]{1,0:T(8,128)(2,1)S(1)} %copy-done.8, bf16[384,512]{1,0:T(8,128)(2,1)S(1)} %copy-done.4, bf16[192,512]{1,0:T(8,128)(2,1)S(1)} %copy-done.10, ...), custom_call_target="tpu_custom_call" | custom-call | tf_op jit(solution)/shard_map/sums_a_0/pallas_call | solution.py:65
  69.8 10.5 %collective-permute-done.12.refs_3_.refs_2_ = bf16[384,512]{1,0:T(8,128)(2,1)} collective-permute-done((bf16[384,512]{1,0:T(8,128)(2,1)}, bf16[384,512]{1,0:T(8,128)(2,1)}, u32[]{:S(2)}, u32[]{:S(2)}) %collective-permute-start.12) | collective-permute-done | bytes 393248 | tf_op jit(solution)/shard_map/ppermute | solution.py:27
  80.3 2.1 %next_grads_2.1 = (bf16[384,512]{1,0:T(8,128)(2,1)S(1)}, bf16[384,512]{1,0:T(8,128)(2,1)S(1)}, f32[8,128]{1,0:T(8,128)S(1)}) custom-call(bf16[3,512,512]{2,1,0:T(8,128)(2,1)S(1)} %copy-done.2, bf16[512,512]{1,0:T(8,128)(2,1)S(1)} %get-tuple-element.95.refs_1_, bf16[384,512]{1,0:T(8,128)(2,1)} %get-tuple-element.111.refs_2_, ...), custom_call_target="tpu_custom_call" | custom-call | tf_op jit(solution)/shard_map/next_grads_2/pallas_call | solution.py:65
  82.5 2.3 %collective-permute-start.15 = (bf16[384,512]{1,0:T(8,128)(2,1)S(1)}, bf16[384,512]{1,0:T(8,128)(2,1)S(1)}, u32[]{:S(2)}, u32[]{:S(2)}) collective-permute-start(bf16[384,512]{1,0:T(8,128)(2,1)S(1)} %get-tuple-element.126.refs_2_), channel_id=1, source_target_pairs={{0,4},{1,5},{2,6},{3,7},{4,0},{5,1},{6,2},{7,3},{8,12},{9,13},{10,... | collective-permute-start | bytes 1179656 | tf_op jit(solution)/shard_map/ppermute | solution.py:27
  84.9 2.4 %next_grads_1_1.1 = (bf16[2048,512]{1,0:T(8,128)(2,1)}, f32[8,128]{1,0:T(8,128)S(1)}) custom-call(bf16[3,512,512]{2,1,0:T(8,128)(2,1)S(1)} %copy-done.2, bf16[512,512]{1,0:T(8,128)(2,1)S(1)} %get-tuple-element.107.refs_5_.refs_1_, bf16[384,512]{1,0:T(8,128)(2,1)} %get-tuple-element.112.refs_5_.refs_2_, ...), custom_call_target="tpu_custom_call", output_to_operand_aliasing={{0}: (4, {})} | custom-call | tf_op jit(solution)/shard_map/next_grads_1_1/pallas_call | solution.py:65
  87.2 2.4 %sums_b_1.1 = (f32[3,512,512]{2,1,0:T(8,128)S(1)}, f32[8,128]{1,0:T(8,128)S(1)}) custom-call(bf16[3,2048,512]{2,1,0:T(8,128)(2,1)} %refs_1_.25, bf16[3,2048,512]{2,1,0:T(8,128)(2,1)} %refs_1_.25, bf16[2,3,2048,512]{3,2,1,0:T(8,128)(2,1)} %bitcast.3, bf16[384,512]{1,0:T(8,128)(2,1)S(1)} %collective-permute-done.13.refs_3_, ...), custom_call_target="tpu_custom_call" | custom-call | tf_op jit(solution)/shard_map/sums_b_1/pallas_call | solution.py:65
  89.6 2.9 %sums_a_2.1 = (f32[2,512,512]{2,1,0:T(8,128)S(1)}, f32[8,128]{1,0:T(8,128)S(1)}) custom-call(bf16[3,2048,512]{2,1,0:T(8,128)(2,1)} %refs_1_.25, bf16[3,2048,512]{2,1,0:T(8,128)(2,1)} %refs_1_.25, bf16[384,512]{1,0:T(8,128)(2,1)} %collective-permute-done.12.refs_3_.refs_2_, bf16[384,512]{1,0:T(8,128)(2,1)S(1)} %get-tuple-element.117.refs_3_.refs_2_, ...), custom_call_target="tpu_custom_call" | custom-call | tf_op jit(solution)/shard_map/sums_a_2/pallas_call | solution.py:65
  92.5 2.0 %next_grads_3.1 = (bf16[448,512]{1,0:T(8,128)(2,1)S(1)}, bf16[256,512]{1,0:T(8,128)(2,1)S(1)}, f32[8,128]{1,0:T(8,128)S(1)}) custom-call(bf16[3,512,512]{2,1,0:T(8,128)(2,1)S(1)} %copy-done.2, bf16[512,512]{1,0:T(8,128)(2,1)S(1)} %get-tuple-element.95.refs_1_, bf16[448,512]{1,0:T(8,128)(2,1)} %get-tuple-element.110.refs_2_, ...), custom_call_target="tpu_custom_call" | custom-call | tf_op jit(solution)/shard_map/next_grads_3/pallas_call | solution.py:65
  94.6 2.5 %collective-permute-start.14 = (bf16[256,512]{1,0:T(8,128)(2,1)S(1)}, bf16[256,512]{1,0:T(8,128)(2,1)S(1)}, u32[]{:S(2)}, u32[]{:S(2)}) collective-permute-start(bf16[256,512]{1,0:T(8,128)(2,1)S(1)} %get-tuple-element.125.refs_2_), channel_id=1, source_target_pairs={{0,4},{1,5},{2,6},{3,7},{4,0},{5,1},{6,2},{7,3},{8,12},{9,13},{10,... | collective-permute-start | bytes 786440 | tf_op jit(solution)/shard_map/ppermute | solution.py:27
  97.2 5.7 %collective-permute-done.16.refs_3_ = bf16[384,512]{1,0:T(8,128)(2,1)S(1)} collective-permute-done((bf16[384,512]{1,0:T(8,128)(2,1)S(1)}, bf16[384,512]{1,0:T(8,128)(2,1)S(1)}, u32[]{:S(2)}, u32[]{:S(2)}) %collective-permute-start.16) | collective-permute-done | bytes 393248 | tf_op jit(solution)/shard_map/ppermute | solution.py:27
  102.9 1.4 next_grads_1_2.1
  104.2 2.4 %sums_b_2.1 = (f32[3,512,512]{2,1,0:T(8,128)S(1)}, f32[8,128]{1,0:T(8,128)S(1)}) custom-call(bf16[3,2048,512]{2,1,0:T(8,128)(2,1)} %refs_1_.25, bf16[3,2048,512]{2,1,0:T(8,128)(2,1)} %refs_1_.25, bf16[2,3,2048,512]{3,2,1,0:T(8,128)(2,1)} %bitcast.4, bf16[384,512]{1,0:T(8,128)(2,1)S(1)} %collective-permute-done.16.refs_3_, ...), custom_call_target="tpu_custom_call" | custom-call | tf_op jit(solution)/shard_map/sums_b_2/pallas_call | solution.py:65
  106.6 1.9 %sums_a_3.1 = (f32[2,512,512]{2,1,0:T(8,128)S(1)}, f32[8,128]{1,0:T(8,128)S(1)}) custom-call(bf16[3,2048,512]{2,1,0:T(8,128)(2,1)} %refs_1_.25, bf16[3,2048,512]{2,1,0:T(8,128)(2,1)} %refs_1_.25, bf16[448,512]{1,0:T(8,128)(2,1)S(1)} %collective-permute-done.11.refs_3_.refs_2_, bf16[448,512]{1,0:T(8,128)(2,1)S(1)} %get-tuple-element.127.refs_3_.refs_2_, ...), custom_call_target="tpu_custom_call" | custom-call | tf_op jit(solution)/shard_map/sums_a_3/pallas_call | solution.py:65
  109.3 1.9 %sums_a_4.1 = (f32[2,512,512]{2,1,0:T(8,128)S(1)}, f32[8,128]{1,0:T(8,128)S(1)}) custom-call(bf16[3,2048,512]{2,1,0:T(8,128)(2,1)} %refs_1_.25, bf16[3,2048,512]{2,1,0:T(8,128)(2,1)} %refs_1_.25, bf16[384,512]{1,0:T(8,128)(2,1)S(1)} %collective-permute-done.15.refs_3_.refs_2_, bf16[384,512]{1,0:T(8,128)(2,1)S(1)} %get-tuple-element.135.refs_3_.refs_2_, ...), custom_call_target="tpu_custom_call" | custom-call | tf_op jit(solution)/shard_map/sums_a_4/pallas_call | solution.py:65
  111.1 6.8 %collective-permute-done.14.refs_3_.refs_2_ = bf16[256,512]{1,0:T(8,128)(2,1)S(1)} collective-permute-done((bf16[256,512]{1,0:T(8,128)(2,1)S(1)}, bf16[256,512]{1,0:T(8,128)(2,1)S(1)}, u32[]{:S(2)}, u32[]{:S(2)}) %collective-permute-start.14) | collective-permute-done | bytes 262176 | tf_op jit(solution)/shard_map/ppermute | solution.py:27
  119.4 1.6 sums_a_5.1
  121.0 1.6 collective-permute-start.17
  122.6 2.5 %collective-permute-start.18 = (bf16[2,128,512]{2,1,0:T(8,128)(2,1)S(1)}, bf16[2,128,512]{2,1,0:T(8,128)(2,1)S(1)}, u32[]{:S(2)}, u32[]{:S(2)}) collective-permute-start(bf16[2,128,512]{2,1,0:T(8,128)(2,1)S(1)} %get-tuple-element.144), channel_id=1, source_target_pairs={{0,16},{8,24},{16,0},{24,8},{1,17},{9,25},{17,1},{25,9},{2,18},{10... | collective-permute-start | bytes 786440 | tf_op jit(solution)/shard_map/ppermute | solution.py:27
  125.1 1.4 next_grads_1_3.1
  126.6 2.5 %sums_b_3.1 = (f32[3,512,512]{2,1,0:T(8,128)S(1)}, f32[8,128]{1,0:T(8,128)S(1)}) custom-call(bf16[3,2048,512]{2,1,0:T(8,128)(2,1)} %refs_1_.25, bf16[3,2048,512]{2,1,0:T(8,128)(2,1)} %refs_1_.25, bf16[2,3,2048,512]{3,2,1,0:T(8,128)(2,1)} %bitcast.5, bf16[448,512]{1,0:T(8,128)(2,1)S(1)} %collective-permute-done.22.refs_3_, ...), custom_call_target="tpu_custom_call" | custom-call | tf_op jit(solution)/shard_map/sums_b_3/pallas_call | solution.py:65
  129.1 1.7 collective-permute-done.21.refs_3_
  132.1 2.4 %sums_b_4.1 = (f32[3,512,512]{2,1,0:T(8,128)S(1)}, f32[8,128]{1,0:T(8,128)S(1)}) custom-call(bf16[3,2048,512]{2,1,0:T(8,128)(2,1)} %refs_1_.25, bf16[3,2048,512]{2,1,0:T(8,128)(2,1)} %refs_1_.25, bf16[2,3,2048,512]{3,2,1,0:T(8,128)(2,1)} %bitcast.6, bf16[384,512]{1,0:T(8,128)(2,1)S(1)} %collective-permute-done.21.refs_3_, ...), custom_call_target="tpu_custom_call" | custom-call | tf_op jit(solution)/shard_map/sums_b_4/pallas_call | solution.py:65
  134.6 1.8 collective-permute-done.20.refs_3_
  137.5 3.0 %sums_b_5.1 = (f32[3,128,512]{2,1,0:T(8,128)S(1)}, bf16[3,128,512]{2,1,0:T(8,128)(2,1)}, bf16[3,128,512]{2,1,0:T(8,128)(2,1)}, bf16[3,128,512]{2,1,0:T(8,128)(2,1)}, f32[8,128]{1,0:T(8,128)S(1)}) custom-call(bf16[3,2048,512]{2,1,0:T(8,128)(2,1)} %refs_1_.25, bf16[3,2048,512]{2,1,0:T(8,128)(2,1)} %refs_1_.25, bf16[2,3,2048,512]{3,2,1,0:T(8,128)(2,1)} %bitcast.7, ...), custom_call_target="tpu_custom_call" | custom-call | tf_op jit(solution)/shard_map/sums_b_5/pallas_call | solution.py:65
  142.0 1.5 collective-permute-start.24
  143.5 1.5 collective-permute-start.25
  146.5 1.6 copy-done.1
  148.1 5.7 %last_grad.1 = (bf16[2048,512]{1,0:T(8,128)(2,1)}, f32[8,128]{1,0:T(8,128)S(1)}) custom-call(bf16[2048,512]{1,0:T(8,128)(2,1)S(1)} %copy-done.1, bf16[2048,512]{1,0:T(8,128)(2,1)} %collective-permute-done.23.refs_1_, bf16[3,512,512]{2,1,0:T(8,128)(2,1)S(1)} %copy-done.2, bf16[2,3,512,512]{3,2,1,0:T(8,128)(2,1)} %bitcast.8, ...), custom_call_target="tpu_custom_call" | custom-call | tf_op jit(solution)/shard_map/last_grad/pallas_call | solution.py:65
  154.1 9.2 %collective-permute-done.25.refs_2_ = bf16[3,128,512]{2,1,0:T(8,128)(2,1)S(1)} collective-permute-done((bf16[3,128,512]{2,1,0:T(8,128)(2,1)}, bf16[3,128,512]{2,1,0:T(8,128)(2,1)S(1)}, u32[]{:S(2)}, u32[]{:S(2)}) %collective-permute-start.25) | collective-permute-done | bytes 393248 | tf_op jit(solution)/shard_map/ppermute | solution.py:27
  164.5 4.0 %collective-permute-done.27.refs_1_ = bf16[128,512]{1,0:T(8,128)(2,1)S(1)} collective-permute-done((bf16[128,512]{1,0:T(8,128)(2,1)S(1)}, bf16[128,512]{1,0:T(8,128)(2,1)S(1)}, u32[]{:S(2)}, u32[]{:S(2)}) %collective-permute-start.27) | collective-permute-done | bytes 131104 | tf_op jit(solution)/shard_map/ppermute | solution.py:27
  168.5 1.8 %store_cross.1 = (f32[3,128,512]{2,1,0:T(8,128)}, f32[8,128]{1,0:T(8,128)}) custom-call(f32[128,512]{1,0:T(8,128)S(1)} %get-tuple-element.172.refs_0_, bf16[128,512]{1,0:T(8,128)(2,1)S(1)} %collective-permute-done.27.refs_1_, bf16[128,512]{1,0:T(8,128)(2,1)} %collective-permute-done.28.refs_2_, f32[8,128]{1,0:T(8,128)S(1)} %get-tuple-element.175.refs_3_), custom_call_target="tpu_custom_call" | custom-call | tf_op jit(solution)/shard_map/store_cross/pallas_call | solution.py:65
  (81 shorter events, 17.7 us)
Async XLA Ops:
  7.2 56.3 %all-gather.5.cloned.1.call-start = ((), (), s32[]{:S(2)}) async-start(), calls=%async_computation | async-start | bytes 18874368 | tf_op jit(solution)/shard_map/all_gather | solution.py:258
  7.9 137.6 %all-gather.7.cloned.1.call-start = ((), (), s32[]{:S(2)}) async-start(), calls=%async_computation.1 | async-start | bytes 4718592 | tf_op jit(solution)/shard_map/all_gather | solution.py:258
  9.9 19.0 %collective-permute-start = (bf16[320,512]{1,0:T(8,128)(2,1)}, bf16[320,512]{1,0:T(8,128)(2,1)S(1)}, u32[]{:S(2)}, u32[]{:S(2)}) collective-permute-start(bf16[320,512]{1,0:T(8,128)(2,1)} %get-tuple-element.90), channel_id=1, source_target_pairs={{0,4},{1,5},{2,6},{3,7},{4,0},{5,1},{6,2},{7,3},{8,12},{9,13},{10,... | collective-permute-start | bytes 983048 | tf_op jit(solution)/shard_map/ppermute | solution.py:27
  14.0 25.4 %collective-permute-start.5 = (bf16[256,512]{1,0:T(8,128)(2,1)}, bf16[256,512]{1,0:T(8,128)(2,1)S(1)}, u32[]{:S(2)}, u32[]{:S(2)}) collective-permute-start(bf16[256,512]{1,0:T(8,128)(2,1)} %get-tuple-element.97), channel_id=1, source_target_pairs={{0,2},{1,3},{2,0},{3,1},{4,6},{5,7},{6,4},{7,5},{8,10},{9,11},{10,... | collective-permute-start | bytes 786440 | tf_op jit(solution)/shard_map/ppermute | solution.py:27
  29.0 0.7 copy-start.15
  31.2 10.4 %copy-start.7 = (bf16[192,512]{1,0:T(8,128)(2,1)}, bf16[192,512]{1,0:T(8,128)(2,1)S(1)}, u32[]{:S(2)}) copy-start(bf16[192,512]{1,0:T(8,128)(2,1)S(1)} %get-tuple-element.103.refs_3_.refs_2_) | copy-start | bytes 589828
  31.2 9.9 %collective-permute-start.1 = (bf16[128,512]{1,0:T(8,128)(2,1)S(1)}, bf16[128,512]{1,0:T(8,128)(2,1)S(1)}, u32[]{:S(2)}, u32[]{:S(2)}) collective-permute-start(bf16[128,512]{1,0:T(8,128)(2,1)S(1)} %get-tuple-element.92.refs_0_), channel_id=1, source_target_pairs={{0,8},{8,0},{16,24},{24,16},{1,9},{9,1},{17,25},{25,17},{2,10},{10... | collective-permute-start | bytes 393224 | tf_op jit(solution)/shard_map/ppermute | solution.py:27
  32.9 23.5 %collective-permute-start.4 = (bf16[384,512]{1,0:T(8,128)(2,1)S(1)}, bf16[384,512]{1,0:T(8,128)(2,1)S(1)}, u32[]{:S(2)}, u32[]{:S(2)}) collective-permute-start(bf16[384,512]{1,0:T(8,128)(2,1)S(1)} %get-tuple-element.96.refs_2_), channel_id=1, source_target_pairs={{0,4},{1,5},{2,6},{3,7},{4,0},{5,1},{6,2},{7,3},{8,12},{9,13},{10,... | collective-permute-start | bytes 1179656 | tf_op jit(solution)/shard_map/ppermute | solution.py:27
  32.9 8.6 %collective-permute-start.2 = (bf16[128,512]{1,0:T(8,128)(2,1)S(1)}, bf16[128,512]{1,0:T(8,128)(2,1)S(1)}, u32[]{:S(2)}, u32[]{:S(2)}) collective-permute-start(bf16[128,512]{1,0:T(8,128)(2,1)S(1)} %get-tuple-element.92.refs_0_), channel_id=1, source_target_pairs={{0,16},{8,24},{16,0},{24,8},{1,17},{9,25},{17,1},{25,9},{2,18},{10... | collective-permute-start | bytes 393224 | tf_op jit(solution)/shard_map/ppermute | solution.py:27
  34.4 7.2 %collective-permute-start.3 = (bf16[128,512]{1,0:T(8,128)(2,1)S(1)}, bf16[128,512]{1,0:T(8,128)(2,1)S(1)}, u32[]{:S(2)}, u32[]{:S(2)}) collective-permute-start(bf16[128,512]{1,0:T(8,128)(2,1)S(1)} %get-tuple-element.92.refs_0_), channel_id=1, source_target_pairs={{0,24},{8,16},{16,8},{24,0},{1,25},{9,17},{17,9},{25,1},{2,26},{10... | collective-permute-start | bytes 393224 | tf_op jit(solution)/shard_map/ppermute | solution.py:27
  34.8 6.8 %copy-start.2 = (bf16[3,512,512]{2,1,0:T(8,128)(2,1)S(1)}, bf16[3,512,512]{2,1,0:T(8,128)(2,1)}, u32[]{:S(2)}) copy-start(bf16[3,512,512]{2,1,0:T(8,128)(2,1)} %refs_2_.5) | copy-start | bytes 4718596
  39.4 9.8 %collective-permute-start.7 = (bf16[1,128,512]{2,1,0:T(8,128)(2,1)S(1)}, bf16[1,128,512]{2,1,0:T(8,128)(2,1)S(1)}, u32[]{:S(2)}, u32[]{:S(2)}) collective-permute-start(bf16[1,128,512]{2,1,0:T(8,128)(2,1)S(1)} %get-tuple-element.99), channel_id=1, source_target_pairs={{0,8},{8,0},{16,24},{24,16},{1,9},{9,1},{17,25},{25,17},{2,10},{10... | collective-permute-start | bytes 393224 | tf_op jit(solution)/shard_map/ppermute | solution.py:27
  41.1 14.0 %collective-permute-start.6 = (bf16[256,512]{1,0:T(8,128)(2,1)S(1)}, bf16[256,512]{1,0:T(8,128)(2,1)S(1)}, u32[]{:S(2)}, u32[]{:S(2)}) collective-permute-start(bf16[256,512]{1,0:T(8,128)(2,1)S(1)} %collective-permute-done.5.refs_0_), channel_id=1, source_target_pairs={{0,8},{8,0},{16,24},{24,16},{1,9},{9,1},{17,25},{25,17},{2,10},{10... | collective-permute-start | bytes 786440 | tf_op jit(solution)/shard_map/ppermute | solution.py:27
  43.5 15.4 %copy-start.9 = (bf16[192,512]{1,0:T(8,128)(2,1)}, bf16[192,512]{1,0:T(8,128)(2,1)S(1)}, u32[]{:S(2)}) copy-start(bf16[192,512]{1,0:T(8,128)(2,1)S(1)} %get-tuple-element.108.refs_6_.refs_4_) | copy-start | bytes 589828
  43.5 12.9 %collective-permute-start.10 = (bf16[192,512]{1,0:T(8,128)(2,1)S(1)}, bf16[192,512]{1,0:T(8,128)(2,1)S(1)}, u32[]{:S(2)}, u32[]{:S(2)}) collective-permute-start(bf16[192,512]{1,0:T(8,128)(2,1)S(1)} %get-tuple-element.108.refs_6_.refs_4_), channel_id=1, source_target_pairs={{0,2},{1,3},{2,0},{3,1},{4,6},{5,7},{6,4},{7,5},{8,10},{9,11},{10,... | collective-permute-start | bytes 589832 | tf_op jit(solution)/shard_map/ppermute | solution.py:27
  47.7 5.7 %collective-permute-start.8 = (bf16[1,128,512]{2,1,0:T(8,128)(2,1)S(1)}, bf16[1,128,512]{2,1,0:T(8,128)(2,1)S(1)}, u32[]{:S(2)}, u32[]{:S(2)}) collective-permute-start(bf16[1,128,512]{2,1,0:T(8,128)(2,1)S(1)} %get-tuple-element.100), channel_id=1, source_target_pairs={{0,16},{8,24},{16,0},{24,8},{1,17},{9,25},{17,1},{25,9},{2,18},{10... | collective-permute-start | bytes 393224 | tf_op jit(solution)/shard_map/ppermute | solution.py:27
  49.2 5.9 %collective-permute-start.9 = (bf16[1,128,512]{2,1,0:T(8,128)(2,1)S(1)}, bf16[1,128,512]{2,1,0:T(8,128)(2,1)S(1)}, u32[]{:S(2)}, u32[]{:S(2)}) collective-permute-start(bf16[1,128,512]{2,1,0:T(8,128)(2,1)S(1)} %get-tuple-element.101), channel_id=1, source_target_pairs={{0,24},{8,16},{16,8},{24,0},{1,25},{9,17},{17,9},{25,1},{2,26},{10... | collective-permute-start | bytes 393224 | tf_op jit(solution)/shard_map/ppermute | solution.py:27
  53.3 27.0 %collective-permute-start.12 = (bf16[384,512]{1,0:T(8,128)(2,1)}, bf16[384,512]{1,0:T(8,128)(2,1)}, u32[]{:S(2)}, u32[]{:S(2)}) collective-permute-start(bf16[384,512]{1,0:T(8,128)(2,1)} %get-tuple-element.111.refs_2_), channel_id=1, source_target_pairs={{0,4},{1,5},{2,6},{3,7},{4,0},{5,1},{6,2},{7,3},{8,12},{9,13},{10,... | collective-permute-start | bytes 1179656 | tf_op jit(solution)/shard_map/ppermute | solution.py:27
  55.1 3.8 %copy-start.11 = (f32[128,512]{1,0:T(8,128)}, f32[128,512]{1,0:T(8,128)S(1)}, u32[]{:S(2)}) copy-start(f32[128,512]{1,0:T(8,128)S(1)} %get-tuple-element.169.refs_2_) | copy-start | bytes 786436
  56.4 2.6 %copy-start.5 = (bf16[192,512]{1,0:T(8,128)(2,1)}, bf16[192,512]{1,0:T(8,128)(2,1)S(1)}, u32[]{:S(2)}) copy-start(bf16[192,512]{1,0:T(8,128)(2,1)S(1)} %collective-permute-done.10.refs_7_.refs_3_) | copy-start | bytes 589828
  56.4 2.6 %copy-start.3 = (bf16[384,512]{1,0:T(8,128)(2,1)}, bf16[384,512]{1,0:T(8,128)(2,1)S(1)}, u32[]{:S(2)}) copy-start(bf16[384,512]{1,0:T(8,128)(2,1)S(1)} %collective-permute-done.4.refs_3_) | copy-start | bytes 1179652
  59.0 1.3 copy-start
  60.3 32.2 %collective-permute-start.11 = (bf16[448,512]{1,0:T(8,128)(2,1)}, bf16[448,512]{1,0:T(8,128)(2,1)S(1)}, u32[]{:S(2)}, u32[]{:S(2)}) collective-permute-start(bf16[448,512]{1,0:T(8,128)(2,1)} %get-tuple-element.110.refs_2_), channel_id=1, source_target_pairs={{0,4},{1,5},{2,6},{3,7},{4,0},{5,1},{6,2},{7,3},{8,12},{9,13},{10,... | collective-permute-start | bytes 1376264 | tf_op jit(solution)/shard_map/ppermute | solution.py:27
  61.0 23.9 %collective-permute-start.13 = (bf16[384,512]{1,0:T(8,128)(2,1)}, bf16[384,512]{1,0:T(8,128)(2,1)S(1)}, u32[]{:S(2)}, u32[]{:S(2)}) collective-permute-start(bf16[384,512]{1,0:T(8,128)(2,1)} %get-tuple-element.112.refs_5_.refs_2_), channel_id=1, source_target_pairs={{0,2},{1,3},{2,0},{3,1},{4,6},{5,7},{6,4},{7,5},{8,10},{9,11},{10,... | collective-permute-start | bytes 1179656 | tf_op jit(solution)/shard_map/ppermute | solution.py:27
  63.5 0.9 copy-start.6
  64.4 1.9 %copy-start.4 = (bf16[384,512]{1,0:T(8,128)(2,1)S(1)}, bf16[384,512]{1,0:T(8,128)(2,1)}, u32[]{:S(2)}) copy-start(bf16[384,512]{1,0:T(8,128)(2,1)} %copy-done.3) | copy-start | bytes 1179652
  64.4 2.0 %copy-start.8 = (bf16[192,512]{1,0:T(8,128)(2,1)S(1)}, bf16[192,512]{1,0:T(8,128)(2,1)}, u32[]{:S(2)}) copy-start(bf16[192,512]{1,0:T(8,128)(2,1)} %copy-done.7) | copy-start | bytes 589828
  64.4 2.0 %copy-start.10 = (bf16[192,512]{1,0:T(8,128)(2,1)S(1)}, bf16[192,512]{1,0:T(8,128)(2,1)}, u32[]{:S(2)}) copy-start(bf16[192,512]{1,0:T(8,128)(2,1)} %copy-done.9) | copy-start | bytes 589828
  82.5 20.4 %collective-permute-start.16 = (bf16[384,512]{1,0:T(8,128)(2,1)S(1)}, bf16[384,512]{1,0:T(8,128)(2,1)S(1)}, u32[]{:S(2)}, u32[]{:S(2)}) collective-permute-start(bf16[384,512]{1,0:T(8,128)(2,1)S(1)} %get-tuple-element.117.refs_3_.refs_2_), channel_id=1, source_target_pairs={{0,2},{1,3},{2,0},{3,1},{4,6},{5,7},{6,4},{7,5},{8,10},{9,11},{10,... | collective-permute-start | bytes 1179656 | tf_op jit(solution)/shard_map/ppermute | solution.py:27
  82.5 26.0 %collective-permute-start.15 = (bf16[384,512]{1,0:T(8,128)(2,1)S(1)}, bf16[384,512]{1,0:T(8,128)(2,1)S(1)}, u32[]{:S(2)}, u32[]{:S(2)}) collective-permute-start(bf16[384,512]{1,0:T(8,128)(2,1)S(1)} %get-tuple-element.126.refs_2_), channel_id=1, source_target_pairs={{0,4},{1,5},{2,6},{3,7},{4,0},{5,1},{6,2},{7,3},{8,12},{9,13},{10,... | collective-permute-start | bytes 1179656 | tf_op jit(solution)/shard_map/ppermute | solution.py:27
  94.5 30.6 %collective-permute-start.22 = (bf16[448,512]{1,0:T(8,128)(2,1)S(1)}, bf16[448,512]{1,0:T(8,128)(2,1)S(1)}, u32[]{:S(2)}, u32[]{:S(2)}) collective-permute-start(bf16[448,512]{1,0:T(8,128)(2,1)S(1)} %get-tuple-element.127.refs_3_.refs_2_), channel_id=1, source_target_pairs={{0,2},{1,3},{2,0},{3,1},{4,6},{5,7},{6,4},{7,5},{8,10},{9,11},{10,... | collective-permute-start | bytes 1376264 | tf_op jit(solution)/shard_map/ppermute | solution.py:27
  94.6 23.3 %collective-permute-start.14 = (bf16[256,512]{1,0:T(8,128)(2,1)S(1)}, bf16[256,512]{1,0:T(8,128)(2,1)S(1)}, u32[]{:S(2)}, u32[]{:S(2)}) collective-permute-start(bf16[256,512]{1,0:T(8,128)(2,1)S(1)} %get-tuple-element.125.refs_2_), channel_id=1, source_target_pairs={{0,4},{1,5},{2,6},{3,7},{4,0},{5,1},{6,2},{7,3},{8,12},{9,13},{10,... | collective-permute-start | bytes 786440 | tf_op jit(solution)/shard_map/ppermute | solution.py:27
  109.2 21.6 %collective-permute-start.21 = (bf16[384,512]{1,0:T(8,128)(2,1)S(1)}, bf16[384,512]{1,0:T(8,128)(2,1)S(1)}, u32[]{:S(2)}, u32[]{:S(2)}) collective-permute-start(bf16[384,512]{1,0:T(8,128)(2,1)S(1)} %get-tuple-element.135.refs_3_.refs_2_), channel_id=1, source_target_pairs={{0,2},{1,3},{2,0},{3,1},{4,6},{5,7},{6,4},{7,5},{8,10},{9,11},{10,... | collective-permute-start | bytes 1179656 | tf_op jit(solution)/shard_map/ppermute | solution.py:27
  118.5 17.8 %collective-permute-start.20 = (bf16[256,512]{1,0:T(8,128)(2,1)S(1)}, bf16[256,512]{1,0:T(8,128)(2,1)S(1)}, u32[]{:S(2)}, u32[]{:S(2)}) collective-permute-start(bf16[256,512]{1,0:T(8,128)(2,1)S(1)} %get-tuple-element.139.refs_3_.refs_2_), channel_id=1, source_target_pairs={{0,2},{1,3},{2,0},{3,1},{4,6},{5,7},{6,4},{7,5},{8,10},{9,11},{10,... | collective-permute-start | bytes 786440 | tf_op jit(solution)/shard_map/ppermute | solution.py:27
  121.0 19.5 %collective-permute-start.17 = (bf16[2,128,512]{2,1,0:T(8,128)(2,1)S(1)}, bf16[2,128,512]{2,1,0:T(8,128)(2,1)S(1)}, u32[]{:S(2)}, u32[]{:S(2)}) collective-permute-start(bf16[2,128,512]{2,1,0:T(8,128)(2,1)S(1)} %get-tuple-element.143), channel_id=1, source_target_pairs={{0,8},{8,0},{16,24},{24,16},{1,9},{9,1},{17,25},{25,17},{2,10},{10... | collective-permute-start | bytes 786440 | tf_op jit(solution)/shard_map/ppermute | solution.py:27
  122.6 17.9 %collective-permute-start.18 = (bf16[2,128,512]{2,1,0:T(8,128)(2,1)S(1)}, bf16[2,128,512]{2,1,0:T(8,128)(2,1)S(1)}, u32[]{:S(2)}, u32[]{:S(2)}) collective-permute-start(bf16[2,128,512]{2,1,0:T(8,128)(2,1)S(1)} %get-tuple-element.144), channel_id=1, source_target_pairs={{0,16},{8,24},{16,0},{24,8},{1,17},{9,25},{17,1},{25,9},{2,18},{10... | collective-permute-start | bytes 786440 | tf_op jit(solution)/shard_map/ppermute | solution.py:27
  125.1 15.4 %collective-permute-start.19 = (bf16[2,128,512]{2,1,0:T(8,128)(2,1)S(1)}, bf16[2,128,512]{2,1,0:T(8,128)(2,1)S(1)}, u32[]{:S(2)}, u32[]{:S(2)}) collective-permute-start(bf16[2,128,512]{2,1,0:T(8,128)(2,1)S(1)} %get-tuple-element.145), channel_id=1, source_target_pairs={{0,24},{8,16},{16,8},{24,0},{1,25},{9,17},{17,9},{25,1},{2,26},{10... | collective-permute-start | bytes 786440 | tf_op jit(solution)/shard_map/ppermute | solution.py:27
  141.3 0.7 copy-start.13
  142.0 4.5 %collective-permute-start.23 = (bf16[2048,512]{1,0:T(8,128)(2,1)}, bf16[2048,512]{1,0:T(8,128)(2,1)}, u32[]{:S(2)}, u32[]{:S(2)}) collective-permute-start(bf16[2048,512]{1,0:T(8,128)(2,1)} %get-tuple-element.159.refs_0_), channel_id=1, source_target_pairs={{0,1},{1,0},{2,3},{3,2},{4,5},{5,4},{6,7},{7,6},{8,9},{9,8},{10,11... | collective-permute-start | bytes 6291464 | tf_op jit(solution)/shard_map/ppermute | solution.py:27
  142.0 12.1 %collective-permute-start.24 = (bf16[3,128,512]{2,1,0:T(8,128)(2,1)}, bf16[3,128,512]{2,1,0:T(8,128)(2,1)S(1)}, u32[]{:S(2)}, u32[]{:S(2)}) collective-permute-start(bf16[3,128,512]{2,1,0:T(8,128)(2,1)} %get-tuple-element.163), channel_id=1, source_target_pairs={{0,8},{8,0},{16,24},{24,16},{1,9},{9,1},{17,25},{25,17},{2,10},{10... | collective-permute-start | bytes 1179656 | tf_op jit(solution)/shard_map/ppermute | solution.py:27
  143.5 19.9 %collective-permute-start.25 = (bf16[3,128,512]{2,1,0:T(8,128)(2,1)}, bf16[3,128,512]{2,1,0:T(8,128)(2,1)S(1)}, u32[]{:S(2)}, u32[]{:S(2)}) collective-permute-start(bf16[3,128,512]{2,1,0:T(8,128)(2,1)} %get-tuple-element.164), channel_id=1, source_target_pairs={{0,16},{8,24},{16,0},{24,8},{1,17},{9,25},{17,1},{25,9},{2,18},{10... | collective-permute-start | bytes 1179656 | tf_op jit(solution)/shard_map/ppermute | solution.py:27
  145.0 18.4 %collective-permute-start.26 = (bf16[3,128,512]{2,1,0:T(8,128)(2,1)}, bf16[3,128,512]{2,1,0:T(8,128)(2,1)S(1)}, u32[]{:S(2)}, u32[]{:S(2)}) collective-permute-start(bf16[3,128,512]{2,1,0:T(8,128)(2,1)} %get-tuple-element.165), channel_id=1, source_target_pairs={{0,24},{8,16},{16,8},{24,0},{1,25},{9,17},{17,9},{25,1},{2,26},{10... | collective-permute-start | bytes 1179656 | tf_op jit(solution)/shard_map/ppermute | solution.py:27
  145.5 19.0 %collective-permute-start.28 = (bf16[128,512]{1,0:T(8,128)(2,1)}, bf16[128,512]{1,0:T(8,128)(2,1)}, u32[]{:S(2)}, u32[]{:S(2)}) collective-permute-start(bf16[128,512]{1,0:T(8,128)(2,1)} %get-tuple-element.174), channel_id=1, source_target_pairs={{0,4},{1,5},{2,6},{3,7},{4,0},{5,1},{6,2},{7,3},{8,12},{9,13},{10,... | collective-permute-start | bytes 393224 | tf_op jit(solution)/shard_map/ppermute | solution.py:27
  146.5 1.6 copy-start.1
  153.8 9.8 %copy-start.12 = (f32[128,512]{1,0:T(8,128)S(1)}, f32[128,512]{1,0:T(8,128)}, u32[]{:S(2)}) copy-start(f32[128,512]{1,0:T(8,128)} %copy-done.11) | copy-start | bytes 786436
  153.8 9.8 %copy-start.14 = (f32[128,512]{1,0:T(8,128)S(1)}, f32[128,512]{1,0:T(8,128)}, u32[]{:S(2)}) copy-start(f32[128,512]{1,0:T(8,128)} %copy-done.13) | copy-start | bytes 786436
  163.5 5.0 %collective-permute-start.27 = (bf16[128,512]{1,0:T(8,128)(2,1)S(1)}, bf16[128,512]{1,0:T(8,128)(2,1)S(1)}, u32[]{:S(2)}, u32[]{:S(2)}) collective-permute-start(bf16[128,512]{1,0:T(8,128)(2,1)S(1)} %get-tuple-element.173), channel_id=1, source_target_pairs={{0,2},{1,3},{2,0},{3,1},{4,6},{5,7},{6,4},{7,5},{8,10},{9,11},{10,... | collective-permute-start | bytes 393224 | tf_op jit(solution)/shard_map/ppermute | solution.py:27
Sparse Core Ops, SparseCore 0:
  9.6 27.5 all-gather.4
  63.6 10.4 all-gather.6

commit v3 on v2

--- a/solution.py
+++ b/solution.py
@@ -86,7 +86,7 @@
     return cuts
 
 
-def cut_out(chain, blocks, name, limit=WHOLE_VMEM):
+def cut_out(chain, blocks, name, limit=WHOLE_VMEM, deps=()):
     flat = [piece for block in blocks for piece in block]
     n = len(flat)
 
@@ -96,7 +96,7 @@
             at = 0
             for _, where, size in block:
                 j = len(copies)
-                target = refs[n + b].at[pl.ds(at, size)]
+                target = refs[n + len(deps) + b].at[pl.ds(at, size)]
                 copy = pltpu.make_async_copy(where(refs[j], size), target, refs[-1].at[j])
                 copy.start()
                 copies.append(copy)
@@ -107,8 +107,8 @@
     return chain(
         body,
         name,
-        [piece[0] for piece in flat],
-        [ANY] * n,
+        [piece[0] for piece in flat] + [in_hbm(a) for a in deps],
+        [ANY] * (n + len(deps)),
         [
             jax.ShapeDtypeStruct((sum(p[2] for p in block), block[0][0].shape[-1]), block[0][0].dtype)
             for block in blocks
@@ -127,16 +127,16 @@
     return lambda ref, size: ref.at[level]
 
 
-def my_share(level, parts):
+def my_share(level):
     def where(ref, size):
-        first = pl.multiple_of(lax.axis_index("wide") % parts * size, size)
+        first = pl.multiple_of(lax.axis_index("wide") * size, size)
         return ref.at[level, pl.ds(first, size)]
 
     return where
 
 
-def place_of(mask, parts):
-    return lambda: (lax.axis_index("wide") ^ mask) % parts
+def place_of(mask):
+    return lambda: lax.axis_index("wide") ^ mask
 
 
 def join_shares(chain, blocks, name):
@@ -162,21 +162,32 @@
     )
 
 
-def next_grads(chain, w_self, jobs, name, into=None, halve=False, fetch=None, deps=()):
+def next_grads(chain, w_self, jobs, name, into=None, fetch=(), deps=(), block=None):
     width = w_self.shape[2]
     operands, in_specs, out_shape, out_specs, scratch, aliases = [], [], [], [], [], {}
     for level, grad, far, far_cross in jobs:
         operands += [w_self, far_cross, grad, far]
         in_specs += [weight_block(w_self, level), WHOLE, WHOLE, WHOLE]
     rows = [job[1].shape[0] for job in jobs]
-    pieces = [size for size, job in zip(rows, jobs) if job[0] != 1]
-    if halve:
-        pieces = [rows[0] // 2] * 2
-    for size in pieces:
-        out_shape.append(jax.ShapeDtypeStruct((size, width), jnp.bfloat16))
+    for size, job in zip(rows, jobs):
+        if job[0] != 1:
+            out_shape.append(jax.ShapeDtypeStruct((size, width), jnp.bfloat16))
+            out_specs.append(WHOLE)
+    n_kept = len(out_shape)
+    for array, _, _, size in fetch:
+        operands.append(array)
+        in_specs.append(ANY)
+        out_shape.append(jax.ShapeDtypeStruct((size, array.shape[-1]), array.dtype))
         out_specs.append(WHOLE)
     operands += deps
     in_specs += [ANY] * len(deps)
+    n_moved = len(fetch) + (2 if block is not None else 0)
+    if n_moved:
+        scratch.append(pltpu.SemaphoreType.DMA((n_moved,)))
+    if block is not None:
+        operands.append(block[0])
+        in_specs.append(ANY)
+        scratch.append(pltpu.VMEM((width, width), jnp.bfloat16))
     if into is not None:
         if not isinstance(into[0], jax.ShapeDtypeStruct):
             aliases[len(operands)] = len(out_shape)
@@ -186,76 +197,65 @@
         out_specs.append(ANY)
         stored = sum(size for size, job in zip(rows, jobs) if job[0] == 1)
         scratch += [pltpu.VMEM((stored, width), jnp.bfloat16), pltpu.SemaphoreType.DMA]
-    if fetch is not None:
-        operands.append(fetch[0])
-        in_specs.append(ANY)
-        out_shape.append(jax.ShapeDtypeStruct((fetch[2], fetch[0].shape[1]), fetch[0].dtype))
-        out_specs.append(WHOLE)
-        scratch.append(pltpu.SemaphoreType.DMA)
 
     def body(*refs):
-        ins, outs = refs[: len(operands)], refs[len(operands) :]
-        outs, scr = outs[: len(out_shape)], outs[len(out_shape) :]
-        if fetch is not None:
-            cut = pltpu.make_async_copy(ins[-1].at[pl.ds(*fetch[1:])], outs[-1], scr[-1])
-            cut.start()
+        ins, rest = refs[: len(operands)], refs[len(operands) :]
+        outs, scr = rest[: len(out_shape)], rest[len(out_shape) :]
+        first = 4 * len(jobs)
+        copies = []
+        for f, (_, index, start, size) in enumerate(fetch):
+            source = ins[first + f].at[(*index, pl.ds(start, size))]
+            copies.append(pltpu.make_async_copy(source, outs[n_kept + f], scr[0].at[f]))
+        if block is not None:
+            source = ins[first + len(fetch) + len(deps)].at[block[1]]
+            copies.append(pltpu.make_async_copy(source, scr[1], scr[0].at[n_moved - 2]))
+        for copy in copies:
+            copy.start()
         at = 0
         for j in range(len(jobs)):
             a_ref, c_ref, grad_ref, far_ref = ins[4 * j : 4 * j + 4]
             total = times_trans(grad_ref[...], a_ref[0]) + times_trans(far_ref[...], c_ref[...])
             total = total.astype(jnp.bfloat16)
             if jobs[j][0] == 1:
-                scr[0][at : at + rows[j]] = total
+                scr[-2][at : at + rows[j]] = total
                 at += rows[j]
-            elif halve:
-                outs[0][...] = total[: pieces[0]]
-                outs[1][...] = total[pieces[0] :]
             else:
                 outs[j][...] = total
+        stores = []
         if into is not None:
-            store = pltpu.make_async_copy(
-                scr[0], outs[len(pieces)].at[pl.ds(into[1], stored)], scr[1]
-            )
-            store.start()
-            store.wait()
-        if fetch is not None:
-            cut.wait()
+            target = outs[-1].at[pl.ds(into[1], stored)]
+            stores.append(pltpu.make_async_copy(scr[-2], target, scr[-1]))
+            stores[-1].start()
+        for copy in copies:
+            copy.wait()
+        if block is not None:
+            target = outs[-1].at[pl.ds(block[2], width)]
+            stores.append(pltpu.make_async_copy(scr[1], target, scr[0].at[n_moved - 1]))
+            stores[-1].start()
+        for copy in stores:
+            copy.wait()
 
     return chain(body, name, operands, in_specs, out_shape, out_specs, scratch, aliases)
 
 
-def last_grad(chain, grad, far, w_self, far_cross):
-    tokens, width = grad.shape
-    steps = max(1, tokens // 512)
+def last_grad(chain, both, far_both, w_self, tokens):
+    width = both.shape[1]
+    steps = max(1, tokens // width)
 
     def body(grad_ref, far_ref, a_ref, c_ref, out_ref):
-        total = times_trans(grad_ref[...], a_ref[0]) + times_trans(far_ref[...], c_ref[0, 0])
+        total = times_trans(grad_ref[...], a_ref[0]) + times_trans(far_ref[...], c_ref[...])
         out_ref[...] = total.astype(jnp.bfloat16)
 
     rows = pl.BlockSpec((tokens // steps, width), lambda i: (i, 0))
     return chain(
         body,
         "last_grad",
-        [grad, far, w_self, far_cross],
-        [rows, rows, weight_block(w_self, 0), cross_block(far_cross)],
-        [jax.ShapeDtypeStruct(grad.shape, grad.dtype)],
+        [in_hbm(both), in_hbm(far_both), w_self, in_hbm(far_both)],
+        [rows, rows, weight_block(w_self, 0), pl.BlockSpec((width, width), lambda i: (tokens // width, 0))],
+        [jax.ShapeDtypeStruct((tokens, width), both.dtype)],
         [rows],
         grid=steps,
     )[0]
-
-
-def cross_block(far_cross):
-    return pl.BlockSpec((1, 1) + far_cross.shape[2:], lambda i: (other_core(), 0, 0, 0))
-
-
-def other_core():
-    return 1 - lax.axis_index("narrow") % 2
-
-
-def both_cores(array):
-    size = lax.axis_size("narrow")
-    pairs = [[i, i + 1] for i in range(0, size, 2)]
-    return lax.all_gather(array, "narrow", axis=0, axis_index_groups=pairs)
 
 
 def weight_block(w_self, level):
@@ -268,7 +268,7 @@
     parts = lax.axis_size("wide")
     share = width // parts
     n = len(pairs)
-    operands = [x for x, _ in xs]
+    operands = [x for x, _, _ in xs]
     in_specs = [ANY] * len(xs)
     for side in sides:
         operands += side if isinstance(side, list) else [in_hbm(side)]
@@ -276,7 +276,7 @@
     if before is not None:
         operands.append(before)
         in_specs.append(WHOLE)
-    buffers = [x for x, _ in xs] + [side for side in sides if not isinstance(side, list)]
+    buffers = [x for x, _, _ in xs] + [side for side in sides if not isinstance(side, list)]
 
     def body(*refs):
         ins, rest = list(refs[: len(operands)]), refs[len(operands) :]
@@ -292,7 +292,7 @@
             copies.append(copy)
             return scratch[0].at[j]
 
-        x_bufs = [fetch(ins.pop(0).at[(*where(), pl.ds(start, rows))]) for _, where in xs]
+        x_bufs = [fetch(ins.pop(0).at[(*at, pl.ds(start - zero, rows))]) for _, at, zero in xs]
         side_refs = []
         for side in sides:
             if isinstance(side, list):
@@ -313,7 +313,7 @@
         if last:
             me = lax.axis_index("wide")
             at = 0
-            for b, many in enumerate(last):
+            for b, many in enumerate(abs(size) for size in last):
                 for k in range(parts):
                     there = pl.multiple_of((me ^ k) * share, share)
                     out = outs[b * parts + k]
@@ -324,7 +324,9 @@
     out_shape = [whole]
     if last:
         out_shape = [
-            jax.ShapeDtypeStruct((many, share, width), jnp.bfloat16 if k else jnp.float32)
+            jax.ShapeDtypeStruct(
+                (abs(many), share, width), jnp.bfloat16 if k or many < 0 else jnp.float32
+            )
             for many in last
             for k in range(parts)
         ]
@@ -365,31 +367,35 @@
     )
 
 
-def store_levels(chain, levels, name):
-    flat, spans = [], []
-    for entry in levels:
-        entry = entry if isinstance(entry, list) else [entry]
-        spans.append((len(flat), len(entry)))
-        flat += entry
-    shape = flat[0].shape[-2:]
+def last_sums(chain, cross_1, terms, self_1, self_2, cross_2):
+    m, n = len(cross_1), len(terms)
+    shape = terms[0].shape[1:]
+
+    def added(refs, j):
+        value = refs[0][j].astype(jnp.float32)
+        for ref in refs[1:]:
+            value = value + ref[j].astype(jnp.float32)
+        return value
 
     def body(*refs):
-        out = refs[len(flat)]
-        for j, (first, many) in enumerate(spans):
-            total = None
-            for ref in refs[first : first + many]:
-                value = ref[...].reshape(shape).astype(jnp.float32)
-                total = value if total is None else total + value
-            out[j] = total
-
+        one, two = refs[:m], refs[m : m + n]
+        self_1_ref, self_2_ref, cross_2_ref, self_ref, cross_ref = refs[m + n :]
+        self_ref[0] = added(two, 0)
+        self_ref[1] = self_1_ref[...]
+        self_ref[2] = self_2_ref[...]
+        cross_ref[0] = added(two, 1)
+        cross_ref[1] = added(one, 0)
+        cross_ref[2] = cross_2_ref[...].astype(jnp.float32)
+
+    levels = jax.ShapeDtypeStruct((LEVELS,) + shape, jnp.float32)
     return chain(
         body,
-        name,
-        flat,
-        [WHOLE] * len(flat),
-        [jax.ShapeDtypeStruct((len(levels),) + shape, jnp.float32)],
-        [WHOLE],
-    )[0]
+        "last_sums",
+        [*cross_1, *terms, self_1, self_2, cross_2],
+        [WHOLE] * (m + n + 3),
+        [levels, levels],
+        [WHOLE, WHOLE],
+    )
 
 
 def local(saved_inputs, cotangent, w_self, w_cross):
@@ -401,9 +407,8 @@
     n = len(cuts)
     z = n - 1
     end = cuts[z][0]
-    far_inputs, far_cross = both_cores(saved_inputs), both_cores(w_cross)
+    far_inputs = swap(saved_inputs, "narrow", 1 << 0)
     saved_inputs, cotangent, w_cross = in_hbm(saved_inputs), in_hbm(cotangent), in_hbm(w_cross)
-    far_inputs, far_cross = in_hbm(far_inputs), in_hbm(far_cross)
     chain = Chain()
     near = [[None] * n for _ in range(LEVELS)]
     far = [[None] * n for _ in range(LEVELS)]
@@ -417,20 +422,30 @@
     def flat(arrays):
         return [a for group in arrays for a in group]
 
-    def at_level(level):
-        return lambda: (level,)
-
-    halves_of = min(2, parts)
-    first, half_1 = cut_out(
+    first, cross_1 = cut_out(
         chain,
         [
-            [(w_cross, my_share(2, parts), share), (cotangent, rows_at(0), cuts[0][1])],
-            [(w_cross, my_share(1, halves_of), width // halves_of)],
+            [(w_cross, my_share(2), share), (cotangent, rows_at(0), cuts[0][1])],
+            [(w_cross, block_of(1), width)],
         ],
         "first_rows",
-    )
+        VMEM_LIMIT,
+    )
+    cross_1 = swap(cross_1, "narrow", 1 << 1)
     first = swap(first, "narrow", 1 << 2)
-    half_1 = swap(half_1, "narrow", 1 << 1)
+    self_2 = weight_sums(
+        chain,
+        [(saved_inputs, (2,), 0)],
+        [[cotangent]],
+        [(0, 0)],
+        0,
+        None,
+        scale,
+        (1,),
+        "self_sums_2",
+    )
+    self_2 = spread(self_2)
+    (self_2,) = add_terms(chain, self_2, "add_self_2", (jnp.float32,))
     share_2, rows, *starts = cut_out(
         chain,
         [
@@ -441,50 +456,37 @@
         ],
         "parted",
         VMEM_LIMIT,
-    )
+        [far_inputs],
+    )
+    far_inputs = in_hbm(far_inputs)
     far[2][0], near[2][0], near[2][1] = [rows], [starts[0]], [starts[1]]
     send(2, 1)
-    shares_2 = [(share_2, place_of(0, parts))]
-    shares_2 += [(swap(share_2, "wide", k), place_of(k, parts)) for k in range(1, parts)]
-    shares_1 = [(half_1, place_of(0, halves_of))]
-    shares_1 += [(swap(half_1, "wide", k), place_of(k, halves_of)) for k in range(1, halves_of)]
-    self_2 = weight_sums(
-        chain,
-        [(saved_inputs, at_level(2))],
-        [[cotangent]],
-        [(0, 0)],
-        0,
-        None,
-        scale,
-        (1,),
-        "self_sums_2",
-    )
-    self_2 = spread(self_2)
-    blocks = [None, None, *join_shares(chain, [shares_2], "join_2")]
+    shares_2 = [(share_2, place_of(0))]
+    shares_2 += [(swap(share_2, "wide", k), place_of(k)) for k in range(1, parts)]
+    blocks = [None, cross_1, *join_shares(chain, [shares_2], "join_2")]
 
     def job(level, k):
         return (level, near[level][k][0], far[level][k][0], blocks[level])
 
-    grad = jax.ShapeDtypeStruct(cotangent.shape, cotangent.dtype)
-
-    def level_1(k):
-        jobs = [(1, a, b, blocks[1]) for a, b in zip(near[1][k], far[1][k])]
-        return next_grads(chain, w_self, jobs, f"next_grads_1_{k}", (grad, cuts[k][0]))[0]
+    grad = jax.ShapeDtypeStruct((tokens + width, width), cotangent.dtype)
+
+    def level_1(ks, block=None):
+        jobs = [job(1, k) for k in ks]
+        into = (grad, cuts[ks[0]][0])
+        return next_grads(chain, w_self, jobs, f"next_grads_1_{ks[0]}", into, (), (), block)
 
     def sums_a(ks, before, last=None):
-        xs = [(saved_inputs, at_level(2)), (saved_inputs, at_level(1))]
+        xs = [(saved_inputs, (2,), 0), (saved_inputs, (1,), 0)]
         sides = [flat(far[2][k] for k in ks), flat(near[1][k] for k in ks)]
         start, name = cuts[ks[0]][0], f"sums_a_{ks[0]}"
         return weight_sums(chain, xs, sides, [(0, 0), (1, 1)], start, before, scale, last, name)
 
-    def sums_b(k, before, last=None):
-        xs = [(saved_inputs, at_level(1)), (saved_inputs, at_level(0))]
-        xs.append((far_inputs, lambda: (other_core(), 0)))
+    def sums_b(ks, before, last=None):
+        xs = [(saved_inputs, (1,), 0), (saved_inputs, (0,), 0), (far_inputs, (0,), 0)]
         pairs = [(0, 0), (1, 1), (2, 1)]
-        start, name = cuts[k][0], f"sums_b_{k}"
-        return weight_sums(
-            chain, xs, [far[1][k], grad], pairs, start, before, scale, last, name
-        )
+        start, name = cuts[ks[0]][0], f"sums_b_{ks[0]}"
+        side = flat(far[1][k] for k in ks)
+        return weight_sums(chain, xs, [side, grad], pairs, start, before, scale, last, name)
 
     sum_a = sum_b = None
     for k in range(n):
@@ -495,41 +497,35 @@
             [job(2, k)] + ([job(1, 0)] if k == 1 else []),
             f"next_grads_{k}",
             (grad, 0) if k == 1 else None,
-            False,
-            (cotangent, *cuts[ahead]) if ahead < n else None,
+            [(cotangent, (), *cuts[ahead])] if ahead < n else [],
         )
+        if k == 1:
+            grad = done.pop()
         if ahead < n:
             near[2][ahead] = [done.pop()]
             send(2, ahead)
-        if k == 1:
-            grad = done.pop()
         near[1][k] = done
         send(1, k)
-        if k == 0:
-            (self_2,) = add_terms(chain, self_2, "add_self_2", (jnp.float32,))
-            (blocks[1],) = join_shares(chain, [shares_1], "join_1")
-        if 2 <= k < z:
-            grad = level_1(k - 1) if k < z - 1 else grad
+        if 2 <= k < z - 1:
+            block = (w_cross, 0, tokens) if k == 2 else None
+            (grad,) = level_1([k - 1], block)
         if 1 <= k < z - 1:
-            (sum_b,) = sums_b(k - 1, sum_b)
+            (sum_b,) = sums_b([k - 1], sum_b)
         if 1 <= k < z:
             (sum_a,) = sums_a([0, 1] if k == 1 else [k], sum_a)
     sum_a = spread(sums_a([z], sum_a, (2,)))
     for k in (z - 2, z - 1):
-        grad = level_1(k)
-        (sum_b,) = sums_b(k, sum_b)
-    grad = level_1(z)
-    sum_b = spread(sums_b(z, sum_b, (3,)))
+        (grad,) = level_1([k])
+        (sum_b,) = sums_b([k], sum_b)
+    (grad,) = level_1([z])
+    terms = sums_b([z], sum_b, (-1, 2))
+    cross_1 = [swap_both(t, k, 1 << 1) for k, t in enumerate(terms[:parts])]
+    sum_c = spread(terms[parts:])
     cross_2, self_1, grad = add_terms(chain, sum_a, "add_a", (jnp.bfloat16, jnp.float32), grad)
     cross_2 = swap(cross_2, "narrow", 1 << 2)
     far_grad = swap(grad, "narrow", 1 << 0)
-    out = last_grad(chain, grad, far_grad, w_self, far_cross)
-    cross_1, self_0, cross_0 = add_terms(
-        chain, sum_b, "add_b", (jnp.bfloat16, jnp.float32, jnp.float32)
-    )
-    cross_1 = swap(cross_1, "narrow", 1 << 1)
-    grad_self = store_levels(chain, [self_0, self_1, self_2], "store_self")
-    grad_cross = store_levels(chain, [cross_0, cross_1, cross_2], "store_cross")
+    out = last_grad(chain, grad, far_grad, w_self, tokens)
+    grad_self, grad_cross = last_sums(chain, cross_1, sum_c, self_1, self_2, cross_2)
     return out, grad_self, grad_cross
 
 

time: 178 us -> 164 us (0.921)
  between operations: 14.5 us -> 0.95 us
  Pallas kernels: 61.3 us -> 51.4 us
  starting transfers between devices: 35.9 us -> 44.5 us
    pallas_call x33 -> x30, Pallas kernels: 61.3 us -> 51.4 us  [__call__(): pl.pallas_call(whole, grid=(grid,), out_shape=[*out_shape, TOKEN], in_spe...]
    ppermute x0 -> x4, starting transfers between devices: none -> 6.3 us  [swap_both(): return lax.ppermute(array, ('wide', 'narrow'), pairs)]
    ppermute x0 -> x4, waiting for transfers between devices: none -> 2.57 us  [swap_both(): return lax.ppermute(array, ('wide', 'narrow'), pairs)]
    ppermute x29 -> x28, starting transfers between devices: 35.9 us -> 38.2 us  [swap(): lax.ppermute(array, axis, [(i, i ^ mask) for i in range(lax.axis_size(axi...]
    unnamed x32 -> x8, local copies, waits for them, and re-layouts: 5.26 us -> 4.21 us
    ppermute x29 -> x28, waiting for transfers between devices: 59.5 us -> 59.3 us  [swap(): lax.ppermute(array, axis, [(i, i ^ mask) for i in range(lax.axis_size(axi...]
  transfers between devices with their start and end apart: 31 -> 32, of which waited for: 13 -> 16; matrix products, arithmetic and copies ran while one was open for 0% -> 0% of each run, Pallas kernels for 34% -> 31%
where the time goes in v3:
time: 164 us; the launch traced here: 163 us
  waiting for transfers between devices  61.9 us (38%)
  Pallas kernels  51.4 us (31%)
  starting transfers between devices  44.5 us (27%)
  local copies, waits for them, and re-layouts  4.21 us (3%)
    ppermute x28, waiting for transfers between devices, swap(): lax.ppermute(array, axis, [(i, i ^ mask) for i in range(lax.axis_size(axi...  59.3 us
    pallas_call x30, Pallas kernels, __call__(): pl.pallas_call(whole, grid=(grid,), out_shape=[*out_shape, TOKEN], in_spe...  51.4 us
    ppermute x28, starting transfers between devices, swap(): lax.ppermute(array, axis, [(i, i ^ mask) for i in range(lax.axis_size(axi...  38.2 us
    ppermute x4, starting transfers between devices, swap_both(): return lax.ppermute(array, ('wide', 'narrow'), pairs)  6.3 us
    unnamed x8, local copies, waits for them, and re-layouts  4.21 us
  transfers between devices with their start and end apart: 32, of which 16 were waited for; matrix products, arithmetic and copies ran while one was open for 0% of the time, Pallas kernels for 31%

profile of v3, /device:TPU:0, one launch (start us, length us, event | category | flops | bytes accessed | tf_op | source)
XLA Modules:
  0.0 163.0 jit_solution(10879646405993169737)
XLA Ops:
  2.4 3.7 %collective-permute-start = (bf16[320,512]{1,0:T(8,128)(2,1)S(1)}, bf16[320,512]{1,0:T(8,128)(2,1)S(1)}, u32[]{:S(2)}, u32[]{:S(2)}) collective-permute-start(bf16[320,512]{1,0:T(8,128)(2,1)S(1)} %get-tuple-element.87), channel_id=1, source_target_pairs={{0,4},{1,5},{2,6},{3,7},{4,0},{5,1},{6,2},{7,3},{8,12},{9,13},{10,... | collective-permute-start | bytes 983048 | tf_op jit(solution)/shard_map/ppermute | solution.py:27
  6.1 4.5 %self_sums_2.1 = (f32[1,128,512]{2,1,0:T(8,128)S(1)}, bf16[1,128,512]{2,1,0:T(8,128)(2,1)S(1)}, bf16[1,128,512]{2,1,0:T(8,128)(2,1)S(1)}, bf16[1,128,512]{2,1,0:T(8,128)(2,1)S(1)}, f32[8,128]{1,0:T(8,128)S(1)}) custom-call(bf16[3,2048,512]{2,1,0:T(8,128)(2,1)} %refs_1_.25, bf16[2048,512]{1,0:T(8,128)(2,1)} %refs_4_.9, f32[8,128]{1,0:T(8,128)S(1)} %get-tuple-element.88.refs_2_), custom_call_target="tpu_custom_call" | custom-call | tf_op jit(solution)/shard_map/self_sums_2/pallas_call | solution.py:65
  10.6 1.6 collective-permute-start.2
  12.2 1.5 collective-permute-start.3
  14.2 2.5 %collective-permute-done.2.refs_1_ = bf16[1,128,512]{2,1,0:T(8,128)(2,1)S(1)} collective-permute-done((bf16[1,128,512]{2,1,0:T(8,128)(2,1)S(1)}, bf16[1,128,512]{2,1,0:T(8,128)(2,1)S(1)}, u32[]{:S(2)}, u32[]{:S(2)}) %collective-permute-start.2) | collective-permute-done | bytes 131104 | tf_op jit(solution)/shard_map/ppermute | solution.py:27
  16.6 1.6 collective-permute-start.9
  18.2 2.1 %collective-permute-done.3.refs_2_ = bf16[1,128,512]{2,1,0:T(8,128)(2,1)S(1)} collective-permute-done((bf16[1,128,512]{2,1,0:T(8,128)(2,1)S(1)}, bf16[1,128,512]{2,1,0:T(8,128)(2,1)S(1)}, u32[]{:S(2)}, u32[]{:S(2)}) %collective-permute-start.3) | collective-permute-done | bytes 131104 | tf_op jit(solution)/shard_map/ppermute | solution.py:27
  21.6 2.6 %copy-done.2 = bf16[3,2048,512]{2,1,0:T(8,128)(2,1)} copy-done((bf16[3,2048,512]{2,1,0:T(8,128)(2,1)}, bf16[3,2048,512]{2,1,0:T(8,128)(2,1)S(1)}, u32[]{:S(2)}) %copy-start.2) | copy-done | bytes 6291480
  24.2 1.6 parted.1
  25.9 1.6 collective-permute-start.5
  27.5 1.5 collective-permute-start.6
  29.4 2.3 %collective-permute-done.5.refs_1_ = bf16[128,512]{1,0:T(8,128)(2,1)S(1)} collective-permute-done((bf16[128,512]{1,0:T(8,128)(2,1)S(1)}, bf16[128,512]{1,0:T(8,128)(2,1)S(1)}, u32[]{:S(2)}, u32[]{:S(2)}) %collective-permute-start.5) | collective-permute-done | bytes 131104 | tf_op jit(solution)/shard_map/ppermute | solution.py:27
  31.8 3.5 %collective-permute-done.6.refs_2_ = bf16[128,512]{1,0:T(8,128)(2,1)S(1)} collective-permute-done((bf16[128,512]{1,0:T(8,128)(2,1)S(1)}, bf16[128,512]{1,0:T(8,128)(2,1)S(1)}, u32[]{:S(2)}, u32[]{:S(2)}) %collective-permute-start.6) | collective-permute-done | bytes 131104 | tf_op jit(solution)/shard_map/ppermute | solution.py:27
  36.4 4.0 %collective-permute-start.10 = (bf16[192,512]{1,0:T(8,128)(2,1)S(1)}, bf16[192,512]{1,0:T(8,128)(2,1)S(1)}, u32[]{:S(2)}, u32[]{:S(2)}) collective-permute-start(bf16[192,512]{1,0:T(8,128)(2,1)S(1)} %get-tuple-element.103.refs_6_.refs_4_), channel_id=1, source_target_pairs={{0,2},{1,3},{2,0},{3,1},{4,6},{5,7},{6,4},{7,5},{8,10},{9,11},{10,... | collective-permute-start | bytes 589832 | tf_op jit(solution)/shard_map/ppermute | solution.py:27
  40.6 7.4 %collective-permute-done.10.refs_7_.refs_3_ = bf16[192,512]{1,0:T(8,128)(2,1)S(1)} collective-permute-done((bf16[192,512]{1,0:T(8,128)(2,1)S(1)}, bf16[192,512]{1,0:T(8,128)(2,1)S(1)}, u32[]{:S(2)}, u32[]{:S(2)}) %collective-permute-start.10) | collective-permute-done | bytes 196640 | tf_op jit(solution)/shard_map/ppermute | solution.py:27
  48.1 7.6 %collective-permute-done.8.refs_3_ = bf16[384,512]{1,0:T(8,128)(2,1)S(1)} collective-permute-done((bf16[384,512]{1,0:T(8,128)(2,1)S(1)}, bf16[384,512]{1,0:T(8,128)(2,1)S(1)}, u32[]{:S(2)}, u32[]{:S(2)}) %collective-permute-start.8) | collective-permute-done | bytes 393248 | tf_op jit(solution)/shard_map/ppermute | solution.py:27
  57.0 1.5 copy-done
  58.6 2.6 %collective-permute-start.13 = (bf16[384,512]{1,0:T(8,128)(2,1)S(1)}, bf16[384,512]{1,0:T(8,128)(2,1)S(1)}, u32[]{:S(2)}, u32[]{:S(2)}) collective-permute-start(bf16[384,512]{1,0:T(8,128)(2,1)S(1)} %get-tuple-element.107.refs_5_.refs_2_), channel_id=1, source_target_pairs={{0,2},{1,3},{2,0},{3,1},{4,6},{5,7},{6,4},{7,5},{8,10},{9,11},{10,... | collective-permute-start | bytes 1179656 | tf_op jit(solution)/shard_map/ppermute | solution.py:27
  61.2 1.9 %sums_b_0.1 = (f32[3,512,512]{2,1,0:T(8,128)S(1)}, f32[8,128]{1,0:T(8,128)S(1)}) custom-call(bf16[3,2048,512]{2,1,0:T(8,128)(2,1)} %refs_1_.25, bf16[3,2048,512]{2,1,0:T(8,128)(2,1)} %refs_1_.25, bf16[3,2048,512]{2,1,0:T(8,128)(2,1)} %copy-done.2, bf16[192,512]{1,0:T(8,128)(2,1)S(1)} %collective-permute-done.10.refs_7_.refs_3_, bf16[2560,512]{1,0:T(8,128)(2,1)} %copy-done, ...), custom_call_target="tpu_custom_call" | custom-call | tf_op jit(solution)/shard_map/sums_b_0/pallas_call | solution.py:65
  63.0 2.3 %sums_a_0.1 = (f32[2,512,512]{2,1,0:T(8,128)S(1)}, f32[8,128]{1,0:T(8,128)S(1)}) custom-call(bf16[3,2048,512]{2,1,0:T(8,128)(2,1)} %refs_1_.25, bf16[3,2048,512]{2,1,0:T(8,128)(2,1)} %refs_1_.25, bf16[192,512]{1,0:T(8,128)(2,1)S(1)} %get-tuple-element.101.refs_3_.refs_2_, bf16[384,512]{1,0:T(8,128)(2,1)S(1)} %collective-permute-done.8.refs_3_, ...), custom_call_target="tpu_custom_call" | custom-call | tf_op jit(solution)/shard_map/sums_a_0/pallas_call | solution.py:65
  65.3 8.6 %collective-permute-done.12.refs_3_.refs_2_ = bf16[384,512]{1,0:T(8,128)(2,1)S(1)} collective-permute-done((bf16[384,512]{1,0:T(8,128)(2,1)S(1)}, bf16[384,512]{1,0:T(8,128)(2,1)S(1)}, u32[]{:S(2)}, u32[]{:S(2)}) %collective-permute-start.12) | collective-permute-done | bytes 393248 | tf_op jit(solution)/shard_map/ppermute | solution.py:27
  75.0 2.6 %collective-permute-start.15 = (bf16[384,512]{1,0:T(8,128)(2,1)S(1)}, bf16[384,512]{1,0:T(8,128)(2,1)S(1)}, u32[]{:S(2)}, u32[]{:S(2)}) collective-permute-start(bf16[384,512]{1,0:T(8,128)(2,1)S(1)} %get-tuple-element.121.refs_2_), channel_id=1, source_target_pairs={{0,4},{1,5},{2,6},{3,7},{4,0},{5,1},{6,2},{7,3},{8,12},{9,13},{10,... | collective-permute-start | bytes 1179656 | tf_op jit(solution)/shard_map/ppermute | solution.py:27
  77.6 2.2 %next_grads_1_1.1 = (bf16[2560,512]{1,0:T(8,128)(2,1)}, f32[8,128]{1,0:T(8,128)S(1)}) custom-call(bf16[3,512,512]{2,1,0:T(8,128)(2,1)S(1)} %copy-done.1, bf16[512,512]{1,0:T(8,128)(2,1)S(1)} %collective-permute-done.9.refs_5_.refs_1_, bf16[384,512]{1,0:T(8,128)(2,1)S(1)} %get-tuple-element.107.refs_5_.refs_2_, ...), custom_call_target="tpu_custom_call", output_to_operand_aliasing={{0}: (5, {})} | custom-call | tf_op jit(solution)/shard_map/next_grads_1_1/pallas_call | solution.py:65
  79.8 2.4 %sums_b_1.1 = (f32[3,512,512]{2,1,0:T(8,128)S(1)}, f32[8,128]{1,0:T(8,128)S(1)}) custom-call(bf16[3,2048,512]{2,1,0:T(8,128)(2,1)} %refs_1_.25, bf16[3,2048,512]{2,1,0:T(8,128)(2,1)} %refs_1_.25, bf16[3,2048,512]{2,1,0:T(8,128)(2,1)} %copy-done.2, bf16[384,512]{1,0:T(8,128)(2,1)S(1)} %collective-permute-done.13.refs_3_, ...), custom_call_target="tpu_custom_call" | custom-call | tf_op jit(solution)/shard_map/sums_b_1/pallas_call | solution.py:65
  82.2 1.9 %sums_a_2.1 = (f32[2,512,512]{2,1,0:T(8,128)S(1)}, f32[8,128]{1,0:T(8,128)S(1)}) custom-call(bf16[3,2048,512]{2,1,0:T(8,128)(2,1)} %refs_1_.25, bf16[3,2048,512]{2,1,0:T(8,128)(2,1)} %refs_1_.25, bf16[384,512]{1,0:T(8,128)(2,1)S(1)} %collective-permute-done.12.refs_3_.refs_2_, bf16[384,512]{1,0:T(8,128)(2,1)S(1)} %get-tuple-element.112.refs_3_.refs_2_, ...), custom_call_target="tpu_custom_call" | custom-call | tf_op jit(solution)/shard_map/sums_a_2/pallas_call | solution.py:65
  85.4 1.9 %collective-permute-start.22 = (bf16[448,512]{1,0:T(8,128)(2,1)S(1)}, bf16[448,512]{1,0:T(8,128)(2,1)S(1)}, u32[]{:S(2)}, u32[]{:S(2)}) collective-permute-start(bf16[448,512]{1,0:T(8,128)(2,1)S(1)} %get-tuple-element.122.refs_3_.refs_2_), channel_id=1, source_target_pairs={{0,2},{1,3},{2,0},{3,1},{4,6},{5,7},{6,4},{7,5},{8,10},{9,11},{10,... | collective-permute-start | bytes 1376264 | tf_op jit(solution)/shard_map/ppermute | solution.py:27
  87.3 1.7 %collective-permute-start.14 = (bf16[256,512]{1,0:T(8,128)(2,1)S(1)}, bf16[256,512]{1,0:T(8,128)(2,1)S(1)}, u32[]{:S(2)}, u32[]{:S(2)}) collective-permute-start(bf16[256,512]{1,0:T(8,128)(2,1)S(1)} %get-tuple-element.120.refs_2_), channel_id=1, source_target_pairs={{0,4},{1,5},{2,6},{3,7},{4,0},{5,1},{6,2},{7,3},{8,12},{9,13},{10,... | collective-permute-start | bytes 786440 | tf_op jit(solution)/shard_map/ppermute | solution.py:27
  89.0 8.4 %collective-permute-done.16.refs_3_ = bf16[384,512]{1,0:T(8,128)(2,1)S(1)} collective-permute-done((bf16[384,512]{1,0:T(8,128)(2,1)S(1)}, bf16[384,512]{1,0:T(8,128)(2,1)S(1)}, u32[]{:S(2)}, u32[]{:S(2)}) %collective-permute-start.16) | collective-permute-done | bytes 393248 | tf_op jit(solution)/shard_map/ppermute | solution.py:27
  98.8 2.4 %sums_b_2.1 = (f32[3,512,512]{2,1,0:T(8,128)S(1)}, f32[8,128]{1,0:T(8,128)S(1)}) custom-call(bf16[3,2048,512]{2,1,0:T(8,128)(2,1)} %refs_1_.25, bf16[3,2048,512]{2,1,0:T(8,128)(2,1)} %refs_1_.25, bf16[3,2048,512]{2,1,0:T(8,128)(2,1)} %copy-done.2, bf16[384,512]{1,0:T(8,128)(2,1)S(1)} %collective-permute-done.16.refs_3_, ...), custom_call_target="tpu_custom_call" | custom-call | tf_op jit(solution)/shard_map/sums_b_2/pallas_call | solution.py:65
  101.2 1.9 %sums_a_3.1 = (f32[2,512,512]{2,1,0:T(8,128)S(1)}, f32[8,128]{1,0:T(8,128)S(1)}) custom-call(bf16[3,2048,512]{2,1,0:T(8,128)(2,1)} %refs_1_.25, bf16[3,2048,512]{2,1,0:T(8,128)(2,1)} %refs_1_.25, bf16[448,512]{1,0:T(8,128)(2,1)S(1)} %collective-permute-done.11.refs_3_.refs_2_, bf16[448,512]{1,0:T(8,128)(2,1)S(1)} %get-tuple-element.122.refs_3_.refs_2_, ...), custom_call_target="tpu_custom_call" | custom-call | tf_op jit(solution)/shard_map/sums_a_3/pallas_call | solution.py:65
  103.8 1.9 %sums_a_4.1 = (f32[2,512,512]{2,1,0:T(8,128)S(1)}, f32[8,128]{1,0:T(8,128)S(1)}) custom-call(bf16[3,2048,512]{2,1,0:T(8,128)(2,1)} %refs_1_.25, bf16[3,2048,512]{2,1,0:T(8,128)(2,1)} %refs_1_.25, bf16[384,512]{1,0:T(8,128)(2,1)S(1)} %collective-permute-done.15.refs_3_.refs_2_, bf16[384,512]{1,0:T(8,128)(2,1)S(1)} %get-tuple-element.130.refs_3_.refs_2_, ...), custom_call_target="tpu_custom_call" | custom-call | tf_op jit(solution)/shard_map/sums_a_4/pallas_call | solution.py:65
  105.7 3.6 %collective-permute-done.14.refs_3_.refs_2_ = bf16[256,512]{1,0:T(8,128)(2,1)S(1)} collective-permute-done((bf16[256,512]{1,0:T(8,128)(2,1)S(1)}, bf16[256,512]{1,0:T(8,128)(2,1)S(1)}, u32[]{:S(2)}, u32[]{:S(2)}) %collective-permute-start.14) | collective-permute-done | bytes 262176 | tf_op jit(solution)/shard_map/ppermute | solution.py:27
  109.8 4.1 %collective-permute-start.20 = (bf16[256,512]{1,0:T(8,128)(2,1)S(1)}, bf16[256,512]{1,0:T(8,128)(2,1)S(1)}, u32[]{:S(2)}, u32[]{:S(2)}) collective-permute-start(bf16[256,512]{1,0:T(8,128)(2,1)S(1)} %get-tuple-element.134.refs_3_.refs_2_), channel_id=1, source_target_pairs={{0,2},{1,3},{2,0},{3,1},{4,6},{5,7},{6,4},{7,5},{8,10},{9,11},{10,... | collective-permute-start | bytes 786440 | tf_op jit(solution)/shard_map/ppermute | solution.py:27
  113.9 1.6 %sums_a_5.1 = (f32[2,128,512]{2,1,0:T(8,128)S(1)}, bf16[2,128,512]{2,1,0:T(8,128)(2,1)S(1)}, bf16[2,128,512]{2,1,0:T(8,128)(2,1)S(1)}, bf16[2,128,512]{2,1,0:T(8,128)(2,1)S(1)}, f32[8,128]{1,0:T(8,128)S(1)}) custom-call(bf16[3,2048,512]{2,1,0:T(8,128)(2,1)} %refs_1_.25, bf16[3,2048,512]{2,1,0:T(8,128)(2,1)} %refs_1_.25, ...), custom_call_target="tpu_custom_call" | custom-call | tf_op jit(solution)/shard_map/sums_a_5/pallas_call | solution.py:65
  116.9 1.5 collective-permute-start.18
  119.1 1.5 next_grads_1_3.1
  120.6 2.5 %sums_b_3.1 = (f32[3,512,512]{2,1,0:T(8,128)S(1)}, f32[8,128]{1,0:T(8,128)S(1)}) custom-call(bf16[3,2048,512]{2,1,0:T(8,128)(2,1)} %refs_1_.25, bf16[3,2048,512]{2,1,0:T(8,128)(2,1)} %refs_1_.25, bf16[3,2048,512]{2,1,0:T(8,128)(2,1)} %copy-done.2, bf16[448,512]{1,0:T(8,128)(2,1)S(1)} %collective-permute-done.22.refs_3_, ...), custom_call_target="tpu_custom_call" | custom-call | tf_op jit(solution)/shard_map/sums_b_3/pallas_call | solution.py:65
  123.5 1.4 next_grads_1_4.1
  124.9 2.4 %sums_b_4.1 = (f32[3,512,512]{2,1,0:T(8,128)S(1)}, f32[8,128]{1,0:T(8,128)S(1)}) custom-call(bf16[3,2048,512]{2,1,0:T(8,128)(2,1)} %refs_1_.25, bf16[3,2048,512]{2,1,0:T(8,128)(2,1)} %refs_1_.25, bf16[3,2048,512]{2,1,0:T(8,128)(2,1)} %copy-done.2, bf16[384,512]{1,0:T(8,128)(2,1)S(1)} %collective-permute-done.21.refs_3_, ...), custom_call_target="tpu_custom_call" | custom-call | tf_op jit(solution)/shard_map/sums_b_4/pallas_call | solution.py:65
  127.3 1.7 %collective-permute-done.20.refs_3_ = bf16[256,512]{1,0:T(8,128)(2,1)S(1)} collective-permute-done((bf16[256,512]{1,0:T(8,128)(2,1)S(1)}, bf16[256,512]{1,0:T(8,128)(2,1)S(1)}, u32[]{:S(2)}, u32[]{:S(2)}) %collective-permute-start.20) | collective-permute-done | bytes 262176 | tf_op jit(solution)/shard_map/ppermute | solution.py:27
  130.2 2.1 %sums_b_5.1 = (bf16[1,128,512]{2,1,0:T(8,128)(2,1)S(1)}, bf16[1,128,512]{2,1,0:T(8,128)(2,1)S(1)}, bf16[1,128,512]{2,1,0:T(8,128)(2,1)S(1)}, bf16[1,128,512]{2,1...) custom-call(bf16[3,2048,512]{2,1,0:T(8,128)(2,1)} %refs_1_.25, ...), custom_call_target="tpu_custom_call" | custom-call | tf_op jit(solution)/shard_map/sums_b_5/pallas_call | solution.py:65
  133.3 2.5 %collective-permute-start.24 = (bf16[1,128,512]{2,1,0:T(8,128)(2,1)S(1)}, bf16[1,128,512]{2,1,0:T(8,128)(2,1)S(1)}, u32[]{:S(2)}, u32[]{:S(2)}) collective-permute-start(bf16[1,128,512]{2,1,0:T(8,128)(2,1)S(1)} %get-tuple-element.157), channel_id=1, source_target_pairs={{0,2},{1,3},{2,0},{3,1},{4,6},{5,7},{6,4},{7,5},{8,10},{9,11},{10,... | collective-permute-start | bytes 393224 | tf_op jit(solution)/shard_map/ppermute | solution.py:37
  137.2 5.0 %collective-permute-done.31.refs_10_ = bf16[128,512]{1,0:T(8,128)(2,1)S(1)} collective-permute-done((bf16[128,512]{1,0:T(8,128)(2,1)S(1)}, bf16[128,512]{1,0:T(8,128)(2,1)S(1)}, u32[]{:S(2)}, u32[]{:S(2)}) %collective-permute-start.31) | collective-permute-done | bytes 131104 | tf_op jit(solution)/shard_map/ppermute | solution.py:27
  143.6 1.4 collective-permute-start.30
  146.6 2.6 %collective-permute-start.27 = (bf16[1,128,512]{2,1,0:T(8,128)(2,1)S(1)}, bf16[1,128,512]{2,1,0:T(8,128)(2,1)S(1)}, u32[]{:S(2)}, u32[]{:S(2)}) collective-permute-start(bf16[1,128,512]{2,1,0:T(8,128)(2,1)S(1)} %get-tuple-element.160), channel_id=1, source_target_pairs={{0,26},{1,27},{2,24},{3,25},{4,30},{5,31},{6,28},{7,29},{8,18},{9,... | collective-permute-start | bytes 393224 | tf_op jit(solution)/shard_map/ppermute | solution.py:37
  149.1 5.9 %last_grad.1 = (bf16[2048,512]{1,0:T(8,128)(2,1)}, f32[8,128]{1,0:T(8,128)S(1)}) custom-call(bf16[2560,512]{1,0:T(8,128)(2,1)} %get-tuple-element.154.refs_0_, bf16[2560,512]{1,0:T(8,128)(2,1)} %copy-done.3, bf16[3,512,512]{2,1,0:T(8,128)(2,1)S(1)} %copy-done.1, bf16[2560,512]{1,0:T(8,128)(2,1)} %copy-done.3, f32[8,128]{1,0:T(8,128)S(1)} %get-tuple-element.155.refs_4_), custom_call_target="tpu_custom_call" | custom-call | tf_op jit(solution)/shard_map/last_grad/pallas_call | solution.py:65
  155.0 1.6 collective-permute-done.27.refs_3_
  156.6 5.1 %collective-permute-done.29.refs_6_ = bf16[2,128,512]{2,1,0:T(8,128)(2,1)S(1)} collective-permute-done((bf16[2,128,512]{2,1,0:T(8,128)(2,1)S(1)}, bf16[2,128,512]{2,1,0:T(8,128)(2,1)S(1)}, u32[]{:S(2)}, u32[]{:S(2)}) %collective-permute-start.29) | collective-permute-done | bytes 262176 | tf_op jit(solution)/shard_map/ppermute | solution.py:27
  (54 shorter events, 21.8 us)
Async XLA Ops:
  0.6 20.9 %collective-permute-start.1 = (bf16[3,2048,512]{2,1,0:T(8,128)(2,1)}, bf16[3,2048,512]{2,1,0:T(8,128)(2,1)S(1)}, u32[]{:S(2)}, u32[]{:S(2)}) collective-permute-start(bf16[3,2048,512]{2,1,0:T(8,128)(2,1)} %refs_1_.25), channel_id=1, source_target_pairs={{0,1},{1,0},{2,3},{3,2},{4,5},{5,4},{6,7},{7,6},{8,9},{9,8},{10,11... | collective-permute-start | bytes 18874376 | tf_op jit(solution)/shard_map/ppermute | solution.py:27
  2.4 19.2 %collective-permute-start = (bf16[320,512]{1,0:T(8,128)(2,1)S(1)}, bf16[320,512]{1,0:T(8,128)(2,1)S(1)}, u32[]{:S(2)}, u32[]{:S(2)}) collective-permute-start(bf16[320,512]{1,0:T(8,128)(2,1)S(1)} %get-tuple-element.87), channel_id=1, source_target_pairs={{0,4},{1,5},{2,6},{3,7},{4,0},{5,1},{6,2},{7,3},{8,12},{9,13},{10,... | collective-permute-start | bytes 983048 | tf_op jit(solution)/shard_map/ppermute | solution.py:27
  10.6 6.0 %collective-permute-start.2 = (bf16[1,128,512]{2,1,0:T(8,128)(2,1)S(1)}, bf16[1,128,512]{2,1,0:T(8,128)(2,1)S(1)}, u32[]{:S(2)}, u32[]{:S(2)}) collective-permute-start(bf16[1,128,512]{2,1,0:T(8,128)(2,1)S(1)} %get-tuple-element.90), channel_id=1, source_target_pairs={{0,8},{8,0},{16,24},{24,16},{1,9},{9,1},{17,25},{25,17},{2,10},{10... | collective-permute-start | bytes 393224 | tf_op jit(solution)/shard_map/ppermute | solution.py:27
  12.2 8.1 %collective-permute-start.3 = (bf16[1,128,512]{2,1,0:T(8,128)(2,1)S(1)}, bf16[1,128,512]{2,1,0:T(8,128)(2,1)S(1)}, u32[]{:S(2)}, u32[]{:S(2)}) collective-permute-start(bf16[1,128,512]{2,1,0:T(8,128)(2,1)S(1)} %get-tuple-element.91), channel_id=1, source_target_pairs={{0,16},{8,24},{16,0},{24,8},{1,17},{9,25},{17,1},{25,9},{2,18},{10... | collective-permute-start | bytes 393224 | tf_op jit(solution)/shard_map/ppermute | solution.py:27
  13.7 6.6 %collective-permute-start.4 = (bf16[1,128,512]{2,1,0:T(8,128)(2,1)S(1)}, bf16[1,128,512]{2,1,0:T(8,128)(2,1)S(1)}, u32[]{:S(2)}, u32[]{:S(2)}) collective-permute-start(bf16[1,128,512]{2,1,0:T(8,128)(2,1)S(1)} %get-tuple-element.92), channel_id=1, source_target_pairs={{0,24},{8,16},{16,8},{24,0},{1,25},{9,17},{17,9},{25,1},{2,26},{10... | collective-permute-start | bytes 393224 | tf_op jit(solution)/shard_map/ppermute | solution.py:27
  16.6 24.0 %collective-permute-start.9 = (bf16[512,512]{1,0:T(8,128)(2,1)S(1)}, bf16[512,512]{1,0:T(8,128)(2,1)S(1)}, u32[]{:S(2)}, u32[]{:S(2)}) collective-permute-start(bf16[512,512]{1,0:T(8,128)(2,1)S(1)} %get-tuple-element.99), channel_id=1, source_target_pairs={{0,2},{1,3},{2,0},{3,1},{4,6},{5,7},{6,4},{7,5},{8,10},{9,11},{10,... | collective-permute-start | bytes 1572872 | tf_op jit(solution)/shard_map/ppermute | solution.py:27
  21.6 2.6 %copy-start.2 = (bf16[3,2048,512]{2,1,0:T(8,128)(2,1)}, bf16[3,2048,512]{2,1,0:T(8,128)(2,1)S(1)}, u32[]{:S(2)}) copy-start(bf16[3,2048,512]{2,1,0:T(8,128)(2,1)S(1)} %collective-permute-done.1.refs_4_.refs_2_) | copy-start | bytes 18874372
  24.2 11.1 %copy-start.1 = (bf16[3,512,512]{2,1,0:T(8,128)(2,1)S(1)}, bf16[3,512,512]{2,1,0:T(8,128)(2,1)}, u32[]{:S(2)}) copy-start(bf16[3,512,512]{2,1,0:T(8,128)(2,1)} %refs_2_.5) | copy-start | bytes 4718596
  25.8 29.9 %collective-permute-start.8 = (bf16[384,512]{1,0:T(8,128)(2,1)S(1)}, bf16[384,512]{1,0:T(8,128)(2,1)S(1)}, u32[]{:S(2)}, u32[]{:S(2)}) collective-permute-start(bf16[384,512]{1,0:T(8,128)(2,1)S(1)} %get-tuple-element.98.refs_2_), channel_id=1, source_target_pairs={{0,4},{1,5},{2,6},{3,7},{4,0},{5,1},{6,2},{7,3},{8,12},{9,13},{10,... | collective-permute-start | bytes 1179656 | tf_op jit(solution)/shard_map/ppermute | solution.py:27
  25.9 5.9 %collective-permute-start.5 = (bf16[128,512]{1,0:T(8,128)(2,1)S(1)}, bf16[128,512]{1,0:T(8,128)(2,1)S(1)}, u32[]{:S(2)}, u32[]{:S(2)}) collective-permute-start(bf16[128,512]{1,0:T(8,128)(2,1)S(1)} %get-tuple-element.95.refs_0_), channel_id=1, source_target_pairs={{0,8},{8,0},{16,24},{24,16},{1,9},{9,1},{17,25},{25,17},{2,10},{10... | collective-permute-start | bytes 393224 | tf_op jit(solution)/shard_map/ppermute | solution.py:27
  27.5 7.8 %collective-permute-start.6 = (bf16[128,512]{1,0:T(8,128)(2,1)S(1)}, bf16[128,512]{1,0:T(8,128)(2,1)S(1)}, u32[]{:S(2)}, u32[]{:S(2)}) collective-permute-start(bf16[128,512]{1,0:T(8,128)(2,1)S(1)} %get-tuple-element.95.refs_0_), channel_id=1, source_target_pairs={{0,16},{8,24},{16,0},{24,8},{1,17},{9,25},{17,1},{25,9},{2,18},{10... | collective-permute-start | bytes 393224 | tf_op jit(solution)/shard_map/ppermute | solution.py:27
  29.0 6.3 %collective-permute-start.7 = (bf16[128,512]{1,0:T(8,128)(2,1)S(1)}, bf16[128,512]{1,0:T(8,128)(2,1)S(1)}, u32[]{:S(2)}, u32[]{:S(2)}) collective-permute-start(bf16[128,512]{1,0:T(8,128)(2,1)S(1)} %get-tuple-element.95.refs_0_), channel_id=1, source_target_pairs={{0,24},{8,16},{16,8},{24,0},{1,25},{9,17},{17,9},{25,1},{2,26},{10... | collective-permute-start | bytes 393224 | tf_op jit(solution)/shard_map/ppermute | solution.py:27
  36.4 11.7 %collective-permute-start.10 = (bf16[192,512]{1,0:T(8,128)(2,1)S(1)}, bf16[192,512]{1,0:T(8,128)(2,1)S(1)}, u32[]{:S(2)}, u32[]{:S(2)}) collective-permute-start(bf16[192,512]{1,0:T(8,128)(2,1)S(1)} %get-tuple-element.103.refs_6_.refs_4_), channel_id=1, source_target_pairs={{0,2},{1,3},{2,0},{3,1},{4,6},{5,7},{6,4},{7,5},{8,10},{9,11},{10,... | collective-permute-start | bytes 589832 | tf_op jit(solution)/shard_map/ppermute | solution.py:27
  40.4 33.5 %collective-permute-start.12 = (bf16[384,512]{1,0:T(8,128)(2,1)S(1)}, bf16[384,512]{1,0:T(8,128)(2,1)S(1)}, u32[]{:S(2)}, u32[]{:S(2)}) collective-permute-start(bf16[384,512]{1,0:T(8,128)(2,1)S(1)} %get-tuple-element.106.refs_2_), channel_id=1, source_target_pairs={{0,4},{1,5},{2,6},{3,7},{4,0},{5,1},{6,2},{7,3},{8,12},{9,13},{10,... | collective-permute-start | bytes 1179656 | tf_op jit(solution)/shard_map/ppermute | solution.py:27
  57.0 1.6 copy-start
  58.6 25.5 %collective-permute-start.11 = (bf16[448,512]{1,0:T(8,128)(2,1)S(1)}, bf16[448,512]{1,0:T(8,128)(2,1)S(1)}, u32[]{:S(2)}, u32[]{:S(2)}) collective-permute-start(bf16[448,512]{1,0:T(8,128)(2,1)S(1)} %get-tuple-element.105.refs_2_), channel_id=1, source_target_pairs={{0,4},{1,5},{2,6},{3,7},{4,0},{5,1},{6,2},{7,3},{8,12},{9,13},{10,... | collective-permute-start | bytes 1376264 | tf_op jit(solution)/shard_map/ppermute | solution.py:27
  58.6 19.0 %collective-permute-start.13 = (bf16[384,512]{1,0:T(8,128)(2,1)S(1)}, bf16[384,512]{1,0:T(8,128)(2,1)S(1)}, u32[]{:S(2)}, u32[]{:S(2)}) collective-permute-start(bf16[384,512]{1,0:T(8,128)(2,1)S(1)} %get-tuple-element.107.refs_5_.refs_2_), channel_id=1, source_target_pairs={{0,2},{1,3},{2,0},{3,1},{4,6},{5,7},{6,4},{7,5},{8,10},{9,11},{10,... | collective-permute-start | bytes 1179656 | tf_op jit(solution)/shard_map/ppermute | solution.py:27
  74.9 22.5 %collective-permute-start.16 = (bf16[384,512]{1,0:T(8,128)(2,1)S(1)}, bf16[384,512]{1,0:T(8,128)(2,1)S(1)}, u32[]{:S(2)}, u32[]{:S(2)}) collective-permute-start(bf16[384,512]{1,0:T(8,128)(2,1)S(1)} %get-tuple-element.112.refs_3_.refs_2_), channel_id=1, source_target_pairs={{0,2},{1,3},{2,0},{3,1},{4,6},{5,7},{6,4},{7,5},{8,10},{9,11},{10,... | collective-permute-start | bytes 1179656 | tf_op jit(solution)/shard_map/ppermute | solution.py:27
  75.0 28.1 %collective-permute-start.15 = (bf16[384,512]{1,0:T(8,128)(2,1)S(1)}, bf16[384,512]{1,0:T(8,128)(2,1)S(1)}, u32[]{:S(2)}, u32[]{:S(2)}) collective-permute-start(bf16[384,512]{1,0:T(8,128)(2,1)S(1)} %get-tuple-element.121.refs_2_), channel_id=1, source_target_pairs={{0,4},{1,5},{2,6},{3,7},{4,0},{5,1},{6,2},{7,3},{8,12},{9,13},{10,... | collective-permute-start | bytes 1179656 | tf_op jit(solution)/shard_map/ppermute | solution.py:27
  85.4 33.0 %collective-permute-start.22 = (bf16[448,512]{1,0:T(8,128)(2,1)S(1)}, bf16[448,512]{1,0:T(8,128)(2,1)S(1)}, u32[]{:S(2)}, u32[]{:S(2)}) collective-permute-start(bf16[448,512]{1,0:T(8,128)(2,1)S(1)} %get-tuple-element.122.refs_3_.refs_2_), channel_id=1, source_target_pairs={{0,2},{1,3},{2,0},{3,1},{4,6},{5,7},{6,4},{7,5},{8,10},{9,11},{10,... | collective-permute-start | bytes 1376264 | tf_op jit(solution)/shard_map/ppermute | solution.py:27
  87.3 22.0 %collective-permute-start.14 = (bf16[256,512]{1,0:T(8,128)(2,1)S(1)}, bf16[256,512]{1,0:T(8,128)(2,1)S(1)}, u32[]{:S(2)}, u32[]{:S(2)}) collective-permute-start(bf16[256,512]{1,0:T(8,128)(2,1)S(1)} %get-tuple-element.120.refs_2_), channel_id=1, source_target_pairs={{0,4},{1,5},{2,6},{3,7},{4,0},{5,1},{6,2},{7,3},{8,12},{9,13},{10,... | collective-permute-start | bytes 786440 | tf_op jit(solution)/shard_map/ppermute | solution.py:27
  103.8 19.7 %collective-permute-start.21 = (bf16[384,512]{1,0:T(8,128)(2,1)S(1)}, bf16[384,512]{1,0:T(8,128)(2,1)S(1)}, u32[]{:S(2)}, u32[]{:S(2)}) collective-permute-start(bf16[384,512]{1,0:T(8,128)(2,1)S(1)} %get-tuple-element.130.refs_3_.refs_2_), channel_id=1, source_target_pairs={{0,2},{1,3},{2,0},{3,1},{4,6},{5,7},{6,4},{7,5},{8,10},{9,11},{10,... | collective-permute-start | bytes 1179656 | tf_op jit(solution)/shard_map/ppermute | solution.py:27
  109.8 19.2 %collective-permute-start.20 = (bf16[256,512]{1,0:T(8,128)(2,1)S(1)}, bf16[256,512]{1,0:T(8,128)(2,1)S(1)}, u32[]{:S(2)}, u32[]{:S(2)}) collective-permute-start(bf16[256,512]{1,0:T(8,128)(2,1)S(1)} %get-tuple-element.134.refs_3_.refs_2_), channel_id=1, source_target_pairs={{0,2},{1,3},{2,0},{3,1},{4,6},{5,7},{6,4},{7,5},{8,10},{9,11},{10,... | collective-permute-start | bytes 786440 | tf_op jit(solution)/shard_map/ppermute | solution.py:27
  115.6 16.7 %collective-permute-start.17 = (bf16[2,128,512]{2,1,0:T(8,128)(2,1)S(1)}, bf16[2,128,512]{2,1,0:T(8,128)(2,1)S(1)}, u32[]{:S(2)}, u32[]{:S(2)}) collective-permute-start(bf16[2,128,512]{2,1,0:T(8,128)(2,1)S(1)} %get-tuple-element.138), channel_id=1, source_target_pairs={{0,8},{8,0},{16,24},{24,16},{1,9},{9,1},{17,25},{25,17},{2,10},{10... | collective-permute-start | bytes 786440 | tf_op jit(solution)/shard_map/ppermute | solution.py:27
  116.9 15.4 %collective-permute-start.18 = (bf16[2,128,512]{2,1,0:T(8,128)(2,1)S(1)}, bf16[2,128,512]{2,1,0:T(8,128)(2,1)S(1)}, u32[]{:S(2)}, u32[]{:S(2)}) collective-permute-start(bf16[2,128,512]{2,1,0:T(8,128)(2,1)S(1)} %get-tuple-element.139), channel_id=1, source_target_pairs={{0,16},{8,24},{16,0},{24,8},{1,17},{9,25},{17,1},{25,9},{2,18},{10... | collective-permute-start | bytes 786440 | tf_op jit(solution)/shard_map/ppermute | solution.py:27
  118.5 13.8 %collective-permute-start.19 = (bf16[2,128,512]{2,1,0:T(8,128)(2,1)S(1)}, bf16[2,128,512]{2,1,0:T(8,128)(2,1)S(1)}, u32[]{:S(2)}, u32[]{:S(2)}) collective-permute-start(bf16[2,128,512]{2,1,0:T(8,128)(2,1)S(1)} %get-tuple-element.140), channel_id=1, source_target_pairs={{0,24},{8,16},{16,8},{24,0},{1,25},{9,17},{17,9},{25,1},{2,26},{10... | collective-permute-start | bytes 786440 | tf_op jit(solution)/shard_map/ppermute | solution.py:27
  132.4 14.1 %collective-permute-start.23 = (bf16[2560,512]{1,0:T(8,128)(2,1)}, bf16[2560,512]{1,0:T(8,128)(2,1)S(1)}, u32[]{:S(2)}, u32[]{:S(2)}) collective-permute-start(bf16[2560,512]{1,0:T(8,128)(2,1)} %get-tuple-element.154.refs_0_), channel_id=1, source_target_pairs={{0,1},{1,0},{2,3},{3,2},{4,5},{5,4},{6,7},{7,6},{8,9},{9,8},{10,11... | collective-permute-start | bytes 7864328 | tf_op jit(solution)/shard_map/ppermute | solution.py:27
  132.5 9.7 %collective-permute-start.31 = (bf16[128,512]{1,0:T(8,128)(2,1)S(1)}, bf16[128,512]{1,0:T(8,128)(2,1)S(1)}, u32[]{:S(2)}, u32[]{:S(2)}) collective-permute-start(bf16[128,512]{1,0:T(8,128)(2,1)S(1)} %get-tuple-element.167), channel_id=1, source_target_pairs={{0,4},{1,5},{2,6},{3,7},{4,0},{5,1},{6,2},{7,3},{8,12},{9,13},{10,... | collective-permute-start | bytes 393224 | tf_op jit(solution)/shard_map/ppermute | solution.py:27
  133.3 10.3 %collective-permute-start.24 = (bf16[1,128,512]{2,1,0:T(8,128)(2,1)S(1)}, bf16[1,128,512]{2,1,0:T(8,128)(2,1)S(1)}, u32[]{:S(2)}, u32[]{:S(2)}) collective-permute-start(bf16[1,128,512]{2,1,0:T(8,128)(2,1)S(1)} %get-tuple-element.157), channel_id=1, source_target_pairs={{0,2},{1,3},{2,0},{3,1},{4,6},{5,7},{6,4},{7,5},{8,10},{9,11},{10,... | collective-permute-start | bytes 393224 | tf_op jit(solution)/shard_map/ppermute | solution.py:37
  135.8 10.3 %collective-permute-start.25 = (bf16[1,128,512]{2,1,0:T(8,128)(2,1)S(1)}, bf16[1,128,512]{2,1,0:T(8,128)(2,1)S(1)}, u32[]{:S(2)}, u32[]{:S(2)}) collective-permute-start(bf16[1,128,512]{2,1,0:T(8,128)(2,1)S(1)} %get-tuple-element.158), channel_id=1, source_target_pairs={{0,10},{1,11},{2,8},{3,9},{4,14},{5,15},{6,12},{7,13},{8,2},{9,3},... | collective-permute-start | bytes 393224 | tf_op jit(solution)/shard_map/ppermute | solution.py:37
  136.5 20.1 %collective-permute-start.28 = (bf16[2,128,512]{2,1,0:T(8,128)(2,1)S(1)}, bf16[2,128,512]{2,1,0:T(8,128)(2,1)S(1)}, u32[]{:S(2)}, u32[]{:S(2)}) collective-permute-start(bf16[2,128,512]{2,1,0:T(8,128)(2,1)S(1)} %get-tuple-element.162), channel_id=1, source_target_pairs={{0,8},{8,0},{16,24},{24,16},{1,9},{9,1},{17,25},{25,17},{2,10},{10... | collective-permute-start | bytes 786440 | tf_op jit(solution)/shard_map/ppermute | solution.py:27
  142.2 19.5 %collective-permute-start.29 = (bf16[2,128,512]{2,1,0:T(8,128)(2,1)S(1)}, bf16[2,128,512]{2,1,0:T(8,128)(2,1)S(1)}, u32[]{:S(2)}, u32[]{:S(2)}) collective-permute-start(bf16[2,128,512]{2,1,0:T(8,128)(2,1)S(1)} %get-tuple-element.163), channel_id=1, source_target_pairs={{0,16},{8,24},{16,0},{24,8},{1,17},{9,25},{17,1},{25,9},{2,18},{10... | collective-permute-start | bytes 786440 | tf_op jit(solution)/shard_map/ppermute | solution.py:27
  143.6 18.1 %collective-permute-start.30 = (bf16[2,128,512]{2,1,0:T(8,128)(2,1)S(1)}, bf16[2,128,512]{2,1,0:T(8,128)(2,1)S(1)}, u32[]{:S(2)}, u32[]{:S(2)}) collective-permute-start(bf16[2,128,512]{2,1,0:T(8,128)(2,1)S(1)} %get-tuple-element.164), channel_id=1, source_target_pairs={{0,24},{8,16},{16,8},{24,0},{1,25},{9,17},{17,9},{25,1},{2,26},{10... | collective-permute-start | bytes 786440 | tf_op jit(solution)/shard_map/ppermute | solution.py:27
  146.0 9.0 %collective-permute-start.26 = (bf16[1,128,512]{2,1,0:T(8,128)(2,1)S(1)}, bf16[1,128,512]{2,1,0:T(8,128)(2,1)S(1)}, u32[]{:S(2)}, u32[]{:S(2)}) collective-permute-start(bf16[1,128,512]{2,1,0:T(8,128)(2,1)S(1)} %get-tuple-element.159), channel_id=1, source_target_pairs={{0,18},{1,19},{2,16},{3,17},{4,22},{5,23},{6,20},{7,21},{8,26},{9,... | collective-permute-start | bytes 393224 | tf_op jit(solution)/shard_map/ppermute | solution.py:37
  146.6 2.6 %copy-start.3 = (bf16[2560,512]{1,0:T(8,128)(2,1)}, bf16[2560,512]{1,0:T(8,128)(2,1)S(1)}, u32[]{:S(2)}) copy-start(bf16[2560,512]{1,0:T(8,128)(2,1)S(1)} %collective-permute-done.23.refs_1_.refs_3_) | copy-start | bytes 7864324
  146.6 10.0 %collective-permute-start.27 = (bf16[1,128,512]{2,1,0:T(8,128)(2,1)S(1)}, bf16[1,128,512]{2,1,0:T(8,128)(2,1)S(1)}, u32[]{:S(2)}, u32[]{:S(2)}) collective-permute-start(bf16[1,128,512]{2,1,0:T(8,128)(2,1)S(1)} %get-tuple-element.160), channel_id=1, source_target_pairs={{0,26},{1,27},{2,24},{3,25},{4,30},{5,31},{6,28},{7,29},{8,18},{9,... | collective-permute-start | bytes 393224 | tf_op jit(solution)/shard_map/ppermute | solution.py:37

commit v4 on v3

--- a/solution.py
+++ b/solution.py
@@ -107,7 +107,7 @@
     return chain(
         body,
         name,
-        [piece[0] for piece in flat] + [in_hbm(a) for a in deps],
+        [piece[0] for piece in flat] + list(deps),
         [ANY] * (n + len(deps)),
         [
             jax.ShapeDtypeStruct((sum(p[2] for p in block), block[0][0].shape[-1]), block[0][0].dtype)
@@ -191,7 +191,7 @@
     if into is not None:
         if not isinstance(into[0], jax.ShapeDtypeStruct):
             aliases[len(operands)] = len(out_shape)
-            operands.append(in_hbm(into[0]))
+            operands.append(into[0])
             in_specs.append(ANY)
         out_shape.append(jax.ShapeDtypeStruct(into[0].shape, into[0].dtype))
         out_specs.append(ANY)
@@ -238,11 +238,11 @@
     return chain(body, name, operands, in_specs, out_shape, out_specs, scratch, aliases)
 
 
-def last_grad(chain, both, far_both, w_self, tokens):
+def last_grad(chain, both, far_both, w_self, tokens, hold):
     width = both.shape[1]
     steps = max(1, tokens // width)
 
-    def body(grad_ref, far_ref, a_ref, c_ref, out_ref):
+    def body(grad_ref, far_ref, a_ref, c_ref, _, out_ref, __):
         total = times_trans(grad_ref[...], a_ref[0]) + times_trans(far_ref[...], c_ref[...])
         out_ref[...] = total.astype(jnp.bfloat16)
 
@@ -250,12 +250,13 @@
     return chain(
         body,
         "last_grad",
-        [in_hbm(both), in_hbm(far_both), w_self, in_hbm(far_both)],
-        [rows, rows, weight_block(w_self, 0), pl.BlockSpec((width, width), lambda i: (tokens // width, 0))],
-        [jax.ShapeDtypeStruct((tokens, width), both.dtype)],
-        [rows],
+        [both, far_both, w_self, far_both, hold],
+        [rows, rows, weight_block(w_self, 0), pl.BlockSpec((width, width), lambda i: (tokens // width, 0)), ANY],
+        [jax.ShapeDtypeStruct((tokens, width), both.dtype), jax.ShapeDtypeStruct(hold.shape, hold.dtype)],
+        [rows, ANY],
+        aliases={4: 1},
         grid=steps,
-    )[0]
+    )
 
 
 def weight_block(w_self, level):
@@ -271,7 +272,7 @@
     operands = [x for x, _, _ in xs]
     in_specs = [ANY] * len(xs)
     for side in sides:
-        operands += side if isinstance(side, list) else [in_hbm(side)]
+        operands += side if isinstance(side, list) else [side]
         in_specs += [WHOLE] * len(side) if isinstance(side, list) else [ANY]
     if before is not None:
         operands.append(before)
@@ -359,7 +360,7 @@
     return chain(
         body,
         name,
-        [*terms, in_hbm(hold)],
+        [*terms, hold],
         [WHOLE] * m + [ANY],
         [*out_shape, jax.ShapeDtypeStruct(hold.shape, hold.dtype)],
         [*out_specs, ANY],
@@ -458,7 +459,6 @@
         VMEM_LIMIT,
         [far_inputs],
     )
-    far_inputs = in_hbm(far_inputs)
     far[2][0], near[2][0], near[2][1] = [rows], [starts[0]], [starts[1]]
     send(2, 1)
     shares_2 = [(share_2, place_of(0))]
@@ -470,10 +470,10 @@
 
     grad = jax.ShapeDtypeStruct((tokens + width, width), cotangent.dtype)
 
-    def level_1(ks, block=None):
+    def level_1(ks, block=None, fetch=()):
         jobs = [job(1, k) for k in ks]
         into = (grad, cuts[ks[0]][0])
-        return next_grads(chain, w_self, jobs, f"next_grads_1_{ks[0]}", into, (), (), block)
+        return next_grads(chain, w_self, jobs, f"next_grads_1_{ks[0]}", into, fetch, (), block)
 
     def sums_a(ks, before, last=None):
         xs = [(saved_inputs, (2,), 0), (saved_inputs, (1,), 0)]
@@ -497,18 +497,20 @@
             [job(2, k)] + ([job(1, 0)] if k == 1 else []),
             f"next_grads_{k}",
             (grad, 0) if k == 1 else None,
-            [(cotangent, (), *cuts[ahead])] if ahead < n else [],
+            [(cotangent, (), *cuts[ahead])] if ahead < min(4, n) else [],
         )
         if k == 1:
             grad = done.pop()
-        if ahead < n:
+        if ahead < min(4, n):
             near[2][ahead] = [done.pop()]
             send(2, ahead)
         near[1][k] = done
         send(1, k)
         if 2 <= k < z - 1:
             block = (w_cross, 0, tokens) if k == 2 else None
-            (grad,) = level_1([k - 1], block)
+            rows, grad = level_1([k - 1], block, [(cotangent, (), *cuts[ahead])])
+            near[2][ahead] = [rows]
+            send(2, ahead)
         if 1 <= k < z - 1:
             (sum_b,) = sums_b([k - 1], sum_b)
         if 1 <= k < z:
@@ -522,9 +524,9 @@
     cross_1 = [swap_both(t, k, 1 << 1) for k, t in enumerate(terms[:parts])]
     sum_c = spread(terms[parts:])
     cross_2, self_1, grad = add_terms(chain, sum_a, "add_a", (jnp.bfloat16, jnp.float32), grad)
+    far_grad = swap(grad, "narrow", 1 << 0)
+    out, cross_2 = last_grad(chain, grad, far_grad, w_self, tokens, cross_2)
     cross_2 = swap(cross_2, "narrow", 1 << 2)
-    far_grad = swap(grad, "narrow", 1 << 0)
-    out = last_grad(chain, grad, far_grad, w_self, tokens)
     grad_self, grad_cross = last_sums(chain, cross_1, sum_c, self_1, self_2, cross_2)
     return out, grad_self, grad_cross
 

time: 164 us -> 155 us (0.945)
  Pallas kernels: 51.4 us -> 43.5 us
  local copies, waits for them, and re-layouts: 4.21 us -> 0.01 us
  starting transfers between devices: 44.5 us -> 47.3 us
    pallas_call x30, Pallas kernels: 51.4 us -> 43.5 us  [__call__(): pl.pallas_call(whole, grid=(grid,), out_shape=[*out_shape, TOKEN], in_spe...]
    ppermute x28, starting transfers between devices: 38.2 us -> 42.8 us  [swap(): lax.ppermute(array, axis, [(i, i ^ mask) for i in range(lax.axis_size(axi...]
    unnamed x8 -> x2, local copies, waits for them, and re-layouts: 4.21 us -> 0.01 us
    ppermute x4, starting transfers between devices: 6.3 us -> 4.48 us  [swap_both(): return lax.ppermute(array, ('wide', 'narrow'), pairs)]
  transfers between devices with their start and end apart: 32 -> 32, of which waited for: 16 -> 18; matrix products, arithmetic and copies ran while one was open for 0% -> 0% of each run, Pallas kernels for 31% -> 27%
where the time goes in v4:
time: 155 us; the launch traced here: 154 us
  waiting for transfers between devices  62.7 us (40%)
  starting transfers between devices  47.3 us (31%)
  Pallas kernels  43.5 us (28%)
    ppermute x28, waiting for transfers between devices, swap(): lax.ppermute(array, axis, [(i, i ^ mask) for i in range(lax.axis_size(axi...  58.9 us
    pallas_call x30, Pallas kernels, __call__(): pl.pallas_call(whole, grid=(grid,), out_shape=[*out_shape, TOKEN], in_spe...  43.5 us
    ppermute x28, starting transfers between devices, swap(): lax.ppermute(array, axis, [(i, i ^ mask) for i in range(lax.axis_size(axi...  42.8 us
    ppermute x4, starting transfers between devices, swap_both(): return lax.ppermute(array, ('wide', 'narrow'), pairs)  4.48 us
    ppermute x4, waiting for transfers between devices, swap_both(): return lax.ppermute(array, ('wide', 'narrow'), pairs)  3.82 us
  transfers between devices with their start and end apart: 32, of which 18 were waited for; matrix products, arithmetic and copies ran while one was open for 0% of the time, Pallas kernels for 27%

profile of v4, /device:TPU:0, one launch (start us, length us, event | category | flops | bytes accessed | tf_op | source)
XLA Modules:
  0.0 154.5 jit_solution(9125634130366186078)
XLA Ops:
  2.4 3.7 %collective-permute-start.1 = (bf16[320,512]{1,0:T(8,128)(2,1)S(1)}, bf16[320,512]{1,0:T(8,128)(2,1)S(1)}, u32[]{:S(2)}, u32[]{:S(2)}) collective-permute-start(bf16[320,512]{1,0:T(8,128)(2,1)S(1)} %get-tuple-element.89), channel_id=1, source_target_pairs={{0,4},{1,5},{2,6},{3,7},{4,0},{5,1},{6,2},{7,3},{8,12},{9,13},{10,... | collective-permute-start | bytes 983048 | tf_op jit(solution)/shard_map/ppermute | solution.py:27
  6.1 4.5 %self_sums_2.1 = (f32[1,128,512]{2,1,0:T(8,128)S(1)}, bf16[1,128,512]{2,1,0:T(8,128)(2,1)S(1)}, bf16[1,128,512]{2,1,0:T(8,128)(2,1)S(1)}, bf16[1,128,512]{2,1,0:T(8,128)(2,1)S(1)}, f32[8,128]{1,0:T(8,128)S(1)}) custom-call(bf16[3,2048,512]{2,1,0:T(8,128)(2,1)} %refs_1_.25, bf16[2048,512]{1,0:T(8,128)(2,1)} %refs_4_.7, f32[8,128]{1,0:T(8,128)S(1)} %get-tuple-element.90.refs_2_), custom_call_target="tpu_custom_call" | custom-call | tf_op jit(solution)/shard_map/self_sums_2/pallas_call | solution.py:65
  10.6 1.6 %collective-permute-start.3 = (bf16[1,128,512]{2,1,0:T(8,128)(2,1)S(1)}, bf16[1,128,512]{2,1,0:T(8,128)(2,1)S(1)}, u32[]{:S(2)}, u32[]{:S(2)}) collective-permute-start(bf16[1,128,512]{2,1,0:T(8,128)(2,1)S(1)} %get-tuple-element.92), channel_id=1, source_target_pairs={{0,8},{8,0},{16,24},{24,16},{1,9},{9,1},{17,25},{25,17},{2,10},{10... | collective-permute-start | bytes 393224 | tf_op jit(solution)/shard_map/ppermute | solution.py:27
  12.2 1.5 collective-permute-start.4
  14.2 2.5 %collective-permute-done.3.refs_1_ = bf16[1,128,512]{2,1,0:T(8,128)(2,1)S(1)} collective-permute-done((bf16[1,128,512]{2,1,0:T(8,128)(2,1)S(1)}, bf16[1,128,512]{2,1,0:T(8,128)(2,1)S(1)}, u32[]{:S(2)}, u32[]{:S(2)}) %collective-permute-start.3) | collective-permute-done | bytes 131104 | tf_op jit(solution)/shard_map/ppermute | solution.py:27
  16.6 1.6 %collective-permute-start = (bf16[512,512]{1,0:T(8,128)(2,1)S(1)}, bf16[512,512]{1,0:T(8,128)(2,1)S(1)}, u32[]{:S(2)}, u32[]{:S(2)}) collective-permute-start(bf16[512,512]{1,0:T(8,128)(2,1)S(1)} %get-tuple-element.88), channel_id=1, source_target_pairs={{0,2},{1,3},{2,0},{3,1},{4,6},{5,7},{6,4},{7,5},{8,10},{9,11},{10,... | collective-permute-start | bytes 1572872 | tf_op jit(solution)/shard_map/ppermute | solution.py:27
  18.2 2.1 %collective-permute-done.4.refs_2_ = bf16[1,128,512]{2,1,0:T(8,128)(2,1)S(1)} collective-permute-done((bf16[1,128,512]{2,1,0:T(8,128)(2,1)S(1)}, bf16[1,128,512]{2,1,0:T(8,128)(2,1)S(1)}, u32[]{:S(2)}, u32[]{:S(2)}) %collective-permute-start.4) | collective-permute-done | bytes 131104 | tf_op jit(solution)/shard_map/ppermute | solution.py:27
  21.6 1.6 %parted.1 = (bf16[128,512]{1,0:T(8,128)(2,1)S(1)}, bf16[192,512]{1,0:T(8,128)(2,1)S(1)}, bf16[192,512]{1,0:T(8,128)(2,1)S(1)}, bf16[384,512]{1,0:T(8,128)(2,1)S(1)}, f32[8,128]{1,0:T(8,128)S(1)}) custom-call(bf16[320,512]{1,0:T(8,128)(2,1)S(1)} %collective-permute-done.1.refs_0_.refs_1_, bf16[320,512]{1,0:T(8,128)(2,1)S(1)} %collective-permute-done.1.refs_0_.refs_1_, ...), custom_call_target="tpu_custom_call" | custom-call | tf_op jit(solution)/shard_map/parted/pallas_call | solution.py:65
  23.2 1.6 %collective-permute-start.6 = (bf16[128,512]{1,0:T(8,128)(2,1)S(1)}, bf16[128,512]{1,0:T(8,128)(2,1)S(1)}, u32[]{:S(2)}, u32[]{:S(2)}) collective-permute-start(bf16[128,512]{1,0:T(8,128)(2,1)S(1)} %get-tuple-element.97.refs_0_), channel_id=1, source_target_pairs={{0,8},{8,0},{16,24},{24,16},{1,9},{9,1},{17,25},{25,17},{2,10},{10... | collective-permute-start | bytes 393224 | tf_op jit(solution)/shard_map/ppermute | solution.py:27
  24.8 1.5 collective-permute-start.7
  26.8 2.3 %collective-permute-done.6.refs_1_ = bf16[128,512]{1,0:T(8,128)(2,1)S(1)} collective-permute-done((bf16[128,512]{1,0:T(8,128)(2,1)S(1)}, bf16[128,512]{1,0:T(8,128)(2,1)S(1)}, u32[]{:S(2)}, u32[]{:S(2)}) %collective-permute-start.6) | collective-permute-done | bytes 131104 | tf_op jit(solution)/shard_map/ppermute | solution.py:27
  29.1 3.5 %collective-permute-done.7.refs_2_ = bf16[128,512]{1,0:T(8,128)(2,1)S(1)} collective-permute-done((bf16[128,512]{1,0:T(8,128)(2,1)S(1)}, bf16[128,512]{1,0:T(8,128)(2,1)S(1)}, u32[]{:S(2)}, u32[]{:S(2)}) %collective-permute-start.7) | collective-permute-done | bytes 131104 | tf_op jit(solution)/shard_map/ppermute | solution.py:27
  33.7 4.0 %collective-permute-start.11 = (bf16[192,512]{1,0:T(8,128)(2,1)S(1)}, bf16[192,512]{1,0:T(8,128)(2,1)S(1)}, u32[]{:S(2)}, u32[]{:S(2)}) collective-permute-start(bf16[192,512]{1,0:T(8,128)(2,1)S(1)} %get-tuple-element.105.refs_6_.refs_4_), channel_id=1, source_target_pairs={{0,2},{1,3},{2,0},{3,1},{4,6},{5,7},{6,4},{7,5},{8,10},{9,11},{10,... | collective-permute-start | bytes 589832 | tf_op jit(solution)/shard_map/ppermute | solution.py:27
  38.0 7.4 %collective-permute-done.11.refs_7_.refs_3_ = bf16[192,512]{1,0:T(8,128)(2,1)S(1)} collective-permute-done((bf16[192,512]{1,0:T(8,128)(2,1)S(1)}, bf16[192,512]{1,0:T(8,128)(2,1)S(1)}, u32[]{:S(2)}, u32[]{:S(2)}) %collective-permute-start.11) | collective-permute-done | bytes 196640 | tf_op jit(solution)/shard_map/ppermute | solution.py:27
  45.4 7.6 %collective-permute-done.10.refs_3_ = bf16[384,512]{1,0:T(8,128)(2,1)S(1)} collective-permute-done((bf16[384,512]{1,0:T(8,128)(2,1)S(1)}, bf16[384,512]{1,0:T(8,128)(2,1)S(1)}, u32[]{:S(2)}, u32[]{:S(2)}) %collective-permute-start.10) | collective-permute-done | bytes 393248 | tf_op jit(solution)/shard_map/ppermute | solution.py:27
  54.8 3.4 %collective-permute-start.14 = (bf16[448,512]{1,0:T(8,128)(2,1)S(1)}, bf16[448,512]{1,0:T(8,128)(2,1)S(1)}, u32[]{:S(2)}, u32[]{:S(2)}) collective-permute-start(bf16[448,512]{1,0:T(8,128)(2,1)S(1)} %get-tuple-element.115.refs_2_), channel_id=1, source_target_pairs={{0,4},{1,5},{2,6},{3,7},{4,0},{5,1},{6,2},{7,3},{8,12},{9,13},{10,... | collective-permute-start | bytes 1376264 | tf_op jit(solution)/shard_map/ppermute | solution.py:27
  58.2 1.7 %sums_b_0.1 = (f32[3,512,512]{2,1,0:T(8,128)S(1)}, f32[8,128]{1,0:T(8,128)S(1)}) custom-call(bf16[3,2048,512]{2,1,0:T(8,128)(2,1)} %refs_1_.25, bf16[3,2048,512]{2,1,0:T(8,128)(2,1)} %refs_1_.25, bf16[3,2048,512]{2,1,0:T(8,128)(2,1)S(1)} %collective-permute-done.2.refs_4_.refs_2_, bf16[192,512]{1,0:T(8,128)(2,1)S(1)} %collective-permute-done.11.refs_7_.refs_3_, ...), custom_call_target="tpu_custom_call" | custom-call | tf_op jit(solution)/shard_map/sums_b_0/pallas_call | solution.py:65
  59.8 2.3 %sums_a_0.1 = (f32[2,512,512]{2,1,0:T(8,128)S(1)}, f32[8,128]{1,0:T(8,128)S(1)}) custom-call(bf16[3,2048,512]{2,1,0:T(8,128)(2,1)} %refs_1_.25, bf16[3,2048,512]{2,1,0:T(8,128)(2,1)} %refs_1_.25, bf16[192,512]{1,0:T(8,128)(2,1)S(1)} %get-tuple-element.101.refs_3_.refs_2_, bf16[384,512]{1,0:T(8,128)(2,1)S(1)} %collective-permute-done.10.refs_3_, ...), custom_call_target="tpu_custom_call" | custom-call | tf_op jit(solution)/shard_map/sums_a_0/pallas_call | solution.py:65
  63.5 11.3 %collective-permute-done.13.refs_3_ = bf16[384,512]{1,0:T(8,128)(2,1)S(1)} collective-permute-done((bf16[384,512]{1,0:T(8,128)(2,1)S(1)}, bf16[384,512]{1,0:T(8,128)(2,1)S(1)}, u32[]{:S(2)}, u32[]{:S(2)}) %collective-permute-start.13) | collective-permute-done | bytes 393248 | tf_op jit(solution)/shard_map/ppermute | solution.py:27
  74.8 1.2 next_grads_1_1.1
  76.1 2.2 %sums_b_1.1 = (f32[3,512,512]{2,1,0:T(8,128)S(1)}, f32[8,128]{1,0:T(8,128)S(1)}) custom-call(bf16[3,2048,512]{2,1,0:T(8,128)(2,1)} %refs_1_.25, bf16[3,2048,512]{2,1,0:T(8,128)(2,1)} %refs_1_.25, bf16[3,2048,512]{2,1,0:T(8,128)(2,1)S(1)} %collective-permute-done.2.refs_4_.refs_2_, bf16[384,512]{1,0:T(8,128)(2,1)S(1)} %collective-permute-done.13.refs_3_, ...), custom_call_target="tpu_custom_call" | custom-call | tf_op jit(solution)/shard_map/sums_b_1/pallas_call | solution.py:65
  78.3 1.9 %sums_a_2.1 = (f32[2,512,512]{2,1,0:T(8,128)S(1)}, f32[8,128]{1,0:T(8,128)S(1)}) custom-call(bf16[3,2048,512]{2,1,0:T(8,128)(2,1)} %refs_1_.25, bf16[3,2048,512]{2,1,0:T(8,128)(2,1)} %refs_1_.25, bf16[384,512]{1,0:T(8,128)(2,1)S(1)} %collective-permute-done.9.refs_3_.refs_2_, bf16[384,512]{1,0:T(8,128)(2,1)S(1)} %get-tuple-element.112.refs_3_.refs_2_, ...), custom_call_target="tpu_custom_call" | custom-call | tf_op jit(solution)/shard_map/sums_a_2/pallas_call | solution.py:65
  81.5 3.2 %collective-permute-start.22 = (bf16[448,512]{1,0:T(8,128)(2,1)S(1)}, bf16[448,512]{1,0:T(8,128)(2,1)S(1)}, u32[]{:S(2)}, u32[]{:S(2)}) collective-permute-start(bf16[448,512]{1,0:T(8,128)(2,1)S(1)} %get-tuple-element.124.refs_3_.refs_2_), channel_id=1, source_target_pairs={{0,2},{1,3},{2,0},{3,1},{4,6},{5,7},{6,4},{7,5},{8,10},{9,11},{10,... | collective-permute-start | bytes 1376264 | tf_op jit(solution)/shard_map/ppermute | solution.py:27
  84.7 6.9 %collective-permute-done.12.refs_3_ = bf16[384,512]{1,0:T(8,128)(2,1)S(1)} collective-permute-done((bf16[384,512]{1,0:T(8,128)(2,1)S(1)}, bf16[384,512]{1,0:T(8,128)(2,1)S(1)}, u32[]{:S(2)}, u32[]{:S(2)}) %collective-permute-start.12) | collective-permute-done | bytes 393248 | tf_op jit(solution)/shard_map/ppermute | solution.py:27
  92.8 2.2 %sums_b_2.1 = (f32[3,512,512]{2,1,0:T(8,128)S(1)}, f32[8,128]{1,0:T(8,128)S(1)}) custom-call(bf16[3,2048,512]{2,1,0:T(8,128)(2,1)} %refs_1_.25, bf16[3,2048,512]{2,1,0:T(8,128)(2,1)} %refs_1_.25, bf16[3,2048,512]{2,1,0:T(8,128)(2,1)S(1)} %collective-permute-done.2.refs_4_.refs_2_, bf16[384,512]{1,0:T(8,128)(2,1)S(1)} %collective-permute-done.12.refs_3_, ...), custom_call_target="tpu_custom_call" | custom-call | tf_op jit(solution)/shard_map/sums_b_2/pallas_call | solution.py:65
  95.0 1.9 %sums_a_3.1 = (f32[2,512,512]{2,1,0:T(8,128)S(1)}, f32[8,128]{1,0:T(8,128)S(1)}) custom-call(bf16[3,2048,512]{2,1,0:T(8,128)(2,1)} %refs_1_.25, bf16[3,2048,512]{2,1,0:T(8,128)(2,1)} %refs_1_.25, bf16[448,512]{1,0:T(8,128)(2,1)S(1)} %collective-permute-done.14.refs_3_.refs_2_, bf16[448,512]{1,0:T(8,128)(2,1)S(1)} %get-tuple-element.124.refs_3_.refs_2_, ...), custom_call_target="tpu_custom_call" | custom-call | tf_op jit(solution)/shard_map/sums_a_3/pallas_call | solution.py:65
  98.4 1.8 %collective-permute-start.21 = (bf16[384,512]{1,0:T(8,128)(2,1)S(1)}, bf16[384,512]{1,0:T(8,128)(2,1)S(1)}, u32[]{:S(2)}, u32[]{:S(2)}) collective-permute-start(bf16[384,512]{1,0:T(8,128)(2,1)S(1)} %get-tuple-element.131.refs_3_.refs_2_), channel_id=1, source_target_pairs={{0,2},{1,3},{2,0},{3,1},{4,6},{5,7},{6,4},{7,5},{8,10},{9,11},{10,... | collective-permute-start | bytes 1179656 | tf_op jit(solution)/shard_map/ppermute | solution.py:27
  100.1 1.9 %sums_a_4.1 = (f32[2,512,512]{2,1,0:T(8,128)S(1)}, f32[8,128]{1,0:T(8,128)S(1)}) custom-call(bf16[3,2048,512]{2,1,0:T(8,128)(2,1)} %refs_1_.25, bf16[3,2048,512]{2,1,0:T(8,128)(2,1)} %refs_1_.25, bf16[384,512]{1,0:T(8,128)(2,1)S(1)} %collective-permute-done.16.refs_3_.refs_2_, bf16[384,512]{1,0:T(8,128)(2,1)S(1)} %get-tuple-element.131.refs_3_.refs_2_, ...), custom_call_target="tpu_custom_call" | custom-call | tf_op jit(solution)/shard_map/sums_a_4/pallas_call | solution.py:65
  102.0 4.6 %collective-permute-done.15.refs_3_.refs_2_ = bf16[256,512]{1,0:T(8,128)(2,1)S(1)} collective-permute-done((bf16[256,512]{1,0:T(8,128)(2,1)S(1)}, bf16[256,512]{1,0:T(8,128)(2,1)S(1)}, u32[]{:S(2)}, u32[]{:S(2)}) %collective-permute-start.15) | collective-permute-done | bytes 262176 | tf_op jit(solution)/shard_map/ppermute | solution.py:27
  107.0 3.9 %collective-permute-start.20 = (bf16[256,512]{1,0:T(8,128)(2,1)S(1)}, bf16[256,512]{1,0:T(8,128)(2,1)S(1)}, u32[]{:S(2)}, u32[]{:S(2)}) collective-permute-start(bf16[256,512]{1,0:T(8,128)(2,1)S(1)} %get-tuple-element.135.refs_3_.refs_2_), channel_id=1, source_target_pairs={{0,2},{1,3},{2,0},{3,1},{4,6},{5,7},{6,4},{7,5},{8,10},{9,11},{10,... | collective-permute-start | bytes 786440 | tf_op jit(solution)/shard_map/ppermute | solution.py:27
  111.0 1.6 %sums_a_5.1 = (f32[2,128,512]{2,1,0:T(8,128)S(1)}, bf16[2,128,512]{2,1,0:T(8,128)(2,1)S(1)}, bf16[2,128,512]{2,1,0:T(8,128)(2,1)S(1)}, bf16[2,128,512]{2,1,0:T(8,128)(2,1)S(1)}, f32[8,128]{1,0:T(8,128)S(1)}) custom-call(bf16[3,2048,512]{2,1,0:T(8,128)(2,1)} %refs_1_.25, bf16[3,2048,512]{2,1,0:T(8,128)(2,1)} %refs_1_.25, ...), custom_call_target="tpu_custom_call" | custom-call | tf_op jit(solution)/shard_map/sums_a_5/pallas_call | solution.py:65
  112.6 1.4 collective-permute-start.17
  114.0 1.5 collective-permute-start.18
  117.2 2.2 %sums_b_3.1 = (f32[3,512,512]{2,1,0:T(8,128)S(1)}, f32[8,128]{1,0:T(8,128)S(1)}) custom-call(bf16[3,2048,512]{2,1,0:T(8,128)(2,1)} %refs_1_.25, bf16[3,2048,512]{2,1,0:T(8,128)(2,1)} %refs_1_.25, bf16[3,2048,512]{2,1,0:T(8,128)(2,1)S(1)} %collective-permute-done.2.refs_4_.refs_2_, bf16[448,512]{1,0:T(8,128)(2,1)S(1)} %collective-permute-done.22.refs_3_, ...), custom_call_target="tpu_custom_call" | custom-call | tf_op jit(solution)/shard_map/sums_b_3/pallas_call | solution.py:65
  120.2 2.2 %sums_b_4.1 = (f32[3,512,512]{2,1,0:T(8,128)S(1)}, f32[8,128]{1,0:T(8,128)S(1)}) custom-call(bf16[3,2048,512]{2,1,0:T(8,128)(2,1)} %refs_1_.25, bf16[3,2048,512]{2,1,0:T(8,128)(2,1)} %refs_1_.25, bf16[3,2048,512]{2,1,0:T(8,128)(2,1)S(1)} %collective-permute-done.2.refs_4_.refs_2_, bf16[384,512]{1,0:T(8,128)(2,1)S(1)} %collective-permute-done.21.refs_3_, ...), custom_call_target="tpu_custom_call" | custom-call | tf_op jit(solution)/shard_map/sums_b_4/pallas_call | solution.py:65
  122.4 2.5 %collective-permute-done.20.refs_3_ = bf16[256,512]{1,0:T(8,128)(2,1)S(1)} collective-permute-done((bf16[256,512]{1,0:T(8,128)(2,1)S(1)}, bf16[256,512]{1,0:T(8,128)(2,1)S(1)}, u32[]{:S(2)}, u32[]{:S(2)}) %collective-permute-start.20) | collective-permute-done | bytes 262176 | tf_op jit(solution)/shard_map/ppermute | solution.py:27
  125.5 1.9 %sums_b_5.1 = (bf16[1,128,512]{2,1,0:T(8,128)(2,1)S(1)}, bf16[1,128,512]{2,1,0:T(8,128)(2,1)S(1)}, bf16[1,128,512]{2,1,0:T(8,128)(2,1)S(1)}, bf16[1,128,512]{2,1...) custom-call(bf16[3,2048,512]{2,1,0:T(8,128)(2,1)} %refs_1_.25, ...), custom_call_target="tpu_custom_call" | custom-call | tf_op jit(solution)/shard_map/sums_b_5/pallas_call | solution.py:65
  127.7 2.8 %collective-permute-start.25 = (bf16[1,128,512]{2,1,0:T(8,128)(2,1)S(1)}, bf16[1,128,512]{2,1,0:T(8,128)(2,1)S(1)}, u32[]{:S(2)}, u32[]{:S(2)}) collective-permute-start(bf16[1,128,512]{2,1,0:T(8,128)(2,1)S(1)} %get-tuple-element.160), channel_id=1, source_target_pairs={{0,10},{1,11},{2,8},{3,9},{4,14},{5,15},{6,12},{7,13},{8,2},{9,3},... | collective-permute-start | bytes 393224 | tf_op jit(solution)/shard_map/ppermute | solution.py:37
  131.2 1.4 collective-permute-start.29
  132.5 1.4 collective-permute-done.24.refs_0_
  134.9 2.4 %collective-permute-done.25.refs_1_ = bf16[1,128,512]{2,1,0:T(8,128)(2,1)S(1)} collective-permute-done((bf16[1,128,512]{2,1,0:T(8,128)(2,1)S(1)}, bf16[1,128,512]{2,1,0:T(8,128)(2,1)S(1)}, u32[]{:S(2)}, u32[]{:S(2)}) %collective-permute-start.25) | collective-permute-done | bytes 131104 | tf_op jit(solution)/shard_map/ppermute | solution.py:37
  137.2 1.9 %collective-permute-start.30 = (bf16[2,128,512]{2,1,0:T(8,128)(2,1)S(1)}, bf16[2,128,512]{2,1,0:T(8,128)(2,1)S(1)}, u32[]{:S(2)}, u32[]{:S(2)}) collective-permute-start(bf16[2,128,512]{2,1,0:T(8,128)(2,1)S(1)} %get-tuple-element.166), channel_id=1, source_target_pairs={{0,24},{8,16},{16,8},{24,0},{1,25},{9,17},{17,9},{25,1},{2,26},{10... | collective-permute-start | bytes 786440 | tf_op jit(solution)/shard_map/ppermute | solution.py:27
  139.9 3.8 %last_grad.1 = (bf16[2048,512]{1,0:T(8,128)(2,1)}, bf16[128,512]{1,0:T(8,128)(2,1)S(1)}, f32[8,128]{1,0:T(8,128)S(1)}) custom-call(bf16[2560,512]{1,0:T(8,128)(2,1)S(1)} %get-tuple-element.155.refs_0_, bf16[2560,512]{1,0:T(8,128)(2,1)S(1)} %collective-permute-done.23.refs_1_.refs_3_, ...), custom_call_target="tpu_custom_call", output_to_operand_aliasing={{1}: (4, {})} | custom-call | tf_op jit(solution)/shard_map/last_grad/pallas_call | solution.py:65
  143.7 4.1 %collective-permute-start.31 = (bf16[128,512]{1,0:T(8,128)(2,1)S(1)}, bf16[128,512]{1,0:T(8,128)(2,1)S(1)}, u32[]{:S(2)}, u32[]{:S(2)}) collective-permute-start(bf16[128,512]{1,0:T(8,128)(2,1)S(1)} %get-tuple-element.169), channel_id=1, source_target_pairs={{0,4},{1,5},{2,6},{3,7},{4,0},{5,1},{6,2},{7,3},{8,12},{9,13},{10,... | collective-permute-start | bytes 393224 | tf_op jit(solution)/shard_map/ppermute | solution.py:27
  147.8 1.3 collective-permute-done.29.refs_6_
  149.1 1.6 %collective-permute-done.30.refs_7_ = bf16[2,128,512]{2,1,0:T(8,128)(2,1)S(1)} collective-permute-done((bf16[2,128,512]{2,1,0:T(8,128)(2,1)S(1)}, bf16[2,128,512]{2,1,0:T(8,128)(2,1)S(1)}, u32[]{:S(2)}, u32[]{:S(2)}) %collective-permute-start.30) | collective-permute-done | bytes 262176 | tf_op jit(solution)/shard_map/ppermute | solution.py:27
  150.8 2.4 %collective-permute-done.31.refs_10_ = bf16[128,512]{1,0:T(8,128)(2,1)S(1)} collective-permute-done((bf16[128,512]{1,0:T(8,128)(2,1)S(1)}, bf16[128,512]{1,0:T(8,128)(2,1)S(1)}, u32[]{:S(2)}, u32[]{:S(2)}) %collective-permute-start.31) | collective-permute-done | bytes 131104 | tf_op jit(solution)/shard_map/ppermute | solution.py:27
  153.2 1.3 last_sums.1
  (48 shorter events, 18.6 us)
Async XLA Ops:
  0.6 20.9 %collective-permute-start.2 = (bf16[3,2048,512]{2,1,0:T(8,128)(2,1)}, bf16[3,2048,512]{2,1,0:T(8,128)(2,1)S(1)}, u32[]{:S(2)}, u32[]{:S(2)}) collective-permute-start(bf16[3,2048,512]{2,1,0:T(8,128)(2,1)} %refs_1_.25), channel_id=1, source_target_pairs={{0,1},{1,0},{2,3},{3,2},{4,5},{5,4},{6,7},{7,6},{8,9},{9,8},{10,11... | collective-permute-start | bytes 18874376 | tf_op jit(solution)/shard_map/ppermute | solution.py:27
  2.4 19.2 %collective-permute-start.1 = (bf16[320,512]{1,0:T(8,128)(2,1)S(1)}, bf16[320,512]{1,0:T(8,128)(2,1)S(1)}, u32[]{:S(2)}, u32[]{:S(2)}) collective-permute-start(bf16[320,512]{1,0:T(8,128)(2,1)S(1)} %get-tuple-element.89), channel_id=1, source_target_pairs={{0,4},{1,5},{2,6},{3,7},{4,0},{5,1},{6,2},{7,3},{8,12},{9,13},{10,... | collective-permute-start | bytes 983048 | tf_op jit(solution)/shard_map/ppermute | solution.py:27
  10.6 6.0 %collective-permute-start.3 = (bf16[1,128,512]{2,1,0:T(8,128)(2,1)S(1)}, bf16[1,128,512]{2,1,0:T(8,128)(2,1)S(1)}, u32[]{:S(2)}, u32[]{:S(2)}) collective-permute-start(bf16[1,128,512]{2,1,0:T(8,128)(2,1)S(1)} %get-tuple-element.92), channel_id=1, source_target_pairs={{0,8},{8,0},{16,24},{24,16},{1,9},{9,1},{17,25},{25,17},{2,10},{10... | collective-permute-start | bytes 393224 | tf_op jit(solution)/shard_map/ppermute | solution.py:27
  12.2 8.1 %collective-permute-start.4 = (bf16[1,128,512]{2,1,0:T(8,128)(2,1)S(1)}, bf16[1,128,512]{2,1,0:T(8,128)(2,1)S(1)}, u32[]{:S(2)}, u32[]{:S(2)}) collective-permute-start(bf16[1,128,512]{2,1,0:T(8,128)(2,1)S(1)} %get-tuple-element.93), channel_id=1, source_target_pairs={{0,16},{8,24},{16,0},{24,8},{1,17},{9,25},{17,1},{25,9},{2,18},{10... | collective-permute-start | bytes 393224 | tf_op jit(solution)/shard_map/ppermute | solution.py:27
  13.7 6.6 %collective-permute-start.5 = (bf16[1,128,512]{2,1,0:T(8,128)(2,1)S(1)}, bf16[1,128,512]{2,1,0:T(8,128)(2,1)S(1)}, u32[]{:S(2)}, u32[]{:S(2)}) collective-permute-start(bf16[1,128,512]{2,1,0:T(8,128)(2,1)S(1)} %get-tuple-element.94), channel_id=1, source_target_pairs={{0,24},{8,16},{16,8},{24,0},{1,25},{9,17},{17,9},{25,1},{2,26},{10... | collective-permute-start | bytes 393224 | tf_op jit(solution)/shard_map/ppermute | solution.py:27
  16.6 21.4 %collective-permute-start = (bf16[512,512]{1,0:T(8,128)(2,1)S(1)}, bf16[512,512]{1,0:T(8,128)(2,1)S(1)}, u32[]{:S(2)}, u32[]{:S(2)}) collective-permute-start(bf16[512,512]{1,0:T(8,128)(2,1)S(1)} %get-tuple-element.88), channel_id=1, source_target_pairs={{0,2},{1,3},{2,0},{3,1},{4,6},{5,7},{6,4},{7,5},{8,10},{9,11},{10,... | collective-permute-start | bytes 1572872 | tf_op jit(solution)/shard_map/ppermute | solution.py:27
  21.6 11.1 %copy-start = (bf16[3,512,512]{2,1,0:T(8,128)(2,1)S(1)}, bf16[3,512,512]{2,1,0:T(8,128)(2,1)}, u32[]{:S(2)}) copy-start(bf16[3,512,512]{2,1,0:T(8,128)(2,1)} %refs_2_.5) | copy-start | bytes 4718596
  23.2 29.9 %collective-permute-start.10 = (bf16[384,512]{1,0:T(8,128)(2,1)S(1)}, bf16[384,512]{1,0:T(8,128)(2,1)S(1)}, u32[]{:S(2)}, u32[]{:S(2)}) collective-permute-start(bf16[384,512]{1,0:T(8,128)(2,1)S(1)} %get-tuple-element.104.refs_2_), channel_id=1, source_target_pairs={{0,4},{1,5},{2,6},{3,7},{4,0},{5,1},{6,2},{7,3},{8,12},{9,13},{10,... | collective-permute-start | bytes 1179656 | tf_op jit(solution)/shard_map/ppermute | solution.py:27
  23.2 5.9 %collective-permute-start.6 = (bf16[128,512]{1,0:T(8,128)(2,1)S(1)}, bf16[128,512]{1,0:T(8,128)(2,1)S(1)}, u32[]{:S(2)}, u32[]{:S(2)}) collective-permute-start(bf16[128,512]{1,0:T(8,128)(2,1)S(1)} %get-tuple-element.97.refs_0_), channel_id=1, source_target_pairs={{0,8},{8,0},{16,24},{24,16},{1,9},{9,1},{17,25},{25,17},{2,10},{10... | collective-permute-start | bytes 393224 | tf_op jit(solution)/shard_map/ppermute | solution.py:27
  24.8 7.8 %collective-permute-start.7 = (bf16[128,512]{1,0:T(8,128)(2,1)S(1)}, bf16[128,512]{1,0:T(8,128)(2,1)S(1)}, u32[]{:S(2)}, u32[]{:S(2)}) collective-permute-start(bf16[128,512]{1,0:T(8,128)(2,1)S(1)} %get-tuple-element.97.refs_0_), channel_id=1, source_target_pairs={{0,16},{8,24},{16,0},{24,8},{1,17},{9,25},{17,1},{25,9},{2,18},{10... | collective-permute-start | bytes 393224 | tf_op jit(solution)/shard_map/ppermute | solution.py:27
  26.4 6.3 %collective-permute-start.8 = (bf16[128,512]{1,0:T(8,128)(2,1)S(1)}, bf16[128,512]{1,0:T(8,128)(2,1)S(1)}, u32[]{:S(2)}, u32[]{:S(2)}) collective-permute-start(bf16[128,512]{1,0:T(8,128)(2,1)S(1)} %get-tuple-element.97.refs_0_), channel_id=1, source_target_pairs={{0,24},{8,16},{16,8},{24,0},{1,25},{9,17},{17,9},{25,1},{2,26},{10... | collective-permute-start | bytes 393224 | tf_op jit(solution)/shard_map/ppermute | solution.py:27
  33.7 11.7 %collective-permute-start.11 = (bf16[192,512]{1,0:T(8,128)(2,1)S(1)}, bf16[192,512]{1,0:T(8,128)(2,1)S(1)}, u32[]{:S(2)}, u32[]{:S(2)}) collective-permute-start(bf16[192,512]{1,0:T(8,128)(2,1)S(1)} %get-tuple-element.105.refs_6_.refs_4_), channel_id=1, source_target_pairs={{0,2},{1,3},{2,0},{3,1},{4,6},{5,7},{6,4},{7,5},{8,10},{9,11},{10,... | collective-permute-start | bytes 589832 | tf_op jit(solution)/shard_map/ppermute | solution.py:27
  37.7 24.4 %collective-permute-start.9 = (bf16[384,512]{1,0:T(8,128)(2,1)S(1)}, bf16[384,512]{1,0:T(8,128)(2,1)S(1)}, u32[]{:S(2)}, u32[]{:S(2)}) collective-permute-start(bf16[384,512]{1,0:T(8,128)(2,1)S(1)} %get-tuple-element.103.refs_2_), channel_id=1, source_target_pairs={{0,4},{1,5},{2,6},{3,7},{4,0},{5,1},{6,2},{7,3},{8,12},{9,13},{10,... | collective-permute-start | bytes 1179656 | tf_op jit(solution)/shard_map/ppermute | solution.py:27
  54.2 20.6 %collective-permute-start.13 = (bf16[384,512]{1,0:T(8,128)(2,1)S(1)}, bf16[384,512]{1,0:T(8,128)(2,1)S(1)}, u32[]{:S(2)}, u32[]{:S(2)}) collective-permute-start(bf16[384,512]{1,0:T(8,128)(2,1)S(1)} %get-tuple-element.107.refs_5_.refs_2_), channel_id=1, source_target_pairs={{0,2},{1,3},{2,0},{3,1},{4,6},{5,7},{6,4},{7,5},{8,10},{9,11},{10,... | collective-permute-start | bytes 1179656 | tf_op jit(solution)/shard_map/ppermute | solution.py:27
  54.8 26.1 %collective-permute-start.14 = (bf16[448,512]{1,0:T(8,128)(2,1)S(1)}, bf16[448,512]{1,0:T(8,128)(2,1)S(1)}, u32[]{:S(2)}, u32[]{:S(2)}) collective-permute-start(bf16[448,512]{1,0:T(8,128)(2,1)S(1)} %get-tuple-element.115.refs_2_), channel_id=1, source_target_pairs={{0,4},{1,5},{2,6},{3,7},{4,0},{5,1},{6,2},{7,3},{8,12},{9,13},{10,... | collective-permute-start | bytes 1376264 | tf_op jit(solution)/shard_map/ppermute | solution.py:27
  62.7 28.9 %collective-permute-start.12 = (bf16[384,512]{1,0:T(8,128)(2,1)S(1)}, bf16[384,512]{1,0:T(8,128)(2,1)S(1)}, u32[]{:S(2)}, u32[]{:S(2)}) collective-permute-start(bf16[384,512]{1,0:T(8,128)(2,1)S(1)} %get-tuple-element.112.refs_3_.refs_2_), channel_id=1, source_target_pairs={{0,2},{1,3},{2,0},{3,1},{4,6},{5,7},{6,4},{7,5},{8,10},{9,11},{10,... | collective-permute-start | bytes 1179656 | tf_op jit(solution)/shard_map/ppermute | solution.py:27
  76.0 21.7 %collective-permute-start.16 = (bf16[384,512]{1,0:T(8,128)(2,1)S(1)}, bf16[384,512]{1,0:T(8,128)(2,1)S(1)}, u32[]{:S(2)}, u32[]{:S(2)}) collective-permute-start(bf16[384,512]{1,0:T(8,128)(2,1)S(1)} %get-tuple-element.123.refs_2_), channel_id=1, source_target_pairs={{0,4},{1,5},{2,6},{3,7},{4,0},{5,1},{6,2},{7,3},{8,12},{9,13},{10,... | collective-permute-start | bytes 1179656 | tf_op jit(solution)/shard_map/ppermute | solution.py:27
  81.5 34.0 %collective-permute-start.22 = (bf16[448,512]{1,0:T(8,128)(2,1)S(1)}, bf16[448,512]{1,0:T(8,128)(2,1)S(1)}, u32[]{:S(2)}, u32[]{:S(2)}) collective-permute-start(bf16[448,512]{1,0:T(8,128)(2,1)S(1)} %get-tuple-element.124.refs_3_.refs_2_), channel_id=1, source_target_pairs={{0,2},{1,3},{2,0},{3,1},{4,6},{5,7},{6,4},{7,5},{8,10},{9,11},{10,... | collective-permute-start | bytes 1376264 | tf_op jit(solution)/shard_map/ppermute | solution.py:27
  92.6 14.0 %collective-permute-start.15 = (bf16[256,512]{1,0:T(8,128)(2,1)S(1)}, bf16[256,512]{1,0:T(8,128)(2,1)S(1)}, u32[]{:S(2)}, u32[]{:S(2)}) collective-permute-start(bf16[256,512]{1,0:T(8,128)(2,1)S(1)} %get-tuple-element.122.refs_2_), channel_id=1, source_target_pairs={{0,4},{1,5},{2,6},{3,7},{4,0},{5,1},{6,2},{7,3},{8,12},{9,13},{10,... | collective-permute-start | bytes 786440 | tf_op jit(solution)/shard_map/ppermute | solution.py:27
  98.4 21.1 %collective-permute-start.21 = (bf16[384,512]{1,0:T(8,128)(2,1)S(1)}, bf16[384,512]{1,0:T(8,128)(2,1)S(1)}, u32[]{:S(2)}, u32[]{:S(2)}) collective-permute-start(bf16[384,512]{1,0:T(8,128)(2,1)S(1)} %get-tuple-element.131.refs_3_.refs_2_), channel_id=1, source_target_pairs={{0,2},{1,3},{2,0},{3,1},{4,6},{5,7},{6,4},{7,5},{8,10},{9,11},{10,... | collective-permute-start | bytes 1179656 | tf_op jit(solution)/shard_map/ppermute | solution.py:27
  107.0 17.9 %collective-permute-start.20 = (bf16[256,512]{1,0:T(8,128)(2,1)S(1)}, bf16[256,512]{1,0:T(8,128)(2,1)S(1)}, u32[]{:S(2)}, u32[]{:S(2)}) collective-permute-start(bf16[256,512]{1,0:T(8,128)(2,1)S(1)} %get-tuple-element.135.refs_3_.refs_2_), channel_id=1, source_target_pairs={{0,2},{1,3},{2,0},{3,1},{4,6},{5,7},{6,4},{7,5},{8,10},{9,11},{10,... | collective-permute-start | bytes 786440 | tf_op jit(solution)/shard_map/ppermute | solution.py:27
  112.6 14.7 %collective-permute-start.17 = (bf16[2,128,512]{2,1,0:T(8,128)(2,1)S(1)}, bf16[2,128,512]{2,1,0:T(8,128)(2,1)S(1)}, u32[]{:S(2)}, u32[]{:S(2)}) collective-permute-start(bf16[2,128,512]{2,1,0:T(8,128)(2,1)S(1)} %get-tuple-element.139), channel_id=1, source_target_pairs={{0,8},{8,0},{16,24},{24,16},{1,9},{9,1},{17,25},{25,17},{2,10},{10... | collective-permute-start | bytes 786440 | tf_op jit(solution)/shard_map/ppermute | solution.py:27
  114.0 13.4 %collective-permute-start.18 = (bf16[2,128,512]{2,1,0:T(8,128)(2,1)S(1)}, bf16[2,128,512]{2,1,0:T(8,128)(2,1)S(1)}, u32[]{:S(2)}, u32[]{:S(2)}) collective-permute-start(bf16[2,128,512]{2,1,0:T(8,128)(2,1)S(1)} %get-tuple-element.140), channel_id=1, source_target_pairs={{0,16},{8,24},{16,0},{24,8},{1,17},{9,25},{17,1},{25,9},{2,18},{10... | collective-permute-start | bytes 786440 | tf_op jit(solution)/shard_map/ppermute | solution.py:27
  115.5 11.9 %collective-permute-start.19 = (bf16[2,128,512]{2,1,0:T(8,128)(2,1)S(1)}, bf16[2,128,512]{2,1,0:T(8,128)(2,1)S(1)}, u32[]{:S(2)}, u32[]{:S(2)}) collective-permute-start(bf16[2,128,512]{2,1,0:T(8,128)(2,1)S(1)} %get-tuple-element.141), channel_id=1, source_target_pairs={{0,24},{8,16},{16,8},{24,0},{1,25},{9,17},{17,9},{25,1},{2,26},{10... | collective-permute-start | bytes 786440 | tf_op jit(solution)/shard_map/ppermute | solution.py:27
  127.5 11.6 %collective-permute-start.23 = (bf16[2560,512]{1,0:T(8,128)(2,1)S(1)}, bf16[2560,512]{1,0:T(8,128)(2,1)S(1)}, u32[]{:S(2)}, u32[]{:S(2)}) collective-permute-start(bf16[2560,512]{1,0:T(8,128)(2,1)S(1)} %get-tuple-element.155.refs_0_), channel_id=1, source_target_pairs={{0,1},{1,0},{2,3},{3,2},{4,5},{5,4},{6,7},{7,6},{8,9},{9,8},{10,11... | collective-permute-start | bytes 7864328 | tf_op jit(solution)/shard_map/ppermute | solution.py:27
  127.6 6.4 %collective-permute-start.24 = (bf16[1,128,512]{2,1,0:T(8,128)(2,1)S(1)}, bf16[1,128,512]{2,1,0:T(8,128)(2,1)S(1)}, u32[]{:S(2)}, u32[]{:S(2)}) collective-permute-start(bf16[1,128,512]{2,1,0:T(8,128)(2,1)S(1)} %get-tuple-element.159), channel_id=1, source_target_pairs={{0,2},{1,3},{2,0},{3,1},{4,6},{5,7},{6,4},{7,5},{8,10},{9,11},{10,... | collective-permute-start | bytes 393224 | tf_op jit(solution)/shard_map/ppermute | solution.py:37
  127.7 9.5 %collective-permute-start.25 = (bf16[1,128,512]{2,1,0:T(8,128)(2,1)S(1)}, bf16[1,128,512]{2,1,0:T(8,128)(2,1)S(1)}, u32[]{:S(2)}, u32[]{:S(2)}) collective-permute-start(bf16[1,128,512]{2,1,0:T(8,128)(2,1)S(1)} %get-tuple-element.160), channel_id=1, source_target_pairs={{0,10},{1,11},{2,8},{3,9},{4,14},{5,15},{6,12},{7,13},{8,2},{9,3},... | collective-permute-start | bytes 393224 | tf_op jit(solution)/shard_map/ppermute | solution.py:37
  130.5 17.3 %collective-permute-start.28 = (bf16[2,128,512]{2,1,0:T(8,128)(2,1)S(1)}, bf16[2,128,512]{2,1,0:T(8,128)(2,1)S(1)}, u32[]{:S(2)}, u32[]{:S(2)}) collective-permute-start(bf16[2,128,512]{2,1,0:T(8,128)(2,1)S(1)} %get-tuple-element.164), channel_id=1, source_target_pairs={{0,8},{8,0},{16,24},{24,16},{1,9},{9,1},{17,25},{25,17},{2,10},{10... | collective-permute-start | bytes 786440 | tf_op jit(solution)/shard_map/ppermute | solution.py:27
  131.2 18.0 %collective-permute-start.29 = (bf16[2,128,512]{2,1,0:T(8,128)(2,1)S(1)}, bf16[2,128,512]{2,1,0:T(8,128)(2,1)S(1)}, u32[]{:S(2)}, u32[]{:S(2)}) collective-permute-start(bf16[2,128,512]{2,1,0:T(8,128)(2,1)S(1)} %get-tuple-element.165), channel_id=1, source_target_pairs={{0,16},{8,24},{16,0},{24,8},{1,17},{9,25},{17,1},{25,9},{2,18},{10... | collective-permute-start | bytes 786440 | tf_op jit(solution)/shard_map/ppermute | solution.py:27
  134.0 9.7 %collective-permute-start.26 = (bf16[1,128,512]{2,1,0:T(8,128)(2,1)S(1)}, bf16[1,128,512]{2,1,0:T(8,128)(2,1)S(1)}, u32[]{:S(2)}, u32[]{:S(2)}) collective-permute-start(bf16[1,128,512]{2,1,0:T(8,128)(2,1)S(1)} %get-tuple-element.161), channel_id=1, source_target_pairs={{0,18},{1,19},{2,16},{3,17},{4,22},{5,23},{6,20},{7,21},{8,26},{9,... | collective-permute-start | bytes 393224 | tf_op jit(solution)/shard_map/ppermute | solution.py:37
  137.2 13.6 %collective-permute-start.30 = (bf16[2,128,512]{2,1,0:T(8,128)(2,1)S(1)}, bf16[2,128,512]{2,1,0:T(8,128)(2,1)S(1)}, u32[]{:S(2)}, u32[]{:S(2)}) collective-permute-start(bf16[2,128,512]{2,1,0:T(8,128)(2,1)S(1)} %get-tuple-element.166), channel_id=1, source_target_pairs={{0,24},{8,16},{16,8},{24,0},{1,25},{9,17},{17,9},{25,1},{2,26},{10... | collective-permute-start | bytes 786440 | tf_op jit(solution)/shard_map/ppermute | solution.py:27
  139.1 8.7 %collective-permute-start.27 = (bf16[1,128,512]{2,1,0:T(8,128)(2,1)S(1)}, bf16[1,128,512]{2,1,0:T(8,128)(2,1)S(1)}, u32[]{:S(2)}, u32[]{:S(2)}) collective-permute-start(bf16[1,128,512]{2,1,0:T(8,128)(2,1)S(1)} %get-tuple-element.162), channel_id=1, source_target_pairs={{0,26},{1,27},{2,24},{3,25},{4,30},{5,31},{6,28},{7,29},{8,18},{9,... | collective-permute-start | bytes 393224 | tf_op jit(solution)/shard_map/ppermute | solution.py:37
  143.7 9.5 %collective-permute-start.31 = (bf16[128,512]{1,0:T(8,128)(2,1)S(1)}, bf16[128,512]{1,0:T(8,128)(2,1)S(1)}, u32[]{:S(2)}, u32[]{:S(2)}) collective-permute-start(bf16[128,512]{1,0:T(8,128)(2,1)S(1)} %get-tuple-element.169), channel_id=1, source_target_pairs={{0,4},{1,5},{2,6},{3,7},{4,0},{5,1},{6,2},{7,3},{8,12},{9,13},{10,... | collective-permute-start | bytes 393224 | tf_op jit(solution)/shard_map/ppermute | solution.py:27

commit v5 on v3

--- a/solution.py
+++ b/solution.py
@@ -12,7 +12,6 @@
 CUTS = (3, 6, 6, 7, 6, 4)
 ROW_TILE = 16
 VMEM_LIMIT = 24 * 1024 * 1024
-WHOLE_VMEM = 60 * 1024 * 1024
 
 ANY = pl.BlockSpec(memory_space=pl.ANY)
 WHOLE = pl.BlockSpec(memory_space=pltpu.VMEM)
@@ -53,7 +52,7 @@
     def __init__(self):
         self.token = None
 
-    def __call__(self, body, name, operands, in_specs, out_shape, out_specs, scratch=(), aliases=None, limit=VMEM_LIMIT, grid=1):
+    def __call__(self, body, name, operands, in_specs, out_shape, out_specs, scratch=(), aliases=None, grid=1):
         n_in, n_out = len(operands), len(out_shape)
         held = [] if self.token is None else [self.token]
 
@@ -70,7 +69,7 @@
             out_specs=[*out_specs, ANY],
             scratch_shapes=list(scratch),
             input_output_aliases=aliases or {},
-            compiler_params=pltpu.CompilerParams(vmem_limit_bytes=limit),
+            compiler_params=pltpu.CompilerParams(vmem_limit_bytes=VMEM_LIMIT),
             name=name,
         )(*operands, *held)
         return outs
@@ -86,7 +85,7 @@
     return cuts
 
 
-def cut_out(chain, blocks, name, limit=WHOLE_VMEM, deps=()):
+def cut_out(chain, blocks, name, deps=()):
     flat = [piece for block in blocks for piece in block]
     n = len(flat)
 
@@ -107,7 +106,7 @@
     return chain(
         body,
         name,
-        [piece[0] for piece in flat] + [in_hbm(a) for a in deps],
+        [piece[0] for piece in flat] + list(deps),
         [ANY] * (n + len(deps)),
         [
             jax.ShapeDtypeStruct((sum(p[2] for p in block), block[0][0].shape[-1]), block[0][0].dtype)
@@ -115,7 +114,6 @@
         ],
         [WHOLE] * len(blocks),
         [pltpu.SemaphoreType.DMA((n,))],
-        limit=limit,
     )
 
 
@@ -162,7 +160,7 @@
     )
 
 
-def next_grads(chain, w_self, jobs, name, into=None, fetch=(), deps=(), block=None):
+def next_grads(chain, w_self, jobs, name, into=None, block=None):
     width = w_self.shape[2]
     operands, in_specs, out_shape, out_specs, scratch, aliases = [], [], [], [], [], {}
     for level, grad, far, far_cross in jobs:
@@ -173,25 +171,14 @@
         if job[0] != 1:
             out_shape.append(jax.ShapeDtypeStruct((size, width), jnp.bfloat16))
             out_specs.append(WHOLE)
-    n_kept = len(out_shape)
-    for array, _, _, size in fetch:
-        operands.append(array)
-        in_specs.append(ANY)
-        out_shape.append(jax.ShapeDtypeStruct((size, array.shape[-1]), array.dtype))
-        out_specs.append(WHOLE)
-    operands += deps
-    in_specs += [ANY] * len(deps)
-    n_moved = len(fetch) + (2 if block is not None else 0)
-    if n_moved:
-        scratch.append(pltpu.SemaphoreType.DMA((n_moved,)))
     if block is not None:
         operands.append(block[0])
         in_specs.append(ANY)
-        scratch.append(pltpu.VMEM((width, width), jnp.bfloat16))
+        scratch += [pltpu.SemaphoreType.DMA((2,)), pltpu.VMEM((width, width), jnp.bfloat16)]
     if into is not None:
         if not isinstance(into[0], jax.ShapeDtypeStruct):
             aliases[len(operands)] = len(out_shape)
-            operands.append(in_hbm(into[0]))
+            operands.append(into[0])
             in_specs.append(ANY)
         out_shape.append(jax.ShapeDtypeStruct(into[0].shape, into[0].dtype))
         out_specs.append(ANY)
@@ -201,16 +188,9 @@
     def body(*refs):
         ins, rest = refs[: len(operands)], refs[len(operands) :]
         outs, scr = rest[: len(out_shape)], rest[len(out_shape) :]
-        first = 4 * len(jobs)
-        copies = []
-        for f, (_, index, start, size) in enumerate(fetch):
-            source = ins[first + f].at[(*index, pl.ds(start, size))]
-            copies.append(pltpu.make_async_copy(source, outs[n_kept + f], scr[0].at[f]))
         if block is not None:
-            source = ins[first + len(fetch) + len(deps)].at[block[1]]
-            copies.append(pltpu.make_async_copy(source, scr[1], scr[0].at[n_moved - 2]))
-        for copy in copies:
-            copy.start()
+            move = pltpu.make_async_copy(ins[4 * len(jobs)].at[block[1]], scr[1], scr[0].at[0])
+            move.start()
         at = 0
         for j in range(len(jobs)):
             a_ref, c_ref, grad_ref, far_ref = ins[4 * j : 4 * j + 4]
@@ -226,11 +206,10 @@
             target = outs[-1].at[pl.ds(into[1], stored)]
             stores.append(pltpu.make_async_copy(scr[-2], target, scr[-1]))
             stores[-1].start()
-        for copy in copies:
-            copy.wait()
         if block is not None:
+            move.wait()
             target = outs[-1].at[pl.ds(block[2], width)]
-            stores.append(pltpu.make_async_copy(scr[1], target, scr[0].at[n_moved - 1]))
+            stores.append(pltpu.make_async_copy(scr[1], target, scr[0].at[1]))
             stores[-1].start()
         for copy in stores:
             copy.wait()
@@ -250,7 +229,7 @@
     return chain(
         body,
         "last_grad",
-        [in_hbm(both), in_hbm(far_both), w_self, in_hbm(far_both)],
+        [both, far_both, w_self, far_both],
         [rows, rows, weight_block(w_self, 0), pl.BlockSpec((width, width), lambda i: (tokens // width, 0))],
         [jax.ShapeDtypeStruct((tokens, width), both.dtype)],
         [rows],
@@ -271,7 +250,7 @@
     operands = [x for x, _, _ in xs]
     in_specs = [ANY] * len(xs)
     for side in sides:
-        operands += side if isinstance(side, list) else [in_hbm(side)]
+        operands += side if isinstance(side, list) else [side]
         in_specs += [WHOLE] * len(side) if isinstance(side, list) else [ANY]
     if before is not None:
         operands.append(before)
@@ -359,11 +338,24 @@
     return chain(
         body,
         name,
-        [*terms, in_hbm(hold)],
+        [*terms, hold],
         [WHOLE] * m + [ANY],
         [*out_shape, jax.ShapeDtypeStruct(hold.shape, hold.dtype)],
         [*out_specs, ANY],
         aliases={m: len(dtypes)},
+    )
+
+
+def hand_on(chain, arrays, deps, name):
+    n = len(arrays)
+    return chain(
+        lambda *refs: None,
+        name,
+        [*arrays, *deps],
+        [ANY] * (n + len(deps)),
+        [jax.ShapeDtypeStruct(a.shape, a.dtype) for a in arrays],
+        [ANY] * n,
+        aliases={j: j for j in range(n)},
     )
 
 
@@ -429,7 +421,6 @@
             [(w_cross, block_of(1), width)],
         ],
         "first_rows",
-        VMEM_LIMIT,
     )
     cross_1 = swap(cross_1, "narrow", 1 << 1)
     first = swap(first, "narrow", 1 << 2)
@@ -455,10 +446,8 @@
             [(cotangent, rows_at(cuts[1][0]), cuts[1][1])],
         ],
         "parted",
-        VMEM_LIMIT,
         [far_inputs],
     )
-    far_inputs = in_hbm(far_inputs)
     far[2][0], near[2][0], near[2][1] = [rows], [starts[0]], [starts[1]]
     send(2, 1)
     shares_2 = [(share_2, place_of(0))]
@@ -473,7 +462,7 @@
     def level_1(ks, block=None):
         jobs = [job(1, k) for k in ks]
         into = (grad, cuts[ks[0]][0])
-        return next_grads(chain, w_self, jobs, f"next_grads_1_{ks[0]}", into, (), (), block)
+        return next_grads(chain, w_self, jobs, f"next_grads_1_{ks[0]}", into, block)
 
     def sums_a(ks, before, last=None):
         xs = [(saved_inputs, (2,), 0), (saved_inputs, (1,), 0)]
@@ -488,27 +477,23 @@
         side = flat(far[1][k] for k in ks)
         return weight_sums(chain, xs, [side, grad], pairs, start, before, scale, last, name)
 
+    def leave(k):
+        rows = (cotangent, rows_at(cuts[k][0]), cuts[k][1])
+        near[2][k] = cut_out(chain, [[rows]], f"rows_{k}")
+        send(2, k)
+
     sum_a = sum_b = None
     for k in range(n):
-        ahead = k + 2
-        done = next_grads(
-            chain,
-            w_self,
-            [job(2, k)] + ([job(1, 0)] if k == 1 else []),
-            f"next_grads_{k}",
-            (grad, 0) if k == 1 else None,
-            [(cotangent, (), *cuts[ahead])] if ahead < n else [],
-        )
+        jobs = [job(2, k)] + ([job(1, 0)] if k == 1 else [])
+        near[1][k] = next_grads(chain, w_self, jobs, f"next_grads_{k}", (grad, 0) if k == 1 else None)
         if k == 1:
-            grad = done.pop()
-        if ahead < n:
-            near[2][ahead] = [done.pop()]
-            send(2, ahead)
-        near[1][k] = done
+            grad = near[1][k].pop()
         send(1, k)
+        if k < 2:
+            leave(k + 2)
         if 2 <= k < z - 1:
-            block = (w_cross, 0, tokens) if k == 2 else None
-            (grad,) = level_1([k - 1], block)
+            (grad,) = level_1([k - 1], (w_cross, 0, tokens) if k == 2 else None)
+            leave(k + 2)
         if 1 <= k < z - 1:
             (sum_b,) = sums_b([k - 1], sum_b)
         if 1 <= k < z:
@@ -519,11 +504,13 @@
         (sum_b,) = sums_b([k], sum_b)
     (grad,) = level_1([z])
     terms = sums_b([z], sum_b, (-1, 2))
-    cross_1 = [swap_both(t, k, 1 << 1) for k, t in enumerate(terms[:parts])]
     sum_c = spread(terms[parts:])
     cross_2, self_1, grad = add_terms(chain, sum_a, "add_a", (jnp.bfloat16, jnp.float32), grad)
+    far_grad = swap(grad, "narrow", 1 << 0)
+    cross_1 = [swap_both(terms[0], 0, 1 << 1)]
+    cross_2, *terms = hand_on(chain, [cross_2, *terms[1:parts]], [far_grad], "rest")
+    cross_1 += [swap_both(t, k, 1 << 1) for k, t in enumerate(terms, 1)]
     cross_2 = swap(cross_2, "narrow", 1 << 2)
-    far_grad = swap(grad, "narrow", 1 << 0)
     out = last_grad(chain, grad, far_grad, w_self, tokens)
     grad_self, grad_cross = last_sums(chain, cross_1, sum_c, self_1, self_2, cross_2)
     return out, grad_self, grad_cross

time: 164 us -> 153 us (0.933)
  Pallas kernels: 51.4 us -> 47.1 us
  local copies, waits for them, and re-layouts: 4.21 us -> 0.01 us
  waiting for transfers between devices: 61.9 us -> 59.5 us
    pallas_call x30 -> x35, Pallas kernels: 51.4 us -> 47.1 us  [__call__(): pl.pallas_call(whole, grid=(grid,), out_shape=[*out_shape, TOKEN], in_spe...]
    unnamed x8 -> x2, local copies, waits for them, and re-layouts: 4.21 us -> 0.01 us
    ppermute x4, starting transfers between devices: 6.3 us -> 2.44 us  [swap_both(): return lax.ppermute(array, ('wide', 'narrow'), pairs)]
    ppermute x28, starting transfers between devices: 38.2 us -> 41.8 us  [swap(): lax.ppermute(array, axis, [(i, i ^ mask) for i in range(lax.axis_size(axi...]
  transfers between devices with their start and end apart: 32 -> 32, of which waited for: 16 -> 17; matrix products, arithmetic and copies ran while one was open for 0% -> 0% of each run, Pallas kernels for 31% -> 30%
where the time goes in v5:
time: 153 us; the launch traced here: 152 us
  waiting for transfers between devices  59.5 us (39%)
  Pallas kernels  47.1 us (31%)
  starting transfers between devices  44.2 us (29%)
    ppermute x28, waiting for transfers between devices, swap(): lax.ppermute(array, axis, [(i, i ^ mask) for i in range(lax.axis_size(axi...  57.7 us
    pallas_call x35, Pallas kernels, __call__(): pl.pallas_call(whole, grid=(grid,), out_shape=[*out_shape, TOKEN], in_spe...  47.1 us
    ppermute x28, starting transfers between devices, swap(): lax.ppermute(array, axis, [(i, i ^ mask) for i in range(lax.axis_size(axi...  41.8 us
  transfers between devices with their start and end apart: 32, of which 17 were waited for; matrix products, arithmetic and copies ran while one was open for 0% of the time, Pallas kernels for 30%

profile of v5, /device:TPU:0, one launch (start us, length us, event | category | flops | bytes accessed | tf_op | source)
XLA Modules:
  0.0 151.8 jit_solution(15034054277530466494)
XLA Ops:
  1.1 1.2 first_rows.1
  2.4 3.7 %collective-permute-start.1 = (bf16[320,512]{1,0:T(8,128)(2,1)S(1)}, bf16[320,512]{1,0:T(8,128)(2,1)S(1)}, u32[]{:S(2)}, u32[]{:S(2)}) collective-permute-start(bf16[320,512]{1,0:T(8,128)(2,1)S(1)} %get-tuple-element.97), channel_id=1, source_target_pairs={{0,4},{1,5},{2,6},{3,7},{4,0},{5,1},{6,2},{7,3},{8,12},{9,13},{10,... | collective-permute-start | bytes 983048 | tf_op jit(solution)/shard_map/ppermute | solution.py:26
  6.1 4.5 %self_sums_2.1 = (f32[1,128,512]{2,1,0:T(8,128)S(1)}, bf16[1,128,512]{2,1,0:T(8,128)(2,1)S(1)}, bf16[1,128,512]{2,1,0:T(8,128)(2,1)S(1)}, bf16[1,128,512]{2,1,0:T(8,128)(2,1)S(1)}, f32[8,128]{1,0:T(8,128)S(1)}) custom-call(bf16[3,2048,512]{2,1,0:T(8,128)(2,1)} %refs_1_.25, bf16[2048,512]{1,0:T(8,128)(2,1)} %refs_0_.43, f32[8,128]{1,0:T(8,128)S(1)} %get-tuple-element.98.refs_2_), custom_call_target="tpu_custom_call" | custom-call | tf_op jit(solution)/shard_map/self_sums_2/pallas_call | solution.py:64
  10.6 1.6 %collective-permute-start.3 = (bf16[1,128,512]{2,1,0:T(8,128)(2,1)S(1)}, bf16[1,128,512]{2,1,0:T(8,128)(2,1)S(1)}, u32[]{:S(2)}, u32[]{:S(2)}) collective-permute-start(bf16[1,128,512]{2,1,0:T(8,128)(2,1)S(1)} %get-tuple-element.100), channel_id=1, source_target_pairs={{0,8},{8,0},{16,24},{24,16},{1,9},{9,1},{17,25},{25,17},{2,10},{10... | collective-permute-start | bytes 393224 | tf_op jit(solution)/shard_map/ppermute | solution.py:26
  12.2 1.5 %collective-permute-start.4 = (bf16[1,128,512]{2,1,0:T(8,128)(2,1)S(1)}, bf16[1,128,512]{2,1,0:T(8,128)(2,1)S(1)}, u32[]{:S(2)}, u32[]{:S(2)}) collective-permute-start(bf16[1,128,512]{2,1,0:T(8,128)(2,1)S(1)} %get-tuple-element.101), channel_id=1, source_target_pairs={{0,16},{8,24},{16,0},{24,8},{1,17},{9,25},{17,1},{25,9},{2,18},{10... | collective-permute-start | bytes 393224 | tf_op jit(solution)/shard_map/ppermute | solution.py:26
  14.2 2.5 %collective-permute-done.3.refs_1_ = bf16[1,128,512]{2,1,0:T(8,128)(2,1)S(1)} collective-permute-done((bf16[1,128,512]{2,1,0:T(8,128)(2,1)S(1)}, bf16[1,128,512]{2,1,0:T(8,128)(2,1)S(1)}, u32[]{:S(2)}, u32[]{:S(2)}) %collective-permute-start.3) | collective-permute-done | bytes 131104 | tf_op jit(solution)/shard_map/ppermute | solution.py:26
  16.6 1.6 %collective-permute-start = (bf16[512,512]{1,0:T(8,128)(2,1)S(1)}, bf16[512,512]{1,0:T(8,128)(2,1)S(1)}, u32[]{:S(2)}, u32[]{:S(2)}) collective-permute-start(bf16[512,512]{1,0:T(8,128)(2,1)S(1)} %get-tuple-element.96), channel_id=1, source_target_pairs={{0,2},{1,3},{2,0},{3,1},{4,6},{5,7},{6,4},{7,5},{8,10},{9,11},{10,... | collective-permute-start | bytes 1572872 | tf_op jit(solution)/shard_map/ppermute | solution.py:26
  18.2 2.1 %collective-permute-done.4.refs_2_ = bf16[1,128,512]{2,1,0:T(8,128)(2,1)S(1)} collective-permute-done((bf16[1,128,512]{2,1,0:T(8,128)(2,1)S(1)}, bf16[1,128,512]{2,1,0:T(8,128)(2,1)S(1)}, u32[]{:S(2)}, u32[]{:S(2)}) %collective-permute-start.4) | collective-permute-done | bytes 131104 | tf_op jit(solution)/shard_map/ppermute | solution.py:26
  20.4 1.2 collective-permute-done.1.refs_0_.refs_1_
  21.6 1.6 %parted.1 = (bf16[128,512]{1,0:T(8,128)(2,1)S(1)}, bf16[192,512]{1,0:T(8,128)(2,1)S(1)}, bf16[192,512]{1,0:T(8,128)(2,1)S(1)}, bf16[384,512]{1,0:T(8,128)(2,1)S(1)}, f32[8,128]{1,0:T(8,128)S(1)}) custom-call(bf16[320,512]{1,0:T(8,128)(2,1)S(1)} %collective-permute-done.1.refs_0_.refs_1_, bf16[320,512]{1,0:T(8,128)(2,1)S(1)} %collective-permute-done.1.refs_0_.refs_1_, ...), custom_call_target="tpu_custom_call" | custom-call | tf_op jit(solution)/shard_map/parted/pallas_call | solution.py:64
  23.2 1.6 %collective-permute-start.6 = (bf16[128,512]{1,0:T(8,128)(2,1)S(1)}, bf16[128,512]{1,0:T(8,128)(2,1)S(1)}, u32[]{:S(2)}, u32[]{:S(2)}) collective-permute-start(bf16[128,512]{1,0:T(8,128)(2,1)S(1)} %get-tuple-element.105.refs_0_), channel_id=1, source_target_pairs={{0,8},{8,0},{16,24},{24,16},{1,9},{9,1},{17,25},{25,17},{2,10},{10... | collective-permute-start | bytes 393224 | tf_op jit(solution)/shard_map/ppermute | solution.py:26
  24.8 1.5 %collective-permute-start.7 = (bf16[128,512]{1,0:T(8,128)(2,1)S(1)}, bf16[128,512]{1,0:T(8,128)(2,1)S(1)}, u32[]{:S(2)}, u32[]{:S(2)}) collective-permute-start(bf16[128,512]{1,0:T(8,128)(2,1)S(1)} %get-tuple-element.105.refs_0_), channel_id=1, source_target_pairs={{0,16},{8,24},{16,0},{24,8},{1,17},{9,25},{17,1},{25,9},{2,18},{10... | collective-permute-start | bytes 393224 | tf_op jit(solution)/shard_map/ppermute | solution.py:26
  26.8 2.3 %collective-permute-done.6.refs_1_ = bf16[128,512]{1,0:T(8,128)(2,1)S(1)} collective-permute-done((bf16[128,512]{1,0:T(8,128)(2,1)S(1)}, bf16[128,512]{1,0:T(8,128)(2,1)S(1)}, u32[]{:S(2)}, u32[]{:S(2)}) %collective-permute-start.6) | collective-permute-done | bytes 131104 | tf_op jit(solution)/shard_map/ppermute | solution.py:26
  29.1 3.5 %collective-permute-done.7.refs_2_ = bf16[128,512]{1,0:T(8,128)(2,1)S(1)} collective-permute-done((bf16[128,512]{1,0:T(8,128)(2,1)S(1)}, bf16[128,512]{1,0:T(8,128)(2,1)S(1)}, u32[]{:S(2)}, u32[]{:S(2)}) %collective-permute-start.7) | collective-permute-done | bytes 131104 | tf_op jit(solution)/shard_map/ppermute | solution.py:26
  33.2 4.0 %collective-permute-start.11 = (bf16[192,512]{1,0:T(8,128)(2,1)S(1)}, bf16[192,512]{1,0:T(8,128)(2,1)S(1)}, u32[]{:S(2)}, u32[]{:S(2)}) collective-permute-start(bf16[192,512]{1,0:T(8,128)(2,1)S(1)} %get-tuple-element.114.refs_6_.refs_4_), channel_id=1, source_target_pairs={{0,2},{1,3},{2,0},{3,1},{4,6},{5,7},{6,4},{7,5},{8,10},{9,11},{10,... | collective-permute-start | bytes 589832 | tf_op jit(solution)/shard_map/ppermute | solution.py:26
  38.5 6.3 %collective-permute-done.11.refs_7_.refs_3_ = bf16[192,512]{1,0:T(8,128)(2,1)S(1)} collective-permute-done((bf16[192,512]{1,0:T(8,128)(2,1)S(1)}, bf16[192,512]{1,0:T(8,128)(2,1)S(1)}, u32[]{:S(2)}, u32[]{:S(2)}) %collective-permute-start.11) | collective-permute-done | bytes 196640 | tf_op jit(solution)/shard_map/ppermute | solution.py:26
  44.9 8.1 %collective-permute-done.10.refs_3_ = bf16[384,512]{1,0:T(8,128)(2,1)S(1)} collective-permute-done((bf16[384,512]{1,0:T(8,128)(2,1)S(1)}, bf16[384,512]{1,0:T(8,128)(2,1)S(1)}, u32[]{:S(2)}, u32[]{:S(2)}) %collective-permute-start.10) | collective-permute-done | bytes 393248 | tf_op jit(solution)/shard_map/ppermute | solution.py:26
  55.8 3.5 %collective-permute-start.14 = (bf16[448,512]{1,0:T(8,128)(2,1)S(1)}, bf16[448,512]{1,0:T(8,128)(2,1)S(1)}, u32[]{:S(2)}, u32[]{:S(2)}) collective-permute-start(bf16[448,512]{1,0:T(8,128)(2,1)S(1)} %get-tuple-element.125.refs_2_), channel_id=1, source_target_pairs={{0,4},{1,5},{2,6},{3,7},{4,0},{5,1},{6,2},{7,3},{8,12},{9,13},{10,... | collective-permute-start | bytes 1376264 | tf_op jit(solution)/shard_map/ppermute | solution.py:26
  59.3 1.7 %sums_b_0.1 = (f32[3,512,512]{2,1,0:T(8,128)S(1)}, f32[8,128]{1,0:T(8,128)S(1)}) custom-call(bf16[3,2048,512]{2,1,0:T(8,128)(2,1)} %refs_1_.25, bf16[3,2048,512]{2,1,0:T(8,128)(2,1)} %refs_1_.25, bf16[3,2048,512]{2,1,0:T(8,128)(2,1)S(1)} %collective-permute-done.2.refs_4_.refs_2_, bf16[192,512]{1,0:T(8,128)(2,1)S(1)} %collective-permute-done.11.refs_7_.refs_3_, ...), custom_call_target="tpu_custom_call" | custom-call | tf_op jit(solution)/shard_map/sums_b_0/pallas_call | solution.py:64
  60.9 2.3 %sums_a_0.1 = (f32[2,512,512]{2,1,0:T(8,128)S(1)}, f32[8,128]{1,0:T(8,128)S(1)}) custom-call(bf16[3,2048,512]{2,1,0:T(8,128)(2,1)} %refs_1_.25, bf16[3,2048,512]{2,1,0:T(8,128)(2,1)} %refs_1_.25, bf16[192,512]{1,0:T(8,128)(2,1)S(1)} %get-tuple-element.109.refs_3_.refs_2_, bf16[384,512]{1,0:T(8,128)(2,1)S(1)} %collective-permute-done.10.refs_3_, ...), custom_call_target="tpu_custom_call" | custom-call | tf_op jit(solution)/shard_map/sums_a_0/pallas_call | solution.py:64
  63.9 10.9 %collective-permute-done.13.refs_3_ = bf16[384,512]{1,0:T(8,128)(2,1)S(1)} collective-permute-done((bf16[384,512]{1,0:T(8,128)(2,1)S(1)}, bf16[384,512]{1,0:T(8,128)(2,1)S(1)}, u32[]{:S(2)}, u32[]{:S(2)}) %collective-permute-start.13) | collective-permute-done | bytes 393248 | tf_op jit(solution)/shard_map/ppermute | solution.py:26
  74.8 1.5 next_grads_1_1.1
  77.4 2.2 %sums_b_1.1 = (f32[3,512,512]{2,1,0:T(8,128)S(1)}, f32[8,128]{1,0:T(8,128)S(1)}) custom-call(bf16[3,2048,512]{2,1,0:T(8,128)(2,1)} %refs_1_.25, bf16[3,2048,512]{2,1,0:T(8,128)(2,1)} %refs_1_.25, bf16[3,2048,512]{2,1,0:T(8,128)(2,1)S(1)} %collective-permute-done.2.refs_4_.refs_2_, bf16[384,512]{1,0:T(8,128)(2,1)S(1)} %collective-permute-done.13.refs_3_, ...), custom_call_target="tpu_custom_call" | custom-call | tf_op jit(solution)/shard_map/sums_b_1/pallas_call | solution.py:64
  79.5 1.9 %sums_a_2.1 = (f32[2,512,512]{2,1,0:T(8,128)S(1)}, f32[8,128]{1,0:T(8,128)S(1)}) custom-call(bf16[3,2048,512]{2,1,0:T(8,128)(2,1)} %refs_1_.25, bf16[3,2048,512]{2,1,0:T(8,128)(2,1)} %refs_1_.25, bf16[384,512]{1,0:T(8,128)(2,1)S(1)} %collective-permute-done.9.refs_3_.refs_2_, bf16[384,512]{1,0:T(8,128)(2,1)S(1)} %get-tuple-element.122.refs_3_.refs_2_, ...), custom_call_target="tpu_custom_call" | custom-call | tf_op jit(solution)/shard_map/sums_a_2/pallas_call | solution.py:64
  82.1 2.5 %collective-permute-start.22 = (bf16[448,512]{1,0:T(8,128)(2,1)S(1)}, bf16[448,512]{1,0:T(8,128)(2,1)S(1)}, u32[]{:S(2)}, u32[]{:S(2)}) collective-permute-start(bf16[448,512]{1,0:T(8,128)(2,1)S(1)} %get-tuple-element.136.refs_3_.refs_2_), channel_id=1, source_target_pairs={{0,2},{1,3},{2,0},{3,1},{4,6},{5,7},{6,4},{7,5},{8,10},{9,11},{10,... | collective-permute-start | bytes 1376264 | tf_op jit(solution)/shard_map/ppermute | solution.py:26
  84.6 6.0 %collective-permute-done.12.refs_3_ = bf16[384,512]{1,0:T(8,128)(2,1)S(1)} collective-permute-done((bf16[384,512]{1,0:T(8,128)(2,1)S(1)}, bf16[384,512]{1,0:T(8,128)(2,1)S(1)}, u32[]{:S(2)}, u32[]{:S(2)}) %collective-permute-start.12) | collective-permute-done | bytes 393248 | tf_op jit(solution)/shard_map/ppermute | solution.py:26
  92.4 1.3 collective-permute-start.15
  93.7 2.2 %sums_b_2.1 = (f32[3,512,512]{2,1,0:T(8,128)S(1)}, f32[8,128]{1,0:T(8,128)S(1)}) custom-call(bf16[3,2048,512]{2,1,0:T(8,128)(2,1)} %refs_1_.25, bf16[3,2048,512]{2,1,0:T(8,128)(2,1)} %refs_1_.25, bf16[3,2048,512]{2,1,0:T(8,128)(2,1)S(1)} %collective-permute-done.2.refs_4_.refs_2_, bf16[384,512]{1,0:T(8,128)(2,1)S(1)} %collective-permute-done.12.refs_3_, ...), custom_call_target="tpu_custom_call" | custom-call | tf_op jit(solution)/shard_map/sums_b_2/pallas_call | solution.py:64
  95.9 1.9 %sums_a_3.1 = (f32[2,512,512]{2,1,0:T(8,128)S(1)}, f32[8,128]{1,0:T(8,128)S(1)}) custom-call(bf16[3,2048,512]{2,1,0:T(8,128)(2,1)} %refs_1_.25, bf16[3,2048,512]{2,1,0:T(8,128)(2,1)} %refs_1_.25, bf16[448,512]{1,0:T(8,128)(2,1)S(1)} %collective-permute-done.14.refs_3_.refs_2_, bf16[448,512]{1,0:T(8,128)(2,1)S(1)} %get-tuple-element.136.refs_3_.refs_2_, ...), custom_call_target="tpu_custom_call" | custom-call | tf_op jit(solution)/shard_map/sums_a_3/pallas_call | solution.py:64
  100.1 1.9 %sums_a_4.1 = (f32[2,512,512]{2,1,0:T(8,128)S(1)}, f32[8,128]{1,0:T(8,128)S(1)}) custom-call(bf16[3,2048,512]{2,1,0:T(8,128)(2,1)} %refs_1_.25, bf16[3,2048,512]{2,1,0:T(8,128)(2,1)} %refs_1_.25, bf16[384,512]{1,0:T(8,128)(2,1)S(1)} %collective-permute-done.16.refs_3_.refs_2_, bf16[384,512]{1,0:T(8,128)(2,1)S(1)} %get-tuple-element.143.refs_3_.refs_2_, ...), custom_call_target="tpu_custom_call" | custom-call | tf_op jit(solution)/shard_map/sums_a_4/pallas_call | solution.py:64
  101.9 5.6 %collective-permute-done.15.refs_3_.refs_2_ = bf16[256,512]{1,0:T(8,128)(2,1)S(1)} collective-permute-done((bf16[256,512]{1,0:T(8,128)(2,1)S(1)}, bf16[256,512]{1,0:T(8,128)(2,1)S(1)}, u32[]{:S(2)}, u32[]{:S(2)}) %collective-permute-start.15) | collective-permute-done | bytes 262176 | tf_op jit(solution)/shard_map/ppermute | solution.py:26
  108.0 3.0 %collective-permute-start.20 = (bf16[256,512]{1,0:T(8,128)(2,1)S(1)}, bf16[256,512]{1,0:T(8,128)(2,1)S(1)}, u32[]{:S(2)}, u32[]{:S(2)}) collective-permute-start(bf16[256,512]{1,0:T(8,128)(2,1)S(1)} %get-tuple-element.147.refs_3_.refs_2_), channel_id=1, source_target_pairs={{0,2},{1,3},{2,0},{3,1},{4,6},{5,7},{6,4},{7,5},{8,10},{9,11},{10,... | collective-permute-start | bytes 786440 | tf_op jit(solution)/shard_map/ppermute | solution.py:26
  111.0 1.6 %sums_a_5.1 = (f32[2,128,512]{2,1,0:T(8,128)S(1)}, bf16[2,128,512]{2,1,0:T(8,128)(2,1)S(1)}, bf16[2,128,512]{2,1,0:T(8,128)(2,1)S(1)}, bf16[2,128,512]{2,1,0:T(8,128)(2,1)S(1)}, f32[8,128]{1,0:T(8,128)S(1)}) custom-call(bf16[3,2048,512]{2,1,0:T(8,128)(2,1)} %refs_1_.25, bf16[3,2048,512]{2,1,0:T(8,128)(2,1)} %refs_1_.25, ...), custom_call_target="tpu_custom_call" | custom-call | tf_op jit(solution)/shard_map/sums_a_5/pallas_call | solution.py:64
  112.7 1.3 collective-permute-start.17
  114.0 1.5 collective-permute-start.18
  117.2 2.2 %sums_b_3.1 = (f32[3,512,512]{2,1,0:T(8,128)S(1)}, f32[8,128]{1,0:T(8,128)S(1)}) custom-call(bf16[3,2048,512]{2,1,0:T(8,128)(2,1)} %refs_1_.25, bf16[3,2048,512]{2,1,0:T(8,128)(2,1)} %refs_1_.25, bf16[3,2048,512]{2,1,0:T(8,128)(2,1)S(1)} %collective-permute-done.2.refs_4_.refs_2_, bf16[448,512]{1,0:T(8,128)(2,1)S(1)} %collective-permute-done.22.refs_3_, ...), custom_call_target="tpu_custom_call" | custom-call | tf_op jit(solution)/shard_map/sums_b_3/pallas_call | solution.py:64
  120.2 2.2 %sums_b_4.1 = (f32[3,512,512]{2,1,0:T(8,128)S(1)}, f32[8,128]{1,0:T(8,128)S(1)}) custom-call(bf16[3,2048,512]{2,1,0:T(8,128)(2,1)} %refs_1_.25, bf16[3,2048,512]{2,1,0:T(8,128)(2,1)} %refs_1_.25, bf16[3,2048,512]{2,1,0:T(8,128)(2,1)S(1)} %collective-permute-done.2.refs_4_.refs_2_, bf16[384,512]{1,0:T(8,128)(2,1)S(1)} %collective-permute-done.21.refs_3_, ...), custom_call_target="tpu_custom_call" | custom-call | tf_op jit(solution)/shard_map/sums_b_4/pallas_call | solution.py:64
  122.4 2.5 %collective-permute-done.20.refs_3_ = bf16[256,512]{1,0:T(8,128)(2,1)S(1)} collective-permute-done((bf16[256,512]{1,0:T(8,128)(2,1)S(1)}, bf16[256,512]{1,0:T(8,128)(2,1)S(1)}, u32[]{:S(2)}, u32[]{:S(2)}) %collective-permute-start.20) | collective-permute-done | bytes 262176 | tf_op jit(solution)/shard_map/ppermute | solution.py:26
  125.5 1.9 %sums_b_5.1 = (bf16[1,128,512]{2,1,0:T(8,128)(2,1)S(1)}, bf16[1,128,512]{2,1,0:T(8,128)(2,1)S(1)}, bf16[1,128,512]{2,1,0:T(8,128)(2,1)S(1)}, bf16[1,128,512]{2,1...) custom-call(bf16[3,2048,512]{2,1,0:T(8,128)(2,1)} %refs_1_.25, ...), custom_call_target="tpu_custom_call" | custom-call | tf_op jit(solution)/shard_map/sums_b_5/pallas_call | solution.py:64
  127.6 1.4 collective-permute-start.28
  129.0 1.5 %collective-permute-start.29 = (bf16[2,128,512]{2,1,0:T(8,128)(2,1)S(1)}, bf16[2,128,512]{2,1,0:T(8,128)(2,1)S(1)}, u32[]{:S(2)}, u32[]{:S(2)}) collective-permute-start(bf16[2,128,512]{2,1,0:T(8,128)(2,1)S(1)} %get-tuple-element.181), channel_id=1, source_target_pairs={{0,16},{8,24},{16,0},{24,8},{1,17},{9,25},{17,1},{25,9},{2,18},{10... | collective-permute-start | bytes 786440 | tf_op jit(solution)/shard_map/ppermute | solution.py:26
  131.2 1.3 collective-permute-done.23.refs_4_.refs_1_.refs_3_
  132.5 1.5 collective-permute-start.25
  134.0 1.9 %collective-permute-done.24.refs_0_ = bf16[1,128,512]{2,1,0:T(8,128)(2,1)S(1)} collective-permute-done((bf16[1,128,512]{2,1,0:T(8,128)(2,1)S(1)}, bf16[1,128,512]{2,1,0:T(8,128)(2,1)S(1)}, u32[]{:S(2)}, u32[]{:S(2)}) %collective-permute-start.24) | collective-permute-done | bytes 131104 | tf_op jit(solution)/shard_map/ppermute | solution.py:36
  136.3 3.1 %collective-permute-done.28.refs_5_ = bf16[2,128,512]{2,1,0:T(8,128)(2,1)S(1)} collective-permute-done((bf16[2,128,512]{2,1,0:T(8,128)(2,1)S(1)}, bf16[2,128,512]{2,1,0:T(8,128)(2,1)S(1)}, u32[]{:S(2)}, u32[]{:S(2)}) %collective-permute-start.28) | collective-permute-done | bytes 262176 | tf_op jit(solution)/shard_map/ppermute | solution.py:26
  139.9 5.5 %collective-permute-start.31 = (bf16[128,512]{1,0:T(8,128)(2,1)S(1)}, bf16[128,512]{1,0:T(8,128)(2,1)S(1)}, u32[]{:S(2)}, u32[]{:S(2)}) collective-permute-start(bf16[128,512]{1,0:T(8,128)(2,1)S(1)} %get-tuple-element.185), channel_id=1, source_target_pairs={{0,4},{1,5},{2,6},{3,7},{4,0},{5,1},{6,2},{7,3},{8,12},{9,13},{10,... | collective-permute-start | bytes 393224 | tf_op jit(solution)/shard_map/ppermute | solution.py:26
  145.5 3.8 %last_grad.1 = (bf16[2048,512]{1,0:T(8,128)(2,1)}, f32[8,128]{1,0:T(8,128)S(1)}) custom-call(bf16[2560,512]{1,0:T(8,128)(2,1)S(1)} %get-tuple-element.167.refs_0_, bf16[2560,512]{1,0:T(8,128)(2,1)S(1)} %collective-permute-done.23.refs_4_.refs_1_.refs_3_, bf16[3,512,512]{2,1,0:T(8,128)(2,1)S(1)} %copy-done, ...), custom_call_target="tpu_custom_call" | custom-call | tf_op jit(solution)/shard_map/last_grad/pallas_call | solution.py:64
  150.6 1.3 last_sums.1
  (53 shorter events, 19.2 us)
Async XLA Ops:
  0.6 20.9 %collective-permute-start.2 = (bf16[3,2048,512]{2,1,0:T(8,128)(2,1)}, bf16[3,2048,512]{2,1,0:T(8,128)(2,1)S(1)}, u32[]{:S(2)}, u32[]{:S(2)}) collective-permute-start(bf16[3,2048,512]{2,1,0:T(8,128)(2,1)} %refs_1_.25), channel_id=1, source_target_pairs={{0,1},{1,0},{2,3},{3,2},{4,5},{5,4},{6,7},{7,6},{8,9},{9,8},{10,11... | collective-permute-start | bytes 18874376 | tf_op jit(solution)/shard_map/ppermute | solution.py:26
  2.4 19.2 %collective-permute-start.1 = (bf16[320,512]{1,0:T(8,128)(2,1)S(1)}, bf16[320,512]{1,0:T(8,128)(2,1)S(1)}, u32[]{:S(2)}, u32[]{:S(2)}) collective-permute-start(bf16[320,512]{1,0:T(8,128)(2,1)S(1)} %get-tuple-element.97), channel_id=1, source_target_pairs={{0,4},{1,5},{2,6},{3,7},{4,0},{5,1},{6,2},{7,3},{8,12},{9,13},{10,... | collective-permute-start | bytes 983048 | tf_op jit(solution)/shard_map/ppermute | solution.py:26
  10.6 6.0 %collective-permute-start.3 = (bf16[1,128,512]{2,1,0:T(8,128)(2,1)S(1)}, bf16[1,128,512]{2,1,0:T(8,128)(2,1)S(1)}, u32[]{:S(2)}, u32[]{:S(2)}) collective-permute-start(bf16[1,128,512]{2,1,0:T(8,128)(2,1)S(1)} %get-tuple-element.100), channel_id=1, source_target_pairs={{0,8},{8,0},{16,24},{24,16},{1,9},{9,1},{17,25},{25,17},{2,10},{10... | collective-permute-start | bytes 393224 | tf_op jit(solution)/shard_map/ppermute | solution.py:26
  12.2 8.1 %collective-permute-start.4 = (bf16[1,128,512]{2,1,0:T(8,128)(2,1)S(1)}, bf16[1,128,512]{2,1,0:T(8,128)(2,1)S(1)}, u32[]{:S(2)}, u32[]{:S(2)}) collective-permute-start(bf16[1,128,512]{2,1,0:T(8,128)(2,1)S(1)} %get-tuple-element.101), channel_id=1, source_target_pairs={{0,16},{8,24},{16,0},{24,8},{1,17},{9,25},{17,1},{25,9},{2,18},{10... | collective-permute-start | bytes 393224 | tf_op jit(solution)/shard_map/ppermute | solution.py:26
  13.7 6.6 %collective-permute-start.5 = (bf16[1,128,512]{2,1,0:T(8,128)(2,1)S(1)}, bf16[1,128,512]{2,1,0:T(8,128)(2,1)S(1)}, u32[]{:S(2)}, u32[]{:S(2)}) collective-permute-start(bf16[1,128,512]{2,1,0:T(8,128)(2,1)S(1)} %get-tuple-element.102), channel_id=1, source_target_pairs={{0,24},{8,16},{16,8},{24,0},{1,25},{9,17},{17,9},{25,1},{2,26},{10... | collective-permute-start | bytes 393224 | tf_op jit(solution)/shard_map/ppermute | solution.py:26
  16.6 21.9 %collective-permute-start = (bf16[512,512]{1,0:T(8,128)(2,1)S(1)}, bf16[512,512]{1,0:T(8,128)(2,1)S(1)}, u32[]{:S(2)}, u32[]{:S(2)}) collective-permute-start(bf16[512,512]{1,0:T(8,128)(2,1)S(1)} %get-tuple-element.96), channel_id=1, source_target_pairs={{0,2},{1,3},{2,0},{3,1},{4,6},{5,7},{6,4},{7,5},{8,10},{9,11},{10,... | collective-permute-start | bytes 1572872 | tf_op jit(solution)/shard_map/ppermute | solution.py:26
  21.6 11.1 %copy-start = (bf16[3,512,512]{2,1,0:T(8,128)(2,1)S(1)}, bf16[3,512,512]{2,1,0:T(8,128)(2,1)}, u32[]{:S(2)}) copy-start(bf16[3,512,512]{2,1,0:T(8,128)(2,1)} %refs_2_.5) | copy-start | bytes 4718596
  23.2 29.9 %collective-permute-start.10 = (bf16[384,512]{1,0:T(8,128)(2,1)S(1)}, bf16[384,512]{1,0:T(8,128)(2,1)S(1)}, u32[]{:S(2)}, u32[]{:S(2)}) collective-permute-start(bf16[384,512]{1,0:T(8,128)(2,1)S(1)} %get-tuple-element.113.refs_2_), channel_id=1, source_target_pairs={{0,4},{1,5},{2,6},{3,7},{4,0},{5,1},{6,2},{7,3},{8,12},{9,13},{10,... | collective-permute-start | bytes 1179656 | tf_op jit(solution)/shard_map/ppermute | solution.py:26
  23.2 5.9 %collective-permute-start.6 = (bf16[128,512]{1,0:T(8,128)(2,1)S(1)}, bf16[128,512]{1,0:T(8,128)(2,1)S(1)}, u32[]{:S(2)}, u32[]{:S(2)}) collective-permute-start(bf16[128,512]{1,0:T(8,128)(2,1)S(1)} %get-tuple-element.105.refs_0_), channel_id=1, source_target_pairs={{0,8},{8,0},{16,24},{24,16},{1,9},{9,1},{17,25},{25,17},{2,10},{10... | collective-permute-start | bytes 393224 | tf_op jit(solution)/shard_map/ppermute | solution.py:26
  24.8 7.8 %collective-permute-start.7 = (bf16[128,512]{1,0:T(8,128)(2,1)S(1)}, bf16[128,512]{1,0:T(8,128)(2,1)S(1)}, u32[]{:S(2)}, u32[]{:S(2)}) collective-permute-start(bf16[128,512]{1,0:T(8,128)(2,1)S(1)} %get-tuple-element.105.refs_0_), channel_id=1, source_target_pairs={{0,16},{8,24},{16,0},{24,8},{1,17},{9,25},{17,1},{25,9},{2,18},{10... | collective-permute-start | bytes 393224 | tf_op jit(solution)/shard_map/ppermute | solution.py:26
  26.4 6.3 %collective-permute-start.8 = (bf16[128,512]{1,0:T(8,128)(2,1)S(1)}, bf16[128,512]{1,0:T(8,128)(2,1)S(1)}, u32[]{:S(2)}, u32[]{:S(2)}) collective-permute-start(bf16[128,512]{1,0:T(8,128)(2,1)S(1)} %get-tuple-element.105.refs_0_), channel_id=1, source_target_pairs={{0,24},{8,16},{16,8},{24,0},{1,25},{9,17},{17,9},{25,1},{2,26},{10... | collective-permute-start | bytes 393224 | tf_op jit(solution)/shard_map/ppermute | solution.py:26
  33.2 11.7 %collective-permute-start.11 = (bf16[192,512]{1,0:T(8,128)(2,1)S(1)}, bf16[192,512]{1,0:T(8,128)(2,1)S(1)}, u32[]{:S(2)}, u32[]{:S(2)}) collective-permute-start(bf16[192,512]{1,0:T(8,128)(2,1)S(1)} %get-tuple-element.114.refs_6_.refs_4_), channel_id=1, source_target_pairs={{0,2},{1,3},{2,0},{3,1},{4,6},{5,7},{6,4},{7,5},{8,10},{9,11},{10,... | collective-permute-start | bytes 589832 | tf_op jit(solution)/shard_map/ppermute | solution.py:26
  38.2 25.0 %collective-permute-start.9 = (bf16[384,512]{1,0:T(8,128)(2,1)S(1)}, bf16[384,512]{1,0:T(8,128)(2,1)S(1)}, u32[]{:S(2)}, u32[]{:S(2)}) collective-permute-start(bf16[384,512]{1,0:T(8,128)(2,1)S(1)} %get-tuple-element.112.refs_2_), channel_id=1, source_target_pairs={{0,4},{1,5},{2,6},{3,7},{4,0},{5,1},{6,2},{7,3},{8,12},{9,13},{10,... | collective-permute-start | bytes 1179656 | tf_op jit(solution)/shard_map/ppermute | solution.py:26
  54.2 20.6 %collective-permute-start.13 = (bf16[384,512]{1,0:T(8,128)(2,1)S(1)}, bf16[384,512]{1,0:T(8,128)(2,1)S(1)}, u32[]{:S(2)}, u32[]{:S(2)}) collective-permute-start(bf16[384,512]{1,0:T(8,128)(2,1)S(1)} %get-tuple-element.116.refs_5_.refs_2_), channel_id=1, source_target_pairs={{0,2},{1,3},{2,0},{3,1},{4,6},{5,7},{6,4},{7,5},{8,10},{9,11},{10,... | collective-permute-start | bytes 1179656 | tf_op jit(solution)/shard_map/ppermute | solution.py:26
  55.8 25.6 %collective-permute-start.14 = (bf16[448,512]{1,0:T(8,128)(2,1)S(1)}, bf16[448,512]{1,0:T(8,128)(2,1)S(1)}, u32[]{:S(2)}, u32[]{:S(2)}) collective-permute-start(bf16[448,512]{1,0:T(8,128)(2,1)S(1)} %get-tuple-element.125.refs_2_), channel_id=1, source_target_pairs={{0,4},{1,5},{2,6},{3,7},{4,0},{5,1},{6,2},{7,3},{8,12},{9,13},{10,... | collective-permute-start | bytes 1376264 | tf_op jit(solution)/shard_map/ppermute | solution.py:26
  63.9 26.8 %collective-permute-start.12 = (bf16[384,512]{1,0:T(8,128)(2,1)S(1)}, bf16[384,512]{1,0:T(8,128)(2,1)S(1)}, u32[]{:S(2)}, u32[]{:S(2)}) collective-permute-start(bf16[384,512]{1,0:T(8,128)(2,1)S(1)} %get-tuple-element.122.refs_3_.refs_2_), channel_id=1, source_target_pairs={{0,2},{1,3},{2,0},{3,1},{4,6},{5,7},{6,4},{7,5},{8,10},{9,11},{10,... | collective-permute-start | bytes 1179656 | tf_op jit(solution)/shard_map/ppermute | solution.py:26
  77.3 21.4 %collective-permute-start.16 = (bf16[384,512]{1,0:T(8,128)(2,1)S(1)}, bf16[384,512]{1,0:T(8,128)(2,1)S(1)}, u32[]{:S(2)}, u32[]{:S(2)}) collective-permute-start(bf16[384,512]{1,0:T(8,128)(2,1)S(1)} %get-tuple-element.135.refs_2_), channel_id=1, source_target_pairs={{0,4},{1,5},{2,6},{3,7},{4,0},{5,1},{6,2},{7,3},{8,12},{9,13},{10,... | collective-permute-start | bytes 1179656 | tf_op jit(solution)/shard_map/ppermute | solution.py:26
  82.1 33.4 %collective-permute-start.22 = (bf16[448,512]{1,0:T(8,128)(2,1)S(1)}, bf16[448,512]{1,0:T(8,128)(2,1)S(1)}, u32[]{:S(2)}, u32[]{:S(2)}) collective-permute-start(bf16[448,512]{1,0:T(8,128)(2,1)S(1)} %get-tuple-element.136.refs_3_.refs_2_), channel_id=1, source_target_pairs={{0,2},{1,3},{2,0},{3,1},{4,6},{5,7},{6,4},{7,5},{8,10},{9,11},{10,... | collective-permute-start | bytes 1376264 | tf_op jit(solution)/shard_map/ppermute | solution.py:26
  92.4 15.1 %collective-permute-start.15 = (bf16[256,512]{1,0:T(8,128)(2,1)S(1)}, bf16[256,512]{1,0:T(8,128)(2,1)S(1)}, u32[]{:S(2)}, u32[]{:S(2)}) collective-permute-start(bf16[256,512]{1,0:T(8,128)(2,1)S(1)} %get-tuple-element.134.refs_2_), channel_id=1, source_target_pairs={{0,4},{1,5},{2,6},{3,7},{4,0},{5,1},{6,2},{7,3},{8,12},{9,13},{10,... | collective-permute-start | bytes 786440 | tf_op jit(solution)/shard_map/ppermute | solution.py:26
  99.3 20.1 %collective-permute-start.21 = (bf16[384,512]{1,0:T(8,128)(2,1)S(1)}, bf16[384,512]{1,0:T(8,128)(2,1)S(1)}, u32[]{:S(2)}, u32[]{:S(2)}) collective-permute-start(bf16[384,512]{1,0:T(8,128)(2,1)S(1)} %get-tuple-element.143.refs_3_.refs_2_), channel_id=1, source_target_pairs={{0,2},{1,3},{2,0},{3,1},{4,6},{5,7},{6,4},{7,5},{8,10},{9,11},{10,... | collective-permute-start | bytes 1179656 | tf_op jit(solution)/shard_map/ppermute | solution.py:26
  108.0 17.0 %collective-permute-start.20 = (bf16[256,512]{1,0:T(8,128)(2,1)S(1)}, bf16[256,512]{1,0:T(8,128)(2,1)S(1)}, u32[]{:S(2)}, u32[]{:S(2)}) collective-permute-start(bf16[256,512]{1,0:T(8,128)(2,1)S(1)} %get-tuple-element.147.refs_3_.refs_2_), channel_id=1, source_target_pairs={{0,2},{1,3},{2,0},{3,1},{4,6},{5,7},{6,4},{7,5},{8,10},{9,11},{10,... | collective-permute-start | bytes 786440 | tf_op jit(solution)/shard_map/ppermute | solution.py:26
  112.7 14.7 %collective-permute-start.17 = (bf16[2,128,512]{2,1,0:T(8,128)(2,1)S(1)}, bf16[2,128,512]{2,1,0:T(8,128)(2,1)S(1)}, u32[]{:S(2)}, u32[]{:S(2)}) collective-permute-start(bf16[2,128,512]{2,1,0:T(8,128)(2,1)S(1)} %get-tuple-element.151), channel_id=1, source_target_pairs={{0,8},{8,0},{16,24},{24,16},{1,9},{9,1},{17,25},{25,17},{2,10},{10... | collective-permute-start | bytes 786440 | tf_op jit(solution)/shard_map/ppermute | solution.py:26
  114.0 13.4 %collective-permute-start.18 = (bf16[2,128,512]{2,1,0:T(8,128)(2,1)S(1)}, bf16[2,128,512]{2,1,0:T(8,128)(2,1)S(1)}, u32[]{:S(2)}, u32[]{:S(2)}) collective-permute-start(bf16[2,128,512]{2,1,0:T(8,128)(2,1)S(1)} %get-tuple-element.152), channel_id=1, source_target_pairs={{0,16},{8,24},{16,0},{24,8},{1,17},{9,25},{17,1},{25,9},{2,18},{10... | collective-permute-start | bytes 786440 | tf_op jit(solution)/shard_map/ppermute | solution.py:26
  115.5 11.9 %collective-permute-start.19 = (bf16[2,128,512]{2,1,0:T(8,128)(2,1)S(1)}, bf16[2,128,512]{2,1,0:T(8,128)(2,1)S(1)}, u32[]{:S(2)}, u32[]{:S(2)}) collective-permute-start(bf16[2,128,512]{2,1,0:T(8,128)(2,1)S(1)} %get-tuple-element.153), channel_id=1, source_target_pairs={{0,24},{8,16},{16,8},{24,0},{1,25},{9,17},{17,9},{25,1},{2,26},{10... | collective-permute-start | bytes 786440 | tf_op jit(solution)/shard_map/ppermute | solution.py:26
  127.5 5.0 %collective-permute-start.23 = (bf16[2560,512]{1,0:T(8,128)(2,1)S(1)}, bf16[2560,512]{1,0:T(8,128)(2,1)S(1)}, u32[]{:S(2)}, u32[]{:S(2)}) collective-permute-start(bf16[2560,512]{1,0:T(8,128)(2,1)S(1)} %get-tuple-element.167.refs_0_), channel_id=1, source_target_pairs={{0,1},{1,0},{2,3},{3,2},{4,5},{5,4},{6,7},{7,6},{8,9},{9,8},{10,11... | collective-permute-start | bytes 7864328 | tf_op jit(solution)/shard_map/ppermute | solution.py:26
  127.6 11.8 %collective-permute-start.28 = (bf16[2,128,512]{2,1,0:T(8,128)(2,1)S(1)}, bf16[2,128,512]{2,1,0:T(8,128)(2,1)S(1)}, u32[]{:S(2)}, u32[]{:S(2)}) collective-permute-start(bf16[2,128,512]{2,1,0:T(8,128)(2,1)S(1)} %get-tuple-element.180), channel_id=1, source_target_pairs={{0,8},{8,0},{16,24},{24,16},{1,9},{9,1},{17,25},{25,17},{2,10},{10... | collective-permute-start | bytes 786440 | tf_op jit(solution)/shard_map/ppermute | solution.py:26
  129.0 10.9 %collective-permute-start.29 = (bf16[2,128,512]{2,1,0:T(8,128)(2,1)S(1)}, bf16[2,128,512]{2,1,0:T(8,128)(2,1)S(1)}, u32[]{:S(2)}, u32[]{:S(2)}) collective-permute-start(bf16[2,128,512]{2,1,0:T(8,128)(2,1)S(1)} %get-tuple-element.181), channel_id=1, source_target_pairs={{0,16},{8,24},{16,0},{24,8},{1,17},{9,25},{17,1},{25,9},{2,18},{10... | collective-permute-start | bytes 786440 | tf_op jit(solution)/shard_map/ppermute | solution.py:26
  130.6 5.3 %collective-permute-start.24 = (bf16[1,128,512]{2,1,0:T(8,128)(2,1)S(1)}, bf16[1,128,512]{2,1,0:T(8,128)(2,1)S(1)}, u32[]{:S(2)}, u32[]{:S(2)}) collective-permute-start(bf16[1,128,512]{2,1,0:T(8,128)(2,1)S(1)} %get-tuple-element.175), channel_id=1, source_target_pairs={{0,2},{1,3},{2,0},{3,1},{4,6},{5,7},{6,4},{7,5},{8,10},{9,11},{10,... | collective-permute-start | bytes 393224 | tf_op jit(solution)/shard_map/ppermute | solution.py:36
  130.6 19.8 %collective-permute-start.30 = (bf16[2,128,512]{2,1,0:T(8,128)(2,1)S(1)}, bf16[2,128,512]{2,1,0:T(8,128)(2,1)S(1)}, u32[]{:S(2)}, u32[]{:S(2)}) collective-permute-start(bf16[2,128,512]{2,1,0:T(8,128)(2,1)S(1)} %get-tuple-element.182), channel_id=1, source_target_pairs={{0,24},{8,16},{16,8},{24,0},{1,25},{9,17},{17,9},{25,1},{2,26},{10... | collective-permute-start | bytes 786440 | tf_op jit(solution)/shard_map/ppermute | solution.py:26
  132.5 17.9 %collective-permute-start.25 = (bf16[1,128,512]{2,1,0:T(8,128)(2,1)S(1)}, bf16[1,128,512]{2,1,0:T(8,128)(2,1)S(1)}, u32[]{:S(2)}, u32[]{:S(2)}) collective-permute-start(bf16[1,128,512]{2,1,0:T(8,128)(2,1)S(1)} %get-tuple-element.176), channel_id=1, source_target_pairs={{0,10},{1,11},{2,8},{3,9},{4,14},{5,15},{6,12},{7,13},{8,2},{9,3},... | collective-permute-start | bytes 393224 | tf_op jit(solution)/shard_map/ppermute | solution.py:36
  135.8 14.6 %collective-permute-start.26 = (bf16[1,128,512]{2,1,0:T(8,128)(2,1)S(1)}, bf16[1,128,512]{2,1,0:T(8,128)(2,1)S(1)}, u32[]{:S(2)}, u32[]{:S(2)}) collective-permute-start(bf16[1,128,512]{2,1,0:T(8,128)(2,1)S(1)} %get-tuple-element.177), channel_id=1, source_target_pairs={{0,18},{1,19},{2,16},{3,17},{4,22},{5,23},{6,20},{7,21},{8,26},{9,... | collective-permute-start | bytes 393224 | tf_op jit(solution)/shard_map/ppermute | solution.py:36
  139.4 11.0 %collective-permute-start.27 = (bf16[1,128,512]{2,1,0:T(8,128)(2,1)S(1)}, bf16[1,128,512]{2,1,0:T(8,128)(2,1)S(1)}, u32[]{:S(2)}, u32[]{:S(2)}) collective-permute-start(bf16[1,128,512]{2,1,0:T(8,128)(2,1)S(1)} %get-tuple-element.178), channel_id=1, source_target_pairs={{0,26},{1,27},{2,24},{3,25},{4,30},{5,31},{6,28},{7,29},{8,18},{9,... | collective-permute-start | bytes 393224 | tf_op jit(solution)/shard_map/ppermute | solution.py:36
  139.9 10.6 %collective-permute-start.31 = (bf16[128,512]{1,0:T(8,128)(2,1)S(1)}, bf16[128,512]{1,0:T(8,128)(2,1)S(1)}, u32[]{:S(2)}, u32[]{:S(2)}) collective-permute-start(bf16[128,512]{1,0:T(8,128)(2,1)S(1)} %get-tuple-element.185), channel_id=1, source_target_pairs={{0,4},{1,5},{2,6},{3,7},{4,0},{5,1},{6,2},{7,3},{8,12},{9,13},{10,... | collective-permute-start | bytes 393224 | tf_op jit(solution)/shard_map/ppermute | solution.py:26

commit v6 on v5

--- a/solution.py
+++ b/solution.py
@@ -370,8 +370,8 @@
         return value
 
     def body(*refs):
-        one, two = refs[:m], refs[m : m + n]
-        self_1_ref, self_2_ref, cross_2_ref, self_ref, cross_ref = refs[m + n :]
+        cross_2_ref, one, two = refs[0], refs[1 : 1 + m], refs[1 + m : 1 + m + n]
+        self_1_ref, self_2_ref, self_ref, cross_ref = refs[1 + m + n :]
         self_ref[0] = added(two, 0)
         self_ref[1] = self_1_ref[...]
         self_ref[2] = self_2_ref[...]
@@ -383,7 +383,7 @@
     return chain(
         body,
         "last_sums",
-        [*cross_1, *terms, self_1, self_2, cross_2],
+        [cross_2, *cross_1, *terms, self_1, self_2],
         [WHOLE] * (m + n + 3),
         [levels, levels],
         [WHOLE, WHOLE],

time: 153 us -> 152 us (level)
  waiting for transfers between devices: 59.5 us -> 57.9 us
    ppermute x4, starting transfers between devices: 2.44 us -> 6.37 us  [swap_both(): return lax.ppermute(array, ('wide', 'narrow'), pairs)]
    ppermute x28, starting transfers between devices: 41.8 us -> 39.1 us  [swap(): lax.ppermute(array, axis, [(i, i ^ mask) for i in range(lax.axis_size(axi...]
  transfers between devices with their start and end apart: 32 -> 32, of which waited for: 17 -> 16; matrix products, arithmetic and copies ran while one was open for 0% -> 0% of each run, Pallas kernels for 30% -> 30%
where the time goes in v6:
time: 152 us; the launch traced here: 151 us
  waiting for transfers between devices  57.9 us (38%)
  Pallas kernels  47.1 us (31%)
  starting transfers between devices  45.5 us (30%)
    ppermute x28, waiting for transfers between devices, swap(): lax.ppermute(array, axis, [(i, i ^ mask) for i in range(lax.axis_size(axi...  57.5 us
    pallas_call x35, Pallas kernels, __call__(): pl.pallas_call(whole, grid=(grid,), out_shape=[*out_shape, TOKEN], in_spe...  47.1 us
    ppermute x28, starting transfers between devices, swap(): lax.ppermute(array, axis, [(i, i ^ mask) for i in range(lax.axis_size(axi...  39.1 us
    ppermute x4, starting transfers between devices, swap_both(): return lax.ppermute(array, ('wide', 'narrow'), pairs)  6.37 us
  transfers between devices with their start and end apart: 32, of which 16 were waited for; matrix products, arithmetic and copies ran while one was open for 0% of the time, Pallas kernels for 30%

profile of v6, /device:TPU:0, one launch (start us, length us, event | category | flops | bytes accessed | tf_op | source)
XLA Modules:
  0.0 151.5 jit_solution(16065914694084647994)
XLA Ops:
  1.1 1.2 first_rows.1
  2.4 3.7 %collective-permute-start.1 = (bf16[320,512]{1,0:T(8,128)(2,1)S(1)}, bf16[320,512]{1,0:T(8,128)(2,1)S(1)}, u32[]{:S(2)}, u32[]{:S(2)}) collective-permute-start(bf16[320,512]{1,0:T(8,128)(2,1)S(1)} %get-tuple-element.97), channel_id=1, source_target_pairs={{0,4},{1,5},{2,6},{3,7},{4,0},{5,1},{6,2},{7,3},{8,12},{9,13},{10,... | collective-permute-start | bytes 983048 | tf_op jit(solution)/shard_map/ppermute | solution.py:26
  6.1 4.5 %self_sums_2.1 = (f32[1,128,512]{2,1,0:T(8,128)S(1)}, bf16[1,128,512]{2,1,0:T(8,128)(2,1)S(1)}, bf16[1,128,512]{2,1,0:T(8,128)(2,1)S(1)}, bf16[1,128,512]{2,1,0:T(8,128)(2,1)S(1)}, f32[8,128]{1,0:T(8,128)S(1)}) custom-call(bf16[3,2048,512]{2,1,0:T(8,128)(2,1)} %refs_1_.25, bf16[2048,512]{1,0:T(8,128)(2,1)} %refs_0_.43, f32[8,128]{1,0:T(8,128)S(1)} %get-tuple-element.98.refs_2_), custom_call_target="tpu_custom_call" | custom-call | tf_op jit(solution)/shard_map/self_sums_2/pallas_call | solution.py:64
  10.6 1.6 %collective-permute-start.3 = (bf16[1,128,512]{2,1,0:T(8,128)(2,1)S(1)}, bf16[1,128,512]{2,1,0:T(8,128)(2,1)S(1)}, u32[]{:S(2)}, u32[]{:S(2)}) collective-permute-start(bf16[1,128,512]{2,1,0:T(8,128)(2,1)S(1)} %get-tuple-element.100), channel_id=1, source_target_pairs={{0,8},{8,0},{16,24},{24,16},{1,9},{9,1},{17,25},{25,17},{2,10},{10... | collective-permute-start | bytes 393224 | tf_op jit(solution)/shard_map/ppermute | solution.py:26
  12.2 1.5 %collective-permute-start.4 = (bf16[1,128,512]{2,1,0:T(8,128)(2,1)S(1)}, bf16[1,128,512]{2,1,0:T(8,128)(2,1)S(1)}, u32[]{:S(2)}, u32[]{:S(2)}) collective-permute-start(bf16[1,128,512]{2,1,0:T(8,128)(2,1)S(1)} %get-tuple-element.101), channel_id=1, source_target_pairs={{0,16},{8,24},{16,0},{24,8},{1,17},{9,25},{17,1},{25,9},{2,18},{10... | collective-permute-start | bytes 393224 | tf_op jit(solution)/shard_map/ppermute | solution.py:26
  14.2 2.5 %collective-permute-done.3.refs_1_ = bf16[1,128,512]{2,1,0:T(8,128)(2,1)S(1)} collective-permute-done((bf16[1,128,512]{2,1,0:T(8,128)(2,1)S(1)}, bf16[1,128,512]{2,1,0:T(8,128)(2,1)S(1)}, u32[]{:S(2)}, u32[]{:S(2)}) %collective-permute-start.3) | collective-permute-done | bytes 131104 | tf_op jit(solution)/shard_map/ppermute | solution.py:26
  16.6 1.6 %collective-permute-start = (bf16[512,512]{1,0:T(8,128)(2,1)S(1)}, bf16[512,512]{1,0:T(8,128)(2,1)S(1)}, u32[]{:S(2)}, u32[]{:S(2)}) collective-permute-start(bf16[512,512]{1,0:T(8,128)(2,1)S(1)} %get-tuple-element.96), channel_id=1, source_target_pairs={{0,2},{1,3},{2,0},{3,1},{4,6},{5,7},{6,4},{7,5},{8,10},{9,11},{10,... | collective-permute-start | bytes 1572872 | tf_op jit(solution)/shard_map/ppermute | solution.py:26
  18.2 2.1 %collective-permute-done.4.refs_2_ = bf16[1,128,512]{2,1,0:T(8,128)(2,1)S(1)} collective-permute-done((bf16[1,128,512]{2,1,0:T(8,128)(2,1)S(1)}, bf16[1,128,512]{2,1,0:T(8,128)(2,1)S(1)}, u32[]{:S(2)}, u32[]{:S(2)}) %collective-permute-start.4) | collective-permute-done | bytes 131104 | tf_op jit(solution)/shard_map/ppermute | solution.py:26
  21.6 1.6 %parted.1 = (bf16[128,512]{1,0:T(8,128)(2,1)S(1)}, bf16[192,512]{1,0:T(8,128)(2,1)S(1)}, bf16[192,512]{1,0:T(8,128)(2,1)S(1)}, bf16[384,512]{1,0:T(8,128)(2,1)S(1)}, f32[8,128]{1,0:T(8,128)S(1)}) custom-call(bf16[320,512]{1,0:T(8,128)(2,1)S(1)} %collective-permute-done.1.refs_0_.refs_1_, bf16[320,512]{1,0:T(8,128)(2,1)S(1)} %collective-permute-done.1.refs_0_.refs_1_, ...), custom_call_target="tpu_custom_call" | custom-call | tf_op jit(solution)/shard_map/parted/pallas_call | solution.py:64
  23.2 1.6 %collective-permute-start.6 = (bf16[128,512]{1,0:T(8,128)(2,1)S(1)}, bf16[128,512]{1,0:T(8,128)(2,1)S(1)}, u32[]{:S(2)}, u32[]{:S(2)}) collective-permute-start(bf16[128,512]{1,0:T(8,128)(2,1)S(1)} %get-tuple-element.105.refs_0_), channel_id=1, source_target_pairs={{0,8},{8,0},{16,24},{24,16},{1,9},{9,1},{17,25},{25,17},{2,10},{10... | collective-permute-start | bytes 393224 | tf_op jit(solution)/shard_map/ppermute | solution.py:26
  24.8 1.5 %collective-permute-start.7 = (bf16[128,512]{1,0:T(8,128)(2,1)S(1)}, bf16[128,512]{1,0:T(8,128)(2,1)S(1)}, u32[]{:S(2)}, u32[]{:S(2)}) collective-permute-start(bf16[128,512]{1,0:T(8,128)(2,1)S(1)} %get-tuple-element.105.refs_0_), channel_id=1, source_target_pairs={{0,16},{8,24},{16,0},{24,8},{1,17},{9,25},{17,1},{25,9},{2,18},{10... | collective-permute-start | bytes 393224 | tf_op jit(solution)/shard_map/ppermute | solution.py:26
  26.8 2.3 %collective-permute-done.6.refs_1_ = bf16[128,512]{1,0:T(8,128)(2,1)S(1)} collective-permute-done((bf16[128,512]{1,0:T(8,128)(2,1)S(1)}, bf16[128,512]{1,0:T(8,128)(2,1)S(1)}, u32[]{:S(2)}, u32[]{:S(2)}) %collective-permute-start.6) | collective-permute-done | bytes 131104 | tf_op jit(solution)/shard_map/ppermute | solution.py:26
  29.1 3.5 %collective-permute-done.7.refs_2_ = bf16[128,512]{1,0:T(8,128)(2,1)S(1)} collective-permute-done((bf16[128,512]{1,0:T(8,128)(2,1)S(1)}, bf16[128,512]{1,0:T(8,128)(2,1)S(1)}, u32[]{:S(2)}, u32[]{:S(2)}) %collective-permute-start.7) | collective-permute-done | bytes 131104 | tf_op jit(solution)/shard_map/ppermute | solution.py:26
  33.2 4.0 %collective-permute-start.11 = (bf16[192,512]{1,0:T(8,128)(2,1)S(1)}, bf16[192,512]{1,0:T(8,128)(2,1)S(1)}, u32[]{:S(2)}, u32[]{:S(2)}) collective-permute-start(bf16[192,512]{1,0:T(8,128)(2,1)S(1)} %get-tuple-element.114.refs_6_.refs_4_), channel_id=1, source_target_pairs={{0,2},{1,3},{2,0},{3,1},{4,6},{5,7},{6,4},{7,5},{8,10},{9,11},{10,... | collective-permute-start | bytes 589832 | tf_op jit(solution)/shard_map/ppermute | solution.py:26
  38.5 6.3 %collective-permute-done.11.refs_7_.refs_3_ = bf16[192,512]{1,0:T(8,128)(2,1)S(1)} collective-permute-done((bf16[192,512]{1,0:T(8,128)(2,1)S(1)}, bf16[192,512]{1,0:T(8,128)(2,1)S(1)}, u32[]{:S(2)}, u32[]{:S(2)}) %collective-permute-start.11) | collective-permute-done | bytes 196640 | tf_op jit(solution)/shard_map/ppermute | solution.py:26
  44.9 8.1 %collective-permute-done.10.refs_3_ = bf16[384,512]{1,0:T(8,128)(2,1)S(1)} collective-permute-done((bf16[384,512]{1,0:T(8,128)(2,1)S(1)}, bf16[384,512]{1,0:T(8,128)(2,1)S(1)}, u32[]{:S(2)}, u32[]{:S(2)}) %collective-permute-start.10) | collective-permute-done | bytes 393248 | tf_op jit(solution)/shard_map/ppermute | solution.py:26
  55.8 3.5 %collective-permute-start.14 = (bf16[448,512]{1,0:T(8,128)(2,1)S(1)}, bf16[448,512]{1,0:T(8,128)(2,1)S(1)}, u32[]{:S(2)}, u32[]{:S(2)}) collective-permute-start(bf16[448,512]{1,0:T(8,128)(2,1)S(1)} %get-tuple-element.125.refs_2_), channel_id=1, source_target_pairs={{0,4},{1,5},{2,6},{3,7},{4,0},{5,1},{6,2},{7,3},{8,12},{9,13},{10,... | collective-permute-start | bytes 1376264 | tf_op jit(solution)/shard_map/ppermute | solution.py:26
  59.3 1.7 %sums_b_0.1 = (f32[3,512,512]{2,1,0:T(8,128)S(1)}, f32[8,128]{1,0:T(8,128)S(1)}) custom-call(bf16[3,2048,512]{2,1,0:T(8,128)(2,1)} %refs_1_.25, bf16[3,2048,512]{2,1,0:T(8,128)(2,1)} %refs_1_.25, bf16[3,2048,512]{2,1,0:T(8,128)(2,1)S(1)} %collective-permute-done.2.refs_4_.refs_2_, bf16[192,512]{1,0:T(8,128)(2,1)S(1)} %collective-permute-done.11.refs_7_.refs_3_, ...), custom_call_target="tpu_custom_call" | custom-call | tf_op jit(solution)/shard_map/sums_b_0/pallas_call | solution.py:64
  60.9 2.3 %sums_a_0.1 = (f32[2,512,512]{2,1,0:T(8,128)S(1)}, f32[8,128]{1,0:T(8,128)S(1)}) custom-call(bf16[3,2048,512]{2,1,0:T(8,128)(2,1)} %refs_1_.25, bf16[3,2048,512]{2,1,0:T(8,128)(2,1)} %refs_1_.25, bf16[192,512]{1,0:T(8,128)(2,1)S(1)} %get-tuple-element.109.refs_3_.refs_2_, bf16[384,512]{1,0:T(8,128)(2,1)S(1)} %collective-permute-done.10.refs_3_, ...), custom_call_target="tpu_custom_call" | custom-call | tf_op jit(solution)/shard_map/sums_a_0/pallas_call | solution.py:64
  63.9 10.9 %collective-permute-done.13.refs_3_ = bf16[384,512]{1,0:T(8,128)(2,1)S(1)} collective-permute-done((bf16[384,512]{1,0:T(8,128)(2,1)S(1)}, bf16[384,512]{1,0:T(8,128)(2,1)S(1)}, u32[]{:S(2)}, u32[]{:S(2)}) %collective-permute-start.13) | collective-permute-done | bytes 393248 | tf_op jit(solution)/shard_map/ppermute | solution.py:26
  74.8 1.5 next_grads_1_1.1
  77.4 2.2 %sums_b_1.1 = (f32[3,512,512]{2,1,0:T(8,128)S(1)}, f32[8,128]{1,0:T(8,128)S(1)}) custom-call(bf16[3,2048,512]{2,1,0:T(8,128)(2,1)} %refs_1_.25, bf16[3,2048,512]{2,1,0:T(8,128)(2,1)} %refs_1_.25, bf16[3,2048,512]{2,1,0:T(8,128)(2,1)S(1)} %collective-permute-done.2.refs_4_.refs_2_, bf16[384,512]{1,0:T(8,128)(2,1)S(1)} %collective-permute-done.13.refs_3_, ...), custom_call_target="tpu_custom_call" | custom-call | tf_op jit(solution)/shard_map/sums_b_1/pallas_call | solution.py:64
  79.5 1.9 %sums_a_2.1 = (f32[2,512,512]{2,1,0:T(8,128)S(1)}, f32[8,128]{1,0:T(8,128)S(1)}) custom-call(bf16[3,2048,512]{2,1,0:T(8,128)(2,1)} %refs_1_.25, bf16[3,2048,512]{2,1,0:T(8,128)(2,1)} %refs_1_.25, bf16[384,512]{1,0:T(8,128)(2,1)S(1)} %collective-permute-done.9.refs_3_.refs_2_, bf16[384,512]{1,0:T(8,128)(2,1)S(1)} %get-tuple-element.122.refs_3_.refs_2_, ...), custom_call_target="tpu_custom_call" | custom-call | tf_op jit(solution)/shard_map/sums_a_2/pallas_call | solution.py:64
  82.1 2.5 %collective-permute-start.22 = (bf16[448,512]{1,0:T(8,128)(2,1)S(1)}, bf16[448,512]{1,0:T(8,128)(2,1)S(1)}, u32[]{:S(2)}, u32[]{:S(2)}) collective-permute-start(bf16[448,512]{1,0:T(8,128)(2,1)S(1)} %get-tuple-element.136.refs_3_.refs_2_), channel_id=1, source_target_pairs={{0,2},{1,3},{2,0},{3,1},{4,6},{5,7},{6,4},{7,5},{8,10},{9,11},{10,... | collective-permute-start | bytes 1376264 | tf_op jit(solution)/shard_map/ppermute | solution.py:26
  84.6 6.0 %collective-permute-done.12.refs_3_ = bf16[384,512]{1,0:T(8,128)(2,1)S(1)} collective-permute-done((bf16[384,512]{1,0:T(8,128)(2,1)S(1)}, bf16[384,512]{1,0:T(8,128)(2,1)S(1)}, u32[]{:S(2)}, u32[]{:S(2)}) %collective-permute-start.12) | collective-permute-done | bytes 393248 | tf_op jit(solution)/shard_map/ppermute | solution.py:26
  92.4 1.3 collective-permute-start.15
  93.7 2.2 %sums_b_2.1 = (f32[3,512,512]{2,1,0:T(8,128)S(1)}, f32[8,128]{1,0:T(8,128)S(1)}) custom-call(bf16[3,2048,512]{2,1,0:T(8,128)(2,1)} %refs_1_.25, bf16[3,2048,512]{2,1,0:T(8,128)(2,1)} %refs_1_.25, bf16[3,2048,512]{2,1,0:T(8,128)(2,1)S(1)} %collective-permute-done.2.refs_4_.refs_2_, bf16[384,512]{1,0:T(8,128)(2,1)S(1)} %collective-permute-done.12.refs_3_, ...), custom_call_target="tpu_custom_call" | custom-call | tf_op jit(solution)/shard_map/sums_b_2/pallas_call | solution.py:64
  95.9 1.9 %sums_a_3.1 = (f32[2,512,512]{2,1,0:T(8,128)S(1)}, f32[8,128]{1,0:T(8,128)S(1)}) custom-call(bf16[3,2048,512]{2,1,0:T(8,128)(2,1)} %refs_1_.25, bf16[3,2048,512]{2,1,0:T(8,128)(2,1)} %refs_1_.25, bf16[448,512]{1,0:T(8,128)(2,1)S(1)} %collective-permute-done.14.refs_3_.refs_2_, bf16[448,512]{1,0:T(8,128)(2,1)S(1)} %get-tuple-element.136.refs_3_.refs_2_, ...), custom_call_target="tpu_custom_call" | custom-call | tf_op jit(solution)/shard_map/sums_a_3/pallas_call | solution.py:64
  100.1 1.9 %sums_a_4.1 = (f32[2,512,512]{2,1,0:T(8,128)S(1)}, f32[8,128]{1,0:T(8,128)S(1)}) custom-call(bf16[3,2048,512]{2,1,0:T(8,128)(2,1)} %refs_1_.25, bf16[3,2048,512]{2,1,0:T(8,128)(2,1)} %refs_1_.25, bf16[384,512]{1,0:T(8,128)(2,1)S(1)} %collective-permute-done.16.refs_3_.refs_2_, bf16[384,512]{1,0:T(8,128)(2,1)S(1)} %get-tuple-element.143.refs_3_.refs_2_, ...), custom_call_target="tpu_custom_call" | custom-call | tf_op jit(solution)/shard_map/sums_a_4/pallas_call | solution.py:64
  101.9 5.6 %collective-permute-done.15.refs_3_.refs_2_ = bf16[256,512]{1,0:T(8,128)(2,1)S(1)} collective-permute-done((bf16[256,512]{1,0:T(8,128)(2,1)S(1)}, bf16[256,512]{1,0:T(8,128)(2,1)S(1)}, u32[]{:S(2)}, u32[]{:S(2)}) %collective-permute-start.15) | collective-permute-done | bytes 262176 | tf_op jit(solution)/shard_map/ppermute | solution.py:26
  108.0 3.0 %collective-permute-start.20 = (bf16[256,512]{1,0:T(8,128)(2,1)S(1)}, bf16[256,512]{1,0:T(8,128)(2,1)S(1)}, u32[]{:S(2)}, u32[]{:S(2)}) collective-permute-start(bf16[256,512]{1,0:T(8,128)(2,1)S(1)} %get-tuple-element.147.refs_3_.refs_2_), channel_id=1, source_target_pairs={{0,2},{1,3},{2,0},{3,1},{4,6},{5,7},{6,4},{7,5},{8,10},{9,11},{10,... | collective-permute-start | bytes 786440 | tf_op jit(solution)/shard_map/ppermute | solution.py:26
  111.0 1.6 %sums_a_5.1 = (f32[2,128,512]{2,1,0:T(8,128)S(1)}, bf16[2,128,512]{2,1,0:T(8,128)(2,1)S(1)}, bf16[2,128,512]{2,1,0:T(8,128)(2,1)S(1)}, bf16[2,128,512]{2,1,0:T(8,128)(2,1)S(1)}, f32[8,128]{1,0:T(8,128)S(1)}) custom-call(bf16[3,2048,512]{2,1,0:T(8,128)(2,1)} %refs_1_.25, bf16[3,2048,512]{2,1,0:T(8,128)(2,1)} %refs_1_.25, ...), custom_call_target="tpu_custom_call" | custom-call | tf_op jit(solution)/shard_map/sums_a_5/pallas_call | solution.py:64
  112.7 1.3 collective-permute-start.17
  114.0 1.5 collective-permute-start.18
  117.2 2.2 %sums_b_3.1 = (f32[3,512,512]{2,1,0:T(8,128)S(1)}, f32[8,128]{1,0:T(8,128)S(1)}) custom-call(bf16[3,2048,512]{2,1,0:T(8,128)(2,1)} %refs_1_.25, bf16[3,2048,512]{2,1,0:T(8,128)(2,1)} %refs_1_.25, bf16[3,2048,512]{2,1,0:T(8,128)(2,1)S(1)} %collective-permute-done.2.refs_4_.refs_2_, bf16[448,512]{1,0:T(8,128)(2,1)S(1)} %collective-permute-done.22.refs_3_, ...), custom_call_target="tpu_custom_call" | custom-call | tf_op jit(solution)/shard_map/sums_b_3/pallas_call | solution.py:64
  120.2 2.2 %sums_b_4.1 = (f32[3,512,512]{2,1,0:T(8,128)S(1)}, f32[8,128]{1,0:T(8,128)S(1)}) custom-call(bf16[3,2048,512]{2,1,0:T(8,128)(2,1)} %refs_1_.25, bf16[3,2048,512]{2,1,0:T(8,128)(2,1)} %refs_1_.25, bf16[3,2048,512]{2,1,0:T(8,128)(2,1)S(1)} %collective-permute-done.2.refs_4_.refs_2_, bf16[384,512]{1,0:T(8,128)(2,1)S(1)} %collective-permute-done.21.refs_3_, ...), custom_call_target="tpu_custom_call" | custom-call | tf_op jit(solution)/shard_map/sums_b_4/pallas_call | solution.py:64
  122.4 2.5 %collective-permute-done.20.refs_3_ = bf16[256,512]{1,0:T(8,128)(2,1)S(1)} collective-permute-done((bf16[256,512]{1,0:T(8,128)(2,1)S(1)}, bf16[256,512]{1,0:T(8,128)(2,1)S(1)}, u32[]{:S(2)}, u32[]{:S(2)}) %collective-permute-start.20) | collective-permute-done | bytes 262176 | tf_op jit(solution)/shard_map/ppermute | solution.py:26
  125.5 1.9 %sums_b_5.1 = (bf16[1,128,512]{2,1,0:T(8,128)(2,1)S(1)}, bf16[1,128,512]{2,1,0:T(8,128)(2,1)S(1)}, bf16[1,128,512]{2,1,0:T(8,128)(2,1)S(1)}, bf16[1,128,512]{2,1...) custom-call(bf16[3,2048,512]{2,1,0:T(8,128)(2,1)} %refs_1_.25, ...), custom_call_target="tpu_custom_call" | custom-call | tf_op jit(solution)/shard_map/sums_b_5/pallas_call | solution.py:64
  127.6 1.4 collective-permute-start.29
  129.0 1.5 %collective-permute-start.30 = (bf16[2,128,512]{2,1,0:T(8,128)(2,1)S(1)}, bf16[2,128,512]{2,1,0:T(8,128)(2,1)S(1)}, u32[]{:S(2)}, u32[]{:S(2)}) collective-permute-start(bf16[2,128,512]{2,1,0:T(8,128)(2,1)S(1)} %get-tuple-element.182), channel_id=1, source_target_pairs={{0,16},{8,24},{16,0},{24,8},{1,17},{9,25},{17,1},{25,9},{2,18},{10... | collective-permute-start | bytes 786440 | tf_op jit(solution)/shard_map/ppermute | solution.py:26
  131.2 1.3 collective-permute-done.23.refs_4_.refs_1_.refs_3_
  132.5 2.9 %collective-permute-start.24 = (bf16[128,512]{1,0:T(8,128)(2,1)S(1)}, bf16[128,512]{1,0:T(8,128)(2,1)S(1)}, u32[]{:S(2)}, u32[]{:S(2)}) collective-permute-start(bf16[128,512]{1,0:T(8,128)(2,1)S(1)} %get-tuple-element.175), channel_id=1, source_target_pairs={{0,4},{1,5},{2,6},{3,7},{4,0},{5,1},{6,2},{7,3},{8,12},{9,13},{10,... | collective-permute-start | bytes 393224 | tf_op jit(solution)/shard_map/ppermute | solution.py:26
  135.8 1.8 %collective-permute-start.26 = (bf16[1,128,512]{2,1,0:T(8,128)(2,1)S(1)}, bf16[1,128,512]{2,1,0:T(8,128)(2,1)S(1)}, u32[]{:S(2)}, u32[]{:S(2)}) collective-permute-start(bf16[1,128,512]{2,1,0:T(8,128)(2,1)S(1)} %get-tuple-element.177), channel_id=1, source_target_pairs={{0,10},{1,11},{2,8},{3,9},{4,14},{5,15},{6,12},{7,13},{8,2},{9,3},... | collective-permute-start | bytes 393224 | tf_op jit(solution)/shard_map/ppermute | solution.py:36
  137.7 1.6 %collective-permute-start.27 = (bf16[1,128,512]{2,1,0:T(8,128)(2,1)S(1)}, bf16[1,128,512]{2,1,0:T(8,128)(2,1)S(1)}, u32[]{:S(2)}, u32[]{:S(2)}) collective-permute-start(bf16[1,128,512]{2,1,0:T(8,128)(2,1)S(1)} %get-tuple-element.178), channel_id=1, source_target_pairs={{0,18},{1,19},{2,16},{3,17},{4,22},{5,23},{6,20},{7,21},{8,26},{9,... | collective-permute-start | bytes 393224 | tf_op jit(solution)/shard_map/ppermute | solution.py:36
  139.6 2.9 %collective-permute-start.28 = (bf16[1,128,512]{2,1,0:T(8,128)(2,1)S(1)}, bf16[1,128,512]{2,1,0:T(8,128)(2,1)S(1)}, u32[]{:S(2)}, u32[]{:S(2)}) collective-permute-start(bf16[1,128,512]{2,1,0:T(8,128)(2,1)S(1)} %get-tuple-element.179), channel_id=1, source_target_pairs={{0,26},{1,27},{2,24},{3,25},{4,30},{5,31},{6,28},{7,29},{8,18},{9,... | collective-permute-start | bytes 393224 | tf_op jit(solution)/shard_map/ppermute | solution.py:36
  142.5 3.8 %last_grad.1 = (bf16[2048,512]{1,0:T(8,128)(2,1)}, f32[8,128]{1,0:T(8,128)S(1)}) custom-call(bf16[2560,512]{1,0:T(8,128)(2,1)S(1)} %get-tuple-element.167.refs_0_, bf16[2560,512]{1,0:T(8,128)(2,1)S(1)} %collective-permute-done.23.refs_4_.refs_1_.refs_3_, bf16[3,512,512]{2,1,0:T(8,128)(2,1)S(1)} %copy-done, ...), custom_call_target="tpu_custom_call" | custom-call | tf_op jit(solution)/shard_map/last_grad/pallas_call | solution.py:64
  146.4 3.8 %collective-permute-done.31.refs_8_ = bf16[2,128,512]{2,1,0:T(8,128)(2,1)S(1)} collective-permute-done((bf16[2,128,512]{2,1,0:T(8,128)(2,1)S(1)}, bf16[2,128,512]{2,1,0:T(8,128)(2,1)S(1)}, u32[]{:S(2)}, u32[]{:S(2)}) %collective-permute-start.31) | collective-permute-done | bytes 262176 | tf_op jit(solution)/shard_map/ppermute | solution.py:26
  150.2 1.3 last_sums.1
  (53 shorter events, 18.9 us)
Async XLA Ops:
  0.6 20.9 %collective-permute-start.2 = (bf16[3,2048,512]{2,1,0:T(8,128)(2,1)}, bf16[3,2048,512]{2,1,0:T(8,128)(2,1)S(1)}, u32[]{:S(2)}, u32[]{:S(2)}) collective-permute-start(bf16[3,2048,512]{2,1,0:T(8,128)(2,1)} %refs_1_.25), channel_id=1, source_target_pairs={{0,1},{1,0},{2,3},{3,2},{4,5},{5,4},{6,7},{7,6},{8,9},{9,8},{10,11... | collective-permute-start | bytes 18874376 | tf_op jit(solution)/shard_map/ppermute | solution.py:26
  2.4 19.2 %collective-permute-start.1 = (bf16[320,512]{1,0:T(8,128)(2,1)S(1)}, bf16[320,512]{1,0:T(8,128)(2,1)S(1)}, u32[]{:S(2)}, u32[]{:S(2)}) collective-permute-start(bf16[320,512]{1,0:T(8,128)(2,1)S(1)} %get-tuple-element.97), channel_id=1, source_target_pairs={{0,4},{1,5},{2,6},{3,7},{4,0},{5,1},{6,2},{7,3},{8,12},{9,13},{10,... | collective-permute-start | bytes 983048 | tf_op jit(solution)/shard_map/ppermute | solution.py:26
  10.6 6.0 %collective-permute-start.3 = (bf16[1,128,512]{2,1,0:T(8,128)(2,1)S(1)}, bf16[1,128,512]{2,1,0:T(8,128)(2,1)S(1)}, u32[]{:S(2)}, u32[]{:S(2)}) collective-permute-start(bf16[1,128,512]{2,1,0:T(8,128)(2,1)S(1)} %get-tuple-element.100), channel_id=1, source_target_pairs={{0,8},{8,0},{16,24},{24,16},{1,9},{9,1},{17,25},{25,17},{2,10},{10... | collective-permute-start | bytes 393224 | tf_op jit(solution)/shard_map/ppermute | solution.py:26
  12.2 8.1 %collective-permute-start.4 = (bf16[1,128,512]{2,1,0:T(8,128)(2,1)S(1)}, bf16[1,128,512]{2,1,0:T(8,128)(2,1)S(1)}, u32[]{:S(2)}, u32[]{:S(2)}) collective-permute-start(bf16[1,128,512]{2,1,0:T(8,128)(2,1)S(1)} %get-tuple-element.101), channel_id=1, source_target_pairs={{0,16},{8,24},{16,0},{24,8},{1,17},{9,25},{17,1},{25,9},{2,18},{10... | collective-permute-start | bytes 393224 | tf_op jit(solution)/shard_map/ppermute | solution.py:26
  13.7 6.6 %collective-permute-start.5 = (bf16[1,128,512]{2,1,0:T(8,128)(2,1)S(1)}, bf16[1,128,512]{2,1,0:T(8,128)(2,1)S(1)}, u32[]{:S(2)}, u32[]{:S(2)}) collective-permute-start(bf16[1,128,512]{2,1,0:T(8,128)(2,1)S(1)} %get-tuple-element.102), channel_id=1, source_target_pairs={{0,24},{8,16},{16,8},{24,0},{1,25},{9,17},{17,9},{25,1},{2,26},{10... | collective-permute-start | bytes 393224 | tf_op jit(solution)/shard_map/ppermute | solution.py:26
  16.6 21.9 %collective-permute-start = (bf16[512,512]{1,0:T(8,128)(2,1)S(1)}, bf16[512,512]{1,0:T(8,128)(2,1)S(1)}, u32[]{:S(2)}, u32[]{:S(2)}) collective-permute-start(bf16[512,512]{1,0:T(8,128)(2,1)S(1)} %get-tuple-element.96), channel_id=1, source_target_pairs={{0,2},{1,3},{2,0},{3,1},{4,6},{5,7},{6,4},{7,5},{8,10},{9,11},{10,... | collective-permute-start | bytes 1572872 | tf_op jit(solution)/shard_map/ppermute | solution.py:26
  21.6 11.1 %copy-start = (bf16[3,512,512]{2,1,0:T(8,128)(2,1)S(1)}, bf16[3,512,512]{2,1,0:T(8,128)(2,1)}, u32[]{:S(2)}) copy-start(bf16[3,512,512]{2,1,0:T(8,128)(2,1)} %refs_2_.5) | copy-start | bytes 4718596
  23.2 29.9 %collective-permute-start.10 = (bf16[384,512]{1,0:T(8,128)(2,1)S(1)}, bf16[384,512]{1,0:T(8,128)(2,1)S(1)}, u32[]{:S(2)}, u32[]{:S(2)}) collective-permute-start(bf16[384,512]{1,0:T(8,128)(2,1)S(1)} %get-tuple-element.113.refs_2_), channel_id=1, source_target_pairs={{0,4},{1,5},{2,6},{3,7},{4,0},{5,1},{6,2},{7,3},{8,12},{9,13},{10,... | collective-permute-start | bytes 1179656 | tf_op jit(solution)/shard_map/ppermute | solution.py:26
  23.2 5.9 %collective-permute-start.6 = (bf16[128,512]{1,0:T(8,128)(2,1)S(1)}, bf16[128,512]{1,0:T(8,128)(2,1)S(1)}, u32[]{:S(2)}, u32[]{:S(2)}) collective-permute-start(bf16[128,512]{1,0:T(8,128)(2,1)S(1)} %get-tuple-element.105.refs_0_), channel_id=1, source_target_pairs={{0,8},{8,0},{16,24},{24,16},{1,9},{9,1},{17,25},{25,17},{2,10},{10... | collective-permute-start | bytes 393224 | tf_op jit(solution)/shard_map/ppermute | solution.py:26
  24.8 7.8 %collective-permute-start.7 = (bf16[128,512]{1,0:T(8,128)(2,1)S(1)}, bf16[128,512]{1,0:T(8,128)(2,1)S(1)}, u32[]{:S(2)}, u32[]{:S(2)}) collective-permute-start(bf16[128,512]{1,0:T(8,128)(2,1)S(1)} %get-tuple-element.105.refs_0_), channel_id=1, source_target_pairs={{0,16},{8,24},{16,0},{24,8},{1,17},{9,25},{17,1},{25,9},{2,18},{10... | collective-permute-start | bytes 393224 | tf_op jit(solution)/shard_map/ppermute | solution.py:26
  26.4 6.3 %collective-permute-start.8 = (bf16[128,512]{1,0:T(8,128)(2,1)S(1)}, bf16[128,512]{1,0:T(8,128)(2,1)S(1)}, u32[]{:S(2)}, u32[]{:S(2)}) collective-permute-start(bf16[128,512]{1,0:T(8,128)(2,1)S(1)} %get-tuple-element.105.refs_0_), channel_id=1, source_target_pairs={{0,24},{8,16},{16,8},{24,0},{1,25},{9,17},{17,9},{25,1},{2,26},{10... | collective-permute-start | bytes 393224 | tf_op jit(solution)/shard_map/ppermute | solution.py:26
  33.2 11.7 %collective-permute-start.11 = (bf16[192,512]{1,0:T(8,128)(2,1)S(1)}, bf16[192,512]{1,0:T(8,128)(2,1)S(1)}, u32[]{:S(2)}, u32[]{:S(2)}) collective-permute-start(bf16[192,512]{1,0:T(8,128)(2,1)S(1)} %get-tuple-element.114.refs_6_.refs_4_), channel_id=1, source_target_pairs={{0,2},{1,3},{2,0},{3,1},{4,6},{5,7},{6,4},{7,5},{8,10},{9,11},{10,... | collective-permute-start | bytes 589832 | tf_op jit(solution)/shard_map/ppermute | solution.py:26
  38.2 25.0 %collective-permute-start.9 = (bf16[384,512]{1,0:T(8,128)(2,1)S(1)}, bf16[384,512]{1,0:T(8,128)(2,1)S(1)}, u32[]{:S(2)}, u32[]{:S(2)}) collective-permute-start(bf16[384,512]{1,0:T(8,128)(2,1)S(1)} %get-tuple-element.112.refs_2_), channel_id=1, source_target_pairs={{0,4},{1,5},{2,6},{3,7},{4,0},{5,1},{6,2},{7,3},{8,12},{9,13},{10,... | collective-permute-start | bytes 1179656 | tf_op jit(solution)/shard_map/ppermute | solution.py:26
  54.2 20.6 %collective-permute-start.13 = (bf16[384,512]{1,0:T(8,128)(2,1)S(1)}, bf16[384,512]{1,0:T(8,128)(2,1)S(1)}, u32[]{:S(2)}, u32[]{:S(2)}) collective-permute-start(bf16[384,512]{1,0:T(8,128)(2,1)S(1)} %get-tuple-element.116.refs_5_.refs_2_), channel_id=1, source_target_pairs={{0,2},{1,3},{2,0},{3,1},{4,6},{5,7},{6,4},{7,5},{8,10},{9,11},{10,... | collective-permute-start | bytes 1179656 | tf_op jit(solution)/shard_map/ppermute | solution.py:26
  55.8 25.6 %collective-permute-start.14 = (bf16[448,512]{1,0:T(8,128)(2,1)S(1)}, bf16[448,512]{1,0:T(8,128)(2,1)S(1)}, u32[]{:S(2)}, u32[]{:S(2)}) collective-permute-start(bf16[448,512]{1,0:T(8,128)(2,1)S(1)} %get-tuple-element.125.refs_2_), channel_id=1, source_target_pairs={{0,4},{1,5},{2,6},{3,7},{4,0},{5,1},{6,2},{7,3},{8,12},{9,13},{10,... | collective-permute-start | bytes 1376264 | tf_op jit(solution)/shard_map/ppermute | solution.py:26
  63.9 26.8 %collective-permute-start.12 = (bf16[384,512]{1,0:T(8,128)(2,1)S(1)}, bf16[384,512]{1,0:T(8,128)(2,1)S(1)}, u32[]{:S(2)}, u32[]{:S(2)}) collective-permute-start(bf16[384,512]{1,0:T(8,128)(2,1)S(1)} %get-tuple-element.122.refs_3_.refs_2_), channel_id=1, source_target_pairs={{0,2},{1,3},{2,0},{3,1},{4,6},{5,7},{6,4},{7,5},{8,10},{9,11},{10,... | collective-permute-start | bytes 1179656 | tf_op jit(solution)/shard_map/ppermute | solution.py:26
  77.3 21.4 %collective-permute-start.16 = (bf16[384,512]{1,0:T(8,128)(2,1)S(1)}, bf16[384,512]{1,0:T(8,128)(2,1)S(1)}, u32[]{:S(2)}, u32[]{:S(2)}) collective-permute-start(bf16[384,512]{1,0:T(8,128)(2,1)S(1)} %get-tuple-element.135.refs_2_), channel_id=1, source_target_pairs={{0,4},{1,5},{2,6},{3,7},{4,0},{5,1},{6,2},{7,3},{8,12},{9,13},{10,... | collective-permute-start | bytes 1179656 | tf_op jit(solution)/shard_map/ppermute | solution.py:26
  82.1 33.4 %collective-permute-start.22 = (bf16[448,512]{1,0:T(8,128)(2,1)S(1)}, bf16[448,512]{1,0:T(8,128)(2,1)S(1)}, u32[]{:S(2)}, u32[]{:S(2)}) collective-permute-start(bf16[448,512]{1,0:T(8,128)(2,1)S(1)} %get-tuple-element.136.refs_3_.refs_2_), channel_id=1, source_target_pairs={{0,2},{1,3},{2,0},{3,1},{4,6},{5,7},{6,4},{7,5},{8,10},{9,11},{10,... | collective-permute-start | bytes 1376264 | tf_op jit(solution)/shard_map/ppermute | solution.py:26
  92.4 15.1 %collective-permute-start.15 = (bf16[256,512]{1,0:T(8,128)(2,1)S(1)}, bf16[256,512]{1,0:T(8,128)(2,1)S(1)}, u32[]{:S(2)}, u32[]{:S(2)}) collective-permute-start(bf16[256,512]{1,0:T(8,128)(2,1)S(1)} %get-tuple-element.134.refs_2_), channel_id=1, source_target_pairs={{0,4},{1,5},{2,6},{3,7},{4,0},{5,1},{6,2},{7,3},{8,12},{9,13},{10,... | collective-permute-start | bytes 786440 | tf_op jit(solution)/shard_map/ppermute | solution.py:26
  99.3 20.1 %collective-permute-start.21 = (bf16[384,512]{1,0:T(8,128)(2,1)S(1)}, bf16[384,512]{1,0:T(8,128)(2,1)S(1)}, u32[]{:S(2)}, u32[]{:S(2)}) collective-permute-start(bf16[384,512]{1,0:T(8,128)(2,1)S(1)} %get-tuple-element.143.refs_3_.refs_2_), channel_id=1, source_target_pairs={{0,2},{1,3},{2,0},{3,1},{4,6},{5,7},{6,4},{7,5},{8,10},{9,11},{10,... | collective-permute-start | bytes 1179656 | tf_op jit(solution)/shard_map/ppermute | solution.py:26
  108.0 17.0 %collective-permute-start.20 = (bf16[256,512]{1,0:T(8,128)(2,1)S(1)}, bf16[256,512]{1,0:T(8,128)(2,1)S(1)}, u32[]{:S(2)}, u32[]{:S(2)}) collective-permute-start(bf16[256,512]{1,0:T(8,128)(2,1)S(1)} %get-tuple-element.147.refs_3_.refs_2_), channel_id=1, source_target_pairs={{0,2},{1,3},{2,0},{3,1},{4,6},{5,7},{6,4},{7,5},{8,10},{9,11},{10,... | collective-permute-start | bytes 786440 | tf_op jit(solution)/shard_map/ppermute | solution.py:26
  112.7 14.7 %collective-permute-start.17 = (bf16[2,128,512]{2,1,0:T(8,128)(2,1)S(1)}, bf16[2,128,512]{2,1,0:T(8,128)(2,1)S(1)}, u32[]{:S(2)}, u32[]{:S(2)}) collective-permute-start(bf16[2,128,512]{2,1,0:T(8,128)(2,1)S(1)} %get-tuple-element.151), channel_id=1, source_target_pairs={{0,8},{8,0},{16,24},{24,16},{1,9},{9,1},{17,25},{25,17},{2,10},{10... | collective-permute-start | bytes 786440 | tf_op jit(solution)/shard_map/ppermute | solution.py:26
  114.0 13.4 %collective-permute-start.18 = (bf16[2,128,512]{2,1,0:T(8,128)(2,1)S(1)}, bf16[2,128,512]{2,1,0:T(8,128)(2,1)S(1)}, u32[]{:S(2)}, u32[]{:S(2)}) collective-permute-start(bf16[2,128,512]{2,1,0:T(8,128)(2,1)S(1)} %get-tuple-element.152), channel_id=1, source_target_pairs={{0,16},{8,24},{16,0},{24,8},{1,17},{9,25},{17,1},{25,9},{2,18},{10... | collective-permute-start | bytes 786440 | tf_op jit(solution)/shard_map/ppermute | solution.py:26
  115.5 11.9 %collective-permute-start.19 = (bf16[2,128,512]{2,1,0:T(8,128)(2,1)S(1)}, bf16[2,128,512]{2,1,0:T(8,128)(2,1)S(1)}, u32[]{:S(2)}, u32[]{:S(2)}) collective-permute-start(bf16[2,128,512]{2,1,0:T(8,128)(2,1)S(1)} %get-tuple-element.153), channel_id=1, source_target_pairs={{0,24},{8,16},{16,8},{24,0},{1,25},{9,17},{17,9},{25,1},{2,26},{10... | collective-permute-start | bytes 786440 | tf_op jit(solution)/shard_map/ppermute | solution.py:26
  127.5 5.0 %collective-permute-start.23 = (bf16[2560,512]{1,0:T(8,128)(2,1)S(1)}, bf16[2560,512]{1,0:T(8,128)(2,1)S(1)}, u32[]{:S(2)}, u32[]{:S(2)}) collective-permute-start(bf16[2560,512]{1,0:T(8,128)(2,1)S(1)} %get-tuple-element.167.refs_0_), channel_id=1, source_target_pairs={{0,1},{1,0},{2,3},{3,2},{4,5},{5,4},{6,7},{7,6},{8,9},{9,8},{10,11... | collective-permute-start | bytes 7864328 | tf_op jit(solution)/shard_map/ppermute | solution.py:26
  127.6 10.1 %collective-permute-start.29 = (bf16[2,128,512]{2,1,0:T(8,128)(2,1)S(1)}, bf16[2,128,512]{2,1,0:T(8,128)(2,1)S(1)}, u32[]{:S(2)}, u32[]{:S(2)}) collective-permute-start(bf16[2,128,512]{2,1,0:T(8,128)(2,1)S(1)} %get-tuple-element.181), channel_id=1, source_target_pairs={{0,8},{8,0},{16,24},{24,16},{1,9},{9,1},{17,25},{25,17},{2,10},{10... | collective-permute-start | bytes 786440 | tf_op jit(solution)/shard_map/ppermute | solution.py:26
  129.0 10.6 %collective-permute-start.30 = (bf16[2,128,512]{2,1,0:T(8,128)(2,1)S(1)}, bf16[2,128,512]{2,1,0:T(8,128)(2,1)S(1)}, u32[]{:S(2)}, u32[]{:S(2)}) collective-permute-start(bf16[2,128,512]{2,1,0:T(8,128)(2,1)S(1)} %get-tuple-element.182), channel_id=1, source_target_pairs={{0,16},{8,24},{16,0},{24,8},{1,17},{9,25},{17,1},{25,9},{2,18},{10... | collective-permute-start | bytes 786440 | tf_op jit(solution)/shard_map/ppermute | solution.py:26
  130.6 5.3 %collective-permute-start.25 = (bf16[1,128,512]{2,1,0:T(8,128)(2,1)S(1)}, bf16[1,128,512]{2,1,0:T(8,128)(2,1)S(1)}, u32[]{:S(2)}, u32[]{:S(2)}) collective-permute-start(bf16[1,128,512]{2,1,0:T(8,128)(2,1)S(1)} %get-tuple-element.176), channel_id=1, source_target_pairs={{0,2},{1,3},{2,0},{3,1},{4,6},{5,7},{6,4},{7,5},{8,10},{9,11},{10,... | collective-permute-start | bytes 393224 | tf_op jit(solution)/shard_map/ppermute | solution.py:36
  130.6 19.6 %collective-permute-start.31 = (bf16[2,128,512]{2,1,0:T(8,128)(2,1)S(1)}, bf16[2,128,512]{2,1,0:T(8,128)(2,1)S(1)}, u32[]{:S(2)}, u32[]{:S(2)}) collective-permute-start(bf16[2,128,512]{2,1,0:T(8,128)(2,1)S(1)} %get-tuple-element.183), channel_id=1, source_target_pairs={{0,24},{8,16},{16,8},{24,0},{1,25},{9,17},{17,9},{25,1},{2,26},{10... | collective-permute-start | bytes 786440 | tf_op jit(solution)/shard_map/ppermute | solution.py:26
  132.5 17.7 %collective-permute-start.24 = (bf16[128,512]{1,0:T(8,128)(2,1)S(1)}, bf16[128,512]{1,0:T(8,128)(2,1)S(1)}, u32[]{:S(2)}, u32[]{:S(2)}) collective-permute-start(bf16[128,512]{1,0:T(8,128)(2,1)S(1)} %get-tuple-element.175), channel_id=1, source_target_pairs={{0,4},{1,5},{2,6},{3,7},{4,0},{5,1},{6,2},{7,3},{8,12},{9,13},{10,... | collective-permute-start | bytes 393224 | tf_op jit(solution)/shard_map/ppermute | solution.py:26
  135.8 14.3 %collective-permute-start.26 = (bf16[1,128,512]{2,1,0:T(8,128)(2,1)S(1)}, bf16[1,128,512]{2,1,0:T(8,128)(2,1)S(1)}, u32[]{:S(2)}, u32[]{:S(2)}) collective-permute-start(bf16[1,128,512]{2,1,0:T(8,128)(2,1)S(1)} %get-tuple-element.177), channel_id=1, source_target_pairs={{0,10},{1,11},{2,8},{3,9},{4,14},{5,15},{6,12},{7,13},{8,2},{9,3},... | collective-permute-start | bytes 393224 | tf_op jit(solution)/shard_map/ppermute | solution.py:36
  137.7 12.5 %collective-permute-start.27 = (bf16[1,128,512]{2,1,0:T(8,128)(2,1)S(1)}, bf16[1,128,512]{2,1,0:T(8,128)(2,1)S(1)}, u32[]{:S(2)}, u32[]{:S(2)}) collective-permute-start(bf16[1,128,512]{2,1,0:T(8,128)(2,1)S(1)} %get-tuple-element.178), channel_id=1, source_target_pairs={{0,18},{1,19},{2,16},{3,17},{4,22},{5,23},{6,20},{7,21},{8,26},{9,... | collective-permute-start | bytes 393224 | tf_op jit(solution)/shard_map/ppermute | solution.py:36
  139.6 10.6 %collective-permute-start.28 = (bf16[1,128,512]{2,1,0:T(8,128)(2,1)S(1)}, bf16[1,128,512]{2,1,0:T(8,128)(2,1)S(1)}, u32[]{:S(2)}, u32[]{:S(2)}) collective-permute-start(bf16[1,128,512]{2,1,0:T(8,128)(2,1)S(1)} %get-tuple-element.179), channel_id=1, source_target_pairs={{0,26},{1,27},{2,24},{3,25},{4,30},{5,31},{6,28},{7,29},{8,18},{9,... | collective-permute-start | bytes 393224 | tf_op jit(solution)/shard_map/ppermute | solution.py:36

commit v7 on v6

--- a/solution.py
+++ b/solution.py
@@ -437,18 +437,17 @@
     )
     self_2 = spread(self_2)
     (self_2,) = add_terms(chain, self_2, "add_self_2", (jnp.float32,))
-    share_2, rows, *starts = cut_out(
+    starts = cut_out(
+        chain, [[(cotangent, rows_at(at), size)] for at, size in cuts[:2]], "rows_0"
+    )
+    share_2, rows = cut_out(
         chain,
-        [
-            [(first, rows_at(0), share)],
-            [(first, rows_at(share), cuts[0][1])],
-            [(cotangent, rows_at(cuts[0][0]), cuts[0][1])],
-            [(cotangent, rows_at(cuts[1][0]), cuts[1][1])],
-        ],
+        [[(first, rows_at(0), share)], [(first, rows_at(share), cuts[0][1])]],
         "parted",
         [far_inputs],
     )
-    far[2][0], near[2][0], near[2][1] = [rows], [starts[0]], [starts[1]]
+    far[2][0], near[2][0] = [rows], [starts[0]]
+    near[2][1] = hand_on(chain, [starts[1]], [], "rows_1")
     send(2, 1)
     shares_2 = [(share_2, place_of(0))]
     shares_2 += [(swap(share_2, "wide", k), place_of(k)) for k in range(1, parts)]

time: 152 us -> 152 us (level)
  starting transfers between devices: 45.5 us -> 47.6 us
  waiting for transfers between devices: 57.9 us -> 56.1 us
    ppermute x28, waiting for transfers between devices: 57.5 us -> 54.2 us  [swap(): lax.ppermute(array, axis, [(i, i ^ mask) for i in range(lax.axis_size(axi...]
    ppermute x28, starting transfers between devices: 39.1 us -> 41.3 us  [swap(): lax.ppermute(array, axis, [(i, i ^ mask) for i in range(lax.axis_size(axi...]
    pallas_call x35 -> x37, Pallas kernels: 47.1 us -> 47.1 us  [__call__(): pl.pallas_call(whole, grid=(grid,), out_shape=[*out_shape, TOKEN], in_spe...]
  transfers between devices with their start and end apart: 32 -> 32, of which waited for: 16 -> 17; matrix products, arithmetic and copies ran while one was open for 0% -> 0% of each run, Pallas kernels for 30% -> 30%
where the time goes in v7:
time: 152 us
  waiting for transfers between devices  56.1 us (37%)
  starting transfers between devices  47.6 us (31%)
  Pallas kernels  47.1 us (31%)
    ppermute x28, waiting for transfers between devices, swap(): lax.ppermute(array, axis, [(i, i ^ mask) for i in range(lax.axis_size(axi...  54.2 us
    pallas_call x37, Pallas kernels, __call__(): pl.pallas_call(whole, grid=(grid,), out_shape=[*out_shape, TOKEN], in_spe...  47.1 us
    ppermute x28, starting transfers between devices, swap(): lax.ppermute(array, axis, [(i, i ^ mask) for i in range(lax.axis_size(axi...  41.3 us
    ppermute x4, starting transfers between devices, swap_both(): return lax.ppermute(array, ('wide', 'narrow'), pairs)  6.33 us
  transfers between devices with their start and end apart: 32, of which 17 were waited for; matrix products, arithmetic and copies ran while one was open for 0% of the time, Pallas kernels for 30%

profile of v7, /device:TPU:0, one launch (start us, length us, event | category | flops | bytes accessed | tf_op | source)
XLA Modules:
  0.0 151.8 jit_solution(3115318630338282371)
XLA Ops:
  1.1 1.2 first_rows.1
  2.4 3.7 %collective-permute-start.1 = (bf16[320,512]{1,0:T(8,128)(2,1)S(1)}, bf16[320,512]{1,0:T(8,128)(2,1)S(1)}, u32[]{:S(2)}, u32[]{:S(2)}) collective-permute-start(bf16[320,512]{1,0:T(8,128)(2,1)S(1)} %get-tuple-element.100), channel_id=1, source_target_pairs={{0,4},{1,5},{2,6},{3,7},{4,0},{5,1},{6,2},{7,3},{8,12},{9,13},{10,... | collective-permute-start | bytes 983048 | tf_op jit(solution)/shard_map/ppermute | solution.py:26
  6.1 4.5 %self_sums_2.1 = (f32[1,128,512]{2,1,0:T(8,128)S(1)}, bf16[1,128,512]{2,1,0:T(8,128)(2,1)S(1)}, bf16[1,128,512]{2,1,0:T(8,128)(2,1)S(1)}, bf16[1,128,512]{2,1,0:T(8,128)(2,1)S(1)}, f32[8,128]{1,0:T(8,128)S(1)}) custom-call(bf16[3,2048,512]{2,1,0:T(8,128)(2,1)} %refs_1_.27, bf16[2048,512]{1,0:T(8,128)(2,1)} %refs_0_.45, f32[8,128]{1,0:T(8,128)S(1)} %get-tuple-element.101.refs_2_), custom_call_target="tpu_custom_call" | custom-call | tf_op jit(solution)/shard_map/self_sums_2/pallas_call | solution.py:64
  10.6 1.6 %collective-permute-start.3 = (bf16[1,128,512]{2,1,0:T(8,128)(2,1)S(1)}, bf16[1,128,512]{2,1,0:T(8,128)(2,1)S(1)}, u32[]{:S(2)}, u32[]{:S(2)}) collective-permute-start(bf16[1,128,512]{2,1,0:T(8,128)(2,1)S(1)} %get-tuple-element.103), channel_id=1, source_target_pairs={{0,8},{8,0},{16,24},{24,16},{1,9},{9,1},{17,25},{25,17},{2,10},{10... | collective-permute-start | bytes 393224 | tf_op jit(solution)/shard_map/ppermute | solution.py:26
  12.2 1.5 %collective-permute-start.4 = (bf16[1,128,512]{2,1,0:T(8,128)(2,1)S(1)}, bf16[1,128,512]{2,1,0:T(8,128)(2,1)S(1)}, u32[]{:S(2)}, u32[]{:S(2)}) collective-permute-start(bf16[1,128,512]{2,1,0:T(8,128)(2,1)S(1)} %get-tuple-element.104), channel_id=1, source_target_pairs={{0,16},{8,24},{16,0},{24,8},{1,17},{9,25},{17,1},{25,9},{2,18},{10... | collective-permute-start | bytes 393224 | tf_op jit(solution)/shard_map/ppermute | solution.py:26
  14.2 2.5 %collective-permute-done.3.refs_1_ = bf16[1,128,512]{2,1,0:T(8,128)(2,1)S(1)} collective-permute-done((bf16[1,128,512]{2,1,0:T(8,128)(2,1)S(1)}, bf16[1,128,512]{2,1,0:T(8,128)(2,1)S(1)}, u32[]{:S(2)}, u32[]{:S(2)}) %collective-permute-start.3) | collective-permute-done | bytes 131104 | tf_op jit(solution)/shard_map/ppermute | solution.py:26
  16.6 1.6 %collective-permute-start = (bf16[512,512]{1,0:T(8,128)(2,1)S(1)}, bf16[512,512]{1,0:T(8,128)(2,1)S(1)}, u32[]{:S(2)}, u32[]{:S(2)}) collective-permute-start(bf16[512,512]{1,0:T(8,128)(2,1)S(1)} %get-tuple-element.99), channel_id=1, source_target_pairs={{0,2},{1,3},{2,0},{3,1},{4,6},{5,7},{6,4},{7,5},{8,10},{9,11},{10,... | collective-permute-start | bytes 1572872 | tf_op jit(solution)/shard_map/ppermute | solution.py:26
  18.2 2.1 %collective-permute-done.4.refs_2_ = bf16[1,128,512]{2,1,0:T(8,128)(2,1)S(1)} collective-permute-done((bf16[1,128,512]{2,1,0:T(8,128)(2,1)S(1)}, bf16[1,128,512]{2,1,0:T(8,128)(2,1)S(1)}, u32[]{:S(2)}, u32[]{:S(2)}) %collective-permute-start.4) | collective-permute-done | bytes 131104 | tf_op jit(solution)/shard_map/ppermute | solution.py:26
  22.4 1.3 collective-permute-start.6
  23.7 1.5 %collective-permute-start.7 = (bf16[128,512]{1,0:T(8,128)(2,1)S(1)}, bf16[128,512]{1,0:T(8,128)(2,1)S(1)}, u32[]{:S(2)}, u32[]{:S(2)}) collective-permute-start(bf16[128,512]{1,0:T(8,128)(2,1)S(1)} %get-tuple-element.109.refs_0_), channel_id=1, source_target_pairs={{0,16},{8,24},{16,0},{24,8},{1,17},{9,25},{17,1},{25,9},{2,18},{10... | collective-permute-start | bytes 393224 | tf_op jit(solution)/shard_map/ppermute | solution.py:26
  25.9 2.1 %collective-permute-done.6.refs_1_ = bf16[128,512]{1,0:T(8,128)(2,1)S(1)} collective-permute-done((bf16[128,512]{1,0:T(8,128)(2,1)S(1)}, bf16[128,512]{1,0:T(8,128)(2,1)S(1)}, u32[]{:S(2)}, u32[]{:S(2)}) %collective-permute-start.6) | collective-permute-done | bytes 131104 | tf_op jit(solution)/shard_map/ppermute | solution.py:26
  28.0 3.5 %collective-permute-done.7.refs_2_ = bf16[128,512]{1,0:T(8,128)(2,1)S(1)} collective-permute-done((bf16[128,512]{1,0:T(8,128)(2,1)S(1)}, bf16[128,512]{1,0:T(8,128)(2,1)S(1)}, u32[]{:S(2)}, u32[]{:S(2)}) %collective-permute-start.7) | collective-permute-done | bytes 131104 | tf_op jit(solution)/shard_map/ppermute | solution.py:26
  32.0 4.0 %collective-permute-start.11 = (bf16[192,512]{1,0:T(8,128)(2,1)S(1)}, bf16[192,512]{1,0:T(8,128)(2,1)S(1)}, u32[]{:S(2)}, u32[]{:S(2)}) collective-permute-start(bf16[192,512]{1,0:T(8,128)(2,1)S(1)} %get-tuple-element.120.refs_6_.refs_4_), channel_id=1, source_target_pairs={{0,2},{1,3},{2,0},{3,1},{4,6},{5,7},{6,4},{7,5},{8,10},{9,11},{10,... | collective-permute-start | bytes 589832 | tf_op jit(solution)/shard_map/ppermute | solution.py:26
  37.4 7.9 %collective-permute-done.11.refs_7_.refs_3_ = bf16[192,512]{1,0:T(8,128)(2,1)S(1)} collective-permute-done((bf16[192,512]{1,0:T(8,128)(2,1)S(1)}, bf16[192,512]{1,0:T(8,128)(2,1)S(1)}, u32[]{:S(2)}, u32[]{:S(2)}) %collective-permute-start.11) | collective-permute-done | bytes 196640 | tf_op jit(solution)/shard_map/ppermute | solution.py:26
  45.3 6.6 %collective-permute-done.10.refs_3_ = bf16[384,512]{1,0:T(8,128)(2,1)S(1)} collective-permute-done((bf16[384,512]{1,0:T(8,128)(2,1)S(1)}, bf16[384,512]{1,0:T(8,128)(2,1)S(1)}, u32[]{:S(2)}, u32[]{:S(2)}) %collective-permute-start.10) | collective-permute-done | bytes 393248 | tf_op jit(solution)/shard_map/ppermute | solution.py:26
  54.2 3.5 %collective-permute-start.14 = (bf16[448,512]{1,0:T(8,128)(2,1)S(1)}, bf16[448,512]{1,0:T(8,128)(2,1)S(1)}, u32[]{:S(2)}, u32[]{:S(2)}) collective-permute-start(bf16[448,512]{1,0:T(8,128)(2,1)S(1)} %get-tuple-element.131.refs_2_), channel_id=1, source_target_pairs={{0,4},{1,5},{2,6},{3,7},{4,0},{5,1},{6,2},{7,3},{8,12},{9,13},{10,... | collective-permute-start | bytes 1376264 | tf_op jit(solution)/shard_map/ppermute | solution.py:26
  57.7 1.7 %sums_b_0.1 = (f32[3,512,512]{2,1,0:T(8,128)S(1)}, f32[8,128]{1,0:T(8,128)S(1)}) custom-call(bf16[3,2048,512]{2,1,0:T(8,128)(2,1)} %refs_1_.27, bf16[3,2048,512]{2,1,0:T(8,128)(2,1)} %refs_1_.27, bf16[3,2048,512]{2,1,0:T(8,128)(2,1)S(1)} %collective-permute-done.2.refs_2_, bf16[192,512]{1,0:T(8,128)(2,1)S(1)} %collective-permute-done.11.refs_7_.refs_3_, ...), custom_call_target="tpu_custom_call" | custom-call | tf_op jit(solution)/shard_map/sums_b_0/pallas_call | solution.py:64
  59.4 2.3 %sums_a_0.1 = (f32[2,512,512]{2,1,0:T(8,128)S(1)}, f32[8,128]{1,0:T(8,128)S(1)}) custom-call(bf16[3,2048,512]{2,1,0:T(8,128)(2,1)} %refs_1_.27, bf16[3,2048,512]{2,1,0:T(8,128)(2,1)} %refs_1_.27, bf16[192,512]{1,0:T(8,128)(2,1)S(1)} %get-tuple-element.115.refs_3_.refs_2_, bf16[384,512]{1,0:T(8,128)(2,1)S(1)} %collective-permute-done.10.refs_3_, ...), custom_call_target="tpu_custom_call" | custom-call | tf_op jit(solution)/shard_map/sums_a_0/pallas_call | solution.py:64
  61.7 8.5 %collective-permute-done.9.refs_3_.refs_2_ = bf16[384,512]{1,0:T(8,128)(2,1)S(1)} collective-permute-done((bf16[384,512]{1,0:T(8,128)(2,1)S(1)}, bf16[384,512]{1,0:T(8,128)(2,1)S(1)}, u32[]{:S(2)}, u32[]{:S(2)}) %collective-permute-start.9) | collective-permute-done | bytes 393248 | tf_op jit(solution)/shard_map/ppermute | solution.py:26
  70.8 1.5 next_grads_1_1.1
  73.3 1.9 %collective-permute-start.16 = (bf16[384,512]{1,0:T(8,128)(2,1)S(1)}, bf16[384,512]{1,0:T(8,128)(2,1)S(1)}, u32[]{:S(2)}, u32[]{:S(2)}) collective-permute-start(bf16[384,512]{1,0:T(8,128)(2,1)S(1)} %get-tuple-element.141.refs_2_), channel_id=1, source_target_pairs={{0,4},{1,5},{2,6},{3,7},{4,0},{5,1},{6,2},{7,3},{8,12},{9,13},{10,... | collective-permute-start | bytes 1179656 | tf_op jit(solution)/shard_map/ppermute | solution.py:26
  75.3 2.2 %sums_b_1.1 = (f32[3,512,512]{2,1,0:T(8,128)S(1)}, f32[8,128]{1,0:T(8,128)S(1)}) custom-call(bf16[3,2048,512]{2,1,0:T(8,128)(2,1)} %refs_1_.27, bf16[3,2048,512]{2,1,0:T(8,128)(2,1)} %refs_1_.27, bf16[3,2048,512]{2,1,0:T(8,128)(2,1)S(1)} %collective-permute-done.2.refs_2_, bf16[384,512]{1,0:T(8,128)(2,1)S(1)} %collective-permute-done.13.refs_3_, ...), custom_call_target="tpu_custom_call" | custom-call | tf_op jit(solution)/shard_map/sums_b_1/pallas_call | solution.py:64
  77.5 1.9 %sums_a_2.1 = (f32[2,512,512]{2,1,0:T(8,128)S(1)}, f32[8,128]{1,0:T(8,128)S(1)}) custom-call(bf16[3,2048,512]{2,1,0:T(8,128)(2,1)} %refs_1_.27, bf16[3,2048,512]{2,1,0:T(8,128)(2,1)} %refs_1_.27, bf16[384,512]{1,0:T(8,128)(2,1)S(1)} %collective-permute-done.9.refs_3_.refs_2_, bf16[384,512]{1,0:T(8,128)(2,1)S(1)} %get-tuple-element.128.refs_3_.refs_2_, ...), custom_call_target="tpu_custom_call" | custom-call | tf_op jit(solution)/shard_map/sums_a_2/pallas_call | solution.py:64
  79.3 9.1 %collective-permute-done.14.refs_3_.refs_2_ = bf16[448,512]{1,0:T(8,128)(2,1)S(1)} collective-permute-done((bf16[448,512]{1,0:T(8,128)(2,1)S(1)}, bf16[448,512]{1,0:T(8,128)(2,1)S(1)}, u32[]{:S(2)}, u32[]{:S(2)}) %collective-permute-start.14) | collective-permute-done | bytes 458784 | tf_op jit(solution)/shard_map/ppermute | solution.py:26
  91.6 3.4 %collective-permute-start.15 = (bf16[256,512]{1,0:T(8,128)(2,1)S(1)}, bf16[256,512]{1,0:T(8,128)(2,1)S(1)}, u32[]{:S(2)}, u32[]{:S(2)}) collective-permute-start(bf16[256,512]{1,0:T(8,128)(2,1)S(1)} %get-tuple-element.140.refs_2_), channel_id=1, source_target_pairs={{0,4},{1,5},{2,6},{3,7},{4,0},{5,1},{6,2},{7,3},{8,12},{9,13},{10,... | collective-permute-start | bytes 786440 | tf_op jit(solution)/shard_map/ppermute | solution.py:26
  95.1 2.2 %sums_b_2.1 = (f32[3,512,512]{2,1,0:T(8,128)S(1)}, f32[8,128]{1,0:T(8,128)S(1)}) custom-call(bf16[3,2048,512]{2,1,0:T(8,128)(2,1)} %refs_1_.27, bf16[3,2048,512]{2,1,0:T(8,128)(2,1)} %refs_1_.27, bf16[3,2048,512]{2,1,0:T(8,128)(2,1)S(1)} %collective-permute-done.2.refs_2_, bf16[384,512]{1,0:T(8,128)(2,1)S(1)} %collective-permute-done.12.refs_3_, ...), custom_call_target="tpu_custom_call" | custom-call | tf_op jit(solution)/shard_map/sums_b_2/pallas_call | solution.py:64
  97.3 1.9 %sums_a_3.1 = (f32[2,512,512]{2,1,0:T(8,128)S(1)}, f32[8,128]{1,0:T(8,128)S(1)}) custom-call(bf16[3,2048,512]{2,1,0:T(8,128)(2,1)} %refs_1_.27, bf16[3,2048,512]{2,1,0:T(8,128)(2,1)} %refs_1_.27, bf16[448,512]{1,0:T(8,128)(2,1)S(1)} %collective-permute-done.14.refs_3_.refs_2_, bf16[448,512]{1,0:T(8,128)(2,1)S(1)} %get-tuple-element.142.refs_3_.refs_2_, ...), custom_call_target="tpu_custom_call" | custom-call | tf_op jit(solution)/shard_map/sums_a_3/pallas_call | solution.py:64
  99.9 1.9 %sums_a_4.1 = (f32[2,512,512]{2,1,0:T(8,128)S(1)}, f32[8,128]{1,0:T(8,128)S(1)}) custom-call(bf16[3,2048,512]{2,1,0:T(8,128)(2,1)} %refs_1_.27, bf16[3,2048,512]{2,1,0:T(8,128)(2,1)} %refs_1_.27, bf16[384,512]{1,0:T(8,128)(2,1)S(1)} %collective-permute-done.16.refs_3_.refs_2_, bf16[384,512]{1,0:T(8,128)(2,1)S(1)} %get-tuple-element.149.refs_3_.refs_2_, ...), custom_call_target="tpu_custom_call" | custom-call | tf_op jit(solution)/shard_map/sums_a_4/pallas_call | solution.py:64
  101.8 4.7 %collective-permute-done.15.refs_3_.refs_2_ = bf16[256,512]{1,0:T(8,128)(2,1)S(1)} collective-permute-done((bf16[256,512]{1,0:T(8,128)(2,1)S(1)}, bf16[256,512]{1,0:T(8,128)(2,1)S(1)}, u32[]{:S(2)}, u32[]{:S(2)}) %collective-permute-start.15) | collective-permute-done | bytes 262176 | tf_op jit(solution)/shard_map/ppermute | solution.py:26
  106.9 3.9 %collective-permute-start.20 = (bf16[256,512]{1,0:T(8,128)(2,1)S(1)}, bf16[256,512]{1,0:T(8,128)(2,1)S(1)}, u32[]{:S(2)}, u32[]{:S(2)}) collective-permute-start(bf16[256,512]{1,0:T(8,128)(2,1)S(1)} %get-tuple-element.153.refs_3_.refs_2_), channel_id=1, source_target_pairs={{0,2},{1,3},{2,0},{3,1},{4,6},{5,7},{6,4},{7,5},{8,10},{9,11},{10,... | collective-permute-start | bytes 786440 | tf_op jit(solution)/shard_map/ppermute | solution.py:26
  110.8 1.6 %sums_a_5.1 = (f32[2,128,512]{2,1,0:T(8,128)S(1)}, bf16[2,128,512]{2,1,0:T(8,128)(2,1)S(1)}, bf16[2,128,512]{2,1,0:T(8,128)(2,1)S(1)}, bf16[2,128,512]{2,1,0:T(8,128)(2,1)S(1)}, f32[8,128]{1,0:T(8,128)S(1)}) custom-call(bf16[3,2048,512]{2,1,0:T(8,128)(2,1)} %refs_1_.27, bf16[3,2048,512]{2,1,0:T(8,128)(2,1)} %refs_1_.27, ...), custom_call_target="tpu_custom_call" | custom-call | tf_op jit(solution)/shard_map/sums_a_5/pallas_call | solution.py:64
  112.5 1.6 %collective-permute-start.17 = (bf16[2,128,512]{2,1,0:T(8,128)(2,1)S(1)}, bf16[2,128,512]{2,1,0:T(8,128)(2,1)S(1)}, u32[]{:S(2)}, u32[]{:S(2)}) collective-permute-start(bf16[2,128,512]{2,1,0:T(8,128)(2,1)S(1)} %get-tuple-element.157), channel_id=1, source_target_pairs={{0,8},{8,0},{16,24},{24,16},{1,9},{9,1},{17,25},{25,17},{2,10},{10... | collective-permute-start | bytes 786440 | tf_op jit(solution)/shard_map/ppermute | solution.py:26
  114.0 1.5 %collective-permute-start.18 = (bf16[2,128,512]{2,1,0:T(8,128)(2,1)S(1)}, bf16[2,128,512]{2,1,0:T(8,128)(2,1)S(1)}, u32[]{:S(2)}, u32[]{:S(2)}) collective-permute-start(bf16[2,128,512]{2,1,0:T(8,128)(2,1)S(1)} %get-tuple-element.158), channel_id=1, source_target_pairs={{0,16},{8,24},{16,0},{24,8},{1,17},{9,25},{17,1},{25,9},{2,18},{10... | collective-permute-start | bytes 786440 | tf_op jit(solution)/shard_map/ppermute | solution.py:26
  117.0 2.2 %sums_b_3.1 = (f32[3,512,512]{2,1,0:T(8,128)S(1)}, f32[8,128]{1,0:T(8,128)S(1)}) custom-call(bf16[3,2048,512]{2,1,0:T(8,128)(2,1)} %refs_1_.27, bf16[3,2048,512]{2,1,0:T(8,128)(2,1)} %refs_1_.27, bf16[3,2048,512]{2,1,0:T(8,128)(2,1)S(1)} %collective-permute-done.2.refs_2_, bf16[448,512]{1,0:T(8,128)(2,1)S(1)} %collective-permute-done.22.refs_3_, ...), custom_call_target="tpu_custom_call" | custom-call | tf_op jit(solution)/shard_map/sums_b_3/pallas_call | solution.py:64
  120.6 2.2 %sums_b_4.1 = (f32[3,512,512]{2,1,0:T(8,128)S(1)}, f32[8,128]{1,0:T(8,128)S(1)}) custom-call(bf16[3,2048,512]{2,1,0:T(8,128)(2,1)} %refs_1_.27, bf16[3,2048,512]{2,1,0:T(8,128)(2,1)} %refs_1_.27, bf16[3,2048,512]{2,1,0:T(8,128)(2,1)S(1)} %collective-permute-done.2.refs_2_, bf16[384,512]{1,0:T(8,128)(2,1)S(1)} %collective-permute-done.21.refs_3_, ...), custom_call_target="tpu_custom_call" | custom-call | tf_op jit(solution)/shard_map/sums_b_4/pallas_call | solution.py:64
  122.8 2.5 %collective-permute-done.20.refs_3_ = bf16[256,512]{1,0:T(8,128)(2,1)S(1)} collective-permute-done((bf16[256,512]{1,0:T(8,128)(2,1)S(1)}, bf16[256,512]{1,0:T(8,128)(2,1)S(1)}, u32[]{:S(2)}, u32[]{:S(2)}) %collective-permute-start.20) | collective-permute-done | bytes 262176 | tf_op jit(solution)/shard_map/ppermute | solution.py:26
  125.8 1.9 %sums_b_5.1 = (bf16[1,128,512]{2,1,0:T(8,128)(2,1)S(1)}, bf16[1,128,512]{2,1,0:T(8,128)(2,1)S(1)}, bf16[1,128,512]{2,1,0:T(8,128)(2,1)S(1)}, bf16[1,128,512]{2,1...) custom-call(bf16[3,2048,512]{2,1,0:T(8,128)(2,1)} %refs_1_.27, ...), custom_call_target="tpu_custom_call" | custom-call | tf_op jit(solution)/shard_map/sums_b_5/pallas_call | solution.py:64
  128.0 1.4 collective-permute-start.29
  129.4 1.5 %collective-permute-start.30 = (bf16[2,128,512]{2,1,0:T(8,128)(2,1)S(1)}, bf16[2,128,512]{2,1,0:T(8,128)(2,1)S(1)}, u32[]{:S(2)}, u32[]{:S(2)}) collective-permute-start(bf16[2,128,512]{2,1,0:T(8,128)(2,1)S(1)} %get-tuple-element.188), channel_id=1, source_target_pairs={{0,16},{8,24},{16,0},{24,8},{1,17},{9,25},{17,1},{25,9},{2,18},{10... | collective-permute-start | bytes 786440 | tf_op jit(solution)/shard_map/ppermute | solution.py:26
  131.5 1.3 collective-permute-done.23.refs_4_.refs_1_.refs_3_
  132.9 2.8 %collective-permute-start.24 = (bf16[128,512]{1,0:T(8,128)(2,1)S(1)}, bf16[128,512]{1,0:T(8,128)(2,1)S(1)}, u32[]{:S(2)}, u32[]{:S(2)}) collective-permute-start(bf16[128,512]{1,0:T(8,128)(2,1)S(1)} %get-tuple-element.181), channel_id=1, source_target_pairs={{0,4},{1,5},{2,6},{3,7},{4,0},{5,1},{6,2},{7,3},{8,12},{9,13},{10,... | collective-permute-start | bytes 393224 | tf_op jit(solution)/shard_map/ppermute | solution.py:26
  136.2 1.8 %collective-permute-start.26 = (bf16[1,128,512]{2,1,0:T(8,128)(2,1)S(1)}, bf16[1,128,512]{2,1,0:T(8,128)(2,1)S(1)}, u32[]{:S(2)}, u32[]{:S(2)}) collective-permute-start(bf16[1,128,512]{2,1,0:T(8,128)(2,1)S(1)} %get-tuple-element.183), channel_id=1, source_target_pairs={{0,10},{1,11},{2,8},{3,9},{4,14},{5,15},{6,12},{7,13},{8,2},{9,3},... | collective-permute-start | bytes 393224 | tf_op jit(solution)/shard_map/ppermute | solution.py:36
  138.0 1.7 %collective-permute-start.27 = (bf16[1,128,512]{2,1,0:T(8,128)(2,1)S(1)}, bf16[1,128,512]{2,1,0:T(8,128)(2,1)S(1)}, u32[]{:S(2)}, u32[]{:S(2)}) collective-permute-start(bf16[1,128,512]{2,1,0:T(8,128)(2,1)S(1)} %get-tuple-element.184), channel_id=1, source_target_pairs={{0,18},{1,19},{2,16},{3,17},{4,22},{5,23},{6,20},{7,21},{8,26},{9,... | collective-permute-start | bytes 393224 | tf_op jit(solution)/shard_map/ppermute | solution.py:36
  140.0 2.9 %collective-permute-start.28 = (bf16[1,128,512]{2,1,0:T(8,128)(2,1)S(1)}, bf16[1,128,512]{2,1,0:T(8,128)(2,1)S(1)}, u32[]{:S(2)}, u32[]{:S(2)}) collective-permute-start(bf16[1,128,512]{2,1,0:T(8,128)(2,1)S(1)} %get-tuple-element.185), channel_id=1, source_target_pairs={{0,26},{1,27},{2,24},{3,25},{4,30},{5,31},{6,28},{7,29},{8,18},{9,... | collective-permute-start | bytes 393224 | tf_op jit(solution)/shard_map/ppermute | solution.py:36
  142.8 3.8 %last_grad.1 = (bf16[2048,512]{1,0:T(8,128)(2,1)}, f32[8,128]{1,0:T(8,128)S(1)}) custom-call(bf16[2560,512]{1,0:T(8,128)(2,1)S(1)} %get-tuple-element.173.refs_0_, bf16[2560,512]{1,0:T(8,128)(2,1)S(1)} %collective-permute-done.23.refs_4_.refs_1_.refs_3_, bf16[3,512,512]{2,1,0:T(8,128)(2,1)S(1)} %copy-done, ...), custom_call_target="tpu_custom_call" | custom-call | tf_op jit(solution)/shard_map/last_grad/pallas_call | solution.py:64
  146.7 2.4 %collective-permute-done.31.refs_8_ = bf16[2,128,512]{2,1,0:T(8,128)(2,1)S(1)} collective-permute-done((bf16[2,128,512]{2,1,0:T(8,128)(2,1)S(1)}, bf16[2,128,512]{2,1,0:T(8,128)(2,1)S(1)}, u32[]{:S(2)}, u32[]{:S(2)}) %collective-permute-start.31) | collective-permute-done | bytes 262176 | tf_op jit(solution)/shard_map/ppermute | solution.py:26
  149.1 1.4 collective-permute-done.28.refs_4_
  150.5 1.3 last_sums.1
  (55 shorter events, 18.8 us)
Async XLA Ops:
  0.6 20.9 %collective-permute-start.2 = (bf16[3,2048,512]{2,1,0:T(8,128)(2,1)}, bf16[3,2048,512]{2,1,0:T(8,128)(2,1)S(1)}, u32[]{:S(2)}, u32[]{:S(2)}) collective-permute-start(bf16[3,2048,512]{2,1,0:T(8,128)(2,1)} %refs_1_.27), channel_id=1, source_target_pairs={{0,1},{1,0},{2,3},{3,2},{4,5},{5,4},{6,7},{7,6},{8,9},{9,8},{10,11... | collective-permute-start | bytes 18874376 | tf_op jit(solution)/shard_map/ppermute | solution.py:26
  2.4 19.2 %collective-permute-start.1 = (bf16[320,512]{1,0:T(8,128)(2,1)S(1)}, bf16[320,512]{1,0:T(8,128)(2,1)S(1)}, u32[]{:S(2)}, u32[]{:S(2)}) collective-permute-start(bf16[320,512]{1,0:T(8,128)(2,1)S(1)} %get-tuple-element.100), channel_id=1, source_target_pairs={{0,4},{1,5},{2,6},{3,7},{4,0},{5,1},{6,2},{7,3},{8,12},{9,13},{10,... | collective-permute-start | bytes 983048 | tf_op jit(solution)/shard_map/ppermute | solution.py:26
  10.6 6.0 %collective-permute-start.3 = (bf16[1,128,512]{2,1,0:T(8,128)(2,1)S(1)}, bf16[1,128,512]{2,1,0:T(8,128)(2,1)S(1)}, u32[]{:S(2)}, u32[]{:S(2)}) collective-permute-start(bf16[1,128,512]{2,1,0:T(8,128)(2,1)S(1)} %get-tuple-element.103), channel_id=1, source_target_pairs={{0,8},{8,0},{16,24},{24,16},{1,9},{9,1},{17,25},{25,17},{2,10},{10... | collective-permute-start | bytes 393224 | tf_op jit(solution)/shard_map/ppermute | solution.py:26
  12.2 8.1 %collective-permute-start.4 = (bf16[1,128,512]{2,1,0:T(8,128)(2,1)S(1)}, bf16[1,128,512]{2,1,0:T(8,128)(2,1)S(1)}, u32[]{:S(2)}, u32[]{:S(2)}) collective-permute-start(bf16[1,128,512]{2,1,0:T(8,128)(2,1)S(1)} %get-tuple-element.104), channel_id=1, source_target_pairs={{0,16},{8,24},{16,0},{24,8},{1,17},{9,25},{17,1},{25,9},{2,18},{10... | collective-permute-start | bytes 393224 | tf_op jit(solution)/shard_map/ppermute | solution.py:26
  13.7 6.6 %collective-permute-start.5 = (bf16[1,128,512]{2,1,0:T(8,128)(2,1)S(1)}, bf16[1,128,512]{2,1,0:T(8,128)(2,1)S(1)}, u32[]{:S(2)}, u32[]{:S(2)}) collective-permute-start(bf16[1,128,512]{2,1,0:T(8,128)(2,1)S(1)} %get-tuple-element.105), channel_id=1, source_target_pairs={{0,24},{8,16},{16,8},{24,0},{1,25},{9,17},{17,9},{25,1},{2,26},{10... | collective-permute-start | bytes 393224 | tf_op jit(solution)/shard_map/ppermute | solution.py:26
  16.6 20.8 %collective-permute-start = (bf16[512,512]{1,0:T(8,128)(2,1)S(1)}, bf16[512,512]{1,0:T(8,128)(2,1)S(1)}, u32[]{:S(2)}, u32[]{:S(2)}) collective-permute-start(bf16[512,512]{1,0:T(8,128)(2,1)S(1)} %get-tuple-element.99), channel_id=1, source_target_pairs={{0,2},{1,3},{2,0},{3,1},{4,6},{5,7},{6,4},{7,5},{8,10},{9,11},{10,... | collective-permute-start | bytes 1572872 | tf_op jit(solution)/shard_map/ppermute | solution.py:26
  21.6 10.0 %copy-start = (bf16[3,512,512]{2,1,0:T(8,128)(2,1)S(1)}, bf16[3,512,512]{2,1,0:T(8,128)(2,1)}, u32[]{:S(2)}) copy-start(bf16[3,512,512]{2,1,0:T(8,128)(2,1)} %refs_2_.3) | copy-start | bytes 4718596
  22.0 29.9 %collective-permute-start.10 = (bf16[384,512]{1,0:T(8,128)(2,1)S(1)}, bf16[384,512]{1,0:T(8,128)(2,1)S(1)}, u32[]{:S(2)}, u32[]{:S(2)}) collective-permute-start(bf16[384,512]{1,0:T(8,128)(2,1)S(1)} %get-tuple-element.119.refs_2_), channel_id=1, source_target_pairs={{0,4},{1,5},{2,6},{3,7},{4,0},{5,1},{6,2},{7,3},{8,12},{9,13},{10,... | collective-permute-start | bytes 1179656 | tf_op jit(solution)/shard_map/ppermute | solution.py:26
  22.4 5.6 %collective-permute-start.6 = (bf16[128,512]{1,0:T(8,128)(2,1)S(1)}, bf16[128,512]{1,0:T(8,128)(2,1)S(1)}, u32[]{:S(2)}, u32[]{:S(2)}) collective-permute-start(bf16[128,512]{1,0:T(8,128)(2,1)S(1)} %get-tuple-element.109.refs_0_), channel_id=1, source_target_pairs={{0,8},{8,0},{16,24},{24,16},{1,9},{9,1},{17,25},{25,17},{2,10},{10... | collective-permute-start | bytes 393224 | tf_op jit(solution)/shard_map/ppermute | solution.py:26
  23.7 7.8 %collective-permute-start.7 = (bf16[128,512]{1,0:T(8,128)(2,1)S(1)}, bf16[128,512]{1,0:T(8,128)(2,1)S(1)}, u32[]{:S(2)}, u32[]{:S(2)}) collective-permute-start(bf16[128,512]{1,0:T(8,128)(2,1)S(1)} %get-tuple-element.109.refs_0_), channel_id=1, source_target_pairs={{0,16},{8,24},{16,0},{24,8},{1,17},{9,25},{17,1},{25,9},{2,18},{10... | collective-permute-start | bytes 393224 | tf_op jit(solution)/shard_map/ppermute | solution.py:26
  25.2 6.3 %collective-permute-start.8 = (bf16[128,512]{1,0:T(8,128)(2,1)S(1)}, bf16[128,512]{1,0:T(8,128)(2,1)S(1)}, u32[]{:S(2)}, u32[]{:S(2)}) collective-permute-start(bf16[128,512]{1,0:T(8,128)(2,1)S(1)} %get-tuple-element.109.refs_0_), channel_id=1, source_target_pairs={{0,24},{8,16},{16,8},{24,0},{1,25},{9,17},{17,9},{25,1},{2,26},{10... | collective-permute-start | bytes 393224 | tf_op jit(solution)/shard_map/ppermute | solution.py:26
  32.0 13.3 %collective-permute-start.11 = (bf16[192,512]{1,0:T(8,128)(2,1)S(1)}, bf16[192,512]{1,0:T(8,128)(2,1)S(1)}, u32[]{:S(2)}, u32[]{:S(2)}) collective-permute-start(bf16[192,512]{1,0:T(8,128)(2,1)S(1)} %get-tuple-element.120.refs_6_.refs_4_), channel_id=1, source_target_pairs={{0,2},{1,3},{2,0},{3,1},{4,6},{5,7},{6,4},{7,5},{8,10},{9,11},{10,... | collective-permute-start | bytes 589832 | tf_op jit(solution)/shard_map/ppermute | solution.py:26
  37.1 33.1 %collective-permute-start.9 = (bf16[384,512]{1,0:T(8,128)(2,1)S(1)}, bf16[384,512]{1,0:T(8,128)(2,1)S(1)}, u32[]{:S(2)}, u32[]{:S(2)}) collective-permute-start(bf16[384,512]{1,0:T(8,128)(2,1)S(1)} %get-tuple-element.118.refs_2_), channel_id=1, source_target_pairs={{0,4},{1,5},{2,6},{3,7},{4,0},{5,1},{6,2},{7,3},{8,12},{9,13},{10,... | collective-permute-start | bytes 1179656 | tf_op jit(solution)/shard_map/ppermute | solution.py:26
  53.1 17.7 %collective-permute-start.13 = (bf16[384,512]{1,0:T(8,128)(2,1)S(1)}, bf16[384,512]{1,0:T(8,128)(2,1)S(1)}, u32[]{:S(2)}, u32[]{:S(2)}) collective-permute-start(bf16[384,512]{1,0:T(8,128)(2,1)S(1)} %get-tuple-element.122.refs_5_.refs_2_), channel_id=1, source_target_pairs={{0,2},{1,3},{2,0},{3,1},{4,6},{5,7},{6,4},{7,5},{8,10},{9,11},{10,... | collective-permute-start | bytes 1179656 | tf_op jit(solution)/shard_map/ppermute | solution.py:26
  54.2 34.3 %collective-permute-start.14 = (bf16[448,512]{1,0:T(8,128)(2,1)S(1)}, bf16[448,512]{1,0:T(8,128)(2,1)S(1)}, u32[]{:S(2)}, u32[]{:S(2)}) collective-permute-start(bf16[448,512]{1,0:T(8,128)(2,1)S(1)} %get-tuple-element.131.refs_2_), channel_id=1, source_target_pairs={{0,4},{1,5},{2,6},{3,7},{4,0},{5,1},{6,2},{7,3},{8,12},{9,13},{10,... | collective-permute-start | bytes 1376264 | tf_op jit(solution)/shard_map/ppermute | solution.py:26
  70.8 19.1 %collective-permute-start.12 = (bf16[384,512]{1,0:T(8,128)(2,1)S(1)}, bf16[384,512]{1,0:T(8,128)(2,1)S(1)}, u32[]{:S(2)}, u32[]{:S(2)}) collective-permute-start(bf16[384,512]{1,0:T(8,128)(2,1)S(1)} %get-tuple-element.128.refs_3_.refs_2_), channel_id=1, source_target_pairs={{0,2},{1,3},{2,0},{3,1},{4,6},{5,7},{6,4},{7,5},{8,10},{9,11},{10,... | collective-permute-start | bytes 1179656 | tf_op jit(solution)/shard_map/ppermute | solution.py:26
  73.3 25.9 %collective-permute-start.16 = (bf16[384,512]{1,0:T(8,128)(2,1)S(1)}, bf16[384,512]{1,0:T(8,128)(2,1)S(1)}, u32[]{:S(2)}, u32[]{:S(2)}) collective-permute-start(bf16[384,512]{1,0:T(8,128)(2,1)S(1)} %get-tuple-element.141.refs_2_), channel_id=1, source_target_pairs={{0,4},{1,5},{2,6},{3,7},{4,0},{5,1},{6,2},{7,3},{8,12},{9,13},{10,... | collective-permute-start | bytes 1179656 | tf_op jit(solution)/shard_map/ppermute | solution.py:26
  89.2 26.4 %collective-permute-start.22 = (bf16[448,512]{1,0:T(8,128)(2,1)S(1)}, bf16[448,512]{1,0:T(8,128)(2,1)S(1)}, u32[]{:S(2)}, u32[]{:S(2)}) collective-permute-start(bf16[448,512]{1,0:T(8,128)(2,1)S(1)} %get-tuple-element.142.refs_3_.refs_2_), channel_id=1, source_target_pairs={{0,2},{1,3},{2,0},{3,1},{4,6},{5,7},{6,4},{7,5},{8,10},{9,11},{10,... | collective-permute-start | bytes 1376264 | tf_op jit(solution)/shard_map/ppermute | solution.py:26
  91.6 14.8 %collective-permute-start.15 = (bf16[256,512]{1,0:T(8,128)(2,1)S(1)}, bf16[256,512]{1,0:T(8,128)(2,1)S(1)}, u32[]{:S(2)}, u32[]{:S(2)}) collective-permute-start(bf16[256,512]{1,0:T(8,128)(2,1)S(1)} %get-tuple-element.140.refs_2_), channel_id=1, source_target_pairs={{0,4},{1,5},{2,6},{3,7},{4,0},{5,1},{6,2},{7,3},{8,12},{9,13},{10,... | collective-permute-start | bytes 786440 | tf_op jit(solution)/shard_map/ppermute | solution.py:26
  99.8 19.9 %collective-permute-start.21 = (bf16[384,512]{1,0:T(8,128)(2,1)S(1)}, bf16[384,512]{1,0:T(8,128)(2,1)S(1)}, u32[]{:S(2)}, u32[]{:S(2)}) collective-permute-start(bf16[384,512]{1,0:T(8,128)(2,1)S(1)} %get-tuple-element.149.refs_3_.refs_2_), channel_id=1, source_target_pairs={{0,2},{1,3},{2,0},{3,1},{4,6},{5,7},{6,4},{7,5},{8,10},{9,11},{10,... | collective-permute-start | bytes 1179656 | tf_op jit(solution)/shard_map/ppermute | solution.py:26
  106.9 18.4 %collective-permute-start.20 = (bf16[256,512]{1,0:T(8,128)(2,1)S(1)}, bf16[256,512]{1,0:T(8,128)(2,1)S(1)}, u32[]{:S(2)}, u32[]{:S(2)}) collective-permute-start(bf16[256,512]{1,0:T(8,128)(2,1)S(1)} %get-tuple-element.153.refs_3_.refs_2_), channel_id=1, source_target_pairs={{0,2},{1,3},{2,0},{3,1},{4,6},{5,7},{6,4},{7,5},{8,10},{9,11},{10,... | collective-permute-start | bytes 786440 | tf_op jit(solution)/shard_map/ppermute | solution.py:26
  112.5 15.2 %collective-permute-start.17 = (bf16[2,128,512]{2,1,0:T(8,128)(2,1)S(1)}, bf16[2,128,512]{2,1,0:T(8,128)(2,1)S(1)}, u32[]{:S(2)}, u32[]{:S(2)}) collective-permute-start(bf16[2,128,512]{2,1,0:T(8,128)(2,1)S(1)} %get-tuple-element.157), channel_id=1, source_target_pairs={{0,8},{8,0},{16,24},{24,16},{1,9},{9,1},{17,25},{25,17},{2,10},{10... | collective-permute-start | bytes 786440 | tf_op jit(solution)/shard_map/ppermute | solution.py:26
  114.0 13.7 %collective-permute-start.18 = (bf16[2,128,512]{2,1,0:T(8,128)(2,1)S(1)}, bf16[2,128,512]{2,1,0:T(8,128)(2,1)S(1)}, u32[]{:S(2)}, u32[]{:S(2)}) collective-permute-start(bf16[2,128,512]{2,1,0:T(8,128)(2,1)S(1)} %get-tuple-element.158), channel_id=1, source_target_pairs={{0,16},{8,24},{16,0},{24,8},{1,17},{9,25},{17,1},{25,9},{2,18},{10... | collective-permute-start | bytes 786440 | tf_op jit(solution)/shard_map/ppermute | solution.py:26
  115.6 12.2 %collective-permute-start.19 = (bf16[2,128,512]{2,1,0:T(8,128)(2,1)S(1)}, bf16[2,128,512]{2,1,0:T(8,128)(2,1)S(1)}, u32[]{:S(2)}, u32[]{:S(2)}) collective-permute-start(bf16[2,128,512]{2,1,0:T(8,128)(2,1)S(1)} %get-tuple-element.159), channel_id=1, source_target_pairs={{0,24},{8,16},{16,8},{24,0},{1,25},{9,17},{17,9},{25,1},{2,26},{10... | collective-permute-start | bytes 786440 | tf_op jit(solution)/shard_map/ppermute | solution.py:26
  127.9 5.0 %collective-permute-start.23 = (bf16[2560,512]{1,0:T(8,128)(2,1)S(1)}, bf16[2560,512]{1,0:T(8,128)(2,1)S(1)}, u32[]{:S(2)}, u32[]{:S(2)}) collective-permute-start(bf16[2560,512]{1,0:T(8,128)(2,1)S(1)} %get-tuple-element.173.refs_0_), channel_id=1, source_target_pairs={{0,1},{1,0},{2,3},{3,2},{4,5},{5,4},{6,7},{7,6},{8,9},{9,8},{10,11... | collective-permute-start | bytes 7864328 | tf_op jit(solution)/shard_map/ppermute | solution.py:26
  128.0 10.0 %collective-permute-start.29 = (bf16[2,128,512]{2,1,0:T(8,128)(2,1)S(1)}, bf16[2,128,512]{2,1,0:T(8,128)(2,1)S(1)}, u32[]{:S(2)}, u32[]{:S(2)}) collective-permute-start(bf16[2,128,512]{2,1,0:T(8,128)(2,1)S(1)} %get-tuple-element.187), channel_id=1, source_target_pairs={{0,8},{8,0},{16,24},{24,16},{1,9},{9,1},{17,25},{25,17},{2,10},{10... | collective-permute-start | bytes 786440 | tf_op jit(solution)/shard_map/ppermute | solution.py:26
  129.4 10.6 %collective-permute-start.30 = (bf16[2,128,512]{2,1,0:T(8,128)(2,1)S(1)}, bf16[2,128,512]{2,1,0:T(8,128)(2,1)S(1)}, u32[]{:S(2)}, u32[]{:S(2)}) collective-permute-start(bf16[2,128,512]{2,1,0:T(8,128)(2,1)S(1)} %get-tuple-element.188), channel_id=1, source_target_pairs={{0,16},{8,24},{16,0},{24,8},{1,17},{9,25},{17,1},{25,9},{2,18},{10... | collective-permute-start | bytes 786440 | tf_op jit(solution)/shard_map/ppermute | solution.py:26
  130.9 5.3 %collective-permute-start.25 = (bf16[1,128,512]{2,1,0:T(8,128)(2,1)S(1)}, bf16[1,128,512]{2,1,0:T(8,128)(2,1)S(1)}, u32[]{:S(2)}, u32[]{:S(2)}) collective-permute-start(bf16[1,128,512]{2,1,0:T(8,128)(2,1)S(1)} %get-tuple-element.182), channel_id=1, source_target_pairs={{0,2},{1,3},{2,0},{3,1},{4,6},{5,7},{6,4},{7,5},{8,10},{9,11},{10,... | collective-permute-start | bytes 393224 | tf_op jit(solution)/shard_map/ppermute | solution.py:36
  130.9 18.2 %collective-permute-start.31 = (bf16[2,128,512]{2,1,0:T(8,128)(2,1)S(1)}, bf16[2,128,512]{2,1,0:T(8,128)(2,1)S(1)}, u32[]{:S(2)}, u32[]{:S(2)}) collective-permute-start(bf16[2,128,512]{2,1,0:T(8,128)(2,1)S(1)} %get-tuple-element.189), channel_id=1, source_target_pairs={{0,24},{8,16},{16,8},{24,0},{1,25},{9,17},{17,9},{25,1},{2,26},{10... | collective-permute-start | bytes 786440 | tf_op jit(solution)/shard_map/ppermute | solution.py:26
  132.9 16.2 %collective-permute-start.24 = (bf16[128,512]{1,0:T(8,128)(2,1)S(1)}, bf16[128,512]{1,0:T(8,128)(2,1)S(1)}, u32[]{:S(2)}, u32[]{:S(2)}) collective-permute-start(bf16[128,512]{1,0:T(8,128)(2,1)S(1)} %get-tuple-element.181), channel_id=1, source_target_pairs={{0,4},{1,5},{2,6},{3,7},{4,0},{5,1},{6,2},{7,3},{8,12},{9,13},{10,... | collective-permute-start | bytes 393224 | tf_op jit(solution)/shard_map/ppermute | solution.py:26
  136.2 12.9 %collective-permute-start.26 = (bf16[1,128,512]{2,1,0:T(8,128)(2,1)S(1)}, bf16[1,128,512]{2,1,0:T(8,128)(2,1)S(1)}, u32[]{:S(2)}, u32[]{:S(2)}) collective-permute-start(bf16[1,128,512]{2,1,0:T(8,128)(2,1)S(1)} %get-tuple-element.183), channel_id=1, source_target_pairs={{0,10},{1,11},{2,8},{3,9},{4,14},{5,15},{6,12},{7,13},{8,2},{9,3},... | collective-permute-start | bytes 393224 | tf_op jit(solution)/shard_map/ppermute | solution.py:36
  138.0 11.1 %collective-permute-start.27 = (bf16[1,128,512]{2,1,0:T(8,128)(2,1)S(1)}, bf16[1,128,512]{2,1,0:T(8,128)(2,1)S(1)}, u32[]{:S(2)}, u32[]{:S(2)}) collective-permute-start(bf16[1,128,512]{2,1,0:T(8,128)(2,1)S(1)} %get-tuple-element.184), channel_id=1, source_target_pairs={{0,18},{1,19},{2,16},{3,17},{4,22},{5,23},{6,20},{7,21},{8,26},{9,... | collective-permute-start | bytes 393224 | tf_op jit(solution)/shard_map/ppermute | solution.py:36
  140.0 10.5 %collective-permute-start.28 = (bf16[1,128,512]{2,1,0:T(8,128)(2,1)S(1)}, bf16[1,128,512]{2,1,0:T(8,128)(2,1)S(1)}, u32[]{:S(2)}, u32[]{:S(2)}) collective-permute-start(bf16[1,128,512]{2,1,0:T(8,128)(2,1)S(1)} %get-tuple-element.185), channel_id=1, source_target_pairs={{0,26},{1,27},{2,24},{3,25},{4,30},{5,31},{6,28},{7,29},{8,18},{9,... | collective-permute-start | bytes 393224 | tf_op jit(solution)/shard_map/ppermute | solution.py:36
